TPU v7x, 32 devices: a whole 2x2x4 slice. The times are simulated.
32 devices in a mesh: genome: 8 (over y, x, core), offset: 4 (over z).
Axes of the slice: x: 2, y: 2, z: 4, core: 2. Of those that a mesh axis runs over, the one named last changes fastest.
Arguments:
- counts: int32 [512, 8, 128, 128], P('genome', 'offset'), may hold values from 1 to 512, as said below
- band_offset: int32 [8], P('offset'), may hold values from 0 to 7, as said below
- bin_mask: int32 [65536], P('genome'), may hold values 0 or 1
- row_factors: float32 [32, 65536], P(None, 'genome'), may hold values from 0.25 to 4
- col_factors: float32 [32, 65536], P(None, 'genome'), may hold values from 0.25 to 4
Outputs:
- bias: float32 [65536], P('genome')
- row_update: float32 [32, 65536], P(None, ('genome', 'offset'))
- col_update: float32 [32, 65536], P(None, ('genome', 'offset'))
Inputs may be any that keep to these rules, and one draw needn't show every extreme that they name: `counts`: only the upper triangle of a tile whose slot has band offset 0 is read. `band_offset`: A permutation of 0 to 7.
All inputs are finite; a program needn't handle non-finite values. No bound on the sum of `bin_mask` on one device may be relied on, other than what follows from the above.
Results may differ from a plain program's by a relative error of at most 0.00011.
Values sent between devices are 32-bit elements; how exact they have to be, the bound alone decides.
No kernel may reach another device: no remote copies, remote signals or barrier semaphores. Data moves between devices by JAX's collectives and lax.ppermute only.
A program may use at most 128 MiB of HBM per device.

v0:
```python
import jax
import jax.numpy as jnp
from jax import lax
from jax.sharding import PartitionSpec as P

ITERS = 3


def shifted(x, axis, by):
    length = lax.axis_size(axis)
    pairs = [(i, i + by) for i in range(length) if 0 <= i + by < length]
    return lax.ppermute(x, axis, pairs)


def mirror_tile(count_block, offset_value):
    edge_size = count_block.shape[-1]
    upper_half = lax.broadcasted_iota(jnp.int32, (edge_size, edge_size), 0) <= lax.broadcasted_iota(
        jnp.int32, (edge_size, edge_size), 1
    )
    mirrored = jnp.where(upper_half, count_block, jnp.swapaxes(count_block, -1, -2))
    return jnp.where(offset_value == 0, mirrored, count_block)


def tile_values(count_block, offset_value, bias_rows, bias_ext):
    bias_cols = lax.dynamic_slice_in_dim(bias_ext, offset_value, bias_rows.shape[0], 0)
    values = mirror_tile(count_block.astype(jnp.float32), offset_value)
    return values * bias_rows[:, :, None] * bias_cols[:, None, :]


def band_coverage(counts, band_offset, bias_rows, bias_ext):
    row_count = counts.shape[0]
    tile_size = counts.shape[2]
    spread = bias_ext.shape[0]
    row_part = jnp.zeros((row_count, tile_size), jnp.float32)
    col_part = jnp.zeros((spread, tile_size), jnp.float32)
    for slot_index in range(counts.shape[1]):
        offset_value = band_offset[slot_index]
        values = tile_values(counts[:, slot_index], offset_value, bias_rows, bias_ext)
        row_part = row_part + jnp.sum(values, axis=2)
        column_terms = jnp.where(offset_value > 0, jnp.sum(values, axis=1), jnp.float32(0.0))
        col_part = col_part + lax.dynamic_update_slice_in_dim(
            jnp.zeros((spread, tile_size), jnp.float32), column_terms, offset_value, 0
        )
    return (row_part, col_part)


def factor_terms(counts, band_offset, bias_rows, bias_ext, mask_rows, mask_ext, w_rows, h_ext):
    factor_count, row_count, tile_size = w_rows.shape
    spread = h_ext.shape[1]
    w_masked = jnp.sum(w_rows * mask_rows[None], axis=2)
    w_num = jnp.zeros((factor_count, row_count, tile_size), jnp.float32)
    h_norm = jnp.zeros((factor_count, row_count), jnp.float32)
    h_num = jnp.zeros((factor_count, spread, tile_size), jnp.float32)
    w_spread = jnp.zeros((factor_count, spread), jnp.float32)
    highest = lax.Precision.HIGHEST
    for slot_index in range(counts.shape[1]):
        offset_value = band_offset[slot_index]
        values = tile_values(counts[:, slot_index], offset_value, bias_rows, bias_ext)
        h_cols = lax.dynamic_slice_in_dim(h_ext, offset_value, row_count, 1)
        m_cols = lax.dynamic_slice_in_dim(mask_ext, offset_value, row_count, 0)
        model_tiles = jnp.einsum("kip,kiq->ipq", w_rows, h_cols, precision=highest)
        ratio_tiles = values / jnp.where(m_cols[:, None, :] > 0, model_tiles, jnp.float32(1.0))
        w_num = w_num + jnp.einsum("ipq,kiq->kip", ratio_tiles, h_cols, precision=highest)
        h_norm = h_norm + jnp.sum(h_cols * m_cols[None], axis=2)
        col_terms = jnp.einsum("kip,ipq->kiq", w_rows, ratio_tiles, precision=highest)
        h_num = h_num + lax.dynamic_update_slice_in_dim(
            jnp.zeros((factor_count, spread, tile_size), jnp.float32), col_terms, offset_value, 1
        )
        w_spread = w_spread + lax.dynamic_update_slice_in_dim(
            jnp.zeros((factor_count, spread), jnp.float32), w_masked, offset_value, 1
        )
    return (w_num, h_norm, h_num, w_spread)


def add_front(main_part, arrived, axis_index):
    span_width = arrived.shape[axis_index]
    front_part = lax.slice_in_dim(main_part, 0, span_width, axis=axis_index) + arrived
    rest_part = lax.slice_in_dim(
        main_part, span_width, main_part.shape[axis_index], axis=axis_index
    )
    return jnp.concatenate([front_part, rest_part], axis=axis_index)


def update_flat(factor, numer, denom, mask_vals):
    live_bins = mask_vals.reshape(1, -1) > 0
    return jnp.where(
        live_bins, factor * numer / jnp.where(live_bins, denom, jnp.float32(1.0)), factor
    )


def per_device(counts, band_offset, bin_mask, row_factors, col_factors):
    row_count = counts.shape[0]
    slot_count = counts.shape[1]
    tile_size = counts.shape[2]
    factor_count = row_factors.shape[0]
    band_count = slot_count * lax.axis_size("offset")
    reach_bins = (band_count - 1) * tile_size
    mask_flat = bin_mask.astype(jnp.float32)
    mask_rows = mask_flat.reshape(row_count, tile_size)
    live_flat = bin_mask > 0
    count_local = jnp.sum(mask_flat)
    bias = mask_flat
    mask_next = mask_flat[:reach_bins]
    for iteration in range(ITERS):
        bias_next = shifted(bias[:reach_bins], "genome", -1)
        if iteration == 0:
            mask_next = bias_next
        bias_ext = jnp.concatenate([bias, bias_next]).reshape(row_count + band_count - 1, tile_size)
        row_part, col_part = band_coverage(
            counts, band_offset, bias.reshape(row_count, tile_size), bias_ext
        )
        main_part = row_part + col_part[:row_count]
        tail_part = col_part[row_count:]
        main_part, tail_part = lax.psum((main_part, tail_part), "offset")
        arrived = shifted(tail_part, "genome", 1)
        coverage = add_front(main_part, arrived, 0)
        coverage = coverage.reshape(-1)
        safe_cover = jnp.where(live_flat, coverage, jnp.float32(1.0))
        cover_total, bins_live = lax.psum((jnp.sum(coverage), count_local), "genome")
        bias = jnp.where(live_flat, bias * (cover_total / bins_live) / safe_cover, jnp.float32(0.0))
    bias_next, col_next = shifted((bias[:reach_bins], col_factors[:, :reach_bins]), "genome", -1)
    bias_ext = jnp.concatenate([bias, bias_next]).reshape(row_count + band_count - 1, tile_size)
    mask_ext = jnp.concatenate([mask_flat, mask_next]).reshape(
        row_count + band_count - 1, tile_size
    )
    w_rows = row_factors.reshape(factor_count, row_count, tile_size)
    h_ext = jnp.concatenate([col_factors, col_next], axis=1).reshape(
        factor_count, row_count + band_count - 1, tile_size
    )
    w_num, h_norm, h_num, w_spread = factor_terms(
        counts,
        band_offset,
        bias.reshape(row_count, tile_size),
        bias_ext,
        mask_rows,
        mask_ext,
        w_rows,
        h_ext,
    )
    num_tail, spread_tail = shifted((h_num[:, row_count:], w_spread[:, row_count:]), "genome", 1)
    h_num = add_front(h_num[:, :row_count], num_tail, 1)
    w_spread = add_front(w_spread[:, :row_count], spread_tail, 1)
    share_bins = row_count * tile_size // lax.axis_size("offset")
    share_start = lax.axis_index("offset") * share_bins
    w_part, h_part = (
        lax.psum_scatter(
            w_num.reshape(factor_count, -1), "offset", scatter_dimension=1, tiled=True
        ),
        lax.psum_scatter(
            h_num.reshape(factor_count, -1), "offset", scatter_dimension=1, tiled=True
        ),
    )
    h_norm, w_spread = lax.psum((h_norm, w_spread), "offset")
    w_den = lax.dynamic_slice_in_dim(
        (h_norm[:, :, None] * mask_rows[None]).reshape(factor_count, -1), share_start, share_bins, 1
    )
    h_den = lax.dynamic_slice_in_dim(
        (w_spread[:, :, None] * mask_rows[None]).reshape(factor_count, -1),
        share_start,
        share_bins,
        1,
    )
    mask_share = lax.dynamic_slice_in_dim(mask_flat, share_start, share_bins, 0)
    row_share = lax.dynamic_slice_in_dim(row_factors, share_start, share_bins, 1)
    col_share = lax.dynamic_slice_in_dim(col_factors, share_start, share_bins, 1)
    row_update = update_flat(row_share, w_part, w_den, mask_share)
    col_update = update_flat(col_share, h_part, h_den, mask_share)
    return (bias, row_update, col_update)


def solution(mesh):
    return jax.shard_map(
        per_device,
        mesh=mesh,
        in_specs=(
            P("genome", "offset", None, None),
            P("offset"),
            P("genome"),
            P(None, "genome"),
            P(None, "genome"),
        ),
        out_specs=(P("genome"), P(None, ("genome", "offset")), P(None, ("genome", "offset"))),
        check_vma=False,
    )
```

profile of v0, /device:TPU:0, one launch (start us, length us, event | category | flops | bytes accessed | tf_op | source)
XLA Modules:
  0.0 312.3 jit_solution(10946181687632182796)
XLA Ops:
  7.2 0.8 convert_bitcast_fusion.1
  8.0 1.3 collective-permute-start
  9.3 0.9 slice.118
  10.2 1.3 collective-permute-start.6
  11.5 1.4 convert_reduce_fusion
  12.9 8.2 %fusion.1 = (f32[64,128,128]{2,1,0:T(8,128)}, s32[64,1,128,128]{3,2,1,0:T(8,128)}) fusion(s32[64,2,128,128]{3,2,1,0:T(8,128)} %param.5), kind=kLoop, calls=%fused_computation.4 | loop fusion | flops 1048576 | bytes 16777216 | tf_op jit(solution)/shard_map/convert_element_type | solution.py:26
  21.1 5.6 %copy.60 = s32[64,1,128,128]{2,3,0,1:T(8,128)} copy(s32[64,1,128,128]{3,2,1,0:T(8,128)} %get-tuple-element.48) | data formatting | bytes 8388608
  26.7 4.8 %convert_bitcast_fusion = f32[64,128,128]{1,2,0:T(8,128)} fusion(s32[64,1,128,128]{2,3,0,1:T(8,128)} %copy.60), kind=kLoop, calls=%fused_computation.13 | loop fusion | flops 1048576 | bytes 8388608 | tf_op jit(solution)/shard_map/convert_element_type | solution.py:26
  37.8 5.6 %copy.39 = f32[64,128,128]{2,1,0:T(8,128)} copy(f32[64,128,128]{1,2,0:T(8,128)} %convert_bitcast_fusion) | data formatting | bytes 8388608 | tf_op jit(solution)/shard_map/convert_element_type | solution.py:26
  43.4 5.6 %copy.41 = f32[64,128,128]{1,2,0:T(8,128)} copy(f32[64,128,128]{2,1,0:T(8,128)} %get-tuple-element.47) | data formatting | bytes 8388608 | tf_op jit(solution)/shard_map/convert_element_type | solution.py:26
  50.3 0.6 broadcast_compare_fusion.1
  51.0 11.3 %fusion.5 = (f32[64,128]{1,0:T(8,128)S(1)}, f32[64,128]{1,0:T(8,128)S(1)}, f32[64,128]{1,0:T(8,128)S(1)}, f32[64,128]{1,0:T(8,128)S(1)}, f32[64,128,128]{1,2,0:T(8,128)}, /*index=5*/f32[64,128,128]{1,2,0:T(8,128)}) fusion(f32[64,128]{1,0:T(8,128)S(1)} %get-tuple-element.58, f32[64,128]{1,0:T(8,128)S(1)} %get-tuple-element.65, ...), kind=kLoop, calls=%fused_computation.17 | loop fusion | flops 14647296 | bytes 25411586 | tf_op jit(solution)/shard_map/reduce_sum | solution.py:39
  62.9 21.1 %all-reduce.3 = (f32[64,128]{1,0:T(8,128)S(1)}, f32[7,128]{1,0:T(8,128)S(1)}) all-reduce(f32[64,128]{1,0:T(8,128)S(1)} %slice_add_fusion.3, f32[7,128]{1,0:T(8,128)S(1)} %slice.129), channel_id=1, replica_groups=mesh['genome'=8,'offset'=4] {'offset'}, use_global_device_ids=true, to_apply=%region_4.5 | all-reduce | flops 9088 | bytes 72704 | tf_op jit(solution)/shard_map/psum | solution.py:114
  84.0 1.3 collective-permute-start.1
  88.4 17.3 %all-reduce = (f32[]{:T(128)}, f32[]{:T(128)}) all-reduce(f32[]{:T(128)S(6)} %reduce_sum.201, f32[]{:T(128)} %convert_reduce_fusion), channel_id=1, replica_groups=mesh['genome'=8,'offset'=4] {'genome'}, use_global_device_ids=true, to_apply=%region_8.9 | all-reduce | flops 2 | bytes 16 | tf_op jit(solution)/shard_map/psum | solution.py:119
  106.9 1.3 collective-permute-start.2
  108.7 3.0 collective-permute-start.9
  111.8 6.9 %fusion.9 = (f32[64,128]{1,0:T(8,128)S(1)}, f32[64,128]{1,0:T(8,128)S(1)}, f32[64,128]{1,0:T(8,128)S(1)}, f32[64,128]{1,0:T(8,128)S(1)}) fusion(f32[64,128,128]{1,2,0:T(8,128)} %get-tuple-element.46, f32[64,128]{1,0:T(8,128)S(1)} %get-tuple-element.56, f32[64,128]{1,0:T(8,128)S(1)} %bitcast.137, f32[64,128]{1,0:T(8,128)S(1)} %get-tuple-element.55, ...), kind=kLoop, calls=%fused_computation.21 | loop fusion | flops 8355840 | bytes 8617984 | tf_op jit(solution)/shard_map/reduce_sum | solution.py:39
  119.3 16.2 %all-reduce.2 = (f32[64,128]{1,0:T(8,128)S(1)}, f32[7,128]{1,0:T(8,128)S(1)}) all-reduce(f32[64,128]{1,0:T(8,128)S(1)} %slice_add_fusion.2, f32[7,128]{1,0:T(8,128)S(1)} %slice.134), channel_id=1, replica_groups=mesh['genome'=8,'offset'=4] {'offset'}, use_global_device_ids=true, to_apply=%region_15.16 | all-reduce | flops 9088 | bytes 72704 | tf_op jit(solution)/shard_map/psum | solution.py:114
  135.5 1.3 collective-permute-start.3
  139.5 16.4 %psum.96 = f32[]{:T(128)} all-reduce(f32[]{:T(128)S(6)} %reduce_sum.209), channel_id=1, replica_groups=mesh['genome'=8,'offset'=4] {'genome'}, use_global_device_ids=true, to_apply=%region_19.20 | all-reduce | flops 1 | bytes 8 | tf_op jit(solution)/shard_map/psum | solution.py:119
  157.2 1.3 collective-permute-start.4
  158.5 0.7 pad_maximum_fusion.1
  159.1 1.1 collective-permute-done.4
  160.3 6.9 %fusion.13 = (f32[64,128]{1,0:T(8,128)S(1)}, f32[64,128]{1,0:T(8,128)S(1)}, f32[64,128]{1,0:T(8,128)S(1)}, f32[64,128]{1,0:T(8,128)S(1)}) fusion(f32[64,128,128]{1,2,0:T(8,128)} %get-tuple-element.46, f32[64,128]{1,0:T(8,128)S(1)} %get-tuple-element.54, f32[64,128]{1,0:T(8,128)S(1)} %bitcast.136, f32[64,128]{1,0:T(8,128)S(1)} %get-tuple-element.53, ...), kind=kLoop, calls=%fused_computation.25 | loop fusion | flops 8355840 | bytes 8617984 | tf_op jit(solution)/shard_map/reduce_sum | solution.py:39
  168.0 1.2 reshape.81
  169.1 1.9 constant_dynamic-slice_fusion.1
  171.1 1.5 multiply_reduce_fusion.1
  172.6 19.3 %all-reduce.1 = (f32[64,128]{1,0:T(8,128)S(1)}, f32[7,128]{1,0:T(8,128)S(1)}, f32[32,64]{0,1:T(8,128)S(1)}, f32[32,64]{1,0:T(8,128)S(1)}) all-reduce(f32[64,128]{1,0:T(8,128)S(1)} %slice_add_fusion.1, f32[7,128]{1,0:T(8,128)S(1)} %slice.139, f32[32,64]{0,1:T(8,128)S(1)} %add.142, ...), channel_id=1, replica_groups=mesh['genome'=8,'offset'=4] {'offset'}, use_global_device_ids=true, to_apply=%region_24.25 | all-reduce | flops 13184 | bytes 105472 | tf_op jit(solution)/shard_map/psum | solution.py:114
  191.8 1.3 collective-permute-start.5
  195.8 16.3 %psum.99 = f32[]{:T(128)} all-reduce(f32[]{:T(128)S(6)} %reduce_sum.216), channel_id=1, replica_groups=mesh['genome'=8,'offset'=4] {'genome'}, use_global_device_ids=true, to_apply=%region_28.29 | all-reduce | flops 1 | bytes 8 | tf_op jit(solution)/shard_map/psum | solution.py:119
  213.5 1.3 collective-permute-start.7
  214.8 1.8 collective-permute-done.7
  216.6 10.9 %bitcast_divide_fusion.1 = f32[64,128,128]{1,2,0:T(8,128)S(1)} fusion(f32[64,128,128]{1,2,0:T(8,128)} %get-tuple-element.45, f32[64,128]{1,0:T(8,128)S(1)} %get-tuple-element.52, f32[64,128]{1,0:T(8,128)S(1)} %bitcast.138, pred[64,128]{1,0:T(8,128)(4,1)S(1)} %copy-done.10, f32[32,64,128]{2,1,0:T(8,128)S(1)} %get-tuple-element.50, f32[32,8192]{1,0:T(8,128)S(1)} %copy-done.4), kind=kOutput, calls=%fused_computation.6 | convolution fusion | flops 406847488 | bytes 10559488 | tf_op jit(solution)/shard_map/kip,kiq->ipq/dot_general | solution.py:61
  227.4 4.2 %fusion.30 = f32[64,32,128]{2,1,0:T(8,128)S(1)} fusion(f32[64,128,128]{1,2,0:T(8,128)S(1)} %bitcast_divide_fusion.1, f32[32,64,128]{2,1,0:T(8,128)S(1)} %get-tuple-element.50), kind=kOutput, calls=%fused_computation.50 | convolution fusion | flops 402653184 | bytes 6291456 | tf_op jit(solution)/shard_map/ipq,kiq->kip/dot_general | solution.py:63
  231.7 11.0 %bitcast_divide_fusion = f32[64,128,128]{1,2,0:T(8,128)S(1)} fusion(f32[64,128,128]{1,2,0:T(8,128)S(1)} %copy-done, f32[64,128]{1,0:T(8,128)S(1)} %get-tuple-element.51, f32[64,128]{1,0:T(8,128)S(1)} %bitcast.139, pred[64,128]{1,0:T(8,128)(4,1)S(1)} %copy-done.9, f32[32,64,128]{2,1,0:T(8,128)S(1)} %get-tuple-element.49, f32[32,8192]{1,0:T(8,128)S(1)} %copy-done.4), kind=kOutput, calls=%fused_computation.5 | convolution fusion | flops 406847488 | bytes 10559488 | tf_op jit(solution)/shard_map/kip,kiq->ipq/dot_general | solution.py:61
  242.7 4.2 %fusion.17 = f32[64,4,8,128]{3,2,1,0:T(8,128)S(1)} fusion(f32[64,32,128]{2,1,0:T(8,128)S(1)} %fusion.30, f32[64,128,128]{1,2,0:T(8,128)S(1)} %bitcast_divide_fusion, f32[32,64,128]{2,1,0:T(8,128)S(1)} %get-tuple-element.49), kind=kOutput, calls=%fused_computation.32 | convolution fusion | flops 402915328 | bytes 7340032 | tf_op jit(solution)/shard_map/ipq,kiq->kip/dot_general | solution.py:63
  246.9 1.1 copy.102
  248.5 8.5 %fusion.16 = f32[32,71,128]{2,0,1:T(8,128)S(1)} fusion(f32[32,71,128]{2,0,1:T(8,128)S(1)} %broadcast.44, s32[]{:T(128)S(6)} %select_n.151, f32[64,128,128]{1,2,0:T(8,128)} %copy-done.1, f32[32,8192]{1,0:T(8,128)S(1)} %copy-done.4), kind=kOutput, calls=%fused_computation.30 | convolution fusion | flops 402653184 | bytes 6291460 | tf_op jit(solution)/shard_map/kip,ipq->kiq/dot_general | solution.py:65
  257.0 6.6 %fusion.15 = f32[32,71,128]{2,0,1:T(8,128)S(1)} fusion(f32[32,71,128]{2,0,1:T(8,128)S(1)} %fusion.16, s32[]{:T(128)S(6)} %select_n.155, f32[64,128,128]{1,2,0:T(8,128)S(1)} %copy-done.3, f32[32,8192]{1,0:T(8,128)S(1)} %copy-done.4), kind=kOutput, calls=%fused_computation.28 | convolution fusion | flops 402915328 | bytes 7340036 | tf_op jit(solution)/shard_map/kip,ipq->kiq/dot_general | solution.py:65
  263.6 3.4 %collective-permute-start.8 = (f32[32,7,128]{2,0,1:T(8,128)S(1)}, f32[32,7,128]{2,0,1:T(8,128)S(1)}, u32[]{:S(2)}, u32[]{:S(2)}) collective-permute-start(f32[32,7,128]{2,0,1:T(8,128)S(1)} %slice.143), channel_id=1, source_target_pairs={{0,4},{4,8},{8,12},{12,16},{16,20},{20,24},{24,28},{1,5},{5,9},{9,... | collective-permute-start | bytes 344072 | tf_op jit(solution)/shard_map/ppermute | solution.py:12
  267.1 0.9 collective-permute-done.8
  268.0 1.1 copy_bitcast_fusion.2
  269.5 0.6 copy.101
  270.4 0.6 copy.100
  271.0 4.2 %reduce-scatter.3.cloned.1.call-done = f32[32,2048]{1,0:T(8,128)} async-done(((f32[32,8192]{1,0:T(8,128)}), f32[32,2048]{1,0:T(8,128)}) %reduce-scatter.3.cloned.1.call-update) | async-done | bytes 262160 | tf_op jit(solution)/shard_map/reduce_scatter | solution.py:146
  275.2 28.2 %reduce-scatter.5.cloned.1.call-done = f32[32,2048]{1,0:T(8,128)} async-done(((f32[32,8192]{1,0:T(8,128)}), f32[32,2048]{1,0:T(8,128)}) %reduce-scatter.5.cloned.1.call-update) | async-done | bytes 262160 | tf_op jit(solution)/shard_map/reduce_scatter | solution.py:149
  303.4 2.0 fusion.39
  (97 shorter events, 9.5 us)
Async XLA Ops:
  7.2 268.1 %reduce-scatter.3.cloned.1.call-start = ((), (), s32[]{:S(2)}) async-start(), calls=%async_computation.2 | async-start | bytes 1310720 | tf_op jit(solution)/shard_map/reduce_scatter | solution.py:146
  8.0 42.3 %collective-permute-start = (f32[896]{0:T(1024)S(1)}, f32[896]{0:T(1024)S(1)}, u32[]{:S(2)}, u32[]{:S(2)}) collective-permute-start(f32[896]{0:T(1024)S(1)} %slice.126), channel_id=1, source_target_pairs={{4,0},{8,4},{12,8},{16,12},{20,16},{24,20},{28,24},{5,1},{9,5},{13... | collective-permute-start | bytes 10760 | tf_op jit(solution)/shard_map/ppermute | solution.py:12
  10.2 157.7 %collective-permute-start.6 = (f32[32,896]{1,0:T(8,128)S(1)}, f32[32,896]{1,0:T(8,128)S(1)}, u32[]{:S(2)}, u32[]{:S(2)}) collective-permute-start(f32[32,896]{1,0:T(8,128)S(1)} %slice.118), channel_id=1, source_target_pairs={{4,0},{8,4},{12,8},{16,12},{20,16},{24,20},{28,24},{5,1},{9,5},{13... | collective-permute-start | bytes 344072 | tf_op jit(solution)/shard_map/ppermute | solution.py:12
  26.6 4.8 %copy-start.4 = (f32[32,8192]{1,0:T(8,128)S(1)}, f32[32,8192]{1,0:T(8,128)}, u32[]{:S(2)}) copy-start(f32[32,8192]{1,0:T(8,128)} %param.8) | copy-start | bytes 3145732
  26.7 5.3 %copy-start.11 = (s32[2]{0:T(128)S(1)}, s32[2]{0:T(128)}, u32[]{:S(2)}) copy-start(s32[2]{0:T(128)} %param.6) | copy-start | bytes 28
  51.0 55.9 %copy-start.6 = (s32[8192]{0:T(1024)S(1)}, s32[8192]{0:T(1024)}, u32[]{:S(2)}) copy-start(s32[8192]{0:T(1024)} %param.7) | copy-start | bytes 98308
  84.0 2.1 collective-permute-start.1
  106.9 4.9 %collective-permute-start.2 = (f32[896]{0:T(1024)S(1)}, f32[896]{0:T(1024)S(1)}, u32[]{:S(2)}, u32[]{:S(2)}) collective-permute-start(f32[896]{0:T(1024)S(1)} %slice.131), channel_id=1, source_target_pairs={{4,0},{8,4},{12,8},{16,12},{20,16},{24,20},{28,24},{5,1},{9,5},{13... | collective-permute-start | bytes 10760 | tf_op jit(solution)/shard_map/ppermute | solution.py:12
  108.7 30.8 %collective-permute-start.9 = (f32[32,7]{1,0:T(8,128)S(1)}, f32[32,7]{1,0:T(8,128)S(1)}, u32[]{:S(2)}, u32[]{:S(2)}) collective-permute-start(f32[32,7]{1,0:T(8,128)S(1)} %slice.146), channel_id=1, source_target_pairs={{0,4},{4,8},{8,12},{12,16},{16,20},{20,24},{24,28},{1,5},{5,9},{9,... | collective-permute-start | bytes 2696 | tf_op jit(solution)/shard_map/ppermute | solution.py:12
  135.5 2.1 collective-permute-start.3
  157.2 3.1 collective-permute-start.4
  160.2 7.6 %copy-start.5 = (f32[32,8192]{1,0:T(8,128)S(1)}, f32[32,8192]{1,0:T(8,128)}, u32[]{:S(2)}) copy-start(f32[32,8192]{1,0:T(8,128)} %param.9) | copy-start | bytes 3145732
  167.9 4.6 %copy-start.8 = (f32[32,64]{1,0:T(8,128)S(1)}, f32[32,64]{1,0:T(8,128)}, u32[]{:S(2)}) copy-start(f32[32,64]{1,0:T(8,128)} %pad_maximum_fusion.1) | copy-start | bytes 24580
  167.9 48.6 %copy-start.10 = (pred[64,128]{1,0:T(8,128)(4,1)S(1)}, pred[64,128]{1,0:T(8,128)(4,1)}, u32[]{:S(2)}) copy-start(pred[64,128]{1,0:T(8,128)(4,1)} %get-tuple-element.35) | copy-start | bytes 24580
  191.8 2.1 collective-permute-start.5
  213.4 18.2 %copy-start.7 = (f32[8192]{0:T(1024)}, f32[8192]{0:T(1024)S(1)}, u32[]{:S(2)}) copy-start(f32[8192]{0:T(1024)S(1)} %fusion.51) | copy-start | bytes 98308
  213.5 3.1 collective-permute-start.7
  227.4 15.3 %copy-start.1 = (f32[64,128,128]{1,2,0:T(8,128)}, f32[64,128,128]{1,2,0:T(8,128)S(1)}, u32[]{:S(2)}) copy-start(f32[64,128,128]{1,2,0:T(8,128)S(1)} %bitcast_divide_fusion.1) | copy-start | bytes 12582916
  227.4 4.2 %copy-start = (f32[64,128,128]{1,2,0:T(8,128)S(1)}, f32[64,128,128]{1,2,0:T(8,128)}, u32[]{:S(2)}) copy-start(f32[64,128,128]{1,2,0:T(8,128)} %get-tuple-element.46) | copy-start | bytes 12582916
  227.4 4.2 %copy-start.9 = (pred[64,128]{1,0:T(8,128)(4,1)S(1)}, pred[64,128]{1,0:T(8,128)(4,1)}, u32[]{:S(2)}) copy-start(pred[64,128]{1,0:T(8,128)(4,1)} %get-tuple-element.57) | copy-start | bytes 24580
  242.7 5.4 %copy-start.2 = (f32[64,128,128]{1,2,0:T(8,128)}, f32[64,128,128]{1,2,0:T(8,128)S(1)}, u32[]{:S(2)}) copy-start(f32[64,128,128]{1,2,0:T(8,128)S(1)} %bitcast_divide_fusion) | copy-start | bytes 12582916
  248.1 55.4 %reduce-scatter.5.cloned.1.call-start = ((), (), s32[]{:S(2)}) async-start(), calls=%async_computation.3 | async-start | bytes 1310720 | tf_op jit(solution)/shard_map/reduce_scatter | solution.py:149
  248.4 8.6 %copy-start.3 = (f32[64,128,128]{1,2,0:T(8,128)S(1)}, f32[64,128,128]{1,2,0:T(8,128)}, u32[]{:S(2)}) copy-start(f32[64,128,128]{1,2,0:T(8,128)} %copy-done.2) | copy-start | bytes 12582916
  263.6 4.3 %collective-permute-start.8 = (f32[32,7,128]{2,0,1:T(8,128)S(1)}, f32[32,7,128]{2,0,1:T(8,128)S(1)}, u32[]{:S(2)}, u32[]{:S(2)}) collective-permute-start(f32[32,7,128]{2,0,1:T(8,128)S(1)} %slice.143), channel_id=1, source_target_pairs={{0,4},{4,8},{8,12},{12,16},{16,20},{20,24},{24,28},{1,5},{5,9},{9,... | collective-permute-start | bytes 344072 | tf_op jit(solution)/shard_map/ppermute | solution.py:12
Sparse Core Ops, SparseCore 0:
  248.2 26.9 reduce-scatter.2
  277.6 25.7 reduce-scatter.4
where the time goes:
time: 313 us; the launch traced here: 312 us
  blocking collectives  107 us (34%)
  other arithmetic  50.5 us (16%)
  matrix products  45.3 us (14%)
  waiting for transfers between devices  36.7 us (12%)
  between operations  28.8 us (9%)
  local copies, waits for them, and re-layouts  27.4 us (9%)
  starting transfers between devices  17 us (5%)
    psum x3, blocking collectives, per_device(): main_part, tail_part = lax.psum((main_part, tail_part), 'offset')  56.5 us
    psum x3, blocking collectives, per_device(): lax.psum((jnp.sum(coverage), count_local), 'genome')  50 us
    reduce_scatter x1, waiting for transfers between devices, per_device(): lax.psum_scatter(h_num.reshape(factor_count, -1), 'offset', scatter_dimen...  28.2 us
    reduce_sum x3, other arithmetic, band_coverage(): row_part = row_part + jnp.sum(values, axis=2)  25.1 us
    dot_general x2, matrix products, factor_terms(): model_tiles = jnp.einsum('kip,kiq->ipq', w_rows, h_cols, precision=highest)  21.9 us
    ppermute x10, starting transfers between devices, shifted(): return lax.ppermute(x, axis, pairs)  16.7 us
    dot_general x2, matrix products, factor_terms(): jnp.einsum('kip,ipq->kiq', w_rows, ratio_tiles, precision=highest)  15.1 us
    convert_element_type x2, other arithmetic, tile_values(): values = mirror_tile(count_block.astype(jnp.float32), offset_value)  13 us
  transfers between devices with their start and end apart: 12, of which 8 were waited for; matrix products, arithmetic and copies ran while one was open for 27% of the time, Pallas kernels for 0%

commit v1 on v0

v1 whole, which is shorter than its diff:
```python
import functools

import jax
import jax.numpy as jnp
from jax import lax
from jax.experimental import pallas as pl
from jax.experimental.pallas import tpu as pltpu
from jax.sharding import PartitionSpec as P

ITERS = 3
STEP = 8
F32 = jnp.float32
BF16 = jnp.bfloat16
VMEM_LIMIT = 48 * 1024 * 1024


def split(x):
    hi = x.astype(BF16)
    lo = (x - hi.astype(F32)).astype(BF16)
    return hi, lo


def tree_sum(parts):
    while len(parts) > 1:
        parts = [a + b for a, b in zip(parts[::2], parts[1::2])]
    return parts[0]


def params():
    return pltpu.CompilerParams(vmem_limit_bytes=VMEM_LIMIT)


def whole(shape):
    return pl.BlockSpec(shape, lambda *_: (0,) * len(shape))


def scale_from(mask, parts):
    cover = tree_sum([p[...] for p in parts])
    live = mask[...] > 0
    return jnp.where(live, 1.0 / jnp.where(live, cover, 1.0), 0.0)


def cover_kernel(first, rows, offs, counts, mask, *refs):
    if first:
        parts, (v_out, edge_out, u_out, acc, weight) = (), refs
    else:
        parts, (v_out, edge_out, u_out, acc, weight) = refs[:-5], refs[-5:]
    step = pl.program_id(0)
    slots = counts.shape[1]
    tile = counts.shape[2]

    @pl.when(step == 0)
    def _():
        u_out[...] = mask[...] if first else scale_from(mask, parts)
        acc[...] = jnp.zeros_like(acc)
        r = lax.broadcasted_iota(jnp.int32, (tile, tile), 0)
        c = lax.broadcasted_iota(jnp.int32, (tile, tile), 1)
        half = jnp.where(r < c, 1.0, jnp.where(r == c, 0.5, 0.0))
        for s in range(slots):
            weight[s] = jnp.where(offs[s] == 0, half, 1.0)

    base = step * STEP
    u_cols = u_out[pl.ds(pl.multiple_of(base, STEP), STEP), :].T

    def tiles(weighted):
        sums = []
        for t in range(STEP):
            u_row = u_cols[:, t : t + 1]
            total = None
            for s in range(slots):
                c = counts[t, s].astype(F32)
                if weighted:
                    c = c * weight[s]
                j = base + t + offs[s]
                term = c * u_out[pl.ds(j, 1), :]
                total = term if total is None else total + term
                acc[pl.ds(j, 1), :] += jnp.sum(c * u_row, axis=0, keepdims=True)
            sums.append(jnp.sum(total, axis=1, keepdims=True))
        acc[pl.ds(pl.multiple_of(base, STEP), STEP), :] += jnp.concatenate(sums, axis=1).T

    on_diagonal = functools.reduce(jnp.logical_or, [offs[s] == 0 for s in range(slots)])

    @pl.when(on_diagonal)
    def _():
        tiles(True)

    @pl.when(jnp.logical_not(on_diagonal))
    def _():
        tiles(False)

    @pl.when(step == pl.num_programs(0) - 1)
    def _():
        pad = acc.shape[0] - rows
        v_out[...] = acc[...]
        edge_out[:pad] = acc[:pad]
        edge_out[pad:] = acc[rows:]


def cover_call(offs, counts, mask_ext, parts):
    rows, slots, tile = counts.shape[:3]
    ext = mask_ext.shape[0]
    flat = jax.ShapeDtypeStruct((ext, tile), F32)
    edge = jax.ShapeDtypeStruct((2 * (ext - rows), tile), F32)
    return pl.pallas_call(
        functools.partial(cover_kernel, not parts, rows),
        grid_spec=pltpu.PrefetchScalarGridSpec(
            num_scalar_prefetch=1,
            grid=(rows // STEP,),
            in_specs=[pl.BlockSpec((STEP, slots, tile, tile), lambda i, *_: (i, 0, 0, 0))]
            + [whole((ext, tile))] * (1 + len(parts)),
            out_specs=[whole((ext, tile)), whole(edge.shape), whole((ext, tile))],
            scratch_shapes=[pltpu.VMEM((ext, tile), F32), pltpu.VMEM((slots, tile, tile), F32)],
        ),
        out_shape=[flat, edge, flat],
        compiler_params=params(),
        name="cover",
    )(offs, counts, mask_ext, *parts)


def ratio_kernel(offs, counts, w_ref, h_ref, hi_out, lo_out):
    step = pl.program_id(0)
    slots, tile = counts.shape[1:3]
    base = step * STEP
    r = lax.broadcasted_iota(jnp.int32, (tile, tile), 0)
    c = lax.broadcasted_iota(jnp.int32, (tile, tile), 1)

    def body(t, carry):
        w_hi, w_lo = split(w_ref[:, pl.ds(pl.multiple_of(t * tile, tile), tile)])
        w4 = jnp.concatenate([w_hi, w_hi, w_lo, w_lo], axis=0).astype(F32).T.astype(BF16)
        for s in range(slots):
            j = base + t + offs[s]
            h_hi, h_lo = split(h_ref[:, pl.ds(pl.multiple_of(j * tile, tile), tile)])
            h4 = jnp.concatenate([h_hi, h_lo, h_hi, h_lo], axis=0)
            model = jnp.dot(w4, h4, preferred_element_type=F32)
            inverse = 1.0 / model
            values = counts[t, s].astype(F32)

            def put(x):
                hi, lo = split(x)
                hi_out[t, :, s * tile : (s + 1) * tile] = hi
                lo_out[t, :, s * tile : (s + 1) * tile] = lo

            @pl.when(offs[s] == 0)
            def _():
                put(jnp.where(r <= c, values, values.T) * inverse)

            @pl.when(offs[s] != 0)
            def _():
                put(values * inverse)

        return carry

    lax.fori_loop(0, STEP, body, 0, unroll=2)


def ratio_call(offs, counts, row_factors, col_ext):
    rows, slots, tile = counts.shape[:3]
    factors = row_factors.shape[0]
    out = jax.ShapeDtypeStruct((rows, tile, slots * tile), BF16)
    block = pl.BlockSpec((STEP, tile, slots * tile), lambda i, *_: (i, 0, 0))
    return pl.pallas_call(
        ratio_kernel,
        grid_spec=pltpu.PrefetchScalarGridSpec(
            num_scalar_prefetch=1,
            grid=(rows // STEP,),
            in_specs=[
                pl.BlockSpec((STEP, slots, tile, tile), lambda i, *_: (i, 0, 0, 0)),
                pl.BlockSpec((factors, STEP * tile), lambda i, *_: (0, i)),
                whole(col_ext.shape),
            ],
            out_specs=[block, block],
        ),
        out_shape=[out, out],
        compiler_params=params(),
        name="ratio",
    )(offs, counts, row_factors, col_ext)


NT = (((1,), (1,)), ((), ()))


def numer_kernel(shares, rows, scal, hi_ref, lo_ref, w_ref, h_ref, mask, *refs):
    offset_count = shares
    parts = refs[:offset_count]
    outs = refs[offset_count:]
    u_out = outs[0]
    w_outs = outs[1 : 1 + shares]
    h_outs = outs[1 + shares : 1 + 2 * shares]
    tail_out = outs[1 + 2 * shares]
    g_all, h_acc = outs[2 + 2 * shares :]
    step = pl.program_id(0)
    me = scal[0]
    share = jnp.bitwise_xor(step, me)
    per = rows // shares
    ext = mask.shape[0]
    tile = mask.shape[1]
    factors = w_ref.shape[0]
    slots = hi_ref.shape[2] // tile
    offs = [scal[1 + s] for s in range(slots)]

    @pl.when(step == 0)
    def _():
        u_out[...] = scale_from(mask, parts)
        h_acc[...] = jnp.zeros_like(h_acc)

        def fill(j, carry):
            x = h_ref[:, pl.ds(pl.multiple_of(j * tile, tile), tile)] * u_out[pl.ds(j, 1), :]
            hi, lo = split(x)
            g_all[j, :factors] = hi
            g_all[j, factors:] = lo
            return carry

        lax.fori_loop(0, ext, fill, 0, unroll=4)

    base = share * per

    def make(t, w_out):
        i = base + t
        u_row = u_out[pl.ds(i, 1), :]
        r_hi = hi_ref[t]
        r_lo = lo_ref[t]
        g = jnp.concatenate([g_all[i + offs[s]] for s in range(slots)], axis=1)
        big = lax.dot_general(g, r_hi, NT, preferred_element_type=F32)
        small = lax.dot_general(g[:factors], r_lo, NT, preferred_element_type=F32)
        w_out[t] = (big[:factors] + big[factors:] + small) * u_row
        a_hi, a_lo = split(w_ref[:, pl.ds(pl.multiple_of(t * tile, tile), tile)] * u_row)
        big = jnp.dot(jnp.concatenate([a_hi, a_lo], axis=0), r_hi, preferred_element_type=F32)
        small = jnp.dot(a_hi, r_lo, preferred_element_type=F32)
        cols = big[:factors] + big[factors:] + small
        for s in range(slots):
            h_acc[i + offs[s]] += cols[:, s * tile : (s + 1) * tile]

    for k in range(shares):

        @pl.when(step == k)
        def _():
            def body(t, carry):
                make(t, w_outs[k])
                return carry

            lax.fori_loop(0, per, body, 0, unroll=4)

    @pl.when(step == shares - 1)
    def _():
        for k in range(shares):
            first = jnp.bitwise_xor(me, k) * per
            for t in range(per):
                h_outs[k][t] = h_acc[first + t] * u_out[pl.ds(first + t, 1), :]
        for t in range(ext - rows):
            tail_out[t] = h_acc[rows + t] * u_out[pl.ds(rows + t, 1), :]


def numer_call(scal, r_hi, r_lo, row_factors, col_ext, mask_ext, parts):
    shares = len(parts)
    rows, tile, wide = r_hi.shape
    factors = row_factors.shape[0]
    ext = mask_ext.shape[0]
    per = rows // shares
    block = pl.BlockSpec((per, tile, wide), lambda i, scal: (jnp.bitwise_xor(i, scal[0]), 0, 0))
    piece = jax.ShapeDtypeStruct((per, factors, tile), F32)
    tail = jax.ShapeDtypeStruct((ext - rows, factors, tile), F32)
    flat = jax.ShapeDtypeStruct((ext, tile), F32)
    outs = [flat] + [piece] * (2 * shares) + [tail]
    res = pl.pallas_call(
        functools.partial(numer_kernel, shares, rows),
        grid_spec=pltpu.PrefetchScalarGridSpec(
            num_scalar_prefetch=1,
            grid=(shares,),
            in_specs=[
                block,
                block,
                pl.BlockSpec((factors, per * tile), lambda i, scal: (0, jnp.bitwise_xor(i, scal[0]))),
                whole(col_ext.shape),
                whole(mask_ext.shape),
            ]
            + [whole((ext, tile))] * shares,
            out_specs=[whole(x.shape) for x in outs],
            scratch_shapes=[
                pltpu.VMEM((ext, 2 * factors, tile), BF16),
                pltpu.VMEM((ext, factors, tile), F32),
            ],
        ),
        out_shape=outs,
        compiler_params=params(),
        name="numer",
    )(scal, r_hi, r_lo, row_factors, col_ext, mask_ext, *parts)
    return res[0], res[1 : 1 + shares], res[1 + shares : 1 + 2 * shares], res[-1]


def xor_exchange(x, axis, k):
    return lax.ppermute(x, axis, [(i, i ^ k) for i in range(lax.axis_size(axis))])


def both_sides(x):
    size = lax.axis_size("genome")
    me = lax.axis_index("genome")
    a = lax.ppermute(x, "genome", [(i, i ^ 1) for i in range(size)])
    b = lax.ppermute(x, "genome", [(i, (((i + 1) ^ 1) - 1) % size) for i in range(size)])
    even = me % 2 == 0
    return jnp.where(even, a, b), jnp.where(even, b, a)


def scatter_sum(pieces):
    size = lax.axis_size("offset")
    if size == 4:
        first = xor_exchange(pieces[2], "offset", 1)
        mine = xor_exchange(pieces[1], "offset", 1)
        far = xor_exchange(pieces[3] + first, "offset", 3)
        return (pieces[0] + mine) + far
    return tree_sum([pieces[0]] + [xor_exchange(pieces[k], "offset", k) for k in range(1, size)])


def per_device(counts, band_offset, bin_mask, row_factors, col_factors):
    rows, slots, tile = counts.shape[:3]
    factors = row_factors.shape[0]
    offset_count = lax.axis_size("offset")
    genome_count = lax.axis_size("genome")
    g = lax.axis_index("genome")
    o = lax.axis_index("offset")
    reach = slots * offset_count - 1
    pad = reach + 1
    offs = band_offset.astype(jnp.int32)
    scal = jnp.concatenate([o.astype(jnp.int32).reshape(1), offs])
    has_next = g < genome_count - 1
    has_prev = g > 0

    mask = bin_mask.astype(F32).reshape(rows, tile)
    mask_next, _ = both_sides(mask[:pad])
    keep = has_next & (lax.broadcasted_iota(jnp.int32, (pad, 1), 0) < reach)
    mask_ext = jnp.concatenate([mask, jnp.where(keep, mask_next, 0.0)])

    ring_left = [(i, (i - 1) % genome_count) for i in range(genome_count)]
    col_next = lax.ppermute(col_factors[:, : pad * tile], "genome", ring_left)
    col_next = jnp.where(has_next, col_next, 1.0)
    col_ext = jnp.concatenate([col_factors, col_next], axis=1)

    scales = []
    parts = []
    for _ in range(ITERS):
        v, edge, u = cover_call(offs, counts, mask_ext, parts)
        scales.append(u[:rows])
        after, before = both_sides(edge)
        front = v[:pad] + jnp.where(has_prev, before[pad:], 0.0)
        back = v[rows:] + jnp.where(has_next, after[:pad], 0.0)
        x = jnp.concatenate([front, v[pad:rows], back])
        parts = [x] + [xor_exchange(x, "offset", k) for k in range(1, offset_count)]

    r_hi, r_lo = ratio_call(offs, counts, row_factors, col_ext)
    u, w_parts, h_parts, tail = numer_call(scal, r_hi, r_lo, row_factors, col_ext, mask_ext, parts)
    u = u[:rows]
    scales.append(u)

    live = mask > 0
    sums = [jnp.sum(mask)]
    for t in range(ITERS):
        sums.append(jnp.sum(jnp.where(live, scales[t] / jnp.where(live, scales[t + 1], 1.0), 0.0)))
    sums = jnp.broadcast_to(jnp.stack(sums)[:, None], (ITERS + 1, tile))
    k = 1
    while k < genome_count:
        sums = sums + xor_exchange(sums, "genome", k)
        k *= 2
    factor = sums[1, 0] / sums[0, 0]
    for t in range(1, ITERS):
        factor = factor * (sums[t + 1, 0] / sums[0, 0])
    bias = jnp.where(live, u * factor, 0.0).reshape(-1)

    arrived = lax.ppermute(tail, "genome", [(i, (i + 1) % genome_count) for i in range(genome_count)])
    per = rows // offset_count
    arrived = jnp.where(has_prev, arrived, 0.0)
    for s in range(-(-pad // per)):
        piece = arrived[s * per : (s + 1) * per]
        h_parts = [
            h.at[: piece.shape[0]].add(jnp.where(jnp.bitwise_xor(o, k) == s, piece, 0.0))
            for k, h in enumerate(h_parts)
        ]

    h_tile = jnp.sum(col_factors.reshape(factors, rows, tile) * mask[None], axis=2)
    w_tile = jnp.sum(row_factors.reshape(factors, rows, tile) * mask[None], axis=2)
    ends = jnp.concatenate([h_tile[:, :pad], w_tile[:, rows - pad :]], axis=1)
    after, before = both_sides(ends)
    h_long = jnp.concatenate([h_tile, jnp.where(has_next, after[:, :pad], 0.0)], axis=1)
    w_long = jnp.concatenate([jnp.where(has_prev, before[:, pad:], 0.0), w_tile], axis=1)
    first = o * per
    w_den = tree_sum([lax.dynamic_slice_in_dim(h_long, first + d, per, 1) for d in range(pad)])
    h_den = tree_sum([lax.dynamic_slice_in_dim(w_long, first + pad - d, per, 1) for d in range(pad)])

    mask_share = lax.dynamic_slice_in_dim(mask, first, per, 0)
    row_share = lax.dynamic_slice_in_dim(row_factors, first * tile, per * tile, 1)
    col_share = lax.dynamic_slice_in_dim(col_factors, first * tile, per * tile, 1)

    def update(share, numer, den):
        live_share = mask_share[None] > 0
        share = share.reshape(factors, per, tile)
        numer = jnp.swapaxes(numer, 0, 1)
        den = jnp.where(live_share, den[:, :, None] * mask_share[None], 1.0)
        new = jnp.where(live_share, share * (numer * factor * factor) / den, share)
        return new.reshape(factors, per * tile)

    row_update = update(row_share, scatter_sum(w_parts), w_den)
    col_update = update(col_share, scatter_sum(h_parts), h_den)
    return bias, row_update, col_update


def solution(mesh):
    return jax.shard_map(
        per_device,
        mesh=mesh,
        in_specs=(
            P("genome", "offset", None, None),
            P("offset"),
            P("genome"),
            P(None, "genome"),
            P(None, "genome"),
        ),
        out_specs=(P("genome"), P(None, ("genome", "offset")), P(None, ("genome", "offset"))),
        check_vma=False,
    )
```

time: 313 us -> 150 us (0.48)
  blocking collectives: 107 us -> 0 us
  Pallas kernels: 0 us -> 66.4 us
  matrix products: 45.3 us -> 0 us
  other arithmetic: 50.5 us -> 10.2 us
  between operations: 28.8 us -> 4.84 us
  local copies, waits for them, and re-layouts: 27.4 us -> 4.29 us
  starting transfers between devices: 17 us -> 31.6 us
  waiting for transfers between devices: 36.7 us -> 31.8 us
    psum x6 -> x0, blocking collectives: 107 us -> none  [the longest x3 56.5 us: per_device(): main_part, tail_part = lax.psum((main_part, tail_part), 'offset')]
    pallas_call x0 -> x5, Pallas kernels: none -> 66.4 us  [the longest x1 30.1 us: ratio_call(): pl.pallas_call(ratio_kernel, grid_spec=pltpu.PrefetchScalarGridSpec(num_s...]
    dot_general x6 -> x0, matrix products: 45.3 us -> none  [the longest x2 21.9 us: factor_terms(): model_tiles = jnp.einsum('kip,kiq->ipq', w_rows, h_cols, precision=highest)]
    reduce_scatter x2 -> x0, waiting for transfers between devices: 32.4 us -> none  [the longest x1 28.2 us: per_device(): lax.psum_scatter(h_num.reshape(factor_count, -1), 'offset', scatter_dimen...]
    reduce_sum x12 -> x3, other arithmetic: 32 us -> 1.85 us  [the longest x1 0.63 us: per_device(): jnp.sum(jnp.where(live, scales[t] / jnp.where(live, scales[t + 1], 1.0),...]
    ppermute x10 -> x30, waiting for transfers between devices: 4.31 us -> 31.8 us  [the longest x18 21 us: xor_exchange(): lax.ppermute(x, axis, [(i, i ^ k) for i in range(lax.axis_size(axis))])]
    ppermute x10 -> x30, starting transfers between devices: 16.7 us -> 31.6 us  [the longest x18 22.1 us: xor_exchange(): lax.ppermute(x, axis, [(i, i ^ k) for i in range(lax.axis_size(axis))])]
    convert_element_type x2 -> x0, other arithmetic: 13 us -> none  [tile_values(): values = mirror_tile(count_block.astype(jnp.float32), offset_value)]
  transfers between devices with their start and end apart: 12 -> 30, of which waited for: 8 -> 14; matrix products, arithmetic and copies ran while one was open for 27% -> 7% of each run, Pallas kernels for 0% -> 38%
where the time goes in v1:
time: 150 us; the launch traced here: 149 us
  Pallas kernels  66.4 us (44%)
  waiting for transfers between devices  31.8 us (21%)
  starting transfers between devices  31.6 us (21%)
  other arithmetic  10.2 us (7%)
  between operations  4.84 us (3%)
  local copies, waits for them, and re-layouts  4.29 us (3%)
    pallas_call x1, Pallas kernels, ratio_call(): pl.pallas_call(ratio_kernel, grid_spec=pltpu.PrefetchScalarGridSpec(num_s...  30.1 us
    pallas_call x3, Pallas kernels, cover_call(): pl.pallas_call(functools.partial(cover_kernel, not parts, rows), grid_spe...  27.6 us
    ppermute x18, starting transfers between devices, xor_exchange(): lax.ppermute(x, axis, [(i, i ^ k) for i in range(lax.axis_size(axis))])  22.1 us
    ppermute x18, waiting for transfers between devices, xor_exchange(): lax.ppermute(x, axis, [(i, i ^ k) for i in range(lax.axis_size(axis))])  21 us
    pallas_call x1, Pallas kernels, numer_call(): pl.pallas_call(functools.partial(numer_kernel, shares, rows), grid_spec=p...  8.62 us
    ppermute x5, starting transfers between devices, both_sides(): lax.ppermute(x, 'genome', [(i, ((i + 1 ^ 1) - 1) % size) for i in range(s...  8.23 us
    ppermute x5, waiting for transfers between devices, both_sides(): lax.ppermute(x, 'genome', [(i, ((i + 1 ^ 1) - 1) % size) for i in range(s...  6.6 us
    ppermute x1, waiting for transfers between devices, per_device(): lax.ppermute(tail, 'genome', [(i, (i + 1) % genome_count) for i in range(...  4.16 us
  transfers between devices with their start and end apart: 30, of which 14 were waited for; matrix products, arithmetic and copies ran while one was open for 7% of the time, Pallas kernels for 38%

profile of v1, /device:TPU:0, one launch (start us, length us, event | category | flops | bytes accessed | tf_op | source)
XLA Modules:
  0.0 149.0 jit_solution(690127878059410505)
XLA Ops:
  0.6 0.9 convert_bitcast_fusion
  1.5 3.3 %collective-permute-start.2 = (f32[8,128]{1,0:T(8,128)S(1)}, f32[8,128]{1,0:T(8,128)S(1)}, u32[]{:S(2)}, u32[]{:S(2)}) collective-permute-start(f32[8,128]{1,0:T(8,128)S(1)} %slice_bitcast_fusion), channel_id=1, source_target_pairs={{0,28},{4,8},{8,4},{12,16},{16,12},{20,24},{24,20},{28,0},{1,29},{... | collective-permute-start | bytes 12296 | tf_op jit(solution)/shard_map/ppermute | solution.py:298
  4.9 1.4 copy.26
  6.9 9.2 %cover.3 = (f32[72,128]{1,0:T(8,128)S(1)}, f32[16,128]{1,0:T(8,128)S(1)}, f32[72,128]{1,0:T(8,128)S(1)}) custom-call(s32[2]{0:T(128)S(1)} %copy-done.1, s32[64,2,128,128]{3,2,1,0:T(8,128)} %counts.7, f32[72,128]{1,0:T(8,128)S(1)} %pad_maximum_fusion.1.mask), custom_call_target="tpu_custom_call" | custom-call | tf_op jit(solution)/shard_map/cover/pallas_call | solution.py:104
  16.1 0.6 collective-permute-start.4
  16.7 1.5 %collective-permute-start.3 = (f32[16,128]{1,0:T(8,128)S(1)}, f32[16,128]{1,0:T(8,128)S(1)}, u32[]{:S(2)}, u32[]{:S(2)}) collective-permute-start(f32[16,128]{1,0:T(8,128)S(1)} %get-tuple-element.75), channel_id=1, source_target_pairs={{0,28},{4,8},{8,4},{12,16},{16,12},{20,24},{24,20},{28,0},{1,29},{... | collective-permute-start | bytes 24584 | tf_op jit(solution)/shard_map/ppermute | solution.py:298
  18.2 0.6 multiply_reduce_fusion.1
  18.9 1.8 %collective-permute-done.3 = f32[16,128]{1,0:T(8,128)S(1)} collective-permute-done((f32[16,128]{1,0:T(8,128)S(1)}, f32[16,128]{1,0:T(8,128)S(1)}, u32[]{:S(2)}, u32[]{:S(2)}) %collective-permute-start.3) | collective-permute-done | bytes 8224 | tf_op jit(solution)/shard_map/ppermute | solution.py:298
  20.7 3.7 %collective-permute-start.7 = (f32[72,128]{1,0:T(8,128)S(1)}, f32[72,128]{1,0:T(8,128)S(1)}, u32[]{:S(2)}, u32[]{:S(2)}) collective-permute-start(f32[72,128]{1,0:T(8,128)S(1)} %pad_maximum_fusion.2.refs_0_), channel_id=1, source_target_pairs={{0,3},{1,2},{2,1},{3,0},{4,7},{5,6},{6,5},{7,4},{8,11},{9,10},{10,... | collective-permute-start | bytes 110600 | tf_op jit(solution)/shard_map/ppermute | solution.py:291
  24.4 0.8 collective-permute-start.5
  25.2 0.8 collective-permute-start.25
  26.0 0.6 collective-permute-done.7.refs_3_
  26.6 2.6 %collective-permute-done.6.refs_2_ = f32[72,128]{1,0:T(8,128)S(1)} collective-permute-done((f32[72,128]{1,0:T(8,128)S(1)}, f32[72,128]{1,0:T(8,128)S(1)}, u32[]{:S(2)}, u32[]{:S(2)}) %collective-permute-start.6) | collective-permute-done | bytes 36896 | tf_op jit(solution)/shard_map/ppermute | solution.py:291
  29.2 9.2 %cover.4 = (f32[72,128]{1,0:T(8,128)S(1)}, f32[16,128]{1,0:T(8,128)S(1)}, f32[72,128]{1,0:T(8,128)S(1)}) custom-call(s32[2]{0:T(128)S(1)} %copy-done.1, s32[64,2,128,128]{3,2,1,0:T(8,128)} %counts.7, f32[72,128]{1,0:T(8,128)S(1)} %pad_maximum_fusion.1.mask, f32[72,128]{1,0:T(8,128)S(1)} %pad_maximum_fusion.2.refs_0_, ...), custom_call_target="tpu_custom_call" | custom-call | tf_op jit(solution)/shard_map/cover/pallas_call | solution.py:104
  38.5 1.1 collective-permute-start.8
  39.7 0.6 convert_reduce_fusion
  40.3 2.3 %collective-permute-done.8 = f32[16,128]{1,0:T(8,128)S(1)} collective-permute-done((f32[16,128]{1,0:T(8,128)S(1)}, f32[16,128]{1,0:T(8,128)S(1)}, u32[]{:S(2)}, u32[]{:S(2)}) %collective-permute-start.8) | collective-permute-done | bytes 8224 | tf_op jit(solution)/shard_map/ppermute | solution.py:298
  42.6 1.5 %collective-permute-start.12 = (f32[72,128]{1,0:T(8,128)S(1)}, f32[72,128]{1,0:T(8,128)S(1)}, u32[]{:S(2)}, u32[]{:S(2)}) collective-permute-start(f32[72,128]{1,0:T(8,128)S(1)} %pad_maximum_fusion.3.refs_0_), channel_id=1, source_target_pairs={{0,3},{1,2},{2,1},{3,0},{4,7},{5,6},{6,5},{7,4},{8,11},{9,10},{10,... | collective-permute-start | bytes 110600 | tf_op jit(solution)/shard_map/ppermute | solution.py:291
  44.1 0.6 collective-permute-start.11
  44.7 2.3 %collective-permute-start.10 = (f32[72,128]{1,0:T(8,128)S(1)}, f32[72,128]{1,0:T(8,128)S(1)}, u32[]{:S(2)}, u32[]{:S(2)}) collective-permute-start(f32[72,128]{1,0:T(8,128)S(1)} %pad_maximum_fusion.3.refs_0_), channel_id=1, source_target_pairs={{0,1},{1,0},{2,3},{3,2},{4,5},{5,4},{6,7},{7,6},{8,9},{9,8},{10,11... | collective-permute-start | bytes 110600 | tf_op jit(solution)/shard_map/ppermute | solution.py:291
  47.0 1.7 %collective-permute-done.12.refs_3_ = f32[72,128]{1,0:T(8,128)S(1)} collective-permute-done((f32[72,128]{1,0:T(8,128)S(1)}, f32[72,128]{1,0:T(8,128)S(1)}, u32[]{:S(2)}, u32[]{:S(2)}) %collective-permute-start.12) | collective-permute-done | bytes 36896 | tf_op jit(solution)/shard_map/ppermute | solution.py:291
  49.4 9.2 %cover.5 = (f32[72,128]{1,0:T(8,128)S(1)}, f32[16,128]{1,0:T(8,128)S(1)}, f32[72,128]{1,0:T(8,128)S(1)}) custom-call(s32[2]{0:T(128)S(1)} %copy-done.1, s32[64,2,128,128]{3,2,1,0:T(8,128)} %counts.7, f32[72,128]{1,0:T(8,128)S(1)} %pad_maximum_fusion.1.mask, f32[72,128]{1,0:T(8,128)S(1)} %pad_maximum_fusion.3.refs_0_, ...), custom_call_target="tpu_custom_call" | custom-call | tf_op jit(solution)/shard_map/cover/pallas_call | solution.py:104
  58.7 1.4 collective-permute-start.13
  60.2 2.6 %collective-permute-done.13 = f32[16,128]{1,0:T(8,128)S(1)} collective-permute-done((f32[16,128]{1,0:T(8,128)S(1)}, f32[16,128]{1,0:T(8,128)S(1)}, u32[]{:S(2)}, u32[]{:S(2)}) %collective-permute-start.13) | collective-permute-done | bytes 8224 | tf_op jit(solution)/shard_map/ppermute | solution.py:298
  62.8 2.4 %collective-permute-start.17 = (f32[72,128]{1,0:T(8,128)S(1)}, f32[72,128]{1,0:T(8,128)S(1)}, u32[]{:S(2)}, u32[]{:S(2)}) collective-permute-start(f32[72,128]{1,0:T(8,128)S(1)} %pad_maximum_fusion.4.refs_0_), channel_id=1, source_target_pairs={{0,3},{1,2},{2,1},{3,0},{4,7},{5,6},{6,5},{7,4},{8,11},{9,10},{10,... | collective-permute-start | bytes 110600 | tf_op jit(solution)/shard_map/ppermute | solution.py:291
  65.2 0.7 collective-permute-start.16
  65.9 1.4 collective-permute-start.15
  67.3 30.1 %ratio.1 = (bf16[64,128,256]{2,1,0:T(8,128)(2,1)}, bf16[64,128,256]{2,1,0:T(8,128)(2,1)}) custom-call(s32[2]{0:T(128)S(1)} %copy-done.1, s32[64,2,128,128]{3,2,1,0:T(8,128)} %counts.7, f32[32,8192]{1,0:T(8,128)S(1)} %copy-done, f32[32,9216]{1,0:T(8,128)S(1)} %pad_maximum_fusion.h_ref), custom_call_target="tpu_custom_call" | custom-call | tf_op jit(solution)/shard_map/ratio/pallas_call | solution.py:161
  97.5 8.6 %numer.1 = (f32[72,128]{1,0:T(8,128)S(1)}, f32[16,32,128]{2,1,0:T(8,128)S(1)}, f32[16,32,128]{2,1,0:T(8,128)S(1)}, f32[16,32,128]{2,1,0:T(8,128)S(1)}, f32[16,32...) custom-call(s32[3]{0:T(128)S(1)} %pad_add_fusion.scal, ...), custom_call_target="tpu_custom_call" | custom-call | tf_op jit(solution)/shard_map/numer/pallas_call | solution.py:264
  106.1 0.6 select_reduce_fusion.2
  106.7 2.6 %pad_maximum_fusion.6 = f32[4]{0:T(128)S(1)} fusion(f32[1]{0:T(128)} %bitcast.6, f32[1]{0:T(128)} %bitcast.5, f32[1]{0:T(128)} %bitcast.4, f32[1]{0:T(128)} %bitcast.3), kind=kLoop, calls=%fused_computation.75 | loop fusion | flops 12 | bytes 32 | tf_op jit(solution)/shard_map/stack | solution.py:357
  110.6 4.2 %collective-permute-done.26 = f32[8,32,128]{2,1,0:T(8,128)S(1)} collective-permute-done((f32[8,32,128]{2,1,0:T(8,128)S(1)}, f32[8,32,128]{2,1,0:T(8,128)S(1)}, u32[]{:S(2)}, u32[]{:S(2)}) %collective-permute-start.26) | collective-permute-done | bytes 131104 | tf_op jit(solution)/shard_map/ppermute | solution.py:367
  115.1 1.3 collective-permute-start.20
  116.8 1.9 %collective-permute-start.21 = (f32[16,32,128]{2,1,0:T(8,128)S(1)}, f32[16,32,128]{2,1,0:T(8,128)S(1)}, u32[]{:S(2)}, u32[]{:S(2)}) collective-permute-start(f32[16,32,128]{2,1,0:T(8,128)S(1)} %get-tuple-element.85), channel_id=1, source_target_pairs={{0,1},{1,0},{2,3},{3,2},{4,5},{5,4},{6,7},{7,6},{8,9},{9,8},{10,11... | collective-permute-start | bytes 786440 | tf_op jit(solution)/shard_map/ppermute | solution.py:291
  118.8 1.9 %collective-permute-start.27 = (f32[16,32,128]{2,1,0:T(8,128)S(1)}, f32[16,32,128]{2,1,0:T(8,128)S(1)}, u32[]{:S(2)}, u32[]{:S(2)}) collective-permute-start(f32[16,32,128]{2,1,0:T(8,128)S(1)} %get-tuple-element.101), channel_id=1, source_target_pairs={{0,1},{1,0},{2,3},{3,2},{4,5},{5,4},{6,7},{7,6},{8,9},{9,8},{10,11... | collective-permute-start | bytes 786440 | tf_op jit(solution)/shard_map/ppermute | solution.py:291
  120.6 1.0 add.259
  121.6 1.8 %collective-permute-start.23 = (f32[16,32,128]{2,1,0:T(8,128)S(1)}, f32[16,32,128]{2,1,0:T(8,128)S(1)}, u32[]{:S(2)}, u32[]{:S(2)}) collective-permute-start(f32[16,32,128]{2,1,0:T(8,128)S(1)} %add.259), channel_id=1, source_target_pairs={{0,3},{1,2},{2,1},{3,0},{4,7},{5,6},{6,5},{7,4},{8,11},{9,10},{10,... | collective-permute-start | bytes 786440 | tf_op jit(solution)/shard_map/ppermute | solution.py:291
  123.4 1.4 collective-permute-done.28
  124.9 1.0 add.288
  125.9 1.8 %collective-permute-start.29 = (f32[16,32,128]{2,1,0:T(8,128)S(1)}, f32[16,32,128]{2,1,0:T(8,128)S(1)}, u32[]{:S(2)}, u32[]{:S(2)}) collective-permute-start(f32[16,32,128]{2,1,0:T(8,128)S(1)} %add.288), channel_id=1, source_target_pairs={{0,3},{1,2},{2,1},{3,0},{4,7},{5,6},{6,5},{7,4},{8,11},{9,10},{10,... | collective-permute-start | bytes 786440 | tf_op jit(solution)/shard_map/ppermute | solution.py:291
  127.7 0.6 fusion.26
  132.2 0.6 select_bitcast_fusion
  132.9 2.8 %collective-permute-done.27 = f32[16,32,128]{2,1,0:T(8,128)S(1)} collective-permute-done((f32[16,32,128]{2,1,0:T(8,128)S(1)}, f32[16,32,128]{2,1,0:T(8,128)S(1)}, u32[]{:S(2)}, u32[]{:S(2)}) %collective-permute-start.27) | collective-permute-done | bytes 262176 | tf_op jit(solution)/shard_map/ppermute | solution.py:291
  135.7 5.6 %collective-permute-done.23 = f32[16,32,128]{2,1,0:T(8,128)S(1)} collective-permute-done((f32[16,32,128]{2,1,0:T(8,128)S(1)}, f32[16,32,128]{2,1,0:T(8,128)S(1)}, u32[]{:S(2)}, u32[]{:S(2)}) %collective-permute-start.23) | collective-permute-done | bytes 262176 | tf_op jit(solution)/shard_map/ppermute | solution.py:291
  141.3 5.1 %collective-permute-done.29 = f32[16,32,128]{2,1,0:T(8,128)S(1)} collective-permute-done((f32[16,32,128]{2,1,0:T(8,128)S(1)}, f32[16,32,128]{2,1,0:T(8,128)S(1)}, u32[]{:S(2)}, u32[]{:S(2)}) %collective-permute-start.29) | collective-permute-done | bytes 262176 | tf_op jit(solution)/shard_map/ppermute | solution.py:291
  146.4 1.2 fusion.1
  147.6 0.7 copy.32
  148.3 0.7 copy.33
  (68 shorter events, 4.0 us)
Async XLA Ops:
  0.6 5.7 %copy-start = (f32[32,8192]{1,0:T(8,128)S(1)}, f32[32,8192]{1,0:T(8,128)}, u32[]{:S(2)}) copy-start(f32[32,8192]{1,0:T(8,128)} %w_ref.3) | copy-start | bytes 3145732
  1.5 5.0 %collective-permute-start.2 = (f32[8,128]{1,0:T(8,128)S(1)}, f32[8,128]{1,0:T(8,128)S(1)}, u32[]{:S(2)}, u32[]{:S(2)}) collective-permute-start(f32[8,128]{1,0:T(8,128)S(1)} %slice_bitcast_fusion), channel_id=1, source_target_pairs={{0,28},{4,8},{8,4},{12,16},{16,12},{20,24},{24,20},{28,0},{1,29},{... | collective-permute-start | bytes 12296 | tf_op jit(solution)/shard_map/ppermute | solution.py:298
  4.8 1.7 %collective-permute-start.1 = (f32[8,128]{1,0:T(8,128)S(1)}, f32[8,128]{1,0:T(8,128)S(1)}, u32[]{:S(2)}, u32[]{:S(2)}) collective-permute-start(f32[8,128]{1,0:T(8,128)S(1)} %slice_bitcast_fusion), channel_id=1, source_target_pairs={{0,4},{4,0},{8,12},{12,8},{16,20},{20,16},{24,28},{28,24},{1,5},{5... | collective-permute-start | bytes 12296 | tf_op jit(solution)/shard_map/ppermute | solution.py:297
  6.3 0.7 copy-start.1
  16.1 2.8 %collective-permute-start.4 = (f32[16,128]{1,0:T(8,128)S(1)}, f32[16,128]{1,0:T(8,128)S(1)}, u32[]{:S(2)}, u32[]{:S(2)}) collective-permute-start(f32[16,128]{1,0:T(8,128)S(1)} %get-tuple-element.75), channel_id=1, source_target_pairs={{0,4},{4,0},{8,12},{12,8},{16,20},{20,16},{24,28},{28,24},{1,5},{5... | collective-permute-start | bytes 24584 | tf_op jit(solution)/shard_map/ppermute | solution.py:297
  16.7 4.0 %collective-permute-start.3 = (f32[16,128]{1,0:T(8,128)S(1)}, f32[16,128]{1,0:T(8,128)S(1)}, u32[]{:S(2)}, u32[]{:S(2)}) collective-permute-start(f32[16,128]{1,0:T(8,128)S(1)} %get-tuple-element.75), channel_id=1, source_target_pairs={{0,28},{4,8},{8,4},{12,16},{16,12},{20,24},{24,20},{28,0},{1,29},{... | collective-permute-start | bytes 24584 | tf_op jit(solution)/shard_map/ppermute | solution.py:298
  20.7 5.9 %collective-permute-start.7 = (f32[72,128]{1,0:T(8,128)S(1)}, f32[72,128]{1,0:T(8,128)S(1)}, u32[]{:S(2)}, u32[]{:S(2)}) collective-permute-start(f32[72,128]{1,0:T(8,128)S(1)} %pad_maximum_fusion.2.refs_0_), channel_id=1, source_target_pairs={{0,3},{1,2},{2,1},{3,0},{4,7},{5,6},{6,5},{7,4},{8,11},{9,10},{10,... | collective-permute-start | bytes 110600 | tf_op jit(solution)/shard_map/ppermute | solution.py:291
  24.4 4.9 %collective-permute-start.6 = (f32[72,128]{1,0:T(8,128)S(1)}, f32[72,128]{1,0:T(8,128)S(1)}, u32[]{:S(2)}, u32[]{:S(2)}) collective-permute-start(f32[72,128]{1,0:T(8,128)S(1)} %pad_maximum_fusion.2.refs_0_), channel_id=1, source_target_pairs={{0,2},{1,3},{2,0},{3,1},{4,6},{5,7},{6,4},{7,5},{8,10},{9,11},{10,... | collective-permute-start | bytes 110600 | tf_op jit(solution)/shard_map/ppermute | solution.py:291
  24.4 4.9 %collective-permute-start.5 = (f32[72,128]{1,0:T(8,128)S(1)}, f32[72,128]{1,0:T(8,128)S(1)}, u32[]{:S(2)}, u32[]{:S(2)}) collective-permute-start(f32[72,128]{1,0:T(8,128)S(1)} %pad_maximum_fusion.2.refs_0_), channel_id=1, source_target_pairs={{0,1},{1,0},{2,3},{3,2},{4,5},{5,4},{6,7},{7,6},{8,9},{9,8},{10,11... | collective-permute-start | bytes 110600 | tf_op jit(solution)/shard_map/ppermute | solution.py:291
  25.2 14.5 %copy-start.3 = (s32[8192]{0:T(1024)S(1)}, s32[8192]{0:T(1024)}, u32[]{:S(2)}) copy-start(s32[8192]{0:T(1024)} %param.15) | copy-start | bytes 98308
  25.2 21.8 %copy-start.2 = (f32[32,8192]{1,0:T(8,128)S(1)}, f32[32,8192]{1,0:T(8,128)}, u32[]{:S(2)}) copy-start(f32[32,8192]{1,0:T(8,128)} %param.17) | copy-start | bytes 3145732
  25.2 84.2 %collective-permute-start.25 = (f32[32,16]{1,0:T(8,128)S(1)}, f32[32,16]{1,0:T(8,128)S(1)}, u32[]{:S(2)}, u32[]{:S(2)}) collective-permute-start(f32[32,16]{1,0:T(8,128)S(1)} %pad_maximum_fusion.5), channel_id=1, source_target_pairs={{0,28},{4,8},{8,4},{12,16},{16,12},{20,24},{24,20},{28,0},{1,29},{... | collective-permute-start | bytes 6152 | tf_op jit(solution)/shard_map/ppermute | solution.py:298
  26.0 83.4 %collective-permute-start.24 = (f32[32,16]{1,0:T(8,128)S(1)}, f32[32,16]{1,0:T(8,128)S(1)}, u32[]{:S(2)}, u32[]{:S(2)}) collective-permute-start(f32[32,16]{1,0:T(8,128)S(1)} %pad_maximum_fusion.5), channel_id=1, source_target_pairs={{0,4},{4,0},{8,12},{12,8},{16,20},{20,16},{24,28},{28,24},{1,5},{5... | collective-permute-start | bytes 6152 | tf_op jit(solution)/shard_map/ppermute | solution.py:297
  38.4 1.8 %collective-permute-start.9 = (f32[16,128]{1,0:T(8,128)S(1)}, f32[16,128]{1,0:T(8,128)S(1)}, u32[]{:S(2)}, u32[]{:S(2)}) collective-permute-start(f32[16,128]{1,0:T(8,128)S(1)} %get-tuple-element.77), channel_id=1, source_target_pairs={{0,4},{4,0},{8,12},{12,8},{16,20},{20,16},{24,28},{28,24},{1,5},{5... | collective-permute-start | bytes 24584 | tf_op jit(solution)/shard_map/ppermute | solution.py:297
  38.5 4.0 %collective-permute-start.8 = (f32[16,128]{1,0:T(8,128)S(1)}, f32[16,128]{1,0:T(8,128)S(1)}, u32[]{:S(2)}, u32[]{:S(2)}) collective-permute-start(f32[16,128]{1,0:T(8,128)S(1)} %get-tuple-element.77), channel_id=1, source_target_pairs={{0,28},{4,8},{8,4},{12,16},{16,12},{20,24},{24,20},{28,0},{1,29},{... | collective-permute-start | bytes 24584 | tf_op jit(solution)/shard_map/ppermute | solution.py:298
  42.6 6.1 %collective-permute-start.12 = (f32[72,128]{1,0:T(8,128)S(1)}, f32[72,128]{1,0:T(8,128)S(1)}, u32[]{:S(2)}, u32[]{:S(2)}) collective-permute-start(f32[72,128]{1,0:T(8,128)S(1)} %pad_maximum_fusion.3.refs_0_), channel_id=1, source_target_pairs={{0,3},{1,2},{2,1},{3,0},{4,7},{5,6},{6,5},{7,4},{8,11},{9,10},{10,... | collective-permute-start | bytes 110600 | tf_op jit(solution)/shard_map/ppermute | solution.py:291
  44.1 5.0 %collective-permute-start.11 = (f32[72,128]{1,0:T(8,128)S(1)}, f32[72,128]{1,0:T(8,128)S(1)}, u32[]{:S(2)}, u32[]{:S(2)}) collective-permute-start(f32[72,128]{1,0:T(8,128)S(1)} %pad_maximum_fusion.3.refs_0_), channel_id=1, source_target_pairs={{0,2},{1,3},{2,0},{3,1},{4,6},{5,7},{6,4},{7,5},{8,10},{9,11},{10,... | collective-permute-start | bytes 110600 | tf_op jit(solution)/shard_map/ppermute | solution.py:291
  44.7 4.7 %collective-permute-start.10 = (f32[72,128]{1,0:T(8,128)S(1)}, f32[72,128]{1,0:T(8,128)S(1)}, u32[]{:S(2)}, u32[]{:S(2)}) collective-permute-start(f32[72,128]{1,0:T(8,128)S(1)} %pad_maximum_fusion.3.refs_0_), channel_id=1, source_target_pairs={{0,1},{1,0},{2,3},{3,2},{4,5},{5,4},{6,7},{7,6},{8,9},{9,8},{10,11... | collective-permute-start | bytes 110600 | tf_op jit(solution)/shard_map/ppermute | solution.py:291
  48.7 17.1 %collective-permute-start = (f32[32,1024]{1,0:T(8,128)S(1)}, f32[32,1024]{1,0:T(8,128)S(1)}, u32[]{:S(2)}, u32[]{:S(2)}) collective-permute-start(f32[32,1024]{1,0:T(8,128)S(1)} %slice.196), channel_id=1, source_target_pairs={{0,28},{4,0},{8,4},{12,8},{16,12},{20,16},{24,20},{28,24},{1,29},{... | collective-permute-start | bytes 393224 | tf_op jit(solution)/shard_map/ppermute | solution.py:333
  58.6 1.6 %collective-permute-start.14 = (f32[16,128]{1,0:T(8,128)S(1)}, f32[16,128]{1,0:T(8,128)S(1)}, u32[]{:S(2)}, u32[]{:S(2)}) collective-permute-start(f32[16,128]{1,0:T(8,128)S(1)} %get-tuple-element.79), channel_id=1, source_target_pairs={{0,4},{4,0},{8,12},{12,8},{16,20},{20,16},{24,28},{28,24},{1,5},{5... | collective-permute-start | bytes 24584 | tf_op jit(solution)/shard_map/ppermute | solution.py:297
  58.7 4.0 %collective-permute-start.13 = (f32[16,128]{1,0:T(8,128)S(1)}, f32[16,128]{1,0:T(8,128)S(1)}, u32[]{:S(2)}, u32[]{:S(2)}) collective-permute-start(f32[16,128]{1,0:T(8,128)S(1)} %get-tuple-element.79), channel_id=1, source_target_pairs={{0,28},{4,8},{8,4},{12,16},{16,12},{20,24},{24,20},{28,0},{1,29},{... | collective-permute-start | bytes 24584 | tf_op jit(solution)/shard_map/ppermute | solution.py:298
  62.8 34.7 %collective-permute-start.17 = (f32[72,128]{1,0:T(8,128)S(1)}, f32[72,128]{1,0:T(8,128)S(1)}, u32[]{:S(2)}, u32[]{:S(2)}) collective-permute-start(f32[72,128]{1,0:T(8,128)S(1)} %pad_maximum_fusion.4.refs_0_), channel_id=1, source_target_pairs={{0,3},{1,2},{2,1},{3,0},{4,7},{5,6},{6,5},{7,4},{8,11},{9,10},{10,... | collective-permute-start | bytes 110600 | tf_op jit(solution)/shard_map/ppermute | solution.py:291
  65.2 32.3 %collective-permute-start.16 = (f32[72,128]{1,0:T(8,128)S(1)}, f32[72,128]{1,0:T(8,128)S(1)}, u32[]{:S(2)}, u32[]{:S(2)}) collective-permute-start(f32[72,128]{1,0:T(8,128)S(1)} %pad_maximum_fusion.4.refs_0_), channel_id=1, source_target_pairs={{0,2},{1,3},{2,0},{3,1},{4,6},{5,7},{6,4},{7,5},{8,10},{9,11},{10,... | collective-permute-start | bytes 110600 | tf_op jit(solution)/shard_map/ppermute | solution.py:291
  65.9 31.6 %collective-permute-start.15 = (f32[72,128]{1,0:T(8,128)S(1)}, f32[72,128]{1,0:T(8,128)S(1)}, u32[]{:S(2)}, u32[]{:S(2)}) collective-permute-start(f32[72,128]{1,0:T(8,128)S(1)} %pad_maximum_fusion.4.refs_0_), channel_id=1, source_target_pairs={{0,1},{1,0},{2,3},{3,2},{4,5},{5,4},{6,7},{7,6},{8,9},{9,8},{10,11... | collective-permute-start | bytes 110600 | tf_op jit(solution)/shard_map/ppermute | solution.py:291
  109.4 1.2 collective-permute-start.18
  109.5 5.3 %collective-permute-start.26 = (f32[8,32,128]{2,1,0:T(8,128)S(1)}, f32[8,32,128]{2,1,0:T(8,128)S(1)}, u32[]{:S(2)}, u32[]{:S(2)}) collective-permute-start(f32[8,32,128]{2,1,0:T(8,128)S(1)} %get-tuple-element.89), channel_id=1, source_target_pairs={{0,4},{4,8},{8,12},{12,16},{16,20},{20,24},{24,28},{28,0},{1,5},{5... | collective-permute-start | bytes 393224 | tf_op jit(solution)/shard_map/ppermute | solution.py:367
  110.0 10.7 %collective-permute-start.22 = (f32[16,32,128]{2,1,0:T(8,128)S(1)}, f32[16,32,128]{2,1,0:T(8,128)}, u32[]{:S(2)}, u32[]{:S(2)}) collective-permute-start(f32[16,32,128]{2,1,0:T(8,128)S(1)} %get-tuple-element.87), channel_id=1, source_target_pairs={{0,1},{1,0},{2,3},{3,2},{4,5},{5,4},{6,7},{7,6},{8,9},{9,8},{10,11... | collective-permute-start | bytes 786440 | tf_op jit(solution)/shard_map/ppermute | solution.py:291
  110.6 4.4 %collective-permute-start.19 = (f32[4,128]{1,0:T(4,128)S(1)}, f32[4,128]{1,0:T(4,128)S(1)}, u32[]{:S(2)}, u32[]{:S(2)}) collective-permute-start(f32[4,128]{1,0:T(4,128)S(1)} %broadcast_add_fusion), channel_id=1, source_target_pairs={{0,8},{4,12},{8,0},{12,4},{16,24},{20,28},{24,16},{28,20},{1,9},{5... | collective-permute-start | bytes 6152 | tf_op jit(solution)/shard_map/ppermute | solution.py:291
  114.9 10.0 %collective-permute-start.28 = (f32[16,32,128]{2,1,0:T(8,128)S(1)}, f32[16,32,128]{2,1,0:T(8,128)}, u32[]{:S(2)}, u32[]{:S(2)}) collective-permute-start(f32[16,32,128]{2,1,0:T(8,128)S(1)} %get-tuple-element.103), channel_id=1, source_target_pairs={{0,1},{1,0},{2,3},{3,2},{4,5},{5,4},{6,7},{7,6},{8,9},{9,8},{10,11... | collective-permute-start | bytes 786440 | tf_op jit(solution)/shard_map/ppermute | solution.py:291
  115.1 3.7 %collective-permute-start.20 = (f32[4,128]{1,0:T(4,128)S(1)}, f32[4,128]{1,0:T(4,128)S(1)}, u32[]{:S(2)}, u32[]{:S(2)}) collective-permute-start(f32[4,128]{1,0:T(4,128)S(1)} %fusion.27), channel_id=1, source_target_pairs={{0,16},{4,20},{8,24},{12,28},{16,0},{20,4},{24,8},{28,12},{1,17},{... | collective-permute-start | bytes 6152 | tf_op jit(solution)/shard_map/ppermute | solution.py:291
  116.8 16.1 %collective-permute-start.21 = (f32[16,32,128]{2,1,0:T(8,128)S(1)}, f32[16,32,128]{2,1,0:T(8,128)S(1)}, u32[]{:S(2)}, u32[]{:S(2)}) collective-permute-start(f32[16,32,128]{2,1,0:T(8,128)S(1)} %get-tuple-element.85), channel_id=1, source_target_pairs={{0,1},{1,0},{2,3},{3,2},{4,5},{5,4},{6,7},{7,6},{8,9},{9,8},{10,11... | collective-permute-start | bytes 786440 | tf_op jit(solution)/shard_map/ppermute | solution.py:291
  118.8 16.9 %collective-permute-start.27 = (f32[16,32,128]{2,1,0:T(8,128)S(1)}, f32[16,32,128]{2,1,0:T(8,128)S(1)}, u32[]{:S(2)}, u32[]{:S(2)}) collective-permute-start(f32[16,32,128]{2,1,0:T(8,128)S(1)} %get-tuple-element.101), channel_id=1, source_target_pairs={{0,1},{1,0},{2,3},{3,2},{4,5},{5,4},{6,7},{7,6},{8,9},{9,8},{10,11... | collective-permute-start | bytes 786440 | tf_op jit(solution)/shard_map/ppermute | solution.py:291
  121.6 19.7 %collective-permute-start.23 = (f32[16,32,128]{2,1,0:T(8,128)S(1)}, f32[16,32,128]{2,1,0:T(8,128)S(1)}, u32[]{:S(2)}, u32[]{:S(2)}) collective-permute-start(f32[16,32,128]{2,1,0:T(8,128)S(1)} %add.259), channel_id=1, source_target_pairs={{0,3},{1,2},{2,1},{3,0},{4,7},{5,6},{6,5},{7,4},{8,11},{9,10},{10,... | collective-permute-start | bytes 786440 | tf_op jit(solution)/shard_map/ppermute | solution.py:291
  125.9 20.5 %collective-permute-start.29 = (f32[16,32,128]{2,1,0:T(8,128)S(1)}, f32[16,32,128]{2,1,0:T(8,128)S(1)}, u32[]{:S(2)}, u32[]{:S(2)}) collective-permute-start(f32[16,32,128]{2,1,0:T(8,128)S(1)} %add.288), channel_id=1, source_target_pairs={{0,3},{1,2},{2,1},{3,0},{4,7},{5,6},{6,5},{7,4},{8,11},{9,10},{10,... | collective-permute-start | bytes 786440 | tf_op jit(solution)/shard_map/ppermute | solution.py:291

commit v2 on v0

v2 whole, which is shorter than its diff:
```python
import functools

import jax
import jax.numpy as jnp
from jax import lax
from jax.experimental import pallas as pl
from jax.experimental.pallas import tpu as pltpu
from jax.sharding import PartitionSpec as P

ITERS = 3
STEP = 8
EARLY = 2
F32 = jnp.float32
BF16 = jnp.bfloat16
VMEM_LIMIT = 20 * 1024 * 1024
NT = (((1,), (1,)), ((), ()))
TN = (((0,), (0,)), ((), ()))


def split(x):
    hi = x.astype(BF16)
    lo = (x - hi.astype(F32)).astype(BF16)
    return hi, lo


def tree_sum(parts):
    while len(parts) > 1:
        parts = [a + b for a, b in zip(parts[::2], parts[1::2])]
    return parts[0]


def params():
    return pltpu.CompilerParams(vmem_limit_bytes=VMEM_LIMIT)


def scale_from(mask, parts):
    cover = tree_sum([p[...] for p in parts])
    live = mask[...] > 0
    return jnp.where(live, 1.0 / jnp.where(live, cover, 1.0), 0.0)


def vmem():
    return pl.BlockSpec(memory_space=pltpu.VMEM)


def kernel_call(body, name, scalars, args, outs, scratch=(), aliases=None, specs=None):
    return pl.pallas_call(
        body,
        grid_spec=pltpu.PrefetchScalarGridSpec(
            num_scalar_prefetch=1,
            grid=(1,),
            in_specs=specs or [vmem() for _ in args],
            out_specs=[vmem() for _ in outs],
            scratch_shapes=list(scratch),
        ),
        out_shape=outs,
        input_output_aliases=aliases or {},
        compiler_params=params(),
        name=name,
    )(scalars, *args)


def by_diagonal(offs, slots, go):
    for s in range(slots):

        @pl.when(offs[s] == 0)
        def _():
            go(s)

    @pl.when(functools.reduce(jnp.logical_and, [offs[s] != 0 for s in range(slots)]))
    def _():
        go(-1)


def tile_value(counts, i, s, diagonal):
    c = counts[i, s].astype(F32)
    if s == diagonal:
        tile = c.shape[0]
        r = lax.broadcasted_iota(jnp.int32, (tile, tile), 0)
        q = lax.broadcasted_iota(jnp.int32, (tile, tile), 1)
        c = jnp.where(r < q, c, jnp.where(r == q, 0.5 * c, 0.0))
    return c


def cover_block(offs, counts, u_ref, acc, base, diagonal, kept=None):
    slots, tile = counts.shape[1:3]
    ones = jnp.ones((8, tile), BF16)
    u_block = u_ref[pl.ds(base, STEP), :]
    u_cols = u_block.T
    u_across = [u_ref[pl.ds(base + offs[s], STEP), :] for s in range(slots)]
    cols = [[] for _ in range(slots)]
    sums = []
    for t in range(STEP):
        total = None
        for s in range(slots):
            c = tile_value(counts, base + t, s, diagonal)
            if kept is not None:
                kept[base + t, s] = c
            term = c * u_across[s][t : t + 1]
            total = term if total is None else total + term
            cols[s].append(jnp.sum(c * u_cols[:, t : t + 1], axis=0, keepdims=True))
        hi, lo = split(total)
        row = lax.dot_general(ones, hi, NT, preferred_element_type=F32)
        row = row + lax.dot_general(ones, lo, NT, preferred_element_type=F32)
        sums.append(row[:1])
    acc[pl.ds(base, STEP), :] += jnp.concatenate(sums, axis=0)
    for s in range(slots):
        acc[pl.ds(base + offs[s], STEP), :] += jnp.concatenate(cols[s], axis=0)


def cover_edge_kernel(first, rows, offs, counts, mask, *refs):
    v_out, edge_out, u_out = refs[-3:]
    pad = mask.shape[0] - rows
    u_out[...] = mask[...] if first else scale_from(mask, refs[:-4])
    v_out[...] = jnp.zeros_like(v_out)

    def go(diagonal):
        for base in list(range(0, pad, STEP)) + list(range(rows - pad, rows, STEP)):
            cover_block(offs, counts, u_out, v_out, base, diagonal)

    if first:
        by_diagonal(offs, counts.shape[1], go)
    else:
        go(-1)
    edge_out[:pad] = v_out[:pad]
    edge_out[pad:] = v_out[rows:]


def cover_main_kernel(first, rows, offs, counts, u_ref, edge_v, v_out, *keep):
    kept = keep[0] if first else None
    pad = edge_v.shape[0] - rows
    v_out[...] = edge_v[...]

    def go(diagonal):
        def body(b, carry):
            cover_block(offs, counts, u_ref, v_out, pl.multiple_of(b * STEP, STEP), diagonal, kept)
            return carry

        lax.fori_loop(pad // STEP, (rows - pad) // STEP, body, 0)
        if first:

            def copy(i, carry):
                for s in range(counts.shape[1]):
                    kept[i, s] = tile_value(counts, i, s, diagonal)
                return carry

            lax.fori_loop(0, pad, copy, 0, unroll=4)
            lax.fori_loop(rows - pad, rows, copy, 0, unroll=4)

    if first:
        by_diagonal(offs, counts.shape[1], go)
    else:
        go(-1)


def cover_edge(offs, counts, mask_ext, parts, after):
    rows, tile = counts.shape[0], counts.shape[2]
    ext = mask_ext.shape[0]
    flat = jax.ShapeDtypeStruct((ext, tile), F32)
    edge = jax.ShapeDtypeStruct((2 * (ext - rows), tile), F32)
    return kernel_call(
        functools.partial(cover_edge_kernel, not parts, rows),
        "cover_edge",
        offs,
        [counts, mask_ext, *parts] + ([after] if parts else []),
        [flat, edge, flat],
    )


def cover_main(offs, counts, u, edge_v, first):
    outs = [jax.ShapeDtypeStruct(u.shape, F32)]
    if first:
        outs.append(pltpu.VMEM(counts.shape, F32))
    return kernel_call(
        functools.partial(cover_main_kernel, first, counts.shape[0]),
        "cover_main",
        offs,
        [counts, u, edge_v],
        outs,
    )


def ratio_kernel(start, count, offs, kept, w_ref, h_ref, after, *refs):
    hi_out, lo_out, h_terms = refs[-3:]
    rows, slots, tile = kept.shape[:3]
    pad = h_ref.shape[1] // tile - rows

    def prepare(j, carry):
        hi, lo = split(h_ref[:, pl.ds(pl.multiple_of(j * tile, tile), tile)])
        h_terms[j - start] = jnp.concatenate([hi, lo, hi, lo], axis=0)
        return carry

    lax.fori_loop(start, start + count + pad, prepare, 0, unroll=4)

    def go(diagonal):
        def body(i, carry):
            hi, lo = split(w_ref[:, pl.ds(pl.multiple_of(i * tile, tile), tile)])
            w_terms = jnp.concatenate([hi, hi, lo, lo], axis=0)
            for s in range(slots):
                model = lax.dot_general(
                    w_terms, h_terms[i - start + offs[s]], TN, preferred_element_type=F32
                )
                values = kept[i, s]
                if s == diagonal:
                    values = values + values.T
                r_hi, r_lo = split(values * (1.0 / model))
                hi_out[i, :, s * tile : (s + 1) * tile] = r_hi
                lo_out[i, :, s * tile : (s + 1) * tile] = r_lo
            return carry

        lax.fori_loop(start, start + count, body, 0, unroll=4)

    by_diagonal(offs, slots, go)


def ratio(offs, kept, row_factors, col_ext, after, earlier, start, count):
    rows, slots, tile = kept.shape[:3]
    factors = row_factors.shape[0]
    pad = col_ext.shape[1] // tile - rows
    out = pltpu.VMEM((rows, tile, slots * tile), BF16)
    return kernel_call(
        functools.partial(ratio_kernel, start, count),
        "ratio",
        offs,
        [kept, row_factors, col_ext, after, *earlier],
        [out, out],
        [pltpu.VMEM((count + pad, 4 * factors, tile), BF16)],
        {5: 0, 6: 1} if earlier else {},
    )


def row_numer(offs, g_all, hi_ref, lo_ref, u_ref, i):
    slots = hi_ref.shape[2] // g_all.shape[2]
    factors = g_all.shape[1] // 2
    g = jnp.concatenate([g_all[i + offs[s]] for s in range(slots)], axis=1)
    big = lax.dot_general(g, hi_ref[i], NT, preferred_element_type=F32)
    small = lax.dot_general(g[:factors], lo_ref[i], NT, preferred_element_type=F32)
    return (big[:factors] + big[factors:] + small) * u_ref[pl.ds(i, 1), :]


def col_numer(w_ref, hi_ref, lo_ref, u_ref, i):
    tile = u_ref.shape[1]
    factors = w_ref.shape[0]
    w = w_ref[:, pl.ds(pl.multiple_of(i * tile, tile), tile)]
    hi, lo = split(w * u_ref[pl.ds(i, 1), :])
    big = jnp.dot(jnp.concatenate([hi, lo], axis=0), hi_ref[i], preferred_element_type=F32)
    small = jnp.dot(hi, lo_ref[i], preferred_element_type=F32)
    return big[:factors] + big[factors:] + small


def col_loop(offs, w_ref, hi_ref, lo_ref, u_ref, acc, start, stop, shift):
    tile = u_ref.shape[1]

    def body(i, carry):
        cols = col_numer(w_ref, hi_ref, lo_ref, u_ref, i)
        for s in range(hi_ref.shape[2] // tile):
            acc[i + offs[s] - shift] += cols[:, s * tile : (s + 1) * tile]
        return carry

    lax.fori_loop(start, stop, body, 0, unroll=4)


def numer_first_kernel(rows, shares, scal, hi_ref, lo_ref, w_ref, h_ref, mask, *refs):
    parts = refs[:shares]
    u_out, g_out, piece_out, tail_out, acc = refs[shares:]
    offs = [scal[1 + s] for s in range(hi_ref.shape[2] // mask.shape[1])]
    ext, tile = mask.shape
    factors = w_ref.shape[0]
    pad = ext - rows
    per = rows // shares
    u_out[...] = scale_from(mask, parts)
    acc[...] = jnp.zeros_like(acc)

    col_loop(offs, w_ref, hi_ref, lo_ref, u_out, acc, rows - pad, rows, rows - pad)
    for t in range(pad):
        tail_out[t] = acc[pad + t] * u_out[rows + t : rows + t + 1, :]

    def fill(j, carry):
        x = h_ref[:, pl.ds(pl.multiple_of(j * tile, tile), tile)] * u_out[pl.ds(j, 1), :]
        hi, lo = split(x)
        g_out[j, :factors] = hi
        g_out[j, factors:] = lo
        return carry

    lax.fori_loop(0, ext, fill, 0, unroll=4)
    first = jnp.bitwise_xor(scal[0], EARLY) * per

    def body(t, carry):
        piece_out[t] = row_numer(offs, g_out, hi_ref, lo_ref, u_out, first + t)
        return carry

    lax.fori_loop(0, per, body, 0, unroll=4)


def numer_row_kernel(order, scal, hi_ref, lo_ref, g_ref, u_ref, *outs):
    offs = [scal[1 + s] for s in range(hi_ref.shape[2] // u_ref.shape[1])]
    per = outs[0].shape[0]
    for k, out in zip(order, outs):
        first = jnp.bitwise_xor(scal[0], k) * per

        def body(t, carry):
            out[t] = row_numer(offs, g_ref, hi_ref, lo_ref, u_ref, first + t)
            return carry

        lax.fori_loop(0, per, body, 0, unroll=4)


def numer_col_kernel(rows, scal, hi_ref, lo_ref, w_ref, u_ref, arrived, *refs):
    outs, acc = refs[:-1], refs[-1]
    offs = [scal[1 + s] for s in range(hi_ref.shape[2] // u_ref.shape[1])]
    per = outs[0].shape[0]
    pad = arrived.shape[0]
    acc[...] = jnp.zeros_like(acc)
    col_loop(offs, w_ref, hi_ref, lo_ref, u_ref, acc, 0, rows, 0)
    for k, out in enumerate(outs):
        share = jnp.bitwise_xor(scal[0], k)
        first = share * per

        def body(t, carry):
            out[t] = acc[first + t] * u_ref[pl.ds(first + t, 1), :]
            return carry

        lax.fori_loop(0, per, body, 0, unroll=4)
        for s in range(-(-pad // per)):

            @pl.when(share == s)
            def _():
                count = min(per, pad - s * per)
                out[:count] += arrived[s * per : s * per + count]


def numer_first(scal, r_hi, r_lo, row_factors, col_ext, mask_ext, parts):
    shares = len(parts)
    rows, tile = r_hi.shape[:2]
    factors = row_factors.shape[0]
    ext = mask_ext.shape[0]
    pad = ext - rows
    outs = [
        jax.ShapeDtypeStruct((ext, tile), F32),
        pltpu.VMEM((ext, 2 * factors, tile), BF16),
        jax.ShapeDtypeStruct((rows // shares, factors, tile), F32),
        jax.ShapeDtypeStruct((pad, factors, tile), F32),
    ]
    return kernel_call(
        functools.partial(numer_first_kernel, rows, shares),
        "numer_first",
        scal,
        [r_hi, r_lo, row_factors, col_ext, mask_ext, *parts],
        outs,
        [pltpu.VMEM((2 * pad, factors, tile), F32)],
    )


def numer_row(scal, r_hi, r_lo, g_all, u, order, shares):
    rows, tile = r_hi.shape[:2]
    piece = jax.ShapeDtypeStruct((rows // shares, g_all.shape[1] // 2, tile), F32)
    return kernel_call(
        functools.partial(numer_row_kernel, order),
        "numer_row",
        scal,
        [r_hi, r_lo, g_all, u],
        [piece] * len(order),
    )


def numer_col(scal, r_hi, r_lo, row_factors, u, arrived, shares):
    rows, tile = r_hi.shape[:2]
    factors = row_factors.shape[0]
    piece = jax.ShapeDtypeStruct((rows // shares, factors, tile), F32)
    return kernel_call(
        functools.partial(numer_col_kernel, rows),
        "numer_col",
        scal,
        [r_hi, r_lo, row_factors, u, arrived],
        [piece] * shares,
        [pltpu.VMEM((u.shape[0], factors, tile), F32)],
    )


def update_kernel(scal, factor_ref, mask, den, scale, *refs):
    terms, out = refs[:-1], refs[-1]
    per, _, tile = terms[0].shape
    c = scale[...]
    for t in range(per):
        at = slice(t * tile, (t + 1) * tile)
        live = mask[pl.ds(scal[0] * per + t, 1), :]
        numer = terms[0][t]
        for term in terms[1:]:
            numer = numer + term[t]
        old = factor_ref[:, at]
        lower = jnp.where(live > 0, den[:, t : t + 1] * live, 1.0)
        out[:, at] = jnp.where(live > 0, old * (numer * c * c) / lower, old)


def update(scal, factors, mask, den, scale, terms):
    count = factors.shape[0]
    per, _, tile = terms[0].shape
    specs = [pl.BlockSpec((count, per * tile), lambda i, scal: (0, scal[0]))]
    specs += [vmem() for _ in range(3 + len(terms))]
    return kernel_call(
        update_kernel,
        "update",
        scal,
        [factors, mask, den, scale, *terms],
        [jax.ShapeDtypeStruct((count, per * tile), F32)],
        specs=specs,
    )[0]


def xor_exchange(x, axis, k):
    return lax.ppermute(x, axis, [(i, i ^ k) for i in range(lax.axis_size(axis))])


def both_sides(x):
    size = lax.axis_size("genome")
    me = lax.axis_index("genome")
    a = lax.ppermute(x, "genome", [(i, i ^ 1) for i in range(size)])
    b = lax.ppermute(x, "genome", [(i, (((i + 1) ^ 1) - 1) % size) for i in range(size)])
    even = me % 2 == 0
    return jnp.where(even, a, b), jnp.where(even, b, a)


def scatter_terms(pieces):
    size = lax.axis_size("offset")
    if size == 4:
        first = xor_exchange(pieces[EARLY], "offset", 1)
        mine = xor_exchange(pieces[1], "offset", 1)
        far = xor_exchange(pieces[3] + first, "offset", 3)
        return [pieces[0], mine, far]
    return [pieces[0]] + [xor_exchange(pieces[k], "offset", k) for k in range(1, size)]


def per_device(counts, band_offset, bin_mask, row_factors, col_factors):
    rows, slots, tile = counts.shape[:3]
    factors = row_factors.shape[0]
    offset_count = lax.axis_size("offset")
    genome_count = lax.axis_size("genome")
    g = lax.axis_index("genome")
    o = lax.axis_index("offset")
    reach = slots * offset_count - 1
    pad = reach + 1
    offs = band_offset.astype(jnp.int32)
    scal = jnp.concatenate([o.astype(jnp.int32).reshape(1), offs])
    has_next = g < genome_count - 1
    has_prev = g > 0

    mask = bin_mask.astype(F32).reshape(rows, tile)
    mask_next, _ = both_sides(mask[:pad])
    keep = has_next & (lax.broadcasted_iota(jnp.int32, (pad, 1), 0) < reach)
    mask_ext = jnp.concatenate([mask, jnp.where(keep, mask_next, 0.0)])

    ring_left = [(i, (i - 1) % genome_count) for i in range(genome_count)]
    col_next = lax.ppermute(col_factors[:, : pad * tile], "genome", ring_left)
    col_next = jnp.where(has_next, col_next, 1.0)
    col_ext = jnp.concatenate([col_factors, col_next], axis=1)

    scales = []
    parts = []
    source = counts
    ratios = []
    cut = [0] + [(rows * (3 * t + 3) // (8 * STEP)) * STEP for t in range(ITERS - 1)] + [rows]
    for t in range(ITERS):
        edge_v, edge, u = cover_edge(offs, source, mask_ext, parts, ratios[0] if ratios else None)
        scales.append(u[:rows])
        after, before = both_sides(edge)
        res = cover_main(offs, source, u, edge_v, t == 0)
        v = res[0]
        if t == 0:
            source = res[1]
        front = v[:pad] + jnp.where(has_prev, before[pad:], 0.0)
        back = v[rows:] + jnp.where(has_next, after[:pad], 0.0)
        x = jnp.concatenate([front, v[pad:rows], back])
        parts = [x] + [xor_exchange(x, "offset", k) for k in range(1, offset_count)]
        ratios = ratio(offs, source, row_factors, col_ext, x, ratios, cut[t], cut[t + 1] - cut[t])

    r_hi, r_lo = ratios
    u_ext, g_all, early, tail = numer_first(
        scal, r_hi, r_lo, row_factors, col_ext, mask_ext, parts
    )
    u = u_ext[:rows]
    scales.append(u)
    arrived = lax.ppermute(tail, "genome", [(i, (i + 1) % genome_count) for i in range(genome_count)])
    arrived = jnp.where(has_prev, arrived, 0.0)
    order = [k for k in (1, 3, 0, *range(4, offset_count))]
    rest = numer_row(scal, r_hi, r_lo, g_all, u_ext, order, offset_count)
    w_parts = dict(zip(order, rest)) | {EARLY: early}
    w_terms = scatter_terms([w_parts[k] for k in range(offset_count)])
    h_parts = numer_col(scal, r_hi, r_lo, row_factors, u_ext, arrived, offset_count)
    h_terms = scatter_terms(h_parts)

    live = mask > 0
    sums = [jnp.sum(mask)]
    for t in range(ITERS):
        sums.append(jnp.sum(jnp.where(live, scales[t] / jnp.where(live, scales[t + 1], 1.0), 0.0)))
    sums = jnp.broadcast_to(jnp.stack(sums)[:, None], (ITERS + 1, tile))
    k = 1
    while k < genome_count:
        sums = sums + xor_exchange(sums, "genome", k)
        k *= 2
    factor = sums[1, 0] / sums[0, 0]
    for t in range(1, ITERS):
        factor = factor * (sums[t + 1, 0] / sums[0, 0])
    bias = jnp.where(live, u * factor, 0.0).reshape(-1)

    per = rows // offset_count
    h_tile = jnp.sum(col_factors.reshape(factors, rows, tile) * mask[None], axis=2)
    w_tile = jnp.sum(row_factors.reshape(factors, rows, tile) * mask[None], axis=2)
    ends = jnp.concatenate([h_tile[:, :pad], w_tile[:, rows - pad :]], axis=1)
    after, before = both_sides(ends)
    h_long = jnp.concatenate([h_tile, jnp.where(has_next, after[:, :pad], 0.0)], axis=1)
    w_long = jnp.concatenate([jnp.where(has_prev, before[:, pad:], 0.0), w_tile], axis=1)
    first = o * per
    w_den = tree_sum([lax.dynamic_slice_in_dim(h_long, first + d, per, 1) for d in range(pad)])
    h_den = tree_sum([lax.dynamic_slice_in_dim(w_long, first + pad - d, per, 1) for d in range(pad)])

    scale = jnp.broadcast_to(factor.reshape(1, 1), (1, tile))
    row_update = update(scal, row_factors, mask, w_den, scale, w_terms)
    col_update = update(scal, col_factors, mask, h_den, scale, h_terms)
    return bias, row_update, col_update


def solution(mesh):
    return jax.shard_map(
        per_device,
        mesh=mesh,
        in_specs=(
            P("genome", "offset", None, None),
            P("offset"),
            P("genome"),
            P(None, "genome"),
            P(None, "genome"),
        ),
        out_specs=(P("genome"), P(None, ("genome", "offset")), P(None, ("genome", "offset"))),
        check_vma=False,
    )
```

time: 313 us -> 132 us (0.42)
  blocking collectives: 107 us -> 0 us
  matrix products: 45.3 us -> 0 us
  other arithmetic: 50.5 us -> 8.47 us
  Pallas kernels: 0 us -> 36 us
  between operations: 28.8 us -> 5.12 us
  waiting for transfers between devices: 36.7 us -> 18.7 us
  starting transfers between devices: 17 us -> 33.6 us
    psum x6 -> x0, blocking collectives: 107 us -> none  [the longest x3 56.5 us: per_device(): main_part, tail_part = lax.psum((main_part, tail_part), 'offset')]
    dot_general x6 -> x0, matrix products: 45.3 us -> none  [the longest x2 21.9 us: factor_terms(): model_tiles = jnp.einsum('kip,kiq->ipq', w_rows, h_cols, precision=highest)]
    pallas_call x0 -> x14, Pallas kernels: none -> 36 us  [kernel_call(): pl.pallas_call(body, grid_spec=pltpu.PrefetchScalarGridSpec(num_scalar_pr...]
    reduce_scatter x2 -> x0, waiting for transfers between devices: 32.4 us -> none  [the longest x1 28.2 us: per_device(): lax.psum_scatter(h_num.reshape(factor_count, -1), 'offset', scatter_dimen...]
    reduce_sum x12 -> x3, other arithmetic: 32 us -> 2 us  [the longest x1 0.71 us: per_device(): jnp.sum(jnp.where(live, scales[t] / jnp.where(live, scales[t + 1], 1.0),...]
    unnamed x28 -> x52, local copies, waits for them, and re-layouts: 7.07 us -> 29.2 us
    ppermute x10 -> x30, starting transfers between devices: 16.7 us -> 33.6 us  [the longest x18 21.5 us: xor_exchange(): lax.ppermute(x, axis, [(i, i ^ k) for i in range(lax.axis_size(axis))])]
    ppermute x10 -> x30, waiting for transfers between devices: 4.31 us -> 18.7 us  [the longest x18 14.1 us: xor_exchange(): lax.ppermute(x, axis, [(i, i ^ k) for i in range(lax.axis_size(axis))])]
  transfers between devices with their start and end apart: 12 -> 30, of which waited for: 8 -> 6; matrix products, arithmetic and copies ran while one was open for 27% -> 7% of each run, Pallas kernels for 0% -> 24%
where the time goes in v2:
time: 132 us
  Pallas kernels  36 us (27%)
  starting transfers between devices  33.6 us (25%)
  local copies, waits for them, and re-layouts  29.9 us (23%)
  waiting for transfers between devices  18.7 us (14%)
  other arithmetic  8.47 us (6%)
  between operations  5.12 us (4%)
    pallas_call x14, Pallas kernels, kernel_call(): pl.pallas_call(body, grid_spec=pltpu.PrefetchScalarGridSpec(num_scalar_pr...  36 us
    unnamed x52, local copies, waits for them, and re-layouts  29.2 us
    ppermute x18, starting transfers between devices, xor_exchange(): lax.ppermute(x, axis, [(i, i ^ k) for i in range(lax.axis_size(axis))])  21.5 us
    ppermute x18, waiting for transfers between devices, xor_exchange(): lax.ppermute(x, axis, [(i, i ^ k) for i in range(lax.axis_size(axis))])  14.1 us
    ppermute x5, starting transfers between devices, both_sides(): lax.ppermute(x, 'genome', [(i, ((i + 1 ^ 1) - 1) % size) for i in range(s...  8.91 us
    ppermute x1, waiting for transfers between devices, per_device(): lax.ppermute(tail, 'genome', [(i, (i + 1) % genome_count) for i in range(...  3.23 us
  transfers between devices with their start and end apart: 30, of which 6 were waited for; matrix products, arithmetic and copies ran while one was open for 7% of the time, Pallas kernels for 24%

profile of v2, /device:TPU:0, one launch (start us, length us, event | category | flops | bytes accessed | tf_op | source)
XLA Modules:
  0.0 131.8 jit_solution(3915573160332300742)
XLA Ops:
  0.6 0.8 convert_bitcast_fusion
  1.9 3.6 %collective-permute-start.1 = (f32[8,128]{1,0:T(8,128)S(1)}, f32[8,128]{1,0:T(8,128)S(1)}, u32[]{:S(2)}, u32[]{:S(2)}) collective-permute-start(f32[8,128]{1,0:T(8,128)S(1)} %slice_bitcast_fusion), channel_id=1, source_target_pairs={{0,28},{4,8},{8,4},{12,16},{16,12},{20,24},{24,20},{28,0},{1,29},{... | collective-permute-start | bytes 12296 | tf_op jit(solution)/shard_map/ppermute | solution.py:418
  5.4 1.3 collective-permute-done.1
  6.8 3.4 %copy-done.14 = s32[64,2,128,128]{3,2,1,0:T(8,128)S(1)} copy-done((s32[64,2,128,128]{3,2,1,0:T(8,128)S(1)}, s32[64,2,128,128]{3,2,1,0:T(8,128)}, u32[]{:S(2)}) %copy-start.14) | copy-done | bytes 8388632
  10.9 1.4 %cover_edge.3 = (f32[72,128]{1,0:T(8,128)S(1)}, f32[16,128]{1,0:T(8,128)S(1)}, f32[72,128]{1,0:T(8,128)S(1)}) custom-call(s32[2]{0:T(128)S(1)} %copy-done.17, s32[64,2,128,128]{3,2,1,0:T(8,128)S(1)} %copy-done.14, f32[72,128]{1,0:T(8,128)S(1)} %pad_maximum_fusion.1.mask), custom_call_target="tpu_custom_call" | custom-call | tf_op jit(solution)/shard_map/cover_edge/pallas_call | solution.py:47
  12.3 2.7 %collective-permute-start.3 = (f32[16,128]{1,0:T(8,128)S(1)}, f32[16,128]{1,0:T(8,128)S(1)}, u32[]{:S(2)}, u32[]{:S(2)}) collective-permute-start(f32[16,128]{1,0:T(8,128)S(1)} %get-tuple-element.35), channel_id=1, source_target_pairs={{0,28},{4,8},{8,4},{12,16},{16,12},{20,24},{24,20},{28,0},{1,29},{... | collective-permute-start | bytes 24584 | tf_op jit(solution)/shard_map/ppermute | solution.py:418
  15.6 3.4 %copy-done.15 = s32[64,2,128,128]{3,2,1,0:T(8,128)S(1)} copy-done((s32[64,2,128,128]{3,2,1,0:T(8,128)S(1)}, s32[64,2,128,128]{3,2,1,0:T(8,128)}, u32[]{:S(2)}) %copy-start.15) | copy-done | bytes 8388632
  18.9 3.4 %cover_main.3 = (f32[72,128]{1,0:T(8,128)S(1)}, f32[64,2,128,128]{3,2,1,0:T(8,128)S(1)}) custom-call(s32[2]{0:T(128)S(1)} %copy-done.18, s32[64,2,128,128]{3,2,1,0:T(8,128)S(1)} %copy-done.15, f32[72,128]{1,0:T(8,128)S(1)} %get-tuple-element.31.u_ref, f32[72,128]{1,0:T(8,128)S(1)} %get-tuple-element.32.edge_v), custom_call_target="tpu_custom_call" | custom-call | tf_op jit(solution)/shard_map/cover_main/pallas_call | solution.py:47
  22.4 2.0 %collective-permute-start.5 = (f32[72,128]{1,0:T(8,128)S(1)}, f32[72,128]{1,0:T(8,128)S(1)}, u32[]{:S(2)}, u32[]{:S(2)}) collective-permute-start(f32[72,128]{1,0:T(8,128)S(1)} %pad_maximum_fusion.2.after.refs_0_), channel_id=1, source_target_pairs={{0,1},{1,0},{2,3},{3,2},{4,5},{5,4},{6,7},{7,6},{8,9},{9,8},{10,11... | collective-permute-start | bytes 110600 | tf_op jit(solution)/shard_map/ppermute | solution.py:411
  24.4 2.3 %collective-permute-start.6 = (f32[72,128]{1,0:T(8,128)S(1)}, f32[72,128]{1,0:T(8,128)S(1)}, u32[]{:S(2)}, u32[]{:S(2)}) collective-permute-start(f32[72,128]{1,0:T(8,128)S(1)} %pad_maximum_fusion.2.after.refs_0_), channel_id=1, source_target_pairs={{0,2},{1,3},{2,0},{3,1},{4,6},{5,7},{6,4},{7,5},{8,10},{9,11},{10,... | collective-permute-start | bytes 110600 | tf_op jit(solution)/shard_map/ppermute | solution.py:411
  26.9 2.7 %ratio.3 = (bf16[64,128,256]{2,1,0:T(8,128)(2,1)S(1)}, bf16[64,128,256]{2,1,0:T(8,128)(2,1)S(1)}) custom-call(s32[2]{0:T(128)S(1)} %copy-done.18, f32[64,2,128,128]{3,2,1,0:T(8,128)S(1)} %get-tuple-element.33.kept.counts, f32[32,8192]{1,0:T(8,128)S(1)} %copy-done.13, f32[32,9216]{1,0:T(8,128)S(1)} %pad_maximum_fusion.h_ref, ...), custom_call_target="tpu_custom_call" | custom-call | tf_op jit(solution)/shard_map/ratio/pallas_call | solution.py:47
  29.9 2.6 %collective-permute-done.7.refs_3_ = f32[72,128]{1,0:T(8,128)S(1)} collective-permute-done((f32[72,128]{1,0:T(8,128)S(1)}, f32[72,128]{1,0:T(8,128)S(1)}, u32[]{:S(2)}, u32[]{:S(2)}) %collective-permute-start.7) | collective-permute-done | bytes 36896 | tf_op jit(solution)/shard_map/ppermute | solution.py:411
  32.4 1.4 %cover_edge.4 = (f32[72,128]{1,0:T(8,128)S(1)}, f32[16,128]{1,0:T(8,128)S(1)}, f32[72,128]{1,0:T(8,128)S(1)}) custom-call(s32[2]{0:T(128)S(1)} %copy-done.18, f32[64,2,128,128]{3,2,1,0:T(8,128)S(1)} %get-tuple-element.33.kept.counts, f32[72,128]{1,0:T(8,128)S(1)} %pad_maximum_fusion.1.mask, f32[72,128]{1,0:T(8,128)S(1)} %pad_maximum_fusion.2.after.refs_0_, ...), custom_call_target="tpu_custom_call" | custom-call | tf_op jit(solution)/shard_map/cover_edge/pallas_call | solution.py:47
  33.9 2.1 %collective-permute-start.9 = (f32[16,128]{1,0:T(8,128)S(1)}, f32[16,128]{1,0:T(8,128)S(1)}, u32[]{:S(2)}, u32[]{:S(2)}) collective-permute-start(f32[16,128]{1,0:T(8,128)S(1)} %get-tuple-element.39), channel_id=1, source_target_pairs={{0,4},{4,0},{8,12},{12,8},{16,20},{20,16},{24,28},{28,24},{1,5},{5... | collective-permute-start | bytes 24584 | tf_op jit(solution)/shard_map/ppermute | solution.py:417
  36.7 3.2 %cover_main.4 = f32[72,128]{1,0:T(8,128)S(1)} custom-call(s32[2]{0:T(128)S(1)} %copy-done.18, f32[64,2,128,128]{3,2,1,0:T(8,128)S(1)} %get-tuple-element.33.kept.counts, f32[72,128]{1,0:T(8,128)S(1)} %get-tuple-element.37.u_ref, f32[72,128]{1,0:T(8,128)S(1)} %get-tuple-element.38.edge_v), custom_call_target="tpu_custom_call" | custom-call | tf_op jit(solution)/shard_map/cover_main/pallas_call | solution.py:47
  40.1 1.5 %collective-permute-start.11 = (f32[72,128]{1,0:T(8,128)S(1)}, f32[72,128]{1,0:T(8,128)S(1)}, u32[]{:S(2)}, u32[]{:S(2)}) collective-permute-start(f32[72,128]{1,0:T(8,128)S(1)} %pad_maximum_fusion.3.after.refs_0_), channel_id=1, source_target_pairs={{0,2},{1,3},{2,0},{3,1},{4,6},{5,7},{6,4},{7,5},{8,10},{9,11},{10,... | collective-permute-start | bytes 110600 | tf_op jit(solution)/shard_map/ppermute | solution.py:411
  41.5 2.9 %collective-permute-start.12 = (f32[72,128]{1,0:T(8,128)S(1)}, f32[72,128]{1,0:T(8,128)S(1)}, u32[]{:S(2)}, u32[]{:S(2)}) collective-permute-start(f32[72,128]{1,0:T(8,128)S(1)} %pad_maximum_fusion.3.after.refs_0_), channel_id=1, source_target_pairs={{0,3},{1,2},{2,1},{3,0},{4,7},{5,6},{6,5},{7,4},{8,11},{9,10},{10,... | collective-permute-start | bytes 110600 | tf_op jit(solution)/shard_map/ppermute | solution.py:411
  45.1 1.1 collective-permute-start.22
  46.2 2.7 %ratio.4 = (bf16[64,128,256]{2,1,0:T(8,128)(2,1)S(1)}, bf16[64,128,256]{2,1,0:T(8,128)(2,1)S(1)}) custom-call(s32[2]{0:T(128)S(1)} %copy-done.18, f32[64,2,128,128]{3,2,1,0:T(8,128)S(1)} %get-tuple-element.33.kept.counts, f32[32,8192]{1,0:T(8,128)S(1)} %copy-done.13, ...), custom_call_target="tpu_custom_call", output_to_operand_aliasing={{0}: (5, {}), {1}: (6, {})} | custom-call | tf_op jit(solution)/shard_map/ratio/pallas_call | solution.py:47
  49.0 1.4 %cover_edge.5 = (f32[72,128]{1,0:T(8,128)S(1)}, f32[16,128]{1,0:T(8,128)S(1)}, f32[72,128]{1,0:T(8,128)S(1)}) custom-call(s32[2]{0:T(128)S(1)} %copy-done.18, f32[64,2,128,128]{3,2,1,0:T(8,128)S(1)} %get-tuple-element.33.kept.counts, f32[72,128]{1,0:T(8,128)S(1)} %pad_maximum_fusion.1.mask, f32[72,128]{1,0:T(8,128)S(1)} %pad_maximum_fusion.3.after.refs_0_, ...), custom_call_target="tpu_custom_call" | custom-call | tf_op jit(solution)/shard_map/cover_edge/pallas_call | solution.py:47
  51.0 1.2 copy-done.8
  52.2 1.6 %collective-permute-start.13 = (f32[16,128]{1,0:T(8,128)S(1)}, f32[16,128]{1,0:T(8,128)S(1)}, u32[]{:S(2)}, u32[]{:S(2)}) collective-permute-start(f32[16,128]{1,0:T(8,128)S(1)} %get-tuple-element.44), channel_id=1, source_target_pairs={{0,28},{4,8},{8,4},{12,16},{16,12},{20,24},{24,20},{28,0},{1,29},{... | collective-permute-start | bytes 24584 | tf_op jit(solution)/shard_map/ppermute | solution.py:418
  54.4 3.4 %copy-done.1 = f32[64,2,128,128]{3,2,1,0:T(8,128)S(1)} copy-done((f32[64,2,128,128]{3,2,1,0:T(8,128)S(1)}, f32[64,2,128,128]{3,2,1,0:T(8,128)}, u32[]{:S(2)}) %copy-start.1) | copy-done | bytes 8388632
  57.8 3.3 %cover_main.5 = f32[72,128]{1,0:T(8,128)S(1)} custom-call(s32[2]{0:T(128)S(1)} %copy-done.18, f32[64,2,128,128]{3,2,1,0:T(8,128)S(1)} %copy-done.1, f32[72,128]{1,0:T(8,128)S(1)} %get-tuple-element.42.u_ref, f32[72,128]{1,0:T(8,128)S(1)} %get-tuple-element.43.edge_v), custom_call_target="tpu_custom_call" | custom-call | tf_op jit(solution)/shard_map/cover_main/pallas_call | solution.py:47
  61.2 1.5 %collective-permute-start.16 = (f32[72,128]{1,0:T(8,128)S(1)}, f32[72,128]{1,0:T(8,128)}, u32[]{:S(2)}, u32[]{:S(2)}) collective-permute-start(f32[72,128]{1,0:T(8,128)S(1)} %pad_maximum_fusion.4.after.refs_0_), channel_id=1, source_target_pairs={{0,2},{1,3},{2,0},{3,1},{4,6},{5,7},{6,4},{7,5},{8,10},{9,11},{10,... | collective-permute-start | bytes 110600 | tf_op jit(solution)/shard_map/ppermute | solution.py:411
  62.7 2.9 %collective-permute-start.17 = (f32[72,128]{1,0:T(8,128)S(1)}, f32[72,128]{1,0:T(8,128)}, u32[]{:S(2)}, u32[]{:S(2)}) collective-permute-start(f32[72,128]{1,0:T(8,128)S(1)} %pad_maximum_fusion.4.after.refs_0_), channel_id=1, source_target_pairs={{0,3},{1,2},{2,1},{3,0},{4,7},{5,6},{6,5},{7,4},{8,11},{9,10},{10,... | collective-permute-start | bytes 110600 | tf_op jit(solution)/shard_map/ppermute | solution.py:411
  65.7 3.4 %copy-done.2 = f32[64,2,128,128]{3,2,1,0:T(8,128)S(1)} copy-done((f32[64,2,128,128]{3,2,1,0:T(8,128)S(1)}, f32[64,2,128,128]{3,2,1,0:T(8,128)}, u32[]{:S(2)}) %copy-start.2) | copy-done | bytes 8388632
  69.0 2.2 %copy-done.4 = bf16[64,128,256]{2,1,0:T(8,128)(2,1)S(1)} copy-done((bf16[64,128,256]{2,1,0:T(8,128)(2,1)S(1)}, bf16[64,128,256]{2,1,0:T(8,128)(2,1)}, u32[]{:S(2)}) %copy-start.4) | copy-done | bytes 4194328
  71.2 2.2 %copy-done.9 = bf16[64,128,256]{2,1,0:T(8,128)(2,1)S(1)} copy-done((bf16[64,128,256]{2,1,0:T(8,128)(2,1)S(1)}, bf16[64,128,256]{2,1,0:T(8,128)(2,1)}, u32[]{:S(2)}) %copy-start.9) | copy-done | bytes 4194328
  73.4 2.0 %ratio.5 = (bf16[64,128,256]{2,1,0:T(8,128)(2,1)S(1)}, bf16[64,128,256]{2,1,0:T(8,128)(2,1)S(1)}) custom-call(s32[2]{0:T(128)S(1)} %copy-done.18, f32[64,2,128,128]{3,2,1,0:T(8,128)S(1)} %copy-done.2, f32[32,8192]{1,0:T(8,128)S(1)} %copy-done.13, f32[32,9216]{1,0:T(8,128)S(1)} %pad_maximum_fusion.h_ref, ...), custom_call_target="tpu_custom_call", output_to_operand_aliasing={{0}: (5, {}), {1}: (6, {})} | custom-call | tf_op jit(solution)/shard_map/ratio/pallas_call | solution.py:47
  75.4 2.0 %copy-done.5 = bf16[64,128,256]{2,1,0:T(8,128)(2,1)} copy-done((bf16[64,128,256]{2,1,0:T(8,128)(2,1)}, bf16[64,128,256]{2,1,0:T(8,128)(2,1)S(1)}, u32[]{:S(2)}) %copy-start.5) | copy-done | bytes 4194328
  77.4 2.0 %copy-done.10 = bf16[64,128,256]{2,1,0:T(8,128)(2,1)} copy-done((bf16[64,128,256]{2,1,0:T(8,128)(2,1)}, bf16[64,128,256]{2,1,0:T(8,128)(2,1)S(1)}, u32[]{:S(2)}) %copy-start.10) | copy-done | bytes 4194328
  79.4 2.2 %copy-done.6 = bf16[64,128,256]{2,1,0:T(8,128)(2,1)S(1)} copy-done((bf16[64,128,256]{2,1,0:T(8,128)(2,1)S(1)}, bf16[64,128,256]{2,1,0:T(8,128)(2,1)}, u32[]{:S(2)}) %copy-start.6) | copy-done | bytes 4194328
  81.6 2.2 %copy-done.11 = bf16[64,128,256]{2,1,0:T(8,128)(2,1)S(1)} copy-done((bf16[64,128,256]{2,1,0:T(8,128)(2,1)S(1)}, bf16[64,128,256]{2,1,0:T(8,128)(2,1)}, u32[]{:S(2)}) %copy-start.11) | copy-done | bytes 4194328
  83.8 3.5 %numer_first.1 = (f32[72,128]{1,0:T(8,128)S(1)}, bf16[72,64,128]{2,1,0:T(8,128)(2,1)S(1)}, f32[16,32,128]{2,1,0:T(8,128)S(1)}, f32[8,32,128]{2,1,0:T(8,128)S(1)}) custom-call(s32[3]{0:T(128)S(1)} %pad_add_fusion.scal, bf16[64,128,256]{2,1,0:T(8,128)(2,1)S(1)} %copy-done.6, bf16[64,128,256]{2,1,0:T(8,128)(2,1)S(1)} %copy-done.11, f32[32,8192]{1,0:T(8,128)S(1)} %copy-done.13, ...), custom_call_target="tpu_custom_call" | custom-call | tf_op jit(solution)/shard_map/numer_first/pallas_call | solution.py:47
  88.0 2.6 %pad_maximum_fusion.6 = f32[4]{0:T(128)S(1)} fusion(f32[1]{0:T(128)} %bitcast.6, f32[1]{0:T(128)} %bitcast.5, f32[1]{0:T(128)} %bitcast.4, f32[1]{0:T(128)} %bitcast.3), kind=kLoop, calls=%fused_computation.58 | loop fusion | flops 12 | bytes 32 | tf_op jit(solution)/shard_map/stack | solution.py:495
  90.7 0.9 fusion.4
  92.2 1.5 %collective-permute-start.19 = (f32[4,128]{1,0:T(4,128)S(1)}, f32[4,128]{1,0:T(4,128)S(1)}, u32[]{:S(2)}, u32[]{:S(2)}) collective-permute-start(f32[4,128]{1,0:T(4,128)S(1)} %broadcast_add_fusion), channel_id=1, source_target_pairs={{0,8},{4,12},{8,0},{12,4},{16,24},{20,28},{24,16},{28,20},{1,9},{5... | collective-permute-start | bytes 6152 | tf_op jit(solution)/shard_map/ppermute | solution.py:411
  93.7 3.2 %collective-permute-done.26 = f32[8,32,128]{2,1,0:T(8,128)S(1)} collective-permute-done((f32[8,32,128]{2,1,0:T(8,128)S(1)}, f32[8,32,128]{2,1,0:T(8,128)S(1)}, u32[]{:S(2)}, u32[]{:S(2)}) %collective-permute-start.26) | collective-permute-done | bytes 131104 | tf_op jit(solution)/shard_map/ppermute | solution.py:482
  97.0 4.3 %numer_col.1 = (f32[16,32,128]{2,1,0:T(8,128)S(1)}, f32[16,32,128]{2,1,0:T(8,128)S(1)}, f32[16,32,128]{2,1,0:T(8,128)S(1)}, f32[16,32,128]{2,1,0:T(8,128)S(1)}) custom-call(s32[3]{0:T(128)S(1)} %pad_add_fusion.scal, bf16[64,128,256]{2,1,0:T(8,128)(2,1)S(1)} %copy-done.7, bf16[64,128,256]{2,1,0:T(8,128)(2,1)S(1)} %copy-done.12, f32[32,8192]{1,0:T(8,128)S(1)} %copy-done.13, ...), custom_call_target="tpu_custom_call" | custom-call | tf_op jit(solution)/shard_map/numer_col/pallas_call | solution.py:47
  102.4 3.9 %numer_row.1 = (f32[16,32,128]{2,1,0:T(8,128)S(1)}, f32[16,32,128]{2,1,0:T(8,128)S(1)}, f32[16,32,128]{2,1,0:T(8,128)S(1)}) custom-call(s32[3]{0:T(128)S(1)} %pad_add_fusion.scal, bf16[64,128,256]{2,1,0:T(8,128)(2,1)S(1)} %copy-done.7, bf16[64,128,256]{2,1,0:T(8,128)(2,1)S(1)} %copy-done.12, bf16[72,64,128]{2,1,0:T(8,128)(2,1)S(1)} %get-tuple-element.49.g_ref, ...), custom_call_target="tpu_custom_call" | custom-call | tf_op jit(solution)/shard_map/numer_row/pallas_call | solution.py:47
  106.3 2.0 %collective-permute-start.23 = (f32[16,32,128]{2,1,0:T(8,128)S(1)}, f32[16,32,128]{2,1,0:T(8,128)S(1)}, u32[]{:S(2)}, u32[]{:S(2)}) collective-permute-start(f32[16,32,128]{2,1,0:T(8,128)S(1)} %get-tuple-element.51), channel_id=1, source_target_pairs={{0,1},{1,0},{2,3},{3,2},{4,5},{5,4},{6,7},{7,6},{8,9},{9,8},{10,11... | collective-permute-start | bytes 786440 | tf_op jit(solution)/shard_map/ppermute | solution.py:411
  108.4 1.0 collective-permute-start.25
  109.4 3.0 %collective-permute-start.29 = (f32[16,32,128]{2,1,0:T(8,128)S(1)}, f32[16,32,128]{2,1,0:T(8,128)S(1)}, u32[]{:S(2)}, u32[]{:S(2)}) collective-permute-start(f32[16,32,128]{2,1,0:T(8,128)S(1)} %add.241), channel_id=1, source_target_pairs={{0,3},{1,2},{2,1},{3,0},{4,7},{5,6},{6,5},{7,4},{8,11},{9,10},{10,... | collective-permute-start | bytes 786440 | tf_op jit(solution)/shard_map/ppermute | solution.py:411
  117.7 9.6 %collective-permute-done.25.refs_2_ = f32[16,32,128]{2,1,0:T(8,128)S(1)} collective-permute-done((f32[16,32,128]{2,1,0:T(8,128)S(1)}, f32[16,32,128]{2,1,0:T(8,128)S(1)}, u32[]{:S(2)}, u32[]{:S(2)}) %collective-permute-start.25) | collective-permute-done | bytes 262176 | tf_op jit(solution)/shard_map/ppermute | solution.py:411
  127.3 1.4 %update.2 = f32[32,2048]{1,0:T(8,128)} custom-call(s32[3]{0:T(128)S(1)} %pad_add_fusion.scal, f32[32,8192]{1,0:T(8,128)S(1)} %copy-done.13, f32[64,128]{1,0:T(8,128)S(1)} %get-tuple-element.73.mask, f32[32,16]{1,0:T(8,128)S(1)} %get-tuple-element.80.den, f32[1,128]{1,0:T(1,128)S(1)} %broadcast_in_dim.59.scale, f32[16,32,128]{2,1,0:T(8,128)S(1)} %get-tuple-element.50.refs_0_, ...), custom_call_target="tpu_custom_call" | custom-call | tf_op jit(solution)/shard_map/update/pallas_call | solution.py:47
  128.7 1.7 %collective-permute-done.27.refs_1_ = f32[16,32,128]{2,1,0:T(8,128)S(1)} collective-permute-done((f32[16,32,128]{2,1,0:T(8,128)S(1)}, f32[16,32,128]{2,1,0:T(8,128)S(1)}, u32[]{:S(2)}, u32[]{:S(2)}) %collective-permute-start.27) | collective-permute-done | bytes 262176 | tf_op jit(solution)/shard_map/ppermute | solution.py:411
  130.4 1.4 %update.3 = f32[32,2048]{1,0:T(8,128)} custom-call(s32[3]{0:T(128)S(1)} %pad_add_fusion.scal, f32[32,8192]{1,0:T(8,128)S(1)} %copy-done.16, f32[64,128]{1,0:T(8,128)S(1)} %get-tuple-element.73.mask, f32[32,16]{1,0:T(8,128)S(1)} %get-tuple-element.79.den, f32[1,128]{1,0:T(1,128)S(1)} %broadcast_in_dim.59.scale, f32[16,32,128]{2,1,0:T(8,128)S(1)} %get-tuple-element.55.refs_0_, ...), custom_call_target="tpu_custom_call" | custom-call | tf_op jit(solution)/shard_map/update/pallas_call | solution.py:47
  (114 shorter events, 9.1 us)
Async XLA Ops:
  1.4 4.0 %collective-permute-start = (f32[8,128]{1,0:T(8,128)S(1)}, f32[8,128]{1,0:T(8,128)S(1)}, u32[]{:S(2)}, u32[]{:S(2)}) collective-permute-start(f32[8,128]{1,0:T(8,128)S(1)} %slice_bitcast_fusion), channel_id=1, source_target_pairs={{0,4},{4,0},{8,12},{12,8},{16,20},{20,16},{24,28},{28,24},{1,5},{5... | collective-permute-start | bytes 12296 | tf_op jit(solution)/shard_map/ppermute | solution.py:417
  1.9 4.9 %collective-permute-start.1 = (f32[8,128]{1,0:T(8,128)S(1)}, f32[8,128]{1,0:T(8,128)S(1)}, u32[]{:S(2)}, u32[]{:S(2)}) collective-permute-start(f32[8,128]{1,0:T(8,128)S(1)} %slice_bitcast_fusion), channel_id=1, source_target_pairs={{0,28},{4,8},{8,4},{12,16},{16,12},{20,24},{24,20},{28,0},{1,29},{... | collective-permute-start | bytes 12296 | tf_op jit(solution)/shard_map/ppermute | solution.py:418
  6.8 3.4 %copy-start.14 = (s32[64,2,128,128]{3,2,1,0:T(8,128)S(1)}, s32[64,2,128,128]{3,2,1,0:T(8,128)}, u32[]{:S(2)}) copy-start(s32[64,2,128,128]{3,2,1,0:T(8,128)} %counts.3) | copy-start | bytes 25165828
  10.9 4.1 %copy-start.16 = (f32[32,8192]{1,0:T(8,128)S(1)}, f32[32,8192]{1,0:T(8,128)}, u32[]{:S(2)}) copy-start(f32[32,8192]{1,0:T(8,128)} %factor_ref.3) | copy-start | bytes 3145732
  10.9 4.5 %copy-start.13 = (f32[32,8192]{1,0:T(8,128)S(1)}, f32[32,8192]{1,0:T(8,128)}, u32[]{:S(2)}) copy-start(f32[32,8192]{1,0:T(8,128)} %w_ref.9) | copy-start | bytes 3145732
  12.3 3.2 %copy-start.18 = (s32[2]{0:T(128)S(1)}, s32[2]{0:T(128)}, u32[]{:S(2)}) copy-start(s32[2]{0:T(128)} %offs.17) | copy-start | bytes 28
  12.3 10.0 %collective-permute-start.3 = (f32[16,128]{1,0:T(8,128)S(1)}, f32[16,128]{1,0:T(8,128)S(1)}, u32[]{:S(2)}, u32[]{:S(2)}) collective-permute-start(f32[16,128]{1,0:T(8,128)S(1)} %get-tuple-element.35), channel_id=1, source_target_pairs={{0,28},{4,8},{8,4},{12,16},{16,12},{20,24},{24,20},{28,0},{1,29},{... | collective-permute-start | bytes 24584 | tf_op jit(solution)/shard_map/ppermute | solution.py:418
  15.0 7.4 %collective-permute-start.4 = (f32[16,128]{1,0:T(8,128)S(1)}, f32[16,128]{1,0:T(8,128)S(1)}, u32[]{:S(2)}, u32[]{:S(2)}) collective-permute-start(f32[16,128]{1,0:T(8,128)S(1)} %get-tuple-element.35), channel_id=1, source_target_pairs={{0,4},{4,0},{8,12},{12,8},{16,20},{20,16},{24,28},{28,24},{1,5},{5... | collective-permute-start | bytes 24584 | tf_op jit(solution)/shard_map/ppermute | solution.py:417
  15.0 11.9 %collective-permute-start.2 = (f32[32,1024]{1,0:T(8,128)S(1)}, f32[32,1024]{1,0:T(8,128)S(1)}, u32[]{:S(2)}, u32[]{:S(2)}) collective-permute-start(f32[32,1024]{1,0:T(8,128)S(1)} %slice.102), channel_id=1, source_target_pairs={{0,28},{4,0},{8,4},{12,8},{16,12},{20,16},{24,20},{28,24},{1,29},{... | collective-permute-start | bytes 393224 | tf_op jit(solution)/shard_map/ppermute | solution.py:453
  15.5 3.4 %copy-start.15 = (s32[64,2,128,128]{3,2,1,0:T(8,128)S(1)}, s32[64,2,128,128]{3,2,1,0:T(8,128)}, u32[]{:S(2)}) copy-start(s32[64,2,128,128]{3,2,1,0:T(8,128)} %counts.3) | copy-start | bytes 25165828
  22.3 26.6 %copy-start = (f32[64,2,128,128]{3,2,1,0:T(8,128)}, f32[64,2,128,128]{3,2,1,0:T(8,128)S(1)}, u32[]{:S(2)}) copy-start(f32[64,2,128,128]{3,2,1,0:T(8,128)S(1)} %get-tuple-element.33.kept.counts) | copy-start | bytes 25165828
  22.4 7.3 %collective-permute-start.5 = (f32[72,128]{1,0:T(8,128)S(1)}, f32[72,128]{1,0:T(8,128)S(1)}, u32[]{:S(2)}, u32[]{:S(2)}) collective-permute-start(f32[72,128]{1,0:T(8,128)S(1)} %pad_maximum_fusion.2.after.refs_0_), channel_id=1, source_target_pairs={{0,1},{1,0},{2,3},{3,2},{4,5},{5,4},{6,7},{7,6},{8,9},{9,8},{10,11... | collective-permute-start | bytes 110600 | tf_op jit(solution)/shard_map/ppermute | solution.py:411
  24.4 5.5 %collective-permute-start.6 = (f32[72,128]{1,0:T(8,128)S(1)}, f32[72,128]{1,0:T(8,128)S(1)}, u32[]{:S(2)}, u32[]{:S(2)}) collective-permute-start(f32[72,128]{1,0:T(8,128)S(1)} %pad_maximum_fusion.2.after.refs_0_), channel_id=1, source_target_pairs={{0,2},{1,3},{2,0},{3,1},{4,6},{5,7},{6,4},{7,5},{8,10},{9,11},{10,... | collective-permute-start | bytes 110600 | tf_op jit(solution)/shard_map/ppermute | solution.py:411
  26.7 5.8 %collective-permute-start.7 = (f32[72,128]{1,0:T(8,128)S(1)}, f32[72,128]{1,0:T(8,128)S(1)}, u32[]{:S(2)}, u32[]{:S(2)}) collective-permute-start(f32[72,128]{1,0:T(8,128)S(1)} %pad_maximum_fusion.2.after.refs_0_), channel_id=1, source_target_pairs={{0,3},{1,2},{2,1},{3,0},{4,7},{5,6},{6,5},{7,4},{8,11},{9,10},{10,... | collective-permute-start | bytes 110600 | tf_op jit(solution)/shard_map/ppermute | solution.py:411
  33.8 6.1 %collective-permute-start.8 = (f32[16,128]{1,0:T(8,128)S(1)}, f32[16,128]{1,0:T(8,128)S(1)}, u32[]{:S(2)}, u32[]{:S(2)}) collective-permute-start(f32[16,128]{1,0:T(8,128)S(1)} %get-tuple-element.39), channel_id=1, source_target_pairs={{0,28},{4,8},{8,4},{12,16},{16,12},{20,24},{24,20},{28,0},{1,29},{... | collective-permute-start | bytes 24584 | tf_op jit(solution)/shard_map/ppermute | solution.py:418
  33.9 6.1 %collective-permute-start.9 = (f32[16,128]{1,0:T(8,128)S(1)}, f32[16,128]{1,0:T(8,128)S(1)}, u32[]{:S(2)}, u32[]{:S(2)}) collective-permute-start(f32[16,128]{1,0:T(8,128)S(1)} %get-tuple-element.39), channel_id=1, source_target_pairs={{0,4},{4,0},{8,12},{12,8},{16,20},{20,16},{24,28},{28,24},{1,5},{5... | collective-permute-start | bytes 24584 | tf_op jit(solution)/shard_map/ppermute | solution.py:417
  36.6 3.3 %copy-start.23 = (f32[32,64]{1,0:T(8,128)}, f32[32,64]{1,0:T(8,128)S(1)}, u32[]{:S(2)}) copy-start(f32[32,64]{1,0:T(8,128)S(1)} %get-tuple-element.63) | copy-start | bytes 24580
  36.6 7.9 %copy-start.21 = (f32[32,64]{1,0:T(8,128)}, f32[32,64]{1,0:T(8,128)S(1)}, u32[]{:S(2)}) copy-start(f32[32,64]{1,0:T(8,128)S(1)} %get-tuple-element.62) | copy-start | bytes 24580
  40.0 8.9 %collective-permute-start.10 = (f32[72,128]{1,0:T(8,128)S(1)}, f32[72,128]{1,0:T(8,128)S(1)}, u32[]{:S(2)}, u32[]{:S(2)}) collective-permute-start(f32[72,128]{1,0:T(8,128)S(1)} %pad_maximum_fusion.3.after.refs_0_), channel_id=1, source_target_pairs={{0,1},{1,0},{2,3},{3,2},{4,5},{5,4},{6,7},{7,6},{8,9},{9,8},{10,11... | collective-permute-start | bytes 110600 | tf_op jit(solution)/shard_map/ppermute | solution.py:411
  40.1 8.9 %collective-permute-start.11 = (f32[72,128]{1,0:T(8,128)S(1)}, f32[72,128]{1,0:T(8,128)S(1)}, u32[]{:S(2)}, u32[]{:S(2)}) collective-permute-start(f32[72,128]{1,0:T(8,128)S(1)} %pad_maximum_fusion.3.after.refs_0_), channel_id=1, source_target_pairs={{0,2},{1,3},{2,0},{3,1},{4,6},{5,7},{6,4},{7,5},{8,10},{9,11},{10,... | collective-permute-start | bytes 110600 | tf_op jit(solution)/shard_map/ppermute | solution.py:411
  41.5 7.4 %collective-permute-start.12 = (f32[72,128]{1,0:T(8,128)S(1)}, f32[72,128]{1,0:T(8,128)S(1)}, u32[]{:S(2)}, u32[]{:S(2)}) collective-permute-start(f32[72,128]{1,0:T(8,128)S(1)} %pad_maximum_fusion.3.after.refs_0_), channel_id=1, source_target_pairs={{0,3},{1,2},{2,1},{3,0},{4,7},{5,6},{6,5},{7,4},{8,11},{9,10},{10,... | collective-permute-start | bytes 110600 | tf_op jit(solution)/shard_map/ppermute | solution.py:411
  45.1 45.6 %collective-permute-start.21 = (f32[32,16]{1,0:T(8,128)}, f32[32,16]{1,0:T(8,128)}, u32[]{:S(2)}, u32[]{:S(2)}) collective-permute-start(f32[32,16]{1,0:T(8,128)} %pad_maximum_fusion.5), channel_id=1, source_target_pairs={{0,4},{4,0},{8,12},{12,8},{16,20},{20,16},{24,28},{28,24},{1,5},{5... | collective-permute-start | bytes 6152 | tf_op jit(solution)/shard_map/ppermute | solution.py:417
  45.1 45.6 %collective-permute-start.22 = (f32[32,16]{1,0:T(8,128)}, f32[32,16]{1,0:T(8,128)}, u32[]{:S(2)}, u32[]{:S(2)}) collective-permute-start(f32[32,16]{1,0:T(8,128)} %pad_maximum_fusion.5), channel_id=1, source_target_pairs={{0,28},{4,8},{8,4},{12,16},{16,12},{20,24},{24,20},{28,0},{1,29},{... | collective-permute-start | bytes 6152 | tf_op jit(solution)/shard_map/ppermute | solution.py:418
  48.9 3.3 %copy-start.8 = (bf16[64,128,256]{2,1,0:T(8,128)(2,1)}, bf16[64,128,256]{2,1,0:T(8,128)(2,1)S(1)}, u32[]{:S(2)}) copy-start(bf16[64,128,256]{2,1,0:T(8,128)(2,1)S(1)} %get-tuple-element.45.refs_1_) | copy-start | bytes 12582916
  48.9 4.8 %copy-start.19 = (s32[8192]{0:T(1024)S(1)}, s32[8192]{0:T(1024)}, u32[]{:S(2)}) copy-start(s32[8192]{0:T(1024)} %param.7) | copy-start | bytes 98308
  52.2 8.9 %collective-permute-start.13 = (f32[16,128]{1,0:T(8,128)S(1)}, f32[16,128]{1,0:T(8,128)S(1)}, u32[]{:S(2)}, u32[]{:S(2)}) collective-permute-start(f32[16,128]{1,0:T(8,128)S(1)} %get-tuple-element.44), channel_id=1, source_target_pairs={{0,28},{4,8},{8,4},{12,16},{16,12},{20,24},{24,20},{28,0},{1,29},{... | collective-permute-start | bytes 24584 | tf_op jit(solution)/shard_map/ppermute | solution.py:418
  53.7 7.3 %collective-permute-start.14 = (f32[16,128]{1,0:T(8,128)S(1)}, f32[16,128]{1,0:T(8,128)S(1)}, u32[]{:S(2)}, u32[]{:S(2)}) collective-permute-start(f32[16,128]{1,0:T(8,128)S(1)} %get-tuple-element.44), channel_id=1, source_target_pairs={{0,4},{4,0},{8,12},{12,8},{16,20},{20,16},{24,28},{28,24},{1,5},{5... | collective-permute-start | bytes 24584 | tf_op jit(solution)/shard_map/ppermute | solution.py:417
  54.4 3.4 %copy-start.1 = (f32[64,2,128,128]{3,2,1,0:T(8,128)S(1)}, f32[64,2,128,128]{3,2,1,0:T(8,128)}, u32[]{:S(2)}) copy-start(f32[64,2,128,128]{3,2,1,0:T(8,128)} %copy-done) | copy-start | bytes 25165828
  61.1 18.3 %collective-permute-start.15 = (f32[72,128]{1,0:T(8,128)S(1)}, f32[72,128]{1,0:T(8,128)S(1)}, u32[]{:S(2)}, u32[]{:S(2)}) collective-permute-start(f32[72,128]{1,0:T(8,128)S(1)} %pad_maximum_fusion.4.after.refs_0_), channel_id=1, source_target_pairs={{0,1},{1,0},{2,3},{3,2},{4,5},{5,4},{6,7},{7,6},{8,9},{9,8},{10,11... | collective-permute-start | bytes 110600 | tf_op jit(solution)/shard_map/ppermute | solution.py:411
  61.2 18.2 %collective-permute-start.16 = (f32[72,128]{1,0:T(8,128)S(1)}, f32[72,128]{1,0:T(8,128)}, u32[]{:S(2)}, u32[]{:S(2)}) collective-permute-start(f32[72,128]{1,0:T(8,128)S(1)} %pad_maximum_fusion.4.after.refs_0_), channel_id=1, source_target_pairs={{0,2},{1,3},{2,0},{3,1},{4,6},{5,7},{6,4},{7,5},{8,10},{9,11},{10,... | collective-permute-start | bytes 110600 | tf_op jit(solution)/shard_map/ppermute | solution.py:411
  62.7 16.7 %collective-permute-start.17 = (f32[72,128]{1,0:T(8,128)S(1)}, f32[72,128]{1,0:T(8,128)}, u32[]{:S(2)}, u32[]{:S(2)}) collective-permute-start(f32[72,128]{1,0:T(8,128)S(1)} %pad_maximum_fusion.4.after.refs_0_), channel_id=1, source_target_pairs={{0,3},{1,2},{2,1},{3,0},{4,7},{5,6},{6,5},{7,4},{8,11},{9,10},{10,... | collective-permute-start | bytes 110600 | tf_op jit(solution)/shard_map/ppermute | solution.py:411
  65.7 3.4 %copy-start.2 = (f32[64,2,128,128]{3,2,1,0:T(8,128)S(1)}, f32[64,2,128,128]{3,2,1,0:T(8,128)}, u32[]{:S(2)}) copy-start(f32[64,2,128,128]{3,2,1,0:T(8,128)} %copy-done) | copy-start | bytes 25165828
  79.4 2.2 %copy-start.6 = (bf16[64,128,256]{2,1,0:T(8,128)(2,1)S(1)}, bf16[64,128,256]{2,1,0:T(8,128)(2,1)}, u32[]{:S(2)}) copy-start(bf16[64,128,256]{2,1,0:T(8,128)(2,1)} %copy-done.5) | copy-start | bytes 12582916
  83.8 3.5 %copy-start.20 = (s32[8192]{0:T(1024)S(1)}, s32[8192]{0:T(1024)}, u32[]{:S(2)}) copy-start(s32[8192]{0:T(1024)} %param.7) | copy-start | bytes 98308
  83.8 13.2 %copy-start.7 = (bf16[64,128,256]{2,1,0:T(8,128)(2,1)S(1)}, bf16[64,128,256]{2,1,0:T(8,128)(2,1)}, u32[]{:S(2)}) copy-start(bf16[64,128,256]{2,1,0:T(8,128)(2,1)} %copy-done.5) | copy-start | bytes 12582916
  83.8 13.2 %copy-start.12 = (bf16[64,128,256]{2,1,0:T(8,128)(2,1)S(1)}, bf16[64,128,256]{2,1,0:T(8,128)(2,1)}, u32[]{:S(2)}) copy-start(bf16[64,128,256]{2,1,0:T(8,128)(2,1)} %copy-done.10) | copy-start | bytes 12582916
  90.7 1.4 %collective-permute-start.18 = (f32[4,128]{1,0:T(4,128)S(1)}, f32[4,128]{1,0:T(4,128)S(1)}, u32[]{:S(2)}, u32[]{:S(2)}) collective-permute-start(f32[4,128]{1,0:T(4,128)S(1)} %broadcast_in_dim.57), channel_id=1, source_target_pairs={{0,4},{4,0},{8,12},{12,8},{16,20},{20,16},{24,28},{28,24},{1,5},{5... | collective-permute-start | bytes 6152 | tf_op jit(solution)/shard_map/ppermute | solution.py:411
  91.6 5.3 %collective-permute-start.26 = (f32[8,32,128]{2,1,0:T(8,128)S(1)}, f32[8,32,128]{2,1,0:T(8,128)S(1)}, u32[]{:S(2)}, u32[]{:S(2)}) collective-permute-start(f32[8,32,128]{2,1,0:T(8,128)S(1)} %get-tuple-element.54), channel_id=1, source_target_pairs={{0,4},{4,8},{8,12},{12,16},{16,20},{20,24},{24,28},{28,0},{1,5},{5... | collective-permute-start | bytes 393224 | tf_op jit(solution)/shard_map/ppermute | solution.py:482
  92.1 16.2 %collective-permute-start.24 = (f32[16,32,128]{2,1,0:T(8,128)S(1)}, f32[16,32,128]{2,1,0:T(8,128)S(1)}, u32[]{:S(2)}, u32[]{:S(2)}) collective-permute-start(f32[16,32,128]{2,1,0:T(8,128)S(1)} %get-tuple-element.53), channel_id=1, source_target_pairs={{0,1},{1,0},{2,3},{3,2},{4,5},{5,4},{6,7},{7,6},{8,9},{9,8},{10,11... | collective-permute-start | bytes 786440 | tf_op jit(solution)/shard_map/ppermute | solution.py:411
  92.2 9.2 %collective-permute-start.19 = (f32[4,128]{1,0:T(4,128)S(1)}, f32[4,128]{1,0:T(4,128)S(1)}, u32[]{:S(2)}, u32[]{:S(2)}) collective-permute-start(f32[4,128]{1,0:T(4,128)S(1)} %broadcast_add_fusion), channel_id=1, source_target_pairs={{0,8},{4,12},{8,0},{12,4},{16,24},{20,28},{24,16},{28,20},{1,9},{5... | collective-permute-start | bytes 6152 | tf_op jit(solution)/shard_map/ppermute | solution.py:411
  97.0 5.0 %copy-start.22 = (f32[32,64]{1,0:T(8,128)S(1)}, f32[32,64]{1,0:T(8,128)}, u32[]{:S(2)}) copy-start(f32[32,64]{1,0:T(8,128)} %copy-done.21) | copy-start | bytes 24580
  97.0 5.0 %copy-start.24 = (f32[32,64]{1,0:T(8,128)S(1)}, f32[32,64]{1,0:T(8,128)}, u32[]{:S(2)}) copy-start(f32[32,64]{1,0:T(8,128)} %copy-done.23) | copy-start | bytes 24580
  101.3 8.1 %collective-permute-start.28 = (f32[16,32,128]{2,1,0:T(8,128)S(1)}, f32[16,32,128]{2,1,0:T(8,128)S(1)}, u32[]{:S(2)}, u32[]{:S(2)}) collective-permute-start(f32[16,32,128]{2,1,0:T(8,128)S(1)} %get-tuple-element.58), channel_id=1, source_target_pairs={{0,1},{1,0},{2,3},{3,2},{4,5},{5,4},{6,7},{7,6},{8,9},{9,8},{10,11... | collective-permute-start | bytes 786440 | tf_op jit(solution)/shard_map/ppermute | solution.py:411
  101.5 6.8 %collective-permute-start.20 = (f32[4,128]{1,0:T(4,128)S(1)}, f32[4,128]{1,0:T(4,128)S(1)}, u32[]{:S(2)}, u32[]{:S(2)}) collective-permute-start(f32[4,128]{1,0:T(4,128)S(1)} %fusion.23), channel_id=1, source_target_pairs={{0,16},{4,20},{8,24},{12,28},{16,0},{20,4},{24,8},{28,12},{1,17},{... | collective-permute-start | bytes 6152 | tf_op jit(solution)/shard_map/ppermute | solution.py:411
  106.3 11.4 %collective-permute-start.23 = (f32[16,32,128]{2,1,0:T(8,128)S(1)}, f32[16,32,128]{2,1,0:T(8,128)S(1)}, u32[]{:S(2)}, u32[]{:S(2)}) collective-permute-start(f32[16,32,128]{2,1,0:T(8,128)S(1)} %get-tuple-element.51), channel_id=1, source_target_pairs={{0,1},{1,0},{2,3},{3,2},{4,5},{5,4},{6,7},{7,6},{8,9},{9,8},{10,11... | collective-permute-start | bytes 786440 | tf_op jit(solution)/shard_map/ppermute | solution.py:411
  108.3 22.1 %collective-permute-start.27 = (f32[16,32,128]{2,1,0:T(8,128)S(1)}, f32[16,32,128]{2,1,0:T(8,128)S(1)}, u32[]{:S(2)}, u32[]{:S(2)}) collective-permute-start(f32[16,32,128]{2,1,0:T(8,128)S(1)} %get-tuple-element.56), channel_id=1, source_target_pairs={{0,1},{1,0},{2,3},{3,2},{4,5},{5,4},{6,7},{7,6},{8,9},{9,8},{10,11... | collective-permute-start | bytes 786440 | tf_op jit(solution)/shard_map/ppermute | solution.py:411
  108.4 18.9 %collective-permute-start.25 = (f32[16,32,128]{2,1,0:T(8,128)S(1)}, f32[16,32,128]{2,1,0:T(8,128)S(1)}, u32[]{:S(2)}, u32[]{:S(2)}) collective-permute-start(f32[16,32,128]{2,1,0:T(8,128)S(1)} %add.231), channel_id=1, source_target_pairs={{0,3},{1,2},{2,1},{3,0},{4,7},{5,6},{6,5},{7,4},{8,11},{9,10},{10,... | collective-permute-start | bytes 786440 | tf_op jit(solution)/shard_map/ppermute | solution.py:411
  109.4 20.9 %collective-permute-start.29 = (f32[16,32,128]{2,1,0:T(8,128)S(1)}, f32[16,32,128]{2,1,0:T(8,128)S(1)}, u32[]{:S(2)}, u32[]{:S(2)}) collective-permute-start(f32[16,32,128]{2,1,0:T(8,128)S(1)} %add.241), channel_id=1, source_target_pairs={{0,3},{1,2},{2,1},{3,0},{4,7},{5,6},{6,5},{7,4},{8,11},{9,10},{10,... | collective-permute-start | bytes 786440 | tf_op jit(solution)/shard_map/ppermute | solution.py:411
  (7 other events, 13.3 us)

commit v3 on v2

--- a/solution.py
+++ b/solution.py
@@ -292,7 +292,10 @@
     lax.fori_loop(0, per, body, 0, unroll=4)
 
 
-def numer_row_kernel(order, scal, hi_ref, lo_ref, g_ref, u_ref, *outs):
+def numer_row_kernel(order, rows, scal, hi_ref, lo_ref, g_ref, *refs):
+    scales = refs[: ITERS + 1]
+    sums_out, outs = refs[ITERS + 1], refs[ITERS + 2 :]
+    u_ref = scales[-1]
     offs = [scal[1 + s] for s in range(hi_ref.shape[2] // u_ref.shape[1])]
     per = outs[0].shape[0]
     for k, out in zip(order, outs):
@@ -303,9 +306,18 @@
             return carry
 
         lax.fori_loop(0, per, body, 0, unroll=4)
-
-
-def numer_col_kernel(rows, scal, hi_ref, lo_ref, w_ref, u_ref, arrived, *refs):
+    sums_out[...] = jnp.zeros_like(sums_out)
+    mask = scales[0][:rows]
+    totals = [mask]
+    for t in range(ITERS):
+        below = jnp.where(mask > 0, scales[t + 1][:rows], 1.0)
+        totals.append(jnp.where(mask > 0, scales[t][:rows] / below, 0.0))
+    for t, total in enumerate(totals):
+        line = jnp.sum(jnp.sum(total, axis=0, keepdims=True), axis=1, keepdims=True)
+        sums_out[t : t + 1, :] = jnp.broadcast_to(line, (1, mask.shape[1]))
+
+
+def numer_col_kernel(rows, scal, hi_ref, lo_ref, w_ref, u_ref, arrived, after, *refs):
     outs, acc = refs[:-1], refs[-1]
     offs = [scal[1 + s] for s in range(hi_ref.shape[2] // u_ref.shape[1])]
     per = outs[0].shape[0]
@@ -351,19 +363,20 @@
     )
 
 
-def numer_row(scal, r_hi, r_lo, g_all, u, order, shares):
+def numer_row(scal, r_hi, r_lo, g_all, scales, order, shares):
     rows, tile = r_hi.shape[:2]
     piece = jax.ShapeDtypeStruct((rows // shares, g_all.shape[1] // 2, tile), F32)
-    return kernel_call(
-        functools.partial(numer_row_kernel, order),
+    res = kernel_call(
+        functools.partial(numer_row_kernel, order, rows),
         "numer_row",
         scal,
-        [r_hi, r_lo, g_all, u],
-        [piece] * len(order),
-    )
-
-
-def numer_col(scal, r_hi, r_lo, row_factors, u, arrived, shares):
+        [r_hi, r_lo, g_all, *scales],
+        [jax.ShapeDtypeStruct((8, tile), F32)] + [piece] * len(order),
+    )
+    return res[0], res[1:]
+
+
+def numer_col(scal, r_hi, r_lo, row_factors, u, arrived, shares, after):
     rows, tile = r_hi.shape[:2]
     factors = row_factors.shape[0]
     piece = jax.ShapeDtypeStruct((rows // shares, factors, tile), F32)
@@ -371,16 +384,25 @@
         functools.partial(numer_col_kernel, rows),
         "numer_col",
         scal,
-        [r_hi, r_lo, row_factors, u, arrived],
+        [r_hi, r_lo, row_factors, u, arrived, after],
         [piece] * shares,
         [pltpu.VMEM((u.shape[0], factors, tile), F32)],
     )
 
 
-def update_kernel(scal, factor_ref, mask, den, scale, *refs):
+def mean_scale(sums):
+    scale = sums[1:2, :] / sums[0:1, :]
+    for t in range(1, ITERS):
+        scale = scale * (sums[t + 1 : t + 2, :] / sums[0:1, :])
+    return scale
+
+
+def update_kernel(scal, factor_ref, mask, den, sums, *refs):
     terms, out = refs[:-1], refs[-1]
     per, _, tile = terms[0].shape
-    c = scale[...]
+    c = mean_scale(sums[...])
+    lanes = den.shape[1]
+    den_here = pltpu.roll(den[...], lax.rem(lanes - scal[0] * per, lanes), 1)
     for t in range(per):
         at = slice(t * tile, (t + 1) * tile)
         live = mask[pl.ds(scal[0] * per + t, 1), :]
@@ -388,11 +410,11 @@
         for term in terms[1:]:
             numer = numer + term[t]
         old = factor_ref[:, at]
-        lower = jnp.where(live > 0, den[:, t : t + 1] * live, 1.0)
+        lower = jnp.where(live > 0, den_here[:, t : t + 1] * live, 1.0)
         out[:, at] = jnp.where(live > 0, old * (numer * c * c) / lower, old)
 
 
-def update(scal, factors, mask, den, scale, terms):
+def update(scal, factors, mask, den, sums, terms):
     count = factors.shape[0]
     per, _, tile = terms[0].shape
     specs = [pl.BlockSpec((count, per * tile), lambda i, scal: (0, scal[0]))]
@@ -401,7 +423,7 @@
         update_kernel,
         "update",
         scal,
-        [factors, mask, den, scale, *terms],
+        [factors, mask, den, sums, *terms],
         [jax.ShapeDtypeStruct((count, per * tile), F32)],
         specs=specs,
     )[0]
@@ -411,13 +433,11 @@
     return lax.ppermute(x, axis, [(i, i ^ k) for i in range(lax.axis_size(axis))])
 
 
-def both_sides(x):
+def both_sides(x, even):
     size = lax.axis_size("genome")
-    me = lax.axis_index("genome")
     a = lax.ppermute(x, "genome", [(i, i ^ 1) for i in range(size)])
     b = lax.ppermute(x, "genome", [(i, (((i + 1) ^ 1) - 1) % size) for i in range(size)])
-    even = me % 2 == 0
-    return jnp.where(even, a, b), jnp.where(even, b, a)
+    return jnp.where(even > 0, a, b), jnp.where(even > 0, b, a)
 
 
 def scatter_terms(pieces):
@@ -436,22 +456,27 @@
     offset_count = lax.axis_size("offset")
     genome_count = lax.axis_size("genome")
     g = lax.axis_index("genome")
-    o = lax.axis_index("offset")
+    o = lax.axis_index("offset").astype(jnp.int32)
     reach = slots * offset_count - 1
     pad = reach + 1
-    offs = band_offset.astype(jnp.int32)
-    scal = jnp.concatenate([o.astype(jnp.int32).reshape(1), offs])
-    has_next = g < genome_count - 1
-    has_prev = g > 0
+
+    line = jnp.broadcast_to(g, (1, tile))
+    even = (line % 2 == 0).astype(F32)
+    has_next = (line < genome_count - 1).astype(F32)
+    has_prev = (line > 0).astype(F32)
+    flags = jnp.concatenate([even, has_next, has_prev])
+    scal = jnp.concatenate([jnp.broadcast_to(o, (1,)), band_offset])
+    flags, scal, band_offset = lax.optimization_barrier((flags, scal, band_offset))
+    even, has_next, has_prev = flags[0:1], flags[1:2], flags[2:3]
 
     mask = bin_mask.astype(F32).reshape(rows, tile)
-    mask_next, _ = both_sides(mask[:pad])
-    keep = has_next & (lax.broadcasted_iota(jnp.int32, (pad, 1), 0) < reach)
-    mask_ext = jnp.concatenate([mask, jnp.where(keep, mask_next, 0.0)])
+    mask_next, _ = both_sides(mask[:pad], even)
+    keep = lax.broadcasted_iota(jnp.int32, (pad, 1), 0) < reach
+    mask_ext = jnp.concatenate([mask, jnp.where(keep, mask_next * has_next, 0.0)])
 
     ring_left = [(i, (i - 1) % genome_count) for i in range(genome_count)]
     col_next = lax.ppermute(col_factors[:, : pad * tile], "genome", ring_left)
-    col_next = jnp.where(has_next, col_next, 1.0)
+    col_next = jnp.where(has_next[:, :1] > 0, col_next, 1.0)
     col_ext = jnp.concatenate([col_factors, col_next], axis=1)
 
     scales = []
@@ -460,62 +485,55 @@
     ratios = []
     cut = [0] + [(rows * (3 * t + 3) // (8 * STEP)) * STEP for t in range(ITERS - 1)] + [rows]
     for t in range(ITERS):
-        edge_v, edge, u = cover_edge(offs, source, mask_ext, parts, ratios[0] if ratios else None)
-        scales.append(u[:rows])
-        after, before = both_sides(edge)
-        res = cover_main(offs, source, u, edge_v, t == 0)
+        edge_v, edge, u = cover_edge(
+            band_offset, source, mask_ext, parts, ratios[0] if ratios else None
+        )
+        scales.append(u)
+        after, before = both_sides(edge, even)
+        res = cover_main(band_offset, source, u, edge_v, t == 0)
         v = res[0]
         if t == 0:
             source = res[1]
-        front = v[:pad] + jnp.where(has_prev, before[pad:], 0.0)
-        back = v[rows:] + jnp.where(has_next, after[:pad], 0.0)
+        front = v[:pad] + before[pad:] * has_prev
+        back = v[rows:] + after[:pad] * has_next
         x = jnp.concatenate([front, v[pad:rows], back])
         parts = [x] + [xor_exchange(x, "offset", k) for k in range(1, offset_count)]
-        ratios = ratio(offs, source, row_factors, col_ext, x, ratios, cut[t], cut[t + 1] - cut[t])
+        ratios = ratio(
+            band_offset, source, row_factors, col_ext, x, ratios, cut[t], cut[t + 1] - cut[t]
+        )
 
     r_hi, r_lo = ratios
-    u_ext, g_all, early, tail = numer_first(
-        scal, r_hi, r_lo, row_factors, col_ext, mask_ext, parts
-    )
-    u = u_ext[:rows]
+    u, g_all, early, tail = numer_first(scal, r_hi, r_lo, row_factors, col_ext, mask_ext, parts)
     scales.append(u)
-    arrived = lax.ppermute(tail, "genome", [(i, (i + 1) % genome_count) for i in range(genome_count)])
-    arrived = jnp.where(has_prev, arrived, 0.0)
+    ring_right = [(i, (i + 1) % genome_count) for i in range(genome_count)]
+    arrived = lax.ppermute(tail, "genome", ring_right) * has_prev
     order = [k for k in (1, 3, 0, *range(4, offset_count))]
-    rest = numer_row(scal, r_hi, r_lo, g_all, u_ext, order, offset_count)
+    sums, rest = numer_row(scal, r_hi, r_lo, g_all, scales, order, offset_count)
     w_parts = dict(zip(order, rest)) | {EARLY: early}
     w_terms = scatter_terms([w_parts[k] for k in range(offset_count)])
-    h_parts = numer_col(scal, r_hi, r_lo, row_factors, u_ext, arrived, offset_count)
+    h_parts = numer_col(scal, r_hi, r_lo, row_factors, u, arrived, offset_count, rest[0])
     h_terms = scatter_terms(h_parts)
 
-    live = mask > 0
-    sums = [jnp.sum(mask)]
-    for t in range(ITERS):
-        sums.append(jnp.sum(jnp.where(live, scales[t] / jnp.where(live, scales[t + 1], 1.0), 0.0)))
-    sums = jnp.broadcast_to(jnp.stack(sums)[:, None], (ITERS + 1, tile))
     k = 1
     while k < genome_count:
         sums = sums + xor_exchange(sums, "genome", k)
         k *= 2
-    factor = sums[1, 0] / sums[0, 0]
-    for t in range(1, ITERS):
-        factor = factor * (sums[t + 1, 0] / sums[0, 0])
-    bias = jnp.where(live, u * factor, 0.0).reshape(-1)
-
-    per = rows // offset_count
+    bias = (u[:rows] * mean_scale(sums)).reshape(-1)
+
     h_tile = jnp.sum(col_factors.reshape(factors, rows, tile) * mask[None], axis=2)
     w_tile = jnp.sum(row_factors.reshape(factors, rows, tile) * mask[None], axis=2)
     ends = jnp.concatenate([h_tile[:, :pad], w_tile[:, rows - pad :]], axis=1)
-    after, before = both_sides(ends)
-    h_long = jnp.concatenate([h_tile, jnp.where(has_next, after[:, :pad], 0.0)], axis=1)
-    w_long = jnp.concatenate([jnp.where(has_prev, before[:, pad:], 0.0), w_tile], axis=1)
-    first = o * per
-    w_den = tree_sum([lax.dynamic_slice_in_dim(h_long, first + d, per, 1) for d in range(pad)])
-    h_den = tree_sum([lax.dynamic_slice_in_dim(w_long, first + pad - d, per, 1) for d in range(pad)])
-
-    scale = jnp.broadcast_to(factor.reshape(1, 1), (1, tile))
-    row_update = update(scal, row_factors, mask, w_den, scale, w_terms)
-    col_update = update(scal, col_factors, mask, h_den, scale, h_terms)
+    after, before = both_sides(ends, even[:, :1])
+    h_long = jnp.concatenate([h_tile, after[:, :pad] * has_next[:, :1]], axis=1)
+    w_long = jnp.concatenate([before[:, pad:] * has_prev[:, :1], w_tile], axis=1)
+    w_den = tree_sum([h_long[:, d : d + rows] for d in range(pad)])
+    h_den = tree_sum([w_long[:, pad - d : pad - d + rows] for d in range(pad)])
+    fill = ((0, 0), (0, -rows % tile))
+    w_den = jnp.pad(w_den, fill)
+    h_den = jnp.pad(h_den, fill)
+
+    row_update = update(scal, row_factors, mask, w_den, sums, w_terms)
+    col_update = update(scal, col_factors, mask, h_den, sums, h_terms)
     return bias, row_update, col_update
 
 

time: 132 us -> 108 us (0.82)
  local copies, waits for them, and re-layouts: 29.9 us -> 6.04 us
  waiting for transfers between devices: 18.7 us -> 24.2 us
  other arithmetic: 8.47 us -> 4.83 us
  between operations: 5.12 us -> 2.38 us
    unnamed x52 -> x10, local copies, waits for them, and re-layouts: 29.2 us -> 4.42 us
    ppermute x18, waiting for transfers between devices: 14.1 us -> 24.2 us  [xor_exchange(): lax.ppermute(x, axis, [(i, i ^ k) for i in range(lax.axis_size(axis))])]
    ppermute x1, waiting for transfers between devices: 3.23 us -> 0.01 us  [per_device(): arrived = lax.ppermute(tail, 'genome', ring_right) * has_prev]
    another operation x1 -> x0, other arithmetic: 2.64 us -> none  [per_device(): sums = jnp.broadcast_to(jnp.stack(sums)[:, None], (ITERS + 1, tile))]
    ppermute x18, starting transfers between devices: 21.5 us -> 23.9 us  [xor_exchange(): lax.ppermute(x, axis, [(i, i ^ k) for i in range(lax.axis_size(axis))])]
    reduce_sum x2 -> x0, other arithmetic: 1.39 us -> none  [the longest x1 0.71 us: per_device(): jnp.sum(jnp.where(live, scales[t] / jnp.where(live, scales[t + 1], 1.0),...]
    mul x0 -> x3, other arithmetic: none -> 1.38 us  [the longest x1 1.37 us: per_device(): before[:, pad:] * has_prev[:, :1]]
  transfers between devices with their start and end apart: 30 -> 30, of which waited for: 6 -> 6; matrix products, arithmetic and copies ran while one was open for 7% -> 6% of each run, Pallas kernels for 24% -> 29%
where the time goes in v3:
time: 108 us
  Pallas kernels  35.7 us (33%)
  starting transfers between devices  34.6 us (32%)
  waiting for transfers between devices  24.2 us (22%)
  local copies, waits for them, and re-layouts  6.04 us (6%)
  other arithmetic  4.83 us (4%)
  between operations  2.38 us (2%)
    pallas_call x14, Pallas kernels, kernel_call(): pl.pallas_call(body, grid_spec=pltpu.PrefetchScalarGridSpec(num_scalar_pr...  35.7 us
    ppermute x18, waiting for transfers between devices, xor_exchange(): lax.ppermute(x, axis, [(i, i ^ k) for i in range(lax.axis_size(axis))])  24.2 us
    ppermute x18, starting transfers between devices, xor_exchange(): lax.ppermute(x, axis, [(i, i ^ k) for i in range(lax.axis_size(axis))])  23.9 us
    ppermute x5, starting transfers between devices, both_sides(): lax.ppermute(x, 'genome', [(i, ((i + 1 ^ 1) - 1) % size) for i in range(s...  8.43 us
    unnamed x10, local copies, waits for them, and re-layouts  4.42 us
    ppermute x5, starting transfers between devices, both_sides(): a = lax.ppermute(x, 'genome', [(i, i ^ 1) for i in range(size)])  2.17 us
  transfers between devices with their start and end apart: 30, of which 6 were waited for; matrix products, arithmetic and copies ran while one was open for 6% of the time, Pallas kernels for 29%

profile of v3, /device:TPU:0, one launch (start us, length us, event | category | flops | bytes accessed | tf_op | source)
XLA Modules:
  0.0 107.7 jit_solution(3967881106210086805)
XLA Ops:
  0.6 0.8 convert_bitcast_fusion
  1.4 0.5 collective-permute-start
  1.9 3.6 %collective-permute-start.1 = (f32[8,128]{1,0:T(8,128)S(1)}, f32[8,128]{1,0:T(8,128)S(1)}, u32[]{:S(2)}, u32[]{:S(2)}) collective-permute-start(f32[8,128]{1,0:T(8,128)S(1)} %slice_bitcast_fusion), channel_id=1, source_target_pairs={{0,28},{4,8},{8,4},{12,16},{16,12},{20,24},{24,20},{28,0},{1,29},{... | collective-permute-start | bytes 12296 | tf_op jit(solution)/shard_map/ppermute | solution.py:439
  5.4 0.9 slice.160
  6.4 0.7 pad_add_fusion.scal
  7.4 3.4 %copy-done.1 = s32[64,2,128,128]{3,2,1,0:T(8,128)S(1)} copy-done((s32[64,2,128,128]{3,2,1,0:T(8,128)S(1)}, s32[64,2,128,128]{3,2,1,0:T(8,128)}, u32[]{:S(2)}) %copy-start.1) | copy-done | bytes 8388632
  10.8 0.7 copy-done.3
  11.5 1.4 %cover_edge.3 = (f32[72,128]{1,0:T(8,128)S(1)}, f32[16,128]{1,0:T(8,128)S(1)}, f32[72,128]{1,0:T(8,128)S(1)}) custom-call(s32[2]{0:T(128)S(1)} %copy-done.3, s32[64,2,128,128]{3,2,1,0:T(8,128)S(1)} %copy-done.1, f32[72,128]{1,0:T(8,128)S(1)} %pad_maximum_fusion.1.mask), custom_call_target="tpu_custom_call" | custom-call | tf_op jit(solution)/shard_map/cover_edge/pallas_call | solution.py:47
  12.9 2.0 %collective-permute-start.3 = (f32[16,128]{1,0:T(8,128)S(1)}, f32[16,128]{1,0:T(8,128)S(1)}, u32[]{:S(2)}, u32[]{:S(2)}) collective-permute-start(f32[16,128]{1,0:T(8,128)S(1)} %get-tuple-element.42), channel_id=1, source_target_pairs={{0,28},{4,8},{8,4},{12,16},{16,12},{20,24},{24,20},{28,0},{1,29},{... | collective-permute-start | bytes 24584 | tf_op jit(solution)/shard_map/ppermute | solution.py:439
  14.9 0.5 fusion.34
  16.1 3.6 %cover_main.3 = (f32[72,128]{1,0:T(8,128)S(1)}, f32[64,2,128,128]{3,2,1,0:T(8,128)S(1)}) custom-call(s32[2]{0:T(128)S(1)} %copy-done.3, s32[64,2,128,128]{3,2,1,0:T(8,128)S(1)} %copy-done.1, f32[72,128]{1,0:T(8,128)S(1)} %get-tuple-element.38.u_ref.refs_0_, f32[72,128]{1,0:T(8,128)S(1)} %get-tuple-element.39.edge_v), custom_call_target="tpu_custom_call" | custom-call | tf_op jit(solution)/shard_map/cover_main/pallas_call | solution.py:47
  19.8 1.4 %collective-permute-start.5 = (f32[72,128]{1,0:T(8,128)S(1)}, f32[72,128]{1,0:T(8,128)S(1)}, u32[]{:S(2)}, u32[]{:S(2)}) collective-permute-start(f32[72,128]{1,0:T(8,128)S(1)} %pad_maximum_fusion.2.after.refs_0_), channel_id=1, source_target_pairs={{0,1},{1,0},{2,3},{3,2},{4,5},{5,4},{6,7},{7,6},{8,9},{9,8},{10,11... | collective-permute-start | bytes 110600 | tf_op jit(solution)/shard_map/ppermute | solution.py:433
  21.2 2.6 %collective-permute-start.6 = (f32[72,128]{1,0:T(8,128)S(1)}, f32[72,128]{1,0:T(8,128)S(1)}, u32[]{:S(2)}, u32[]{:S(2)}) collective-permute-start(f32[72,128]{1,0:T(8,128)S(1)} %pad_maximum_fusion.2.after.refs_0_), channel_id=1, source_target_pairs={{0,2},{1,3},{2,0},{3,1},{4,6},{5,7},{6,4},{7,5},{8,10},{9,11},{10,... | collective-permute-start | bytes 110600 | tf_op jit(solution)/shard_map/ppermute | solution.py:433
  23.8 0.4 collective-permute-start.7
  24.4 2.8 %ratio.3 = (bf16[64,128,256]{2,1,0:T(8,128)(2,1)S(1)}, bf16[64,128,256]{2,1,0:T(8,128)(2,1)S(1)}) custom-call(s32[2]{0:T(128)S(1)} %copy-done.3, f32[64,2,128,128]{3,2,1,0:T(8,128)S(1)} %get-tuple-element.40.kept.counts, f32[32,8192]{1,0:T(8,128)S(1)} %copy-done, f32[32,9216]{1,0:T(8,128)S(1)} %pad_maximum_fusion.h_ref, ...), custom_call_target="tpu_custom_call" | custom-call | tf_op jit(solution)/shard_map/ratio/pallas_call | solution.py:47
  27.2 2.4 %collective-permute-done.7.refs_3_ = f32[72,128]{1,0:T(8,128)S(1)} collective-permute-done((f32[72,128]{1,0:T(8,128)S(1)}, f32[72,128]{1,0:T(8,128)S(1)}, u32[]{:S(2)}, u32[]{:S(2)}) %collective-permute-start.7) | collective-permute-done | bytes 36896 | tf_op jit(solution)/shard_map/ppermute | solution.py:433
  29.6 1.4 %cover_edge.4 = (f32[72,128]{1,0:T(8,128)S(1)}, f32[16,128]{1,0:T(8,128)S(1)}, f32[72,128]{1,0:T(8,128)S(1)}) custom-call(s32[2]{0:T(128)S(1)} %copy-done.3, f32[64,2,128,128]{3,2,1,0:T(8,128)S(1)} %get-tuple-element.40.kept.counts, f32[72,128]{1,0:T(8,128)S(1)} %pad_maximum_fusion.1.mask, f32[72,128]{1,0:T(8,128)S(1)} %pad_maximum_fusion.2.after.refs_0_, ...), custom_call_target="tpu_custom_call" | custom-call | tf_op jit(solution)/shard_map/cover_edge/pallas_call | solution.py:47
  31.0 1.3 %collective-permute-start.9 = (f32[16,128]{1,0:T(8,128)S(1)}, f32[16,128]{1,0:T(8,128)S(1)}, u32[]{:S(2)}, u32[]{:S(2)}) collective-permute-start(f32[16,128]{1,0:T(8,128)S(1)} %get-tuple-element.46), channel_id=1, source_target_pairs={{0,4},{4,0},{8,12},{12,8},{16,20},{20,16},{24,28},{28,24},{1,5},{5... | collective-permute-start | bytes 24584 | tf_op jit(solution)/shard_map/ppermute | solution.py:438
  32.3 3.2 %cover_main.4 = f32[72,128]{1,0:T(8,128)S(1)} custom-call(s32[2]{0:T(128)S(1)} %copy-done.3, f32[64,2,128,128]{3,2,1,0:T(8,128)S(1)} %get-tuple-element.40.kept.counts, f32[72,128]{1,0:T(8,128)S(1)} %get-tuple-element.44.u_ref.refs_1_, f32[72,128]{1,0:T(8,128)S(1)} %get-tuple-element.45.edge_v), custom_call_target="tpu_custom_call" | custom-call | tf_op jit(solution)/shard_map/cover_main/pallas_call | solution.py:47
  35.7 1.5 %collective-permute-start.11 = (f32[72,128]{1,0:T(8,128)S(1)}, f32[72,128]{1,0:T(8,128)S(1)}, u32[]{:S(2)}, u32[]{:S(2)}) collective-permute-start(f32[72,128]{1,0:T(8,128)S(1)} %pad_maximum_fusion.3.after.refs_0_), channel_id=1, source_target_pairs={{0,2},{1,3},{2,0},{3,1},{4,6},{5,7},{6,4},{7,5},{8,10},{9,11},{10,... | collective-permute-start | bytes 110600 | tf_op jit(solution)/shard_map/ppermute | solution.py:433
  37.2 2.9 %collective-permute-start.12 = (f32[72,128]{1,0:T(8,128)S(1)}, f32[72,128]{1,0:T(8,128)S(1)}, u32[]{:S(2)}, u32[]{:S(2)}) collective-permute-start(f32[72,128]{1,0:T(8,128)S(1)} %pad_maximum_fusion.3.after.refs_0_), channel_id=1, source_target_pairs={{0,3},{1,2},{2,1},{3,0},{4,7},{5,6},{6,5},{7,4},{8,11},{9,10},{10,... | collective-permute-start | bytes 110600 | tf_op jit(solution)/shard_map/ppermute | solution.py:433
  40.5 2.8 %ratio.4 = (bf16[64,128,256]{2,1,0:T(8,128)(2,1)S(1)}, bf16[64,128,256]{2,1,0:T(8,128)(2,1)S(1)}) custom-call(s32[2]{0:T(128)S(1)} %copy-done.3, f32[64,2,128,128]{3,2,1,0:T(8,128)S(1)} %get-tuple-element.40.kept.counts, f32[32,8192]{1,0:T(8,128)S(1)} %copy-done, ...), custom_call_target="tpu_custom_call", output_to_operand_aliasing={{0}: (5, {}), {1}: (6, {})} | custom-call | tf_op jit(solution)/shard_map/ratio/pallas_call | solution.py:47
  43.3 1.4 %cover_edge.5 = (f32[72,128]{1,0:T(8,128)S(1)}, f32[16,128]{1,0:T(8,128)S(1)}, f32[72,128]{1,0:T(8,128)S(1)}) custom-call(s32[2]{0:T(128)S(1)} %copy-done.3, f32[64,2,128,128]{3,2,1,0:T(8,128)S(1)} %get-tuple-element.40.kept.counts, f32[72,128]{1,0:T(8,128)S(1)} %pad_maximum_fusion.1.mask, f32[72,128]{1,0:T(8,128)S(1)} %pad_maximum_fusion.3.after.refs_0_, ...), custom_call_target="tpu_custom_call" | custom-call | tf_op jit(solution)/shard_map/cover_edge/pallas_call | solution.py:47
  44.7 0.5 collective-permute-start.13
  45.6 0.6 multiply_reduce_fusion.1
  46.3 3.3 %cover_main.5 = f32[72,128]{1,0:T(8,128)S(1)} custom-call(s32[2]{0:T(128)S(1)} %copy-done.3, f32[64,2,128,128]{3,2,1,0:T(8,128)S(1)} %get-tuple-element.40.kept.counts, f32[72,128]{1,0:T(8,128)S(1)} %get-tuple-element.49.u_ref.refs_2_, f32[72,128]{1,0:T(8,128)S(1)} %get-tuple-element.50.edge_v), custom_call_target="tpu_custom_call" | custom-call | tf_op jit(solution)/shard_map/cover_main/pallas_call | solution.py:47
  49.7 3.1 %collective-permute-start.16 = (f32[72,128]{1,0:T(8,128)S(1)}, f32[72,128]{1,0:T(8,128)S(1)}, u32[]{:S(2)}, u32[]{:S(2)}) collective-permute-start(f32[72,128]{1,0:T(8,128)S(1)} %pad_maximum_fusion.4.after.refs_0_), channel_id=1, source_target_pairs={{0,2},{1,3},{2,0},{3,1},{4,6},{5,7},{6,4},{7,5},{8,10},{9,11},{10,... | collective-permute-start | bytes 110600 | tf_op jit(solution)/shard_map/ppermute | solution.py:433
  52.8 1.3 %collective-permute-start.17 = (f32[72,128]{1,0:T(8,128)S(1)}, f32[72,128]{1,0:T(8,128)S(1)}, u32[]{:S(2)}, u32[]{:S(2)}) collective-permute-start(f32[72,128]{1,0:T(8,128)S(1)} %pad_maximum_fusion.4.after.refs_0_), channel_id=1, source_target_pairs={{0,3},{1,2},{2,1},{3,0},{4,7},{5,6},{6,5},{7,4},{8,11},{9,10},{10,... | collective-permute-start | bytes 110600 | tf_op jit(solution)/shard_map/ppermute | solution.py:433
  54.2 2.3 %collective-permute-start.22 = (f32[32,16]{1,0:T(8,128)S(1)}, f32[32,16]{1,0:T(8,128)S(1)}, u32[]{:S(2)}, u32[]{:S(2)}) collective-permute-start(f32[32,16]{1,0:T(8,128)S(1)} %pad_maximum_fusion.7), channel_id=1, source_target_pairs={{0,28},{4,8},{8,4},{12,16},{16,12},{20,24},{24,20},{28,0},{1,29},{... | collective-permute-start | bytes 6152 | tf_op jit(solution)/shard_map/ppermute | solution.py:439
  57.1 2.1 %ratio.5 = (bf16[64,128,256]{2,1,0:T(8,128)(2,1)S(1)}, bf16[64,128,256]{2,1,0:T(8,128)(2,1)S(1)}) custom-call(s32[2]{0:T(128)S(1)} %copy-done.3, f32[64,2,128,128]{3,2,1,0:T(8,128)S(1)} %get-tuple-element.40.kept.counts, f32[32,8192]{1,0:T(8,128)S(1)} %copy-done, ...), custom_call_target="tpu_custom_call", output_to_operand_aliasing={{0}: (5, {}), {1}: (6, {})} | custom-call | tf_op jit(solution)/shard_map/ratio/pallas_call | solution.py:47
  59.2 2.4 %numer_first.1 = (f32[72,128]{1,0:T(8,128)S(1)}, bf16[72,64,128]{2,1,0:T(8,128)(2,1)S(1)}, f32[16,32,128]{2,1,0:T(8,128)S(1)}, f32[8,32,128]{2,1,0:T(8,128)S(1)}) custom-call(s32[3]{0:T(128)S(1)} %pad_add_fusion.scal, bf16[64,128,256]{2,1,0:T(8,128)(2,1)S(1)} %get-tuple-element.53.hi_ref, bf16[64,128,256]{2,1,0:T(8,128)(2,1)S(1)} %get-tuple-element.54.lo_ref, ...), custom_call_target="tpu_custom_call" | custom-call | tf_op jit(solution)/shard_map/numer_first/pallas_call | solution.py:47
  61.6 4.0 %numer_row.1 = (f32[8,128]{1,0:T(8,128)S(1)}, f32[16,32,128]{2,1,0:T(8,128)S(1)}, f32[16,32,128]{2,1,0:T(8,128)S(1)}, f32[16,32,128]{2,1,0:T(8,128)S(1)}) custom-call(s32[3]{0:T(128)S(1)} %pad_add_fusion.scal, bf16[64,128,256]{2,1,0:T(8,128)(2,1)S(1)} %get-tuple-element.53.hi_ref, bf16[64,128,256]{2,1,0:T(8,128)(2,1)S(1)} %get-tuple-element.54.lo_ref, ...), custom_call_target="tpu_custom_call" | custom-call | tf_op jit(solution)/shard_map/numer_row/pallas_call | solution.py:47
  65.7 0.7 collective-permute-start.18
  66.3 1.4 %fusion.10 = (f32[32,8]{1,0:T(8,128)S(1)}, f32[32,8]{1,0:T(8,128)S(1)}) fusion(f32[32,16]{1,0:T(8,128)S(1)} %collective-permute-done.21, f32[32,16]{1,0:T(8,128)S(1)} %collective-permute-done.22, f32[]{:T(128)} %bitcast.11, pred[]{:T(512)} %bitcast.9, f32[]{:T(128)} %bitcast.10), kind=kLoop, calls=%fused_computation.31 | loop fusion | flops 1024 | bytes 6153 | tf_op jit(solution)/shard_map/mul | solution.py:528
  67.7 1.8 %collective-permute-start.19 = (f32[8,128]{1,0:T(8,128)S(1)}, f32[8,128]{1,0:T(8,128)S(1)}, u32[]{:S(2)}, u32[]{:S(2)}) collective-permute-start(f32[8,128]{1,0:T(8,128)S(1)} %add.93), channel_id=1, source_target_pairs={{0,8},{4,12},{8,0},{12,4},{16,24},{20,28},{24,16},{28,20},{1,9},{5... | collective-permute-start | bytes 12296 | tf_op jit(solution)/shard_map/ppermute | solution.py:433
  69.6 4.3 %numer_col.1 = (f32[16,32,128]{2,1,0:T(8,128)S(1)}, f32[16,32,128]{2,1,0:T(8,128)S(1)}, f32[16,32,128]{2,1,0:T(8,128)S(1)}, f32[16,32,128]{2,1,0:T(8,128)S(1)}) custom-call(s32[3]{0:T(128)S(1)} %pad_add_fusion.scal, bf16[64,128,256]{2,1,0:T(8,128)(2,1)S(1)} %get-tuple-element.53.hi_ref, bf16[64,128,256]{2,1,0:T(8,128)(2,1)S(1)} %get-tuple-element.54.lo_ref, ...), custom_call_target="tpu_custom_call" | custom-call | tf_op jit(solution)/shard_map/numer_col/pallas_call | solution.py:47
  73.9 2.0 %collective-permute-start.28 = (f32[16,32,128]{2,1,0:T(8,128)S(1)}, f32[16,32,128]{2,1,0:T(8,128)S(1)}, u32[]{:S(2)}, u32[]{:S(2)}) collective-permute-start(f32[16,32,128]{2,1,0:T(8,128)S(1)} %get-tuple-element.66), channel_id=1, source_target_pairs={{0,1},{1,0},{2,3},{3,2},{4,5},{5,4},{6,7},{7,6},{8,9},{9,8},{10,11... | collective-permute-start | bytes 786440 | tf_op jit(solution)/shard_map/ppermute | solution.py:433
  76.0 1.2 %collective-permute-start.20 = (f32[8,128]{1,0:T(8,128)S(1)}, f32[8,128]{1,0:T(8,128)S(1)}, u32[]{:S(2)}, u32[]{:S(2)}) collective-permute-start(f32[8,128]{1,0:T(8,128)S(1)} %add.94), channel_id=1, source_target_pairs={{0,16},{4,20},{8,24},{12,28},{16,0},{20,4},{24,8},{28,12},{1,17},{... | collective-permute-start | bytes 12296 | tf_op jit(solution)/shard_map/ppermute | solution.py:433
  77.6 2.1 %collective-permute-done.20 = f32[8,128]{1,0:T(8,128)S(1)} collective-permute-done((f32[8,128]{1,0:T(8,128)S(1)}, f32[8,128]{1,0:T(8,128)S(1)}, u32[]{:S(2)}, u32[]{:S(2)}) %collective-permute-start.20) | collective-permute-done | bytes 4128 | tf_op jit(solution)/shard_map/ppermute | solution.py:433
  79.9 2.3 %collective-permute-start.25 = (f32[16,32,128]{2,1,0:T(8,128)S(1)}, f32[16,32,128]{2,1,0:T(8,128)S(1)}, u32[]{:S(2)}, u32[]{:S(2)}) collective-permute-start(f32[16,32,128]{2,1,0:T(8,128)S(1)} %add.103), channel_id=1, source_target_pairs={{0,3},{1,2},{2,1},{3,0},{4,7},{5,6},{6,5},{7,4},{8,11},{9,10},{10,... | collective-permute-start | bytes 786440 | tf_op jit(solution)/shard_map/ppermute | solution.py:433
  82.2 1.0 collective-permute-done.28
  83.2 2.3 %collective-permute-start.29 = (f32[16,32,128]{2,1,0:T(8,128)S(1)}, f32[16,32,128]{2,1,0:T(8,128)S(1)}, u32[]{:S(2)}, u32[]{:S(2)}) collective-permute-start(f32[16,32,128]{2,1,0:T(8,128)S(1)} %add.111), channel_id=1, source_target_pairs={{0,3},{1,2},{2,1},{3,0},{4,7},{5,6},{6,5},{7,4},{8,11},{9,10},{10,... | collective-permute-start | bytes 786440 | tf_op jit(solution)/shard_map/ppermute | solution.py:433
  85.5 0.6 multiply_bitcast_fusion
  86.1 2.7 %collective-permute-done.23.refs_1_ = f32[16,32,128]{2,1,0:T(8,128)S(1)} collective-permute-done((f32[16,32,128]{2,1,0:T(8,128)S(1)}, f32[16,32,128]{2,1,0:T(8,128)S(1)}, u32[]{:S(2)}, u32[]{:S(2)}) %collective-permute-start.23) | collective-permute-done | bytes 262176 | tf_op jit(solution)/shard_map/ppermute | solution.py:433
  88.8 13.4 %collective-permute-done.25.refs_2_ = f32[16,32,128]{2,1,0:T(8,128)S(1)} collective-permute-done((f32[16,32,128]{2,1,0:T(8,128)S(1)}, f32[16,32,128]{2,1,0:T(8,128)S(1)}, u32[]{:S(2)}, u32[]{:S(2)}) %collective-permute-start.25) | collective-permute-done | bytes 262176 | tf_op jit(solution)/shard_map/ppermute | solution.py:433
  102.2 1.5 %update.2 = f32[32,2048]{1,0:T(8,128)} custom-call(s32[3]{0:T(128)S(1)} %pad_add_fusion.scal, f32[32,8192]{1,0:T(8,128)S(1)} %copy-done, f32[64,128]{1,0:T(8,128)S(1)} %get-tuple-element.77.mask, f32[32,128]{1,0:T(8,128)S(1)} %pad.7.den, f32[8,128]{1,0:T(8,128)S(1)} %add.95.sums, f32[16,32,128]{2,1,0:T(8,128)S(1)} %get-tuple-element.58.refs_0_, ...), custom_call_target="tpu_custom_call" | custom-call | tf_op jit(solution)/shard_map/update/pallas_call | solution.py:47
  103.7 2.5 %collective-permute-done.29.refs_2_ = f32[16,32,128]{2,1,0:T(8,128)S(1)} collective-permute-done((f32[16,32,128]{2,1,0:T(8,128)S(1)}, f32[16,32,128]{2,1,0:T(8,128)S(1)}, u32[]{:S(2)}, u32[]{:S(2)}) %collective-permute-start.29) | collective-permute-done | bytes 262176 | tf_op jit(solution)/shard_map/ppermute | solution.py:433
  106.2 1.5 %update.3 = f32[32,2048]{1,0:T(8,128)} custom-call(s32[3]{0:T(128)S(1)} %pad_add_fusion.scal, f32[32,8192]{1,0:T(8,128)S(1)} %copy-done.2, f32[64,128]{1,0:T(8,128)S(1)} %get-tuple-element.77.mask, f32[32,128]{1,0:T(8,128)S(1)} %pad.8.den, f32[8,128]{1,0:T(8,128)S(1)} %add.95.sums, f32[16,32,128]{2,1,0:T(8,128)S(1)} %get-tuple-element.63.refs_0_, ...), custom_call_target="tpu_custom_call" | custom-call | tf_op jit(solution)/shard_map/update/pallas_call | solution.py:47
  (75 shorter events, 2.3 us)
Async XLA Ops:
  1.4 5.9 %collective-permute-start = (f32[8,128]{1,0:T(8,128)S(1)}, f32[8,128]{1,0:T(8,128)S(1)}, u32[]{:S(2)}, u32[]{:S(2)}) collective-permute-start(f32[8,128]{1,0:T(8,128)S(1)} %slice_bitcast_fusion), channel_id=1, source_target_pairs={{0,4},{4,0},{8,12},{12,8},{16,20},{20,16},{24,28},{28,24},{1,5},{5... | collective-permute-start | bytes 12296 | tf_op jit(solution)/shard_map/ppermute | solution.py:438
  1.9 5.5 %collective-permute-start.1 = (f32[8,128]{1,0:T(8,128)S(1)}, f32[8,128]{1,0:T(8,128)S(1)}, u32[]{:S(2)}, u32[]{:S(2)}) collective-permute-start(f32[8,128]{1,0:T(8,128)S(1)} %slice_bitcast_fusion), channel_id=1, source_target_pairs={{0,28},{4,8},{8,4},{12,16},{16,12},{20,24},{24,20},{28,0},{1,29},{... | collective-permute-start | bytes 12296 | tf_op jit(solution)/shard_map/ppermute | solution.py:439
  6.3 17.9 %collective-permute-start.2 = (f32[32,1024]{1,0:T(8,128)S(1)}, f32[32,1024]{1,0:T(8,128)S(1)}, u32[]{:S(2)}, u32[]{:S(2)}) collective-permute-start(f32[32,1024]{1,0:T(8,128)S(1)} %slice.160), channel_id=1, source_target_pairs={{0,28},{4,0},{8,4},{12,8},{16,12},{20,16},{24,20},{28,24},{1,29},{... | collective-permute-start | bytes 393224 | tf_op jit(solution)/shard_map/ppermute | solution.py:478
  7.4 3.4 %copy-start.1 = (s32[64,2,128,128]{3,2,1,0:T(8,128)S(1)}, s32[64,2,128,128]{3,2,1,0:T(8,128)}, u32[]{:S(2)}) copy-start(s32[64,2,128,128]{3,2,1,0:T(8,128)} %counts.3) | copy-start | bytes 25165828
  10.8 0.7 copy-start.3
  12.9 6.9 %collective-permute-start.3 = (f32[16,128]{1,0:T(8,128)S(1)}, f32[16,128]{1,0:T(8,128)S(1)}, u32[]{:S(2)}, u32[]{:S(2)}) collective-permute-start(f32[16,128]{1,0:T(8,128)S(1)} %get-tuple-element.42), channel_id=1, source_target_pairs={{0,28},{4,8},{8,4},{12,16},{16,12},{20,24},{24,20},{28,0},{1,29},{... | collective-permute-start | bytes 24584 | tf_op jit(solution)/shard_map/ppermute | solution.py:439
  14.9 4.8 %collective-permute-start.4 = (f32[16,128]{1,0:T(8,128)S(1)}, f32[16,128]{1,0:T(8,128)S(1)}, u32[]{:S(2)}, u32[]{:S(2)}) collective-permute-start(f32[16,128]{1,0:T(8,128)S(1)} %get-tuple-element.42), channel_id=1, source_target_pairs={{0,4},{4,0},{8,12},{12,8},{16,20},{20,16},{24,28},{28,24},{1,5},{5... | collective-permute-start | bytes 24584 | tf_op jit(solution)/shard_map/ppermute | solution.py:438
  16.1 8.2 %copy-start.2 = (f32[32,8192]{1,0:T(8,128)S(1)}, f32[32,8192]{1,0:T(8,128)}, u32[]{:S(2)}) copy-start(f32[32,8192]{1,0:T(8,128)} %factor_ref.3) | copy-start | bytes 3145732
  16.1 8.2 %copy-start = (f32[32,8192]{1,0:T(8,128)S(1)}, f32[32,8192]{1,0:T(8,128)}, u32[]{:S(2)}) copy-start(f32[32,8192]{1,0:T(8,128)} %w_ref.9) | copy-start | bytes 3145732
  19.8 7.4 %collective-permute-start.5 = (f32[72,128]{1,0:T(8,128)S(1)}, f32[72,128]{1,0:T(8,128)S(1)}, u32[]{:S(2)}, u32[]{:S(2)}) collective-permute-start(f32[72,128]{1,0:T(8,128)S(1)} %pad_maximum_fusion.2.after.refs_0_), channel_id=1, source_target_pairs={{0,1},{1,0},{2,3},{3,2},{4,5},{5,4},{6,7},{7,6},{8,9},{9,8},{10,11... | collective-permute-start | bytes 110600 | tf_op jit(solution)/shard_map/ppermute | solution.py:433
  21.2 5.9 %collective-permute-start.6 = (f32[72,128]{1,0:T(8,128)S(1)}, f32[72,128]{1,0:T(8,128)S(1)}, u32[]{:S(2)}, u32[]{:S(2)}) collective-permute-start(f32[72,128]{1,0:T(8,128)S(1)} %pad_maximum_fusion.2.after.refs_0_), channel_id=1, source_target_pairs={{0,2},{1,3},{2,0},{3,1},{4,6},{5,7},{6,4},{7,5},{8,10},{9,11},{10,... | collective-permute-start | bytes 110600 | tf_op jit(solution)/shard_map/ppermute | solution.py:433
  23.8 5.8 %collective-permute-start.7 = (f32[72,128]{1,0:T(8,128)S(1)}, f32[72,128]{1,0:T(8,128)S(1)}, u32[]{:S(2)}, u32[]{:S(2)}) collective-permute-start(f32[72,128]{1,0:T(8,128)S(1)} %pad_maximum_fusion.2.after.refs_0_), channel_id=1, source_target_pairs={{0,3},{1,2},{2,1},{3,0},{4,7},{5,6},{6,5},{7,4},{8,11},{9,10},{10,... | collective-permute-start | bytes 110600 | tf_op jit(solution)/shard_map/ppermute | solution.py:433
  31.0 4.6 %collective-permute-start.8 = (f32[16,128]{1,0:T(8,128)S(1)}, f32[16,128]{1,0:T(8,128)S(1)}, u32[]{:S(2)}, u32[]{:S(2)}) collective-permute-start(f32[16,128]{1,0:T(8,128)S(1)} %get-tuple-element.46), channel_id=1, source_target_pairs={{0,28},{4,8},{8,4},{12,16},{16,12},{20,24},{24,20},{28,0},{1,29},{... | collective-permute-start | bytes 24584 | tf_op jit(solution)/shard_map/ppermute | solution.py:439
  31.0 4.6 %collective-permute-start.9 = (f32[16,128]{1,0:T(8,128)S(1)}, f32[16,128]{1,0:T(8,128)S(1)}, u32[]{:S(2)}, u32[]{:S(2)}) collective-permute-start(f32[16,128]{1,0:T(8,128)S(1)} %get-tuple-element.46), channel_id=1, source_target_pairs={{0,4},{4,0},{8,12},{12,8},{16,20},{20,16},{24,28},{28,24},{1,5},{5... | collective-permute-start | bytes 24584 | tf_op jit(solution)/shard_map/ppermute | solution.py:438
  35.6 7.6 %collective-permute-start.10 = (f32[72,128]{1,0:T(8,128)S(1)}, f32[72,128]{1,0:T(8,128)S(1)}, u32[]{:S(2)}, u32[]{:S(2)}) collective-permute-start(f32[72,128]{1,0:T(8,128)S(1)} %pad_maximum_fusion.3.after.refs_0_), channel_id=1, source_target_pairs={{0,1},{1,0},{2,3},{3,2},{4,5},{5,4},{6,7},{7,6},{8,9},{9,8},{10,11... | collective-permute-start | bytes 110600 | tf_op jit(solution)/shard_map/ppermute | solution.py:433
  35.7 7.6 %collective-permute-start.11 = (f32[72,128]{1,0:T(8,128)S(1)}, f32[72,128]{1,0:T(8,128)S(1)}, u32[]{:S(2)}, u32[]{:S(2)}) collective-permute-start(f32[72,128]{1,0:T(8,128)S(1)} %pad_maximum_fusion.3.after.refs_0_), channel_id=1, source_target_pairs={{0,2},{1,3},{2,0},{3,1},{4,6},{5,7},{6,4},{7,5},{8,10},{9,11},{10,... | collective-permute-start | bytes 110600 | tf_op jit(solution)/shard_map/ppermute | solution.py:433
  37.2 6.1 %collective-permute-start.12 = (f32[72,128]{1,0:T(8,128)S(1)}, f32[72,128]{1,0:T(8,128)S(1)}, u32[]{:S(2)}, u32[]{:S(2)}) collective-permute-start(f32[72,128]{1,0:T(8,128)S(1)} %pad_maximum_fusion.3.after.refs_0_), channel_id=1, source_target_pairs={{0,3},{1,2},{2,1},{3,0},{4,7},{5,6},{6,5},{7,4},{8,11},{9,10},{10,... | collective-permute-start | bytes 110600 | tf_op jit(solution)/shard_map/ppermute | solution.py:433
  44.7 4.9 %collective-permute-start.13 = (f32[16,128]{1,0:T(8,128)S(1)}, f32[16,128]{1,0:T(8,128)S(1)}, u32[]{:S(2)}, u32[]{:S(2)}) collective-permute-start(f32[16,128]{1,0:T(8,128)S(1)} %get-tuple-element.51), channel_id=1, source_target_pairs={{0,28},{4,8},{8,4},{12,16},{16,12},{20,24},{24,20},{28,0},{1,29},{... | collective-permute-start | bytes 24584 | tf_op jit(solution)/shard_map/ppermute | solution.py:439
  45.2 4.3 %collective-permute-start.14 = (f32[16,128]{1,0:T(8,128)S(1)}, f32[16,128]{1,0:T(8,128)S(1)}, u32[]{:S(2)}, u32[]{:S(2)}) collective-permute-start(f32[16,128]{1,0:T(8,128)S(1)} %get-tuple-element.51), channel_id=1, source_target_pairs={{0,4},{4,0},{8,12},{12,8},{16,20},{20,16},{24,28},{28,24},{1,5},{5... | collective-permute-start | bytes 24584 | tf_op jit(solution)/shard_map/ppermute | solution.py:438
  49.6 9.5 %collective-permute-start.15 = (f32[72,128]{1,0:T(8,128)S(1)}, f32[72,128]{1,0:T(8,128)S(1)}, u32[]{:S(2)}, u32[]{:S(2)}) collective-permute-start(f32[72,128]{1,0:T(8,128)S(1)} %pad_maximum_fusion.4.after.refs_0_), channel_id=1, source_target_pairs={{0,1},{1,0},{2,3},{3,2},{4,5},{5,4},{6,7},{7,6},{8,9},{9,8},{10,11... | collective-permute-start | bytes 110600 | tf_op jit(solution)/shard_map/ppermute | solution.py:433
  49.7 9.5 %collective-permute-start.16 = (f32[72,128]{1,0:T(8,128)S(1)}, f32[72,128]{1,0:T(8,128)S(1)}, u32[]{:S(2)}, u32[]{:S(2)}) collective-permute-start(f32[72,128]{1,0:T(8,128)S(1)} %pad_maximum_fusion.4.after.refs_0_), channel_id=1, source_target_pairs={{0,2},{1,3},{2,0},{3,1},{4,6},{5,7},{6,4},{7,5},{8,10},{9,11},{10,... | collective-permute-start | bytes 110600 | tf_op jit(solution)/shard_map/ppermute | solution.py:433
  52.8 6.4 %collective-permute-start.17 = (f32[72,128]{1,0:T(8,128)S(1)}, f32[72,128]{1,0:T(8,128)S(1)}, u32[]{:S(2)}, u32[]{:S(2)}) collective-permute-start(f32[72,128]{1,0:T(8,128)S(1)} %pad_maximum_fusion.4.after.refs_0_), channel_id=1, source_target_pairs={{0,3},{1,2},{2,1},{3,0},{4,7},{5,6},{6,5},{7,4},{8,11},{9,10},{10,... | collective-permute-start | bytes 110600 | tf_op jit(solution)/shard_map/ppermute | solution.py:433
  54.1 12.2 %collective-permute-start.21 = (f32[32,16]{1,0:T(8,128)S(1)}, f32[32,16]{1,0:T(8,128)S(1)}, u32[]{:S(2)}, u32[]{:S(2)}) collective-permute-start(f32[32,16]{1,0:T(8,128)S(1)} %pad_maximum_fusion.7), channel_id=1, source_target_pairs={{0,4},{4,0},{8,12},{12,8},{16,20},{20,16},{24,28},{28,24},{1,5},{5... | collective-permute-start | bytes 6152 | tf_op jit(solution)/shard_map/ppermute | solution.py:438
  54.2 12.2 %collective-permute-start.22 = (f32[32,16]{1,0:T(8,128)S(1)}, f32[32,16]{1,0:T(8,128)S(1)}, u32[]{:S(2)}, u32[]{:S(2)}) collective-permute-start(f32[32,16]{1,0:T(8,128)S(1)} %pad_maximum_fusion.7), channel_id=1, source_target_pairs={{0,28},{4,8},{8,4},{12,16},{16,12},{20,24},{24,20},{28,0},{1,29},{... | collective-permute-start | bytes 6152 | tf_op jit(solution)/shard_map/ppermute | solution.py:439
  61.6 8.0 %collective-permute-start.26 = (f32[8,32,128]{2,1,0:T(8,128)S(1)}, f32[8,32,128]{2,1,0:T(8,128)S(1)}, u32[]{:S(2)}, u32[]{:S(2)}) collective-permute-start(f32[8,32,128]{2,1,0:T(8,128)S(1)} %get-tuple-element.62), channel_id=1, source_target_pairs={{0,4},{4,8},{8,12},{12,16},{16,20},{20,24},{24,28},{28,0},{1,5},{5... | collective-permute-start | bytes 393224 | tf_op jit(solution)/shard_map/ppermute | solution.py:509
  65.7 2.1 %collective-permute-start.18 = (f32[8,128]{1,0:T(8,128)S(1)}, f32[8,128]{1,0:T(8,128)S(1)}, u32[]{:S(2)}, u32[]{:S(2)}) collective-permute-start(f32[8,128]{1,0:T(8,128)S(1)} %get-tuple-element.57), channel_id=1, source_target_pairs={{0,4},{4,0},{8,12},{12,8},{16,20},{20,16},{24,28},{28,24},{1,5},{5... | collective-permute-start | bytes 12296 | tf_op jit(solution)/shard_map/ppermute | solution.py:433
  67.7 12.1 %collective-permute-start.24 = (f32[16,32,128]{2,1,0:T(8,128)S(1)}, f32[16,32,128]{2,1,0:T(8,128)S(1)}, u32[]{:S(2)}, u32[]{:S(2)}) collective-permute-start(f32[16,32,128]{2,1,0:T(8,128)S(1)} %get-tuple-element.61), channel_id=1, source_target_pairs={{0,1},{1,0},{2,3},{3,2},{4,5},{5,4},{6,7},{7,6},{8,9},{9,8},{10,11... | collective-permute-start | bytes 786440 | tf_op jit(solution)/shard_map/ppermute | solution.py:433
  67.7 8.3 %collective-permute-start.19 = (f32[8,128]{1,0:T(8,128)S(1)}, f32[8,128]{1,0:T(8,128)S(1)}, u32[]{:S(2)}, u32[]{:S(2)}) collective-permute-start(f32[8,128]{1,0:T(8,128)S(1)} %add.93), channel_id=1, source_target_pairs={{0,8},{4,12},{8,0},{12,4},{16,24},{20,28},{24,16},{28,20},{1,9},{5... | collective-permute-start | bytes 12296 | tf_op jit(solution)/shard_map/ppermute | solution.py:433
  73.9 9.3 %collective-permute-start.28 = (f32[16,32,128]{2,1,0:T(8,128)S(1)}, f32[16,32,128]{2,1,0:T(8,128)S(1)}, u32[]{:S(2)}, u32[]{:S(2)}) collective-permute-start(f32[16,32,128]{2,1,0:T(8,128)S(1)} %get-tuple-element.66), channel_id=1, source_target_pairs={{0,1},{1,0},{2,3},{3,2},{4,5},{5,4},{6,7},{7,6},{8,9},{9,8},{10,11... | collective-permute-start | bytes 786440 | tf_op jit(solution)/shard_map/ppermute | solution.py:433
  76.0 3.7 %collective-permute-start.20 = (f32[8,128]{1,0:T(8,128)S(1)}, f32[8,128]{1,0:T(8,128)S(1)}, u32[]{:S(2)}, u32[]{:S(2)}) collective-permute-start(f32[8,128]{1,0:T(8,128)S(1)} %add.94), channel_id=1, source_target_pairs={{0,16},{4,20},{8,24},{12,28},{16,0},{20,4},{24,8},{28,12},{1,17},{... | collective-permute-start | bytes 12296 | tf_op jit(solution)/shard_map/ppermute | solution.py:433
  77.4 11.4 %collective-permute-start.23 = (f32[16,32,128]{2,1,0:T(8,128)S(1)}, f32[16,32,128]{2,1,0:T(8,128)S(1)}, u32[]{:S(2)}, u32[]{:S(2)}) collective-permute-start(f32[16,32,128]{2,1,0:T(8,128)S(1)} %get-tuple-element.59.after), channel_id=1, source_target_pairs={{0,1},{1,0},{2,3},{3,2},{4,5},{5,4},{6,7},{7,6},{8,9},{9,8},{10,11... | collective-permute-start | bytes 786440 | tf_op jit(solution)/shard_map/ppermute | solution.py:433
  79.7 23.9 %collective-permute-start.27 = (f32[16,32,128]{2,1,0:T(8,128)S(1)}, f32[16,32,128]{2,1,0:T(8,128)S(1)}, u32[]{:S(2)}, u32[]{:S(2)}) collective-permute-start(f32[16,32,128]{2,1,0:T(8,128)S(1)} %get-tuple-element.64), channel_id=1, source_target_pairs={{0,1},{1,0},{2,3},{3,2},{4,5},{5,4},{6,7},{7,6},{8,9},{9,8},{10,11... | collective-permute-start | bytes 786440 | tf_op jit(solution)/shard_map/ppermute | solution.py:433
  79.9 22.3 %collective-permute-start.25 = (f32[16,32,128]{2,1,0:T(8,128)S(1)}, f32[16,32,128]{2,1,0:T(8,128)S(1)}, u32[]{:S(2)}, u32[]{:S(2)}) collective-permute-start(f32[16,32,128]{2,1,0:T(8,128)S(1)} %add.103), channel_id=1, source_target_pairs={{0,3},{1,2},{2,1},{3,0},{4,7},{5,6},{6,5},{7,4},{8,11},{9,10},{10,... | collective-permute-start | bytes 786440 | tf_op jit(solution)/shard_map/ppermute | solution.py:433
  83.2 23.0 %collective-permute-start.29 = (f32[16,32,128]{2,1,0:T(8,128)S(1)}, f32[16,32,128]{2,1,0:T(8,128)S(1)}, u32[]{:S(2)}, u32[]{:S(2)}) collective-permute-start(f32[16,32,128]{2,1,0:T(8,128)S(1)} %add.111), channel_id=1, source_target_pairs={{0,3},{1,2},{2,1},{3,0},{4,7},{5,6},{6,5},{7,4},{8,11},{9,10},{10,... | collective-permute-start | bytes 786440 | tf_op jit(solution)/shard_map/ppermute | solution.py:433

commit v4 on v3

v4 whole, which is shorter than its diff:
```python
import functools

import jax
import jax.numpy as jnp
from jax import lax
from jax.experimental import pallas as pl
from jax.experimental.pallas import tpu as pltpu
from jax.sharding import PartitionSpec as P

ITERS = 3
STEP = 8
F32 = jnp.float32
BF16 = jnp.bfloat16
VMEM_LIMIT = 20 * 1024 * 1024
NT = (((1,), (1,)), ((), ()))
TN = (((0,), (0,)), ((), ()))


def split(x):
    hi = x.astype(BF16)
    lo = (x - hi.astype(F32)).astype(BF16)
    return hi, lo


def tree_sum(parts):
    while len(parts) > 1:
        parts = [a + b for a, b in zip(parts[::2], parts[1::2])]
    return parts[0]


def params():
    return pltpu.CompilerParams(vmem_limit_bytes=VMEM_LIMIT)


def scale_from(mask, parts):
    cover = tree_sum([p[...] for p in parts])
    live = mask[...] > 0
    return jnp.where(live, 1.0 / jnp.where(live, cover, 1.0), 0.0)


def vmem():
    return pl.BlockSpec(memory_space=pltpu.VMEM)


def kernel_call(body, name, scalars, args, outs, scratch=(), aliases=None, specs=None):
    return pl.pallas_call(
        body,
        grid_spec=pltpu.PrefetchScalarGridSpec(
            num_scalar_prefetch=1,
            grid=(1,),
            in_specs=specs or [vmem() for _ in args],
            out_specs=[vmem() for _ in outs],
            scratch_shapes=list(scratch),
        ),
        out_shape=outs,
        input_output_aliases=aliases or {},
        compiler_params=params(),
        name=name,
    )(scalars, *args)


def offsets(scal, slots):
    return [scal[1 + s] for s in range(slots)]


def by_diagonal(offs, slots, go):
    for s in range(slots):

        @pl.when(offs[s] == 0)
        def _():
            go(s)

    @pl.when(functools.reduce(jnp.logical_and, [offs[s] != 0 for s in range(slots)]))
    def _():
        go(-1)


def tile_value(counts, i, s, diagonal):
    c = counts[i, s].astype(F32)
    if s == diagonal:
        tile = c.shape[0]
        r = lax.broadcasted_iota(jnp.int32, (tile, tile), 0)
        q = lax.broadcasted_iota(jnp.int32, (tile, tile), 1)
        c = jnp.where(r < q, c, jnp.where(r == q, 0.5 * c, 0.0))
    return c


def cover_block(offs, counts, u_ref, acc, base, diagonal, at, kept=None):
    slots, tile = counts.shape[1:3]
    ones = jnp.ones((8, tile), BF16)
    u_block = u_ref[pl.ds(base, STEP), :]
    u_cols = u_block.T
    u_across = [u_ref[pl.ds(base + offs[s], STEP), :] for s in range(slots)]
    cols = [[] for _ in range(slots)]
    sums = []
    for t in range(STEP):
        total = None
        for s in range(slots):
            c = tile_value(counts, at + t, s, diagonal)
            if kept is not None:
                kept[base + t, s] = c
            term = c * u_across[s][t : t + 1]
            total = term if total is None else total + term
            cols[s].append(jnp.sum(c * u_cols[:, t : t + 1], axis=0, keepdims=True))
        hi, lo = split(total)
        row = lax.dot_general(ones, hi, NT, preferred_element_type=F32)
        row = row + lax.dot_general(ones, lo, NT, preferred_element_type=F32)
        sums.append(row[:1])
    acc[pl.ds(base, STEP), :] += jnp.concatenate(sums, axis=0)
    for s in range(slots):
        acc[pl.ds(base + offs[s], STEP), :] += jnp.concatenate(cols[s], axis=0)


def block_copies(hbm, buffer, sems, bases):
    return [
        pltpu.make_async_copy(
            hbm.at[pl.ds(base, STEP)], buffer.at[pl.ds(k * STEP, STEP)], sems.at[k]
        )
        for k, base in enumerate(bases)
    ]


def edge_bases(rows, pad):
    return list(range(0, pad, STEP)) + list(range(rows - pad, rows, STEP))


def write_edge(v_out, edge_out, rows):
    pad = v_out.shape[0] - rows
    edge_out[:pad] = v_out[:pad]
    edge_out[pad:] = v_out[rows:]


def first_edge_kernel(scal, hbm, u_ref, v_out, edge_out, kept, buffer, sems):
    rows, slots = hbm.shape[:2]
    offs = offsets(scal, slots)
    bases = edge_bases(rows, u_ref.shape[0] - rows)
    copies = block_copies(hbm, buffer, sems, bases)
    for copy in copies:
        copy.start()
    v_out[...] = jnp.zeros_like(v_out)
    for copy in copies:
        copy.wait()

    def go(diagonal):
        for k, base in enumerate(bases):
            cover_block(offs, buffer, u_ref, v_out, base, diagonal, k * STEP, kept)

    by_diagonal(offs, slots, go)
    write_edge(v_out, edge_out, rows)


def first_main_kernel(scal, hbm, u_ref, edge_v, kept_in, v_out, kept, buffer, sems):
    rows, slots = hbm.shape[:2]
    offs = offsets(scal, slots)
    pad = u_ref.shape[0] - rows
    bases = list(range(pad, rows - pad, STEP))
    copies = block_copies(hbm, buffer, sems, bases)
    for copy in copies:
        copy.start()
    v_out[...] = edge_v[...]

    def go(diagonal):
        for k, base in enumerate(bases):
            copies[k].wait()
            cover_block(offs, buffer, u_ref, v_out, base, diagonal, k * STEP, kept)

    by_diagonal(offs, slots, go)


def edge_kernel(scal, kept, mask, *refs):
    v_out, edge_out, u_out = refs[-3:]
    rows, slots = kept.shape[:2]
    offs = offsets(scal, slots)
    u_out[...] = scale_from(mask, refs[:-4])
    v_out[...] = jnp.zeros_like(v_out)
    for base in edge_bases(rows, mask.shape[0] - rows):
        cover_block(offs, kept, u_out, v_out, base, -1, base)
    write_edge(v_out, edge_out, rows)


def main_kernel(scal, kept, u_ref, edge_v, v_out):
    rows, slots = kept.shape[:2]
    offs = offsets(scal, slots)
    pad = edge_v.shape[0] - rows
    v_out[...] = edge_v[...]
    for base in range(pad, rows - pad, STEP):
        cover_block(offs, kept, u_ref, v_out, base, -1, base)


def first_edge(scal, counts, u):
    rows, slots, tile = counts.shape[:3]
    ext = u.shape[0]
    pad = ext - rows
    outs = [
        jax.ShapeDtypeStruct(u.shape, F32),
        jax.ShapeDtypeStruct((2 * pad, tile), F32),
        pltpu.VMEM(counts.shape, F32),
    ]
    return kernel_call(
        first_edge_kernel,
        "first_edge",
        scal,
        [counts, u],
        outs,
        [
            pltpu.VMEM((2 * pad, slots, tile, tile), counts.dtype),
            pltpu.SemaphoreType.DMA((2 * pad // STEP,)),
        ],
        specs=[pl.BlockSpec(memory_space=pltpu.HBM), vmem()],
    )


def first_main(scal, counts, u, edge_v, kept):
    rows, slots, tile = counts.shape[:3]
    inner = rows - 2 * (u.shape[0] - rows)
    outs = [jax.ShapeDtypeStruct(u.shape, F32), pltpu.VMEM(counts.shape, F32)]
    return kernel_call(
        first_main_kernel,
        "first_main",
        scal,
        [counts, u, edge_v, kept],
        outs,
        [
            pltpu.VMEM((inner, slots, tile, tile), counts.dtype),
            pltpu.SemaphoreType.DMA((inner // STEP,)),
        ],
        aliases={4: 1},
        specs=[pl.BlockSpec(memory_space=pltpu.HBM), vmem(), vmem(), vmem()],
    )


def cover_edge(scal, kept, mask_ext, parts, after):
    rows, tile = kept.shape[0], kept.shape[2]
    flat = jax.ShapeDtypeStruct(mask_ext.shape, F32)
    edge = jax.ShapeDtypeStruct((2 * (mask_ext.shape[0] - rows), tile), F32)
    args = [kept, mask_ext, *parts, after]
    return kernel_call(edge_kernel, "cover_edge", scal, args, [flat, edge, flat])


def cover_main(scal, kept, u, edge_v):
    outs = [jax.ShapeDtypeStruct(u.shape, F32)]
    return kernel_call(main_kernel, "cover_main", scal, [kept, u, edge_v], outs)[0]


def ratio_kernel(start, count, scal, kept, w_ref, h_ref, after, *refs):
    hi_out, lo_out, h_terms = refs[-3:]
    rows, slots, tile = kept.shape[:3]
    offs = offsets(scal, slots)
    pad = h_ref.shape[1] // tile - rows

    def prepare(j, carry):
        hi, lo = split(h_ref[:, pl.ds(pl.multiple_of(j * tile, tile), tile)])
        h_terms[j - start] = jnp.concatenate([hi, lo, hi, lo], axis=0)
        return carry

    lax.fori_loop(start, start + count + pad, prepare, 0, unroll=4)

    def go(diagonal):
        def body(i, carry):
            hi, lo = split(w_ref[:, pl.ds(pl.multiple_of(i * tile, tile), tile)])
            w_terms = jnp.concatenate([hi, hi, lo, lo], axis=0)
            for s in range(slots):
                model = lax.dot_general(
                    w_terms, h_terms[i - start + offs[s]], TN, preferred_element_type=F32
                )
                values = kept[i, s]
                if s == diagonal:
                    values = values + values.T
                r_hi, r_lo = split(values * (1.0 / model))
                hi_out[i, :, s * tile : (s + 1) * tile] = r_hi
                lo_out[i, :, s * tile : (s + 1) * tile] = r_lo
            return carry

        lax.fori_loop(start, start + count, body, 0, unroll=4)

    by_diagonal(offs, slots, go)


def ratio(scal, kept, row_factors, col_ext, after, earlier, start, count):
    rows, slots, tile = kept.shape[:3]
    factors = row_factors.shape[0]
    pad = col_ext.shape[1] // tile - rows
    out = pltpu.VMEM((rows, tile, slots * tile), BF16)
    return kernel_call(
        functools.partial(ratio_kernel, start, count),
        "ratio",
        scal,
        [kept, row_factors, col_ext, after, *earlier],
        [out, out],
        [pltpu.VMEM((count + pad, 4 * factors, tile), BF16)],
        {5: 0, 6: 1} if earlier else {},
    )


def row_numer(offs, g_all, hi_ref, lo_ref, u_ref, i):
    slots = hi_ref.shape[2] // g_all.shape[2]
    factors = g_all.shape[1] // 2
    g = jnp.concatenate([g_all[i + offs[s]] for s in range(slots)], axis=1)
    big = lax.dot_general(g, hi_ref[i], NT, preferred_element_type=F32)
    small = lax.dot_general(g[:factors], lo_ref[i], NT, preferred_element_type=F32)
    return (big[:factors] + big[factors:] + small) * u_ref[pl.ds(i, 1), :]


def col_numer(w_ref, hi_ref, lo_ref, u_ref, i):
    tile = u_ref.shape[1]
    factors = w_ref.shape[0]
    w = w_ref[:, pl.ds(pl.multiple_of(i * tile, tile), tile)]
    hi, lo = split(w * u_ref[pl.ds(i, 1), :])
    big = jnp.dot(jnp.concatenate([hi, lo], axis=0), hi_ref[i], preferred_element_type=F32)
    small = jnp.dot(hi, lo_ref[i], preferred_element_type=F32)
    return big[:factors] + big[factors:] + small


def col_loop(offs, w_ref, hi_ref, lo_ref, u_ref, acc, start, stop, shift):
    tile = u_ref.shape[1]

    def body(i, carry):
        cols = col_numer(w_ref, hi_ref, lo_ref, u_ref, i)
        for s in range(hi_ref.shape[2] // tile):
            acc[i + offs[s] - shift] += cols[:, s * tile : (s + 1) * tile]
        return carry

    lax.fori_loop(start, stop, body, 0, unroll=4)


def row_pieces(scal, offs, g_ref, hi_ref, lo_ref, u_ref, order, outs):
    for k, out in zip(order, outs):
        per = out.shape[0]
        first = jnp.bitwise_xor(scal[0], k) * per

        def body(t, carry):
            out[t] = row_numer(offs, g_ref, hi_ref, lo_ref, u_ref, first + t)
            return carry

        lax.fori_loop(0, per, body, 0, unroll=4)


def numer_col_kernel(shares, scal, hi_ref, lo_ref, w_ref, mask, *refs):
    parts, scales, refs = refs[:shares], refs[shares : shares + ITERS], refs[shares + ITERS :]
    u_out, tail_out, sums_out = refs[:3]
    outs, acc = refs[3:-1], refs[-1]
    rows = hi_ref.shape[0]
    ext, tile = mask.shape
    offs = offsets(scal, hi_ref.shape[2] // tile)
    per = rows // shares
    u_out[...] = scale_from(mask, parts)
    acc[...] = jnp.zeros_like(acc)
    col_loop(offs, w_ref, hi_ref, lo_ref, u_out, acc, 0, rows, 0)
    for k, out in enumerate(outs):
        first = jnp.bitwise_xor(scal[0], k) * per

        def body(t, carry):
            out[t] = acc[first + t] * u_out[pl.ds(first + t, 1), :]
            return carry

        lax.fori_loop(0, per, body, 0, unroll=4)
    for t in range(ext - rows):
        tail_out[t] = acc[rows + t] * u_out[rows + t : rows + t + 1, :]
    pad = ext - rows
    lane = lax.broadcasted_iota(jnp.int32, tail_out.shape[1:], 1)
    ends = jnp.zeros(tail_out.shape[1:], F32)
    for t in range(pad):
        ends = jnp.where(lane == t, tile_sum(w_ref, mask, rows - pad + t), ends)
    tail_out[pad] = ends
    write_sums(sums_out, [*scales, u_out], rows)


def write_sums(sums_out, scales, rows):
    sums_out[...] = jnp.zeros_like(sums_out)
    mask = scales[0][:rows]
    totals = [mask]
    for t in range(ITERS):
        below = jnp.where(mask > 0, scales[t + 1][:rows], 1.0)
        totals.append(jnp.where(mask > 0, scales[t][:rows] / below, 0.0))
    for t, total in enumerate(totals):
        line = jnp.sum(jnp.sum(total, axis=0, keepdims=True), axis=1, keepdims=True)
        sums_out[t : t + 1, :] = jnp.broadcast_to(line, (1, mask.shape[1]))


def numer_row_kernel(scal, hi_ref, lo_ref, h_ref, *refs):
    u_ref, outs, terms = refs[0], refs[1:-1], refs[-1]
    ext, tile = u_ref.shape
    factors = h_ref.shape[0]
    offs = offsets(scal, hi_ref.shape[2] // tile)

    def fill(j, carry):
        x = h_ref[:, pl.ds(pl.multiple_of(j * tile, tile), tile)] * u_ref[pl.ds(j, 1), :]
        hi, lo = split(x)
        terms[j, :factors] = hi
        terms[j, factors:] = lo
        return carry

    lax.fori_loop(0, ext, fill, 0, unroll=4)
    row_pieces(scal, offs, terms, hi_ref, lo_ref, u_ref, range(len(outs)), outs)


def numer_col(scal, r_hi, r_lo, row_factors, mask_ext, parts, scales):
    shares = len(parts)
    rows, tile = r_hi.shape[:2]
    factors = row_factors.shape[0]
    ext = mask_ext.shape[0]
    piece = jax.ShapeDtypeStruct((rows // shares, factors, tile), F32)
    outs = [
        jax.ShapeDtypeStruct((ext, tile), F32),
        jax.ShapeDtypeStruct((ext - rows + 1, factors, tile), F32),
        jax.ShapeDtypeStruct((8, tile), F32),
    ]
    res = kernel_call(
        functools.partial(numer_col_kernel, shares),
        "numer_col",
        scal,
        [r_hi, r_lo, row_factors, mask_ext, *parts, *scales],
        outs + [piece] * shares,
        [pltpu.VMEM((ext, factors, tile), F32)],
    )
    return *res[:3], res[3:]


def numer_row(scal, r_hi, r_lo, col_ext, u, shares):
    rows, tile = r_hi.shape[:2]
    factors = col_ext.shape[0]
    piece = jax.ShapeDtypeStruct((rows // shares, factors, tile), F32)
    return kernel_call(
        numer_row_kernel,
        "numer_row",
        scal,
        [r_hi, r_lo, col_ext, u],
        [piece] * shares,
        [pltpu.VMEM((u.shape[0], 2 * factors, tile), BF16)],
    )


def mean_scale(sums):
    scale = sums[1:2, :] / sums[0:1, :]
    for t in range(1, ITERS):
        scale = scale * (sums[t + 1 : t + 2, :] / sums[0:1, :])
    return scale


def tile_sum(factor_ref, mask, j):
    tile = mask.shape[1]
    x = factor_ref[:, pl.ds(pl.multiple_of(j * tile, tile), tile)] * mask[pl.ds(j, 1), :]
    return jnp.sum(x, axis=1, keepdims=True)


def windows(sums, per):
    return [tree_sum(sums[t : t + len(sums) - per]) for t in range(per)]


def write_coefficient(old_ref, mask, first, lowers, times_out, plus_out):
    tile = mask.shape[1]
    for t, lower in enumerate(lowers):
        live = mask[pl.ds(first + t, 1), :]
        old = old_ref[:, t * tile : (t + 1) * tile]
        times_out[t] = jnp.where(live > 0, old / jnp.where(live > 0, lower * live, 1.0), 0.0)
        plus_out[t] = jnp.where(live > 0, 0.0, old)


def row_coefficient_kernel(pad, scal, old_ref, mask, other, times_out, plus_out):
    per = times_out.shape[0]
    first = scal[0] * per
    sums = [tile_sum(other, mask, first + t) for t in range(per + pad)]
    write_coefficient(old_ref, mask, first, windows(sums, per), times_out, plus_out)


def col_coefficient_kernel(pad, scal, old_ref, mask, other, ends, times_out, plus_out):
    per = times_out.shape[0]
    first = scal[0] * per
    sums = []
    for j in range(1, per + pad):
        total = tile_sum(other, mask, jnp.maximum(first - pad + j, 0))
        for start in range(0, pad, per):
            if start + j < pad:
                before = jnp.where(scal[scal.shape[0] - 1] > 0, ends[:, start + j : start + j + 1], 0.0)
                total = jnp.where(first == start, before, total)
        sums.append(total)
    sums.append(jnp.zeros_like(sums[0]))
    write_coefficient(old_ref, mask, first, windows(sums, per), times_out, plus_out)


def coefficient(kernel, scal, shares, old, mask_ext, other, *ends):
    factors = old.shape[0]
    tile = mask_ext.shape[1]
    rows = old.shape[1] // tile
    per = rows // shares
    specs = [pl.BlockSpec((factors, per * tile), lambda i, scal: (0, scal[0]))]
    specs += [vmem() for _ in range(2 + len(ends))]
    return kernel_call(
        functools.partial(kernel, mask_ext.shape[0] - rows),
        "coefficient",
        scal,
        [old, mask_ext, other, *ends],
        [jax.ShapeDtypeStruct((per, factors, tile), F32)] * 2,
        specs=specs,
    )


def update_kernel(scal, sums, times, plus, *refs):
    terms, out = refs[:-1], refs[-1]
    per, _, tile = times.shape
    c = mean_scale(sums[...])
    for t in range(per):
        numer = terms[0][t]
        for term in terms[1:]:
            numer = numer + term[t]
        out[:, t * tile : (t + 1) * tile] = times[t] * (numer * c * c) + plus[t]


def update(scal, sums, times, plus, terms):
    per, count, tile = terms[0].shape
    return kernel_call(
        update_kernel,
        "update",
        scal,
        [sums, times, plus, *terms],
        [jax.ShapeDtypeStruct((count, per * tile), F32)],
    )[0]


def xor_exchange(x, axis, k):
    return lax.ppermute(x, axis, [(i, i ^ k) for i in range(lax.axis_size(axis))])


def both_sides(x, even):
    size = lax.axis_size("genome")
    a = lax.ppermute(x, "genome", [(i, i ^ 1) for i in range(size)])
    b = lax.ppermute(x, "genome", [(i, (((i + 1) ^ 1) - 1) % size) for i in range(size)])
    return jnp.where(even > 0, a, b), jnp.where(even > 0, b, a)


def scatter_terms(pieces, extra=None, across=None):
    size = lax.axis_size("offset")

    def piece(k):
        return pieces[k] if extra is None else put(pieces[k], extra[k])

    def put(x, y):
        return x.at[: y.shape[0]].add(y)

    if size == 4:
        far = pieces[3] + xor_exchange(pieces[2], "offset", 1)
        if extra is not None:
            far = put(far, extra[3] + across)
        moved = xor_exchange(far, "offset", 3)
        return [piece(0), xor_exchange(piece(1), "offset", 1), moved], far
    moved = [xor_exchange(piece(k), "offset", k) for k in range(1, size)]
    return [piece(0), *moved], moved[0]


def per_device(counts, band_offset, bin_mask, row_factors, col_factors):
    rows, slots, tile = counts.shape[:3]
    factors = row_factors.shape[0]
    offset_count = lax.axis_size("offset")
    genome_count = lax.axis_size("genome")
    g = lax.axis_index("genome")
    o = lax.axis_index("offset").astype(jnp.int32)
    reach = slots * offset_count - 1
    pad = reach + 1

    line = jnp.broadcast_to(g, (1, tile))
    even = (line % 2 == 0).astype(F32)
    has_next = (line < genome_count - 1).astype(F32)
    has_prev = (line > 0).astype(F32)
    count = offset_count * -(-pad * offset_count // rows)
    index = lax.broadcasted_iota(jnp.int32, (count, tile), 0)
    share, k = index // offset_count, index % offset_count
    mine = (jnp.bitwise_xor(share, k) == o).astype(F32) * has_prev
    flags = jnp.concatenate([even, has_next, has_prev, mine])
    before = jnp.broadcast_to((g > 0).astype(jnp.int32), (1,))
    scal = jnp.concatenate([jnp.broadcast_to(o, (1,)), band_offset, before])
    flags, scal, bin_mask = lax.optimization_barrier((flags, scal, bin_mask))
    even, has_next, has_prev = flags[0:1], flags[1:2], flags[2:3]
    mine = flags[3:]

    mask = bin_mask.astype(F32).reshape(rows, tile)
    mask_next, _ = both_sides(mask[:pad], even)
    keep = lax.broadcasted_iota(jnp.int32, (pad, 1), 0) < reach
    mask_ext = jnp.concatenate([mask, jnp.where(keep, mask_next * has_next, 0.0)])

    scales = []
    ratios = []
    cut = [0] + [(rows * (3 * t + 3) // (8 * STEP)) * STEP for t in range(ITERS - 1)] + [rows]
    for t in range(ITERS):
        if t == 0:
            u = mask_ext
            counts = pltpu.with_memory_space_constraint(counts, pltpu.HBM)
            edge_v, edge, kept = first_edge(scal, counts, u)
        else:
            edge_v, edge, u = cover_edge(scal, kept, mask_ext, parts, ratios[0])
        scales.append(u)
        after, before = both_sides(edge, even)
        if t == 0:
            v, kept = first_main(scal, counts, u, edge_v, kept)
            col_late, _ = lax.optimization_barrier((col_factors, v))
            ring_left = [(i, (i - 1) % genome_count) for i in range(genome_count)]
            col_next = lax.ppermute(col_late[:, : pad * tile], "genome", ring_left)
            col_next = jnp.where(has_next[:, :1] > 0, col_next, 1.0)
            col_ext = jnp.concatenate([col_factors, col_next], axis=1)
        else:
            v = cover_main(scal, kept, u, edge_v)
        front = v[:pad] + before[pad:] * has_prev
        back = v[rows:] + after[:pad] * has_next
        x = jnp.concatenate([front, v[pad:rows], back])
        parts = [x] + [xor_exchange(x, "offset", k) for k in range(1, offset_count)]
        ratios = ratio(
            scal, kept, row_factors, col_ext, x, ratios, cut[t], cut[t + 1] - cut[t]
        )

    r_hi, r_lo = ratios
    u, tail, sums, h_parts = numer_col(scal, r_hi, r_lo, row_factors, mask_ext, parts, scales)
    w_parts = numer_row(scal, r_hi, r_lo, col_ext, u, offset_count)
    per = rows // offset_count

    right = [(i, (i + 1) % genome_count) for i in range(genome_count)]
    arrived = lax.ppermute(tail, "genome", right)
    if offset_count == 4 and pad <= per:
        diagonal = [
            (i * 4 + j, (i + 1) % genome_count * 4 + (j ^ 1))
            for i in range(genome_count)
            for j in range(4)
        ]
        across = lax.ppermute(tail[:pad], ("genome", "offset"), diagonal)
        extra = [arrived[:pad] * mine[k : k + 1] for k in range(4)]
        h_terms, half_way = scatter_terms(h_parts, extra, across * mine[3:4])
    else:
        h_parts = list(h_parts)
        for s in range(-(-pad // per)):
            piece = arrived[s * per : min(pad, (s + 1) * per)]
            for k in range(offset_count):
                at = s * offset_count + k
                h_parts[k] = h_parts[k].at[: piece.shape[0]].add(piece * mine[at : at + 1])
        h_terms, half_way = scatter_terms(h_parts)
    w_terms, half_way_too = scatter_terms(w_parts)

    sums, _ = lax.optimization_barrier((sums, half_way_too))
    sums = jnp.sum(lax.all_gather(sums, "genome"), axis=0)
    bias = (u[:rows] * mean_scale(sums)).reshape(-1)

    row_terms = coefficient(
        row_coefficient_kernel, scal, offset_count, row_factors, mask_ext, col_ext
    )
    col_terms = coefficient(
        col_coefficient_kernel, scal, offset_count, col_factors, mask_ext, row_factors, arrived[pad]
    )
    col_update = update(scal, sums, *col_terms, h_terms)
    row_update = update(scal, sums, *row_terms, w_terms)
    return bias, row_update, col_update


def solution(mesh):
    return jax.shard_map(
        per_device,
        mesh=mesh,
        in_specs=(
            P("genome", "offset", None, None),
            P("offset"),
            P("genome"),
            P(None, "genome"),
            P(None, "genome"),
        ),
        out_specs=(P("genome"), P(None, ("genome", "offset")), P(None, ("genome", "offset"))),
        check_vma=False,
    )
```

time: 108 us -> 106 us (0.981)
  blocking collectives: 0 us -> 8.95 us
  local copies, waits for them, and re-layouts: 6.04 us -> 0.57 us
  starting transfers between devices: 34.6 us -> 30.4 us
  other arithmetic: 4.83 us -> 2.77 us
  Pallas kernels: 35.7 us -> 37.7 us
    all_gather x0 -> x1, blocking collectives: none -> 8.95 us  [per_device(): sums = jnp.sum(lax.all_gather(sums, 'genome'), axis=0)]
    ppermute x18 -> x15, starting transfers between devices: 23.9 us -> 17.8 us  [xor_exchange(): lax.ppermute(x, axis, [(i, i ^ k) for i in range(lax.axis_size(axis))])]
    unnamed x10 -> x4, local copies, waits for them, and re-layouts: 4.42 us -> 0.01 us
    ppermute x18 -> x15, waiting for transfers between devices: 24.2 us -> 20.2 us  [xor_exchange(): lax.ppermute(x, axis, [(i, i ^ k) for i in range(lax.axis_size(axis))])]
    ppermute x2 -> x3, starting transfers between devices: 0.07 us -> 2.61 us  [the longest x1 2.42 us: per_device(): across = lax.ppermute(tail[:pad], ('genome', 'offset'), diagonal)]
    ppermute x5 -> x4, starting transfers between devices: 8.43 us -> 6.33 us  [both_sides(): lax.ppermute(x, 'genome', [(i, ((i + 1 ^ 1) - 1) % size) for i in range(s...]
    pallas_call x14 -> x15, Pallas kernels: 35.7 us -> 37.7 us  [kernel_call(): pl.pallas_call(body, grid_spec=pltpu.PrefetchScalarGridSpec(num_scalar_pr...]
    ppermute x2 -> x3, waiting for transfers between devices: 0.01 us -> 1.73 us  [the longest x1 1.73 us: per_device(): across = lax.ppermute(tail[:pad], ('genome', 'offset'), diagonal)]
  transfers between devices with their start and end apart: 30 -> 26, of which waited for: 6 -> 7; matrix products, arithmetic and copies ran while one was open for 6% -> 1% of each run, Pallas kernels for 29% -> 25%
where the time goes in v4:
time: 106 us; the launch traced here: 105 us
  Pallas kernels  37.7 us (36%)
  starting transfers between devices  30.4 us (29%)
  waiting for transfers between devices  23.3 us (22%)
  blocking collectives  8.95 us (8%)
  other arithmetic  2.77 us (3%)
  between operations  1.69 us (2%)
    pallas_call x15, Pallas kernels, kernel_call(): pl.pallas_call(body, grid_spec=pltpu.PrefetchScalarGridSpec(num_scalar_pr...  37.7 us
    ppermute x15, waiting for transfers between devices, xor_exchange(): lax.ppermute(x, axis, [(i, i ^ k) for i in range(lax.axis_size(axis))])  20.2 us
    ppermute x15, starting transfers between devices, xor_exchange(): lax.ppermute(x, axis, [(i, i ^ k) for i in range(lax.axis_size(axis))])  17.8 us
    all_gather x1, blocking collectives, per_device(): sums = jnp.sum(lax.all_gather(sums, 'genome'), axis=0)  8.95 us
    ppermute x4, starting transfers between devices, both_sides(): lax.ppermute(x, 'genome', [(i, ((i + 1 ^ 1) - 1) % size) for i in range(s...  6.33 us
    ppermute x4, starting transfers between devices, both_sides(): a = lax.ppermute(x, 'genome', [(i, i ^ 1) for i in range(size)])  3.62 us
    ppermute x1, starting transfers between devices, per_device(): across = lax.ppermute(tail[:pad], ('genome', 'offset'), diagonal)  2.42 us
  transfers between devices with their start and end apart: 26, of which 7 were waited for; matrix products, arithmetic and copies ran while one was open for 1% of the time, Pallas kernels for 25%

profile of v4, /device:TPU:0, one launch (start us, length us, event | category | flops | bytes accessed | tf_op | source)
XLA Modules:
  0.0 105.3 jit_solution(11013866346273709657)
XLA Ops:
  0.7 0.1 maximum_maximum_fusion
  0.9 0.7 pad_add_fusion.scal
  1.7 0.8 convert_bitcast_fusion
  2.4 0.5 collective-permute-start
  2.9 3.6 %collective-permute-start.1 = (f32[8,128]{1,0:T(8,128)S(1)}, f32[8,128]{1,0:T(8,128)S(1)}, u32[]{:S(2)}, u32[]{:S(2)}) collective-permute-start(f32[8,128]{1,0:T(8,128)S(1)} %slice_bitcast_fusion.1), channel_id=1, source_target_pairs={{0,28},{4,8},{8,4},{12,16},{16,12},{20,24},{24,20},{28,0},{1,29},{... | collective-permute-start | bytes 12296 | tf_op jit(solution)/shard_map/ppermute | solution.py:527
  6.5 1.3 %collective-permute-done.1 = f32[8,128]{1,0:T(8,128)S(1)} collective-permute-done((f32[8,128]{1,0:T(8,128)S(1)}, f32[8,128]{1,0:T(8,128)S(1)}, u32[]{:S(2)}, u32[]{:S(2)}) %collective-permute-start.1) | collective-permute-done | bytes 4128 | tf_op jit(solution)/shard_map/ppermute | solution.py:527
  7.8 3.0 %first_edge.1 = (f32[72,128]{1,0:T(8,128)S(1)}, f32[16,128]{1,0:T(8,128)S(1)}, f32[64,2,128,128]{3,2,1,0:T(8,128)S(1)}) custom-call(s32[4]{0:T(128)S(1)} %pad_add_fusion.scal, s32[64,2,128,128]{3,2,1,0:T(8,128)} %hbm.3, f32[72,128]{1,0:T(8,128)S(1)} %pad_maximum_fusion.1.u_ref.mask.refs_4_), custom_call_target="tpu_custom_call" | custom-call | tf_op jit(solution)/shard_map/first_edge/pallas_call | solution.py:46
  10.8 2.7 %collective-permute-start.3 = (f32[16,128]{1,0:T(8,128)S(1)}, f32[16,128]{1,0:T(8,128)S(1)}, u32[]{:S(2)}, u32[]{:S(2)}) collective-permute-start(f32[16,128]{1,0:T(8,128)S(1)} %get-tuple-element.84), channel_id=1, source_target_pairs={{0,28},{4,8},{8,4},{12,16},{16,12},{20,24},{24,20},{28,0},{1,29},{... | collective-permute-start | bytes 24584 | tf_op jit(solution)/shard_map/ppermute | solution.py:527
  13.5 0.5 slice.193
  14.7 4.7 %first_main.1 = (f32[72,128]{1,0:T(8,128)S(1)}, f32[64,2,128,128]{3,2,1,0:T(8,128)S(1)}) custom-call(s32[4]{0:T(128)S(1)} %pad_add_fusion.scal, s32[64,2,128,128]{3,2,1,0:T(8,128)} %hbm.3, f32[72,128]{1,0:T(8,128)S(1)} %pad_maximum_fusion.1.u_ref.mask.refs_4_, f32[72,128]{1,0:T(8,128)S(1)} %get-tuple-element.79.edge_v, ...), custom_call_target="tpu_custom_call", output_to_operand_aliasing={{1}: (4, {})} | custom-call | tf_op jit(solution)/shard_map/first_main/pallas_call | solution.py:46
  19.4 0.1 collective-permute-start.2
  19.6 1.9 %collective-permute-start.5 = (f32[72,128]{1,0:T(8,128)S(1)}, f32[72,128]{1,0:T(8,128)S(1)}, u32[]{:S(2)}, u32[]{:S(2)}) collective-permute-start(f32[72,128]{1,0:T(8,128)S(1)} %pad_maximum_fusion.2.after.refs_0_), channel_id=1, source_target_pairs={{0,1},{1,0},{2,3},{3,2},{4,5},{5,4},{6,7},{7,6},{8,9},{9,8},{10,11... | collective-permute-start | bytes 110600 | tf_op jit(solution)/shard_map/ppermute | solution.py:521
  21.4 2.5 %collective-permute-start.6 = (f32[72,128]{1,0:T(8,128)S(1)}, f32[72,128]{1,0:T(8,128)S(1)}, u32[]{:S(2)}, u32[]{:S(2)}) collective-permute-start(f32[72,128]{1,0:T(8,128)S(1)} %pad_maximum_fusion.2.after.refs_0_), channel_id=1, source_target_pairs={{0,2},{1,3},{2,0},{3,1},{4,6},{5,7},{6,4},{7,5},{8,10},{9,11},{10,... | collective-permute-start | bytes 110600 | tf_op jit(solution)/shard_map/ppermute | solution.py:521
  23.9 0.1 collective-permute-start.7
  24.0 0.1 pad_maximum_fusion.h_ref.other
  24.1 2.9 %ratio.3 = (bf16[64,128,256]{2,1,0:T(8,128)(2,1)S(1)}, bf16[64,128,256]{2,1,0:T(8,128)(2,1)S(1)}) custom-call(s32[4]{0:T(128)S(1)} %pad_add_fusion.scal, f32[64,2,128,128]{3,2,1,0:T(8,128)S(1)} %get-tuple-element.81.kept, f32[32,8192]{1,0:T(8,128)S(1)} %copy-done, f32[32,9216]{1,0:T(8,128)S(1)} %pad_maximum_fusion.h_ref.other, ...), custom_call_target="tpu_custom_call" | custom-call | tf_op jit(solution)/shard_map/ratio/pallas_call | solution.py:46
  27.1 2.6 %collective-permute-done.7.refs_3_ = f32[72,128]{1,0:T(8,128)S(1)} collective-permute-done((f32[72,128]{1,0:T(8,128)S(1)}, f32[72,128]{1,0:T(8,128)S(1)}, u32[]{:S(2)}, u32[]{:S(2)}) %collective-permute-start.7) | collective-permute-done | bytes 36896 | tf_op jit(solution)/shard_map/ppermute | solution.py:521
  29.7 1.4 %cover_edge.2 = (f32[72,128]{1,0:T(8,128)S(1)}, f32[16,128]{1,0:T(8,128)S(1)}, f32[72,128]{1,0:T(8,128)S(1)}) custom-call(s32[4]{0:T(128)S(1)} %pad_add_fusion.scal, f32[64,2,128,128]{3,2,1,0:T(8,128)S(1)} %get-tuple-element.81.kept, f32[72,128]{1,0:T(8,128)S(1)} %pad_maximum_fusion.1.u_ref.mask.refs_4_, f32[72,128]{1,0:T(8,128)S(1)} %pad_maximum_fusion.2.after.refs_0_, ...), custom_call_target="tpu_custom_call" | custom-call | tf_op jit(solution)/shard_map/cover_edge/pallas_call | solution.py:46
  31.1 2.1 %collective-permute-start.9 = (f32[16,128]{1,0:T(8,128)S(1)}, f32[16,128]{1,0:T(8,128)S(1)}, u32[]{:S(2)}, u32[]{:S(2)}) collective-permute-start(f32[16,128]{1,0:T(8,128)S(1)} %get-tuple-element.88), channel_id=1, source_target_pairs={{0,4},{4,0},{8,12},{12,8},{16,20},{20,16},{24,28},{28,24},{1,5},{5... | collective-permute-start | bytes 24584 | tf_op jit(solution)/shard_map/ppermute | solution.py:526
  33.2 2.8 %cover_main.2 = f32[72,128]{1,0:T(8,128)S(1)} custom-call(s32[4]{0:T(128)S(1)} %pad_add_fusion.scal, f32[64,2,128,128]{3,2,1,0:T(8,128)S(1)} %get-tuple-element.81.kept, f32[72,128]{1,0:T(8,128)S(1)} %get-tuple-element.86.u_ref.refs_5_, f32[72,128]{1,0:T(8,128)S(1)} %get-tuple-element.87.edge_v), custom_call_target="tpu_custom_call" | custom-call | tf_op jit(solution)/shard_map/cover_main/pallas_call | solution.py:46
  36.1 1.6 %collective-permute-start.11 = (f32[72,128]{1,0:T(8,128)S(1)}, f32[72,128]{1,0:T(8,128)S(1)}, u32[]{:S(2)}, u32[]{:S(2)}) collective-permute-start(f32[72,128]{1,0:T(8,128)S(1)} %pad_maximum_fusion.3.after.refs_0_), channel_id=1, source_target_pairs={{0,2},{1,3},{2,0},{3,1},{4,6},{5,7},{6,4},{7,5},{8,10},{9,11},{10,... | collective-permute-start | bytes 110600 | tf_op jit(solution)/shard_map/ppermute | solution.py:521
  37.8 2.7 %collective-permute-start.12 = (f32[72,128]{1,0:T(8,128)S(1)}, f32[72,128]{1,0:T(8,128)S(1)}, u32[]{:S(2)}, u32[]{:S(2)}) collective-permute-start(f32[72,128]{1,0:T(8,128)S(1)} %pad_maximum_fusion.3.after.refs_0_), channel_id=1, source_target_pairs={{0,3},{1,2},{2,1},{3,0},{4,7},{5,6},{6,5},{7,4},{8,11},{9,10},{10,... | collective-permute-start | bytes 110600 | tf_op jit(solution)/shard_map/ppermute | solution.py:521
  40.5 2.7 %ratio.4 = (bf16[64,128,256]{2,1,0:T(8,128)(2,1)S(1)}, bf16[64,128,256]{2,1,0:T(8,128)(2,1)S(1)}) custom-call(s32[4]{0:T(128)S(1)} %pad_add_fusion.scal, f32[64,2,128,128]{3,2,1,0:T(8,128)S(1)} %get-tuple-element.81.kept, f32[32,8192]{1,0:T(8,128)S(1)} %copy-done, ...), custom_call_target="tpu_custom_call", output_to_operand_aliasing={{0}: (5, {}), {1}: (6, {})} | custom-call | tf_op jit(solution)/shard_map/ratio/pallas_call | solution.py:46
  43.2 0.3 collective-permute-done.12.refs_3_
  43.5 1.4 %cover_edge.3 = (f32[72,128]{1,0:T(8,128)S(1)}, f32[16,128]{1,0:T(8,128)S(1)}, f32[72,128]{1,0:T(8,128)S(1)}) custom-call(s32[4]{0:T(128)S(1)} %pad_add_fusion.scal, f32[64,2,128,128]{3,2,1,0:T(8,128)S(1)} %get-tuple-element.81.kept, f32[72,128]{1,0:T(8,128)S(1)} %pad_maximum_fusion.1.u_ref.mask.refs_4_, f32[72,128]{1,0:T(8,128)S(1)} %pad_maximum_fusion.3.after.refs_0_, ...), custom_call_target="tpu_custom_call" | custom-call | tf_op jit(solution)/shard_map/cover_edge/pallas_call | solution.py:46
  45.0 1.1 %collective-permute-start.14 = (f32[16,128]{1,0:T(8,128)S(1)}, f32[16,128]{1,0:T(8,128)S(1)}, u32[]{:S(2)}, u32[]{:S(2)}) collective-permute-start(f32[16,128]{1,0:T(8,128)S(1)} %get-tuple-element.93), channel_id=1, source_target_pairs={{0,4},{4,0},{8,12},{12,8},{16,20},{20,16},{24,28},{28,24},{1,5},{5... | collective-permute-start | bytes 24584 | tf_op jit(solution)/shard_map/ppermute | solution.py:526
  46.1 2.8 %cover_main.3 = f32[72,128]{1,0:T(8,128)S(1)} custom-call(s32[4]{0:T(128)S(1)} %pad_add_fusion.scal, f32[64,2,128,128]{3,2,1,0:T(8,128)S(1)} %get-tuple-element.81.kept, f32[72,128]{1,0:T(8,128)S(1)} %get-tuple-element.91.u_ref.refs_6_, f32[72,128]{1,0:T(8,128)S(1)} %get-tuple-element.92.edge_v), custom_call_target="tpu_custom_call" | custom-call | tf_op jit(solution)/shard_map/cover_main/pallas_call | solution.py:46
  49.1 3.3 %collective-permute-start.16 = (f32[72,128]{1,0:T(8,128)S(1)}, f32[72,128]{1,0:T(8,128)S(1)}, u32[]{:S(2)}, u32[]{:S(2)}) collective-permute-start(f32[72,128]{1,0:T(8,128)S(1)} %pad_maximum_fusion.4.after.refs_0_), channel_id=1, source_target_pairs={{0,2},{1,3},{2,0},{3,1},{4,6},{5,7},{6,4},{7,5},{8,10},{9,11},{10,... | collective-permute-start | bytes 110600 | tf_op jit(solution)/shard_map/ppermute | solution.py:521
  52.3 1.1 %collective-permute-start.17 = (f32[72,128]{1,0:T(8,128)S(1)}, f32[72,128]{1,0:T(8,128)S(1)}, u32[]{:S(2)}, u32[]{:S(2)}) collective-permute-start(f32[72,128]{1,0:T(8,128)S(1)} %pad_maximum_fusion.4.after.refs_0_), channel_id=1, source_target_pairs={{0,3},{1,2},{2,1},{3,0},{4,7},{5,6},{6,5},{7,4},{8,11},{9,10},{10,... | collective-permute-start | bytes 110600 | tf_op jit(solution)/shard_map/ppermute | solution.py:521
  53.4 2.0 %ratio.5 = (bf16[64,128,256]{2,1,0:T(8,128)(2,1)S(1)}, bf16[64,128,256]{2,1,0:T(8,128)(2,1)S(1)}) custom-call(s32[4]{0:T(128)S(1)} %pad_add_fusion.scal, f32[64,2,128,128]{3,2,1,0:T(8,128)S(1)} %get-tuple-element.81.kept, f32[32,8192]{1,0:T(8,128)S(1)} %copy-done, ...), custom_call_target="tpu_custom_call", output_to_operand_aliasing={{0}: (5, {}), {1}: (6, {})} | custom-call | tf_op jit(solution)/shard_map/ratio/pallas_call | solution.py:46
  55.4 2.7 %collective-permute-done.17.refs_3_ = f32[72,128]{1,0:T(8,128)S(1)} collective-permute-done((f32[72,128]{1,0:T(8,128)S(1)}, f32[72,128]{1,0:T(8,128)S(1)}, u32[]{:S(2)}, u32[]{:S(2)}) %collective-permute-start.17) | collective-permute-done | bytes 36896 | tf_op jit(solution)/shard_map/ppermute | solution.py:521
  58.1 4.4 %numer_col.1 = (f32[72,128]{1,0:T(8,128)S(1)}, f32[9,32,128]{2,1,0:T(8,128)S(1)}, f32[8,128]{1,0:T(8,128)S(1)}, f32[16,32,128]{2,1,0:T(8,128)S(1)}, f32[16,32,12...) custom-call(s32[4]{0:T(128)S(1)} %pad_add_fusion.scal, ...), custom_call_target="tpu_custom_call" | custom-call | tf_op jit(solution)/shard_map/numer_col/pallas_call | solution.py:46
  62.6 0.7 coefficient.2
  63.4 2.4 %collective-permute-start.24 = (f32[8,32,128]{2,1,0:T(8,128)S(1)}, f32[8,32,128]{2,1,0:T(8,128)S(1)}, u32[]{:S(2)}, u32[]{:S(2)}) collective-permute-start(f32[8,32,128]{2,1,0:T(8,128)S(1)} %slice.224), channel_id=1, source_target_pairs={{0,5},{1,4},{2,7},{3,6},{4,9},{5,8},{6,11},{7,10},{8,13},{9,12},{1... | collective-permute-start | bytes 393224 | tf_op jit(solution)/shard_map/ppermute | solution.py:622
  65.8 5.4 %numer_row.1 = (f32[16,32,128]{2,1,0:T(8,128)S(1)}, f32[16,32,128]{2,1,0:T(8,128)S(1)}, f32[16,32,128]{2,1,0:T(8,128)S(1)}, f32[16,32,128]{2,1,0:T(8,128)S(1)}) custom-call(s32[4]{0:T(128)S(1)} %pad_add_fusion.scal, bf16[64,128,256]{2,1,0:T(8,128)(2,1)S(1)} %get-tuple-element.95.hi_ref, bf16[64,128,256]{2,1,0:T(8,128)(2,1)S(1)} %get-tuple-element.96.lo_ref, ...), custom_call_target="tpu_custom_call" | custom-call | tf_op jit(solution)/shard_map/numer_row/pallas_call | solution.py:46
  71.2 0.3 collective-permute-start.18
  71.5 1.7 %collective-permute-start.19 = (f32[16,32,128]{2,1,0:T(8,128)S(1)}, f32[16,32,128]{2,1,0:T(8,128)S(1)}, u32[]{:S(2)}, u32[]{:S(2)}) collective-permute-start(f32[16,32,128]{2,1,0:T(8,128)S(1)} %get-tuple-element.105), channel_id=1, source_target_pairs={{0,1},{1,0},{2,3},{3,2},{4,5},{5,4},{6,7},{7,6},{8,9},{9,8},{10,11... | collective-permute-start | bytes 786440 | tf_op jit(solution)/shard_map/ppermute | solution.py:521
  73.2 0.9 coefficient.3
  74.2 1.7 %collective-permute-done.24 = f32[8,32,128]{2,1,0:T(8,128)S(1)} collective-permute-done((f32[8,32,128]{2,1,0:T(8,128)S(1)}, f32[8,32,128]{2,1,0:T(8,128)S(1)}, u32[]{:S(2)}, u32[]{:S(2)}) %collective-permute-start.24) | collective-permute-done | bytes 131104 | tf_op jit(solution)/shard_map/ppermute | solution.py:622
  76.0 0.1 fusion
  76.1 1.2 %collective-permute-start.25 = (f32[16,32,128]{2,1,0:T(8,128)S(1)}, f32[16,32,128]{2,1,0:T(8,128)S(1)}, u32[]{:S(2)}, u32[]{:S(2)}) collective-permute-start(f32[16,32,128]{2,1,0:T(8,128)S(1)} %get-tuple-element.113), channel_id=1, source_target_pairs={{0,3},{1,2},{2,1},{3,0},{4,7},{5,6},{6,5},{7,4},{8,11},{9,10},{10,... | collective-permute-start | bytes 786440 | tf_op jit(solution)/shard_map/ppermute | solution.py:521
  77.3 3.2 %collective-permute-done.18 = f32[16,32,128]{2,1,0:T(8,128)S(1)} collective-permute-done((f32[16,32,128]{2,1,0:T(8,128)S(1)}, f32[16,32,128]{2,1,0:T(8,128)S(1)}, u32[]{:S(2)}, u32[]{:S(2)}) %collective-permute-start.18) | collective-permute-done | bytes 262176 | tf_op jit(solution)/shard_map/ppermute | solution.py:521
  80.5 1.1 %collective-permute-start.20 = (f32[16,32,128]{2,1,0:T(8,128)S(1)}, f32[16,32,128]{2,1,0:T(8,128)S(1)}, u32[]{:S(2)}, u32[]{:S(2)}) collective-permute-start(f32[16,32,128]{2,1,0:T(8,128)S(1)} %add.72), channel_id=1, source_target_pairs={{0,3},{1,2},{2,1},{3,0},{4,7},{5,6},{6,5},{7,4},{8,11},{9,10},{10,... | collective-permute-start | bytes 786440 | tf_op jit(solution)/shard_map/ppermute | solution.py:521
  81.6 9.0 %all-gather = f32[64,128]{1,0:T(8,128)S(1)} all-gather(f32[8,128]{1,0:T(8,128)S(1)} %get-tuple-element.101), channel_id=2, replica_groups=mesh['genome'=8,'offset'=4] {'genome'}, dimensions={0}, use_global_device_ids=true | all-gather | bytes 36864 | tf_op jit(solution)/shard_map/all_gather | solution.py:636
  90.6 0.6 multiply_bitcast_fusion
  91.2 11.4 %collective-permute-done.22.refs_1_ = f32[16,32,128]{2,1,0:T(8,128)S(1)} collective-permute-done((f32[16,32,128]{2,1,0:T(8,128)S(1)}, f32[16,32,128]{2,1,0:T(8,128)S(1)}, u32[]{:S(2)}, u32[]{:S(2)}) %collective-permute-start.22) | collective-permute-done | bytes 262176 | tf_op jit(solution)/shard_map/ppermute | solution.py:521
  102.7 1.3 %update.3 = f32[32,2048]{1,0:T(8,128)} custom-call(s32[4]{0:T(128)S(1)} %pad_add_fusion.scal, f32[8,128]{1,0:T(8,128)S(1)} %bitcast_reduce_fusion.sums, f32[16,32,128]{2,1,0:T(8,128)S(1)} %get-tuple-element.107.times, f32[16,32,128]{2,1,0:T(8,128)S(1)} %get-tuple-element.108.plus, f32[16,32,128]{2,1,0:T(8,128)S(1)} %get-tuple-element.115.refs_0_, ...), custom_call_target="tpu_custom_call" | custom-call | tf_op jit(solution)/shard_map/update/pallas_call | solution.py:46
  104.0 1.3 %update.2 = f32[32,2048]{1,0:T(8,128)} custom-call(s32[4]{0:T(128)S(1)} %pad_add_fusion.scal, f32[8,128]{1,0:T(8,128)S(1)} %bitcast_reduce_fusion.sums, f32[16,32,128]{2,1,0:T(8,128)S(1)} %get-tuple-element.102.times, f32[16,32,128]{2,1,0:T(8,128)S(1)} %get-tuple-element.103.plus, f32[16,32,128]{2,1,0:T(8,128)S(1)} %get-tuple-element.104.refs_0_, ...), custom_call_target="tpu_custom_call" | custom-call | tf_op jit(solution)/shard_map/update/pallas_call | solution.py:46
  (59 shorter events, 1.0 us)
Async XLA Ops:
  2.4 4.0 %collective-permute-start = (f32[8,128]{1,0:T(8,128)S(1)}, f32[8,128]{1,0:T(8,128)S(1)}, u32[]{:S(2)}, u32[]{:S(2)}) collective-permute-start(f32[8,128]{1,0:T(8,128)S(1)} %slice_bitcast_fusion.1), channel_id=1, source_target_pairs={{0,4},{4,0},{8,12},{12,8},{16,20},{20,16},{24,28},{28,24},{1,5},{5... | collective-permute-start | bytes 12296 | tf_op jit(solution)/shard_map/ppermute | solution.py:526
  2.9 4.9 %collective-permute-start.1 = (f32[8,128]{1,0:T(8,128)S(1)}, f32[8,128]{1,0:T(8,128)S(1)}, u32[]{:S(2)}, u32[]{:S(2)}) collective-permute-start(f32[8,128]{1,0:T(8,128)S(1)} %slice_bitcast_fusion.1), channel_id=1, source_target_pairs={{0,28},{4,8},{8,4},{12,16},{16,12},{20,24},{24,20},{28,0},{1,29},{... | collective-permute-start | bytes 12296 | tf_op jit(solution)/shard_map/ppermute | solution.py:527
  10.8 8.7 %collective-permute-start.3 = (f32[16,128]{1,0:T(8,128)S(1)}, f32[16,128]{1,0:T(8,128)S(1)}, u32[]{:S(2)}, u32[]{:S(2)}) collective-permute-start(f32[16,128]{1,0:T(8,128)S(1)} %get-tuple-element.84), channel_id=1, source_target_pairs={{0,28},{4,8},{8,4},{12,16},{16,12},{20,24},{24,20},{28,0},{1,29},{... | collective-permute-start | bytes 24584 | tf_op jit(solution)/shard_map/ppermute | solution.py:527
  13.5 6.1 %collective-permute-start.4 = (f32[16,128]{1,0:T(8,128)S(1)}, f32[16,128]{1,0:T(8,128)S(1)}, u32[]{:S(2)}, u32[]{:S(2)}) collective-permute-start(f32[16,128]{1,0:T(8,128)S(1)} %get-tuple-element.84), channel_id=1, source_target_pairs={{0,4},{4,0},{8,12},{12,8},{16,20},{20,16},{24,28},{28,24},{1,5},{5... | collective-permute-start | bytes 24584 | tf_op jit(solution)/shard_map/ppermute | solution.py:526
  14.7 4.7 %copy-start.1 = (f32[32,8192]{1,0:T(8,128)S(1)}, f32[32,8192]{1,0:T(8,128)}, u32[]{:S(2)}) copy-start(f32[32,8192]{1,0:T(8,128)} %old_ref.3) | copy-start | bytes 3145732
  14.7 9.5 %copy-start = (f32[32,8192]{1,0:T(8,128)S(1)}, f32[32,8192]{1,0:T(8,128)}, u32[]{:S(2)}) copy-start(f32[32,8192]{1,0:T(8,128)} %other.1) | copy-start | bytes 3145732
  19.4 4.6 %collective-permute-start.2 = (f32[32,1024]{1,0:T(8,128)S(1)}, f32[32,1024]{1,0:T(8,128)S(1)}, u32[]{:S(2)}, u32[]{:S(2)}) collective-permute-start(f32[32,1024]{1,0:T(8,128)S(1)} %slice.194), channel_id=1, source_target_pairs={{0,28},{4,0},{8,4},{12,8},{16,12},{20,16},{24,20},{28,24},{1,29},{... | collective-permute-start | bytes 393224 | tf_op jit(solution)/shard_map/ppermute | solution.py:596
  19.6 7.4 %collective-permute-start.5 = (f32[72,128]{1,0:T(8,128)S(1)}, f32[72,128]{1,0:T(8,128)S(1)}, u32[]{:S(2)}, u32[]{:S(2)}) collective-permute-start(f32[72,128]{1,0:T(8,128)S(1)} %pad_maximum_fusion.2.after.refs_0_), channel_id=1, source_target_pairs={{0,1},{1,0},{2,3},{3,2},{4,5},{5,4},{6,7},{7,6},{8,9},{9,8},{10,11... | collective-permute-start | bytes 110600 | tf_op jit(solution)/shard_map/ppermute | solution.py:521
  21.4 5.6 %collective-permute-start.6 = (f32[72,128]{1,0:T(8,128)S(1)}, f32[72,128]{1,0:T(8,128)S(1)}, u32[]{:S(2)}, u32[]{:S(2)}) collective-permute-start(f32[72,128]{1,0:T(8,128)S(1)} %pad_maximum_fusion.2.after.refs_0_), channel_id=1, source_target_pairs={{0,2},{1,3},{2,0},{3,1},{4,6},{5,7},{6,4},{7,5},{8,10},{9,11},{10,... | collective-permute-start | bytes 110600 | tf_op jit(solution)/shard_map/ppermute | solution.py:521
  23.9 5.8 %collective-permute-start.7 = (f32[72,128]{1,0:T(8,128)S(1)}, f32[72,128]{1,0:T(8,128)S(1)}, u32[]{:S(2)}, u32[]{:S(2)}) collective-permute-start(f32[72,128]{1,0:T(8,128)S(1)} %pad_maximum_fusion.2.after.refs_0_), channel_id=1, source_target_pairs={{0,3},{1,2},{2,1},{3,0},{4,7},{5,6},{6,5},{7,4},{8,11},{9,10},{10,... | collective-permute-start | bytes 110600 | tf_op jit(solution)/shard_map/ppermute | solution.py:521
  31.0 5.0 %collective-permute-start.8 = (f32[16,128]{1,0:T(8,128)S(1)}, f32[16,128]{1,0:T(8,128)S(1)}, u32[]{:S(2)}, u32[]{:S(2)}) collective-permute-start(f32[16,128]{1,0:T(8,128)S(1)} %get-tuple-element.88), channel_id=1, source_target_pairs={{0,28},{4,8},{8,4},{12,16},{16,12},{20,24},{24,20},{28,0},{1,29},{... | collective-permute-start | bytes 24584 | tf_op jit(solution)/shard_map/ppermute | solution.py:527
  31.1 4.9 %collective-permute-start.9 = (f32[16,128]{1,0:T(8,128)S(1)}, f32[16,128]{1,0:T(8,128)S(1)}, u32[]{:S(2)}, u32[]{:S(2)}) collective-permute-start(f32[16,128]{1,0:T(8,128)S(1)} %get-tuple-element.88), channel_id=1, source_target_pairs={{0,4},{4,0},{8,12},{12,8},{16,20},{20,16},{24,28},{28,24},{1,5},{5... | collective-permute-start | bytes 24584 | tf_op jit(solution)/shard_map/ppermute | solution.py:526
  36.1 7.1 %collective-permute-start.10 = (f32[72,128]{1,0:T(8,128)S(1)}, f32[72,128]{1,0:T(8,128)S(1)}, u32[]{:S(2)}, u32[]{:S(2)}) collective-permute-start(f32[72,128]{1,0:T(8,128)S(1)} %pad_maximum_fusion.3.after.refs_0_), channel_id=1, source_target_pairs={{0,1},{1,0},{2,3},{3,2},{4,5},{5,4},{6,7},{7,6},{8,9},{9,8},{10,11... | collective-permute-start | bytes 110600 | tf_op jit(solution)/shard_map/ppermute | solution.py:521
  36.1 7.1 %collective-permute-start.11 = (f32[72,128]{1,0:T(8,128)S(1)}, f32[72,128]{1,0:T(8,128)S(1)}, u32[]{:S(2)}, u32[]{:S(2)}) collective-permute-start(f32[72,128]{1,0:T(8,128)S(1)} %pad_maximum_fusion.3.after.refs_0_), channel_id=1, source_target_pairs={{0,2},{1,3},{2,0},{3,1},{4,6},{5,7},{6,4},{7,5},{8,10},{9,11},{10,... | collective-permute-start | bytes 110600 | tf_op jit(solution)/shard_map/ppermute | solution.py:521
  37.8 5.8 %collective-permute-start.12 = (f32[72,128]{1,0:T(8,128)S(1)}, f32[72,128]{1,0:T(8,128)S(1)}, u32[]{:S(2)}, u32[]{:S(2)}) collective-permute-start(f32[72,128]{1,0:T(8,128)S(1)} %pad_maximum_fusion.3.after.refs_0_), channel_id=1, source_target_pairs={{0,3},{1,2},{2,1},{3,0},{4,7},{5,6},{6,5},{7,4},{8,11},{9,10},{10,... | collective-permute-start | bytes 110600 | tf_op jit(solution)/shard_map/ppermute | solution.py:521
  44.9 4.0 %collective-permute-start.13 = (f32[16,128]{1,0:T(8,128)S(1)}, f32[16,128]{1,0:T(8,128)S(1)}, u32[]{:S(2)}, u32[]{:S(2)}) collective-permute-start(f32[16,128]{1,0:T(8,128)S(1)} %get-tuple-element.93), channel_id=1, source_target_pairs={{0,28},{4,8},{8,4},{12,16},{16,12},{20,24},{24,20},{28,0},{1,29},{... | collective-permute-start | bytes 24584 | tf_op jit(solution)/shard_map/ppermute | solution.py:527
  45.0 4.0 %collective-permute-start.14 = (f32[16,128]{1,0:T(8,128)S(1)}, f32[16,128]{1,0:T(8,128)S(1)}, u32[]{:S(2)}, u32[]{:S(2)}) collective-permute-start(f32[16,128]{1,0:T(8,128)S(1)} %get-tuple-element.93), channel_id=1, source_target_pairs={{0,4},{4,0},{8,12},{12,8},{16,20},{20,16},{24,28},{28,24},{1,5},{5... | collective-permute-start | bytes 24584 | tf_op jit(solution)/shard_map/ppermute | solution.py:526
  49.0 6.4 %collective-permute-start.15 = (f32[72,128]{1,0:T(8,128)S(1)}, f32[72,128]{1,0:T(8,128)S(1)}, u32[]{:S(2)}, u32[]{:S(2)}) collective-permute-start(f32[72,128]{1,0:T(8,128)S(1)} %pad_maximum_fusion.4.after.refs_0_), channel_id=1, source_target_pairs={{0,1},{1,0},{2,3},{3,2},{4,5},{5,4},{6,7},{7,6},{8,9},{9,8},{10,11... | collective-permute-start | bytes 110600 | tf_op jit(solution)/shard_map/ppermute | solution.py:521
  49.1 6.4 %collective-permute-start.16 = (f32[72,128]{1,0:T(8,128)S(1)}, f32[72,128]{1,0:T(8,128)S(1)}, u32[]{:S(2)}, u32[]{:S(2)}) collective-permute-start(f32[72,128]{1,0:T(8,128)S(1)} %pad_maximum_fusion.4.after.refs_0_), channel_id=1, source_target_pairs={{0,2},{1,3},{2,0},{3,1},{4,6},{5,7},{6,4},{7,5},{8,10},{9,11},{10,... | collective-permute-start | bytes 110600 | tf_op jit(solution)/shard_map/ppermute | solution.py:521
  52.3 5.8 %collective-permute-start.17 = (f32[72,128]{1,0:T(8,128)S(1)}, f32[72,128]{1,0:T(8,128)S(1)}, u32[]{:S(2)}, u32[]{:S(2)}) collective-permute-start(f32[72,128]{1,0:T(8,128)S(1)} %pad_maximum_fusion.4.after.refs_0_), channel_id=1, source_target_pairs={{0,3},{1,2},{2,1},{3,0},{4,7},{5,6},{6,5},{7,4},{8,11},{9,10},{10,... | collective-permute-start | bytes 110600 | tf_op jit(solution)/shard_map/ppermute | solution.py:521
  62.5 10.8 %collective-permute-start.21 = (f32[9,32,128]{2,1,0:T(8,128)S(1)}, f32[9,32,128]{2,1,0:T(8,128)S(1)}, u32[]{:S(2)}, u32[]{:S(2)}) collective-permute-start(f32[9,32,128]{2,1,0:T(8,128)S(1)} %get-tuple-element.106), channel_id=1, source_target_pairs={{0,4},{4,8},{8,12},{12,16},{16,20},{20,24},{24,28},{28,0},{1,5},{5... | collective-permute-start | bytes 442376 | tf_op jit(solution)/shard_map/ppermute | solution.py:615
  62.5 11.6 %collective-permute-start.23 = (f32[16,32,128]{2,1,0:T(8,128)S(1)}, f32[16,32,128]{2,1,0:T(8,128)S(1)}, u32[]{:S(2)}, u32[]{:S(2)}) collective-permute-start(f32[16,32,128]{2,1,0:T(8,128)S(1)} %get-tuple-element.112), channel_id=1, source_target_pairs={{0,1},{1,0},{2,3},{3,2},{4,5},{5,4},{6,7},{7,6},{8,9},{9,8},{10,11... | collective-permute-start | bytes 786440 | tf_op jit(solution)/shard_map/ppermute | solution.py:521
  63.4 12.6 %collective-permute-start.24 = (f32[8,32,128]{2,1,0:T(8,128)S(1)}, f32[8,32,128]{2,1,0:T(8,128)S(1)}, u32[]{:S(2)}, u32[]{:S(2)}) collective-permute-start(f32[8,32,128]{2,1,0:T(8,128)S(1)} %slice.224), channel_id=1, source_target_pairs={{0,5},{1,4},{2,7},{3,6},{4,9},{5,8},{6,11},{7,10},{8,13},{9,12},{1... | collective-permute-start | bytes 393224 | tf_op jit(solution)/shard_map/ppermute | solution.py:622
  71.2 9.3 %collective-permute-start.18 = (f32[16,32,128]{2,1,0:T(8,128)S(1)}, f32[16,32,128]{2,1,0:T(8,128)S(1)}, u32[]{:S(2)}, u32[]{:S(2)}) collective-permute-start(f32[16,32,128]{2,1,0:T(8,128)S(1)} %get-tuple-element.100), channel_id=1, source_target_pairs={{0,1},{1,0},{2,3},{3,2},{4,5},{5,4},{6,7},{7,6},{8,9},{9,8},{10,11... | collective-permute-start | bytes 786440 | tf_op jit(solution)/shard_map/ppermute | solution.py:521
  71.5 32.5 %collective-permute-start.19 = (f32[16,32,128]{2,1,0:T(8,128)S(1)}, f32[16,32,128]{2,1,0:T(8,128)S(1)}, u32[]{:S(2)}, u32[]{:S(2)}) collective-permute-start(f32[16,32,128]{2,1,0:T(8,128)S(1)} %get-tuple-element.105), channel_id=1, source_target_pairs={{0,1},{1,0},{2,3},{3,2},{4,5},{5,4},{6,7},{7,6},{8,9},{9,8},{10,11... | collective-permute-start | bytes 786440 | tf_op jit(solution)/shard_map/ppermute | solution.py:521
  76.0 26.6 %collective-permute-start.22 = (f32[16,32,128]{2,1,0:T(8,128)S(1)}, f32[16,32,128]{2,1,0:T(8,128)S(1)}, u32[]{:S(2)}, u32[]{:S(2)}) collective-permute-start(f32[16,32,128]{2,1,0:T(8,128)S(1)} %get-tuple-element.114), channel_id=1, source_target_pairs={{0,1},{1,0},{2,3},{3,2},{4,5},{5,4},{6,7},{7,6},{8,9},{9,8},{10,11... | collective-permute-start | bytes 786440 | tf_op jit(solution)/shard_map/ppermute | solution.py:521
  76.1 26.6 %collective-permute-start.25 = (f32[16,32,128]{2,1,0:T(8,128)S(1)}, f32[16,32,128]{2,1,0:T(8,128)S(1)}, u32[]{:S(2)}, u32[]{:S(2)}) collective-permute-start(f32[16,32,128]{2,1,0:T(8,128)S(1)} %get-tuple-element.113), channel_id=1, source_target_pairs={{0,3},{1,2},{2,1},{3,0},{4,7},{5,6},{6,5},{7,4},{8,11},{9,10},{10,... | collective-permute-start | bytes 786440 | tf_op jit(solution)/shard_map/ppermute | solution.py:521
  80.5 23.5 %collective-permute-start.20 = (f32[16,32,128]{2,1,0:T(8,128)S(1)}, f32[16,32,128]{2,1,0:T(8,128)S(1)}, u32[]{:S(2)}, u32[]{:S(2)}) collective-permute-start(f32[16,32,128]{2,1,0:T(8,128)S(1)} %add.72), channel_id=1, source_target_pairs={{0,3},{1,2},{2,1},{3,0},{4,7},{5,6},{6,5},{7,4},{8,11},{9,10},{10,... | collective-permute-start | bytes 786440 | tf_op jit(solution)/shard_map/ppermute | solution.py:521

commit v5 on v4

--- a/solution.py
+++ b/solution.py
@@ -9,6 +9,7 @@
 
 ITERS = 3
 STEP = 8
+EARLY = 2
 F32 = jnp.float32
 BF16 = jnp.bfloat16
 VMEM_LIMIT = 20 * 1024 * 1024
@@ -33,7 +34,7 @@
 
 
 def scale_from(mask, parts):
-    cover = tree_sum([p[...] for p in parts])
+    cover = tree_sum([p[...] for p in parts[:1] + parts[:0:-1]])
     live = mask[...] > 0
     return jnp.where(live, 1.0 / jnp.where(live, cover, 1.0), 0.0)
 
@@ -130,41 +131,38 @@
     edge_out[pad:] = v_out[rows:]
 
 
-def first_edge_kernel(scal, hbm, u_ref, v_out, edge_out, kept, buffer, sems):
+def first_main_kernel(scal, hbm, mask, v_out, kept, buffer, sems):
     rows, slots = hbm.shape[:2]
     offs = offsets(scal, slots)
-    bases = edge_bases(rows, u_ref.shape[0] - rows)
+    pad = v_out.shape[0] - rows
+    inner = list(range(pad, rows - pad, STEP))
+    bases = inner + edge_bases(rows, pad)
     copies = block_copies(hbm, buffer, sems, bases)
     for copy in copies:
         copy.start()
     v_out[...] = jnp.zeros_like(v_out)
-    for copy in copies:
-        copy.wait()
-
-    def go(diagonal):
-        for k, base in enumerate(bases):
-            cover_block(offs, buffer, u_ref, v_out, base, diagonal, k * STEP, kept)
-
-    by_diagonal(offs, slots, go)
-    write_edge(v_out, edge_out, rows)
-
-
-def first_main_kernel(scal, hbm, u_ref, edge_v, kept_in, v_out, kept, buffer, sems):
-    rows, slots = hbm.shape[:2]
-    offs = offsets(scal, slots)
-    pad = u_ref.shape[0] - rows
-    bases = list(range(pad, rows - pad, STEP))
-    copies = block_copies(hbm, buffer, sems, bases)
-    for copy in copies:
-        copy.start()
-    v_out[...] = edge_v[...]
 
     def go(diagonal):
         for k, base in enumerate(bases):
             copies[k].wait()
-            cover_block(offs, buffer, u_ref, v_out, base, diagonal, k * STEP, kept)
+            at = k * STEP
+            if base in inner:
+                cover_block(offs, buffer, mask, v_out, base, diagonal, at, kept)
+            else:
+                for t in range(STEP):
+                    for s in range(slots):
+                        kept[base + t, s] = tile_value(buffer, at + t, s, diagonal)
 
     by_diagonal(offs, slots, go)
+
+
+def first_edge_kernel(scal, kept, u_ref, inner_v, v_out, edge_out):
+    rows, slots = kept.shape[:2]
+    offs = offsets(scal, slots)
+    v_out[...] = inner_v[...]
+    for base in edge_bases(rows, u_ref.shape[0] - rows):
+        cover_block(offs, kept, u_ref, v_out, base, -1, base)
+    write_edge(v_out, edge_out, rows)
 
 
 def edge_kernel(scal, kept, mask, *refs):
@@ -187,46 +185,25 @@
         cover_block(offs, kept, u_ref, v_out, base, -1, base)
 
 
-def first_edge(scal, counts, u):
+def first_main(scal, counts, mask, ext):
     rows, slots, tile = counts.shape[:3]
-    ext = u.shape[0]
-    pad = ext - rows
-    outs = [
-        jax.ShapeDtypeStruct(u.shape, F32),
-        jax.ShapeDtypeStruct((2 * pad, tile), F32),
-        pltpu.VMEM(counts.shape, F32),
-    ]
-    return kernel_call(
-        first_edge_kernel,
-        "first_edge",
-        scal,
-        [counts, u],
-        outs,
-        [
-            pltpu.VMEM((2 * pad, slots, tile, tile), counts.dtype),
-            pltpu.SemaphoreType.DMA((2 * pad // STEP,)),
-        ],
-        specs=[pl.BlockSpec(memory_space=pltpu.HBM), vmem()],
-    )
-
-
-def first_main(scal, counts, u, edge_v, kept):
-    rows, slots, tile = counts.shape[:3]
-    inner = rows - 2 * (u.shape[0] - rows)
-    outs = [jax.ShapeDtypeStruct(u.shape, F32), pltpu.VMEM(counts.shape, F32)]
+    outs = [jax.ShapeDtypeStruct((ext, tile), F32), pltpu.VMEM(counts.shape, F32)]
     return kernel_call(
         first_main_kernel,
         "first_main",
         scal,
-        [counts, u, edge_v, kept],
+        [counts, mask],
         outs,
-        [
-            pltpu.VMEM((inner, slots, tile, tile), counts.dtype),
-            pltpu.SemaphoreType.DMA((inner // STEP,)),
-        ],
-        aliases={4: 1},
-        specs=[pl.BlockSpec(memory_space=pltpu.HBM), vmem(), vmem(), vmem()],
-    )
+        [pltpu.VMEM(counts.shape, counts.dtype), pltpu.SemaphoreType.DMA((rows // STEP,))],
+        specs=[pl.BlockSpec(memory_space=pltpu.HBM), vmem()],
+    )
+
+
+def first_edge(scal, kept, u, inner_v):
+    rows, tile = kept.shape[0], kept.shape[2]
+    flat = jax.ShapeDtypeStruct(u.shape, F32)
+    edge = jax.ShapeDtypeStruct((2 * (u.shape[0] - rows), tile), F32)
+    return kernel_call(first_edge_kernel, "first_edge", scal, [kept, u, inner_v], [flat, edge])
 
 
 def cover_edge(scal, kept, mask_ext, parts, after):
@@ -242,11 +219,14 @@
     return kernel_call(main_kernel, "cover_main", scal, [kept, u, edge_v], outs)[0]
 
 
-def ratio_kernel(start, count, scal, kept, w_ref, h_ref, after, *refs):
-    hi_out, lo_out, h_terms = refs[-3:]
-    rows, slots, tile = kept.shape[:3]
+def ratio_kernel(start, count, pad, scal, kept, w_ref, h_ref, after, *refs):
+    slots, tile = kept.shape[1:3]
     offs = offsets(scal, slots)
-    pad = h_ref.shape[1] // tile - rows
+    if start == 0:
+        hi_out, lo_out, same, h_terms = refs
+        same[...] = after[...]
+    else:
+        hi_out, lo_out, h_terms = refs[-3:]
 
     def prepare(j, carry):
         hi, lo = split(h_ref[:, pl.ds(pl.multiple_of(j * tile, tile), tile)])
@@ -279,14 +259,14 @@
 def ratio(scal, kept, row_factors, col_ext, after, earlier, start, count):
     rows, slots, tile = kept.shape[:3]
     factors = row_factors.shape[0]
-    pad = col_ext.shape[1] // tile - rows
+    pad = after.shape[0] - rows
     out = pltpu.VMEM((rows, tile, slots * tile), BF16)
     return kernel_call(
-        functools.partial(ratio_kernel, start, count),
+        functools.partial(ratio_kernel, start, count, pad),
         "ratio",
         scal,
         [kept, row_factors, col_ext, after, *earlier],
-        [out, out],
+        [out, out] + [jax.ShapeDtypeStruct(after.shape, F32)] * (start == 0),
         [pltpu.VMEM((count + pad, 4 * factors, tile), BF16)],
         {5: 0, 6: 1} if earlier else {},
     )
@@ -311,16 +291,17 @@
     return big[:factors] + big[factors:] + small
 
 
-def col_loop(offs, w_ref, hi_ref, lo_ref, u_ref, acc, start, stop, shift):
+def col_loop(offs, w_ref, hi_ref, lo_ref, u_ref, acc, start, count, shift):
     tile = u_ref.shape[1]
 
-    def body(i, carry):
+    def body(n, carry):
+        i = start + n
         cols = col_numer(w_ref, hi_ref, lo_ref, u_ref, i)
         for s in range(hi_ref.shape[2] // tile):
             acc[i + offs[s] - shift] += cols[:, s * tile : (s + 1) * tile]
         return carry
 
-    lax.fori_loop(start, stop, body, 0, unroll=4)
+    lax.fori_loop(0, count, body, 0, unroll=4)
 
 
 def row_pieces(scal, offs, g_ref, hi_ref, lo_ref, u_ref, order, outs):
@@ -335,34 +316,73 @@
         lax.fori_loop(0, per, body, 0, unroll=4)
 
 
-def numer_col_kernel(shares, scal, hi_ref, lo_ref, w_ref, mask, *refs):
-    parts, scales, refs = refs[:shares], refs[shares : shares + ITERS], refs[shares + ITERS :]
-    u_out, tail_out, sums_out = refs[:3]
-    outs, acc = refs[3:-1], refs[-1]
+def scaled_terms(h_ref, u_ref, terms, start, count):
+    tile = u_ref.shape[1]
+    factors = h_ref.shape[0]
+
+    def fill(n, carry):
+        j = start + n
+        x = h_ref[:, pl.ds(pl.multiple_of(j * tile, tile), tile)] * u_ref[pl.ds(j, 1), :]
+        hi, lo = split(x)
+        terms[j, :factors] = hi
+        terms[j, factors:] = lo
+        return carry
+
+    lax.fori_loop(0, count, fill, 0, unroll=4)
+
+
+def numer_first_kernel(k, shares, scal, hi_ref, lo_ref, w_ref, mask, *refs):
+    parts, scales = refs[:shares], refs[shares : shares + ITERS]
+    u_out, tail_out, sums_out, out, acc = refs[shares + ITERS :]
     rows = hi_ref.shape[0]
     ext, tile = mask.shape
     offs = offsets(scal, hi_ref.shape[2] // tile)
     per = rows // shares
+    pad = ext - rows
     u_out[...] = scale_from(mask, parts)
+
     acc[...] = jnp.zeros_like(acc)
-    col_loop(offs, w_ref, hi_ref, lo_ref, u_out, acc, 0, rows, 0)
-    for k, out in enumerate(outs):
-        first = jnp.bitwise_xor(scal[0], k) * per
-
-        def body(t, carry):
-            out[t] = acc[first + t] * u_out[pl.ds(first + t, 1), :]
-            return carry
-
-        lax.fori_loop(0, per, body, 0, unroll=4)
-    for t in range(ext - rows):
-        tail_out[t] = acc[rows + t] * u_out[rows + t : rows + t + 1, :]
-    pad = ext - rows
+    col_loop(offs, w_ref, hi_ref, lo_ref, u_out, acc, rows - pad, pad, rows - pad)
+    for t in range(pad):
+        tail_out[t] = acc[pad + t] * u_out[rows + t : rows + t + 1, :]
     lane = lax.broadcasted_iota(jnp.int32, tail_out.shape[1:], 1)
     ends = jnp.zeros(tail_out.shape[1:], F32)
     for t in range(pad):
         ends = jnp.where(lane == t, tile_sum(w_ref, mask, rows - pad + t), ends)
     tail_out[pad] = ends
+
+    first = jnp.bitwise_xor(scal[0], k) * per
+    acc[...] = jnp.zeros_like(acc)
+    block = min(per, pad)
+    col_loop(offs, w_ref, hi_ref, lo_ref, u_out, acc, first, per, first - pad)
+    for q in range(1, pad // block + 1):
+
+        @pl.when(first >= q * block)
+        def _():
+            start = first - q * block
+            col_loop(offs, w_ref, hi_ref, lo_ref, u_out, acc, start, block, first - pad)
+
+    for t in range(per):
+        out[t] = acc[pad + t] * u_out[pl.ds(first + t, 1), :]
     write_sums(sums_out, [*scales, u_out], rows)
+
+
+def numer_col_kernel(order, scal, hi_ref, lo_ref, w_ref, u_ref, after, *refs):
+    outs, acc = refs[:-1], refs[-1]
+    rows = hi_ref.shape[0]
+    tile = u_ref.shape[1]
+    offs = offsets(scal, hi_ref.shape[2] // tile)
+    per = outs[0].shape[0]
+    acc[...] = jnp.zeros_like(acc)
+    col_loop(offs, w_ref, hi_ref, lo_ref, u_ref, acc, 0, rows, 0)
+    for k, out in zip(order, outs):
+        first = jnp.bitwise_xor(scal[0], k) * per
+
+        def body(t, carry):
+            out[t] = acc[first + t] * u_ref[pl.ds(first + t, 1), :]
+            return carry
+
+        lax.fori_loop(0, per, body, 0, unroll=4)
 
 
 def write_sums(sums_out, scales, rows):
@@ -377,43 +397,48 @@
         sums_out[t : t + 1, :] = jnp.broadcast_to(line, (1, mask.shape[1]))
 
 
-def numer_row_kernel(scal, hi_ref, lo_ref, h_ref, *refs):
-    u_ref, outs, terms = refs[0], refs[1:-1], refs[-1]
+def numer_row_kernel(scal, hi_ref, lo_ref, h_ref, u_ref, *refs):
+    outs, terms = refs[:-1], refs[-1]
     ext, tile = u_ref.shape
-    factors = h_ref.shape[0]
     offs = offsets(scal, hi_ref.shape[2] // tile)
-
-    def fill(j, carry):
-        x = h_ref[:, pl.ds(pl.multiple_of(j * tile, tile), tile)] * u_ref[pl.ds(j, 1), :]
-        hi, lo = split(x)
-        terms[j, :factors] = hi
-        terms[j, factors:] = lo
-        return carry
-
-    lax.fori_loop(0, ext, fill, 0, unroll=4)
+    scaled_terms(h_ref, u_ref, terms, 0, ext)
     row_pieces(scal, offs, terms, hi_ref, lo_ref, u_ref, range(len(outs)), outs)
 
 
-def numer_col(scal, r_hi, r_lo, row_factors, mask_ext, parts, scales):
+def numer_first(scal, r_hi, r_lo, row_factors, mask_ext, parts, scales, k):
     shares = len(parts)
     rows, tile = r_hi.shape[:2]
     factors = row_factors.shape[0]
     ext = mask_ext.shape[0]
+    pad = ext - rows
+    per = rows // shares
+    return kernel_call(
+        functools.partial(numer_first_kernel, k, shares),
+        "numer_first",
+        scal,
+        [r_hi, r_lo, row_factors, mask_ext, *parts, *scales],
+        [
+            jax.ShapeDtypeStruct((ext, tile), F32),
+            jax.ShapeDtypeStruct((pad + 1, factors, tile), F32),
+            jax.ShapeDtypeStruct((8, tile), F32),
+            jax.ShapeDtypeStruct((per, factors, tile), F32),
+        ],
+        [pltpu.VMEM((per + 2 * pad, factors, tile), F32)],
+    )
+
+
+def numer_col(scal, r_hi, r_lo, row_factors, u, after, order, shares):
+    rows, tile = r_hi.shape[:2]
+    factors = row_factors.shape[0]
     piece = jax.ShapeDtypeStruct((rows // shares, factors, tile), F32)
-    outs = [
-        jax.ShapeDtypeStruct((ext, tile), F32),
-        jax.ShapeDtypeStruct((ext - rows + 1, factors, tile), F32),
-        jax.ShapeDtypeStruct((8, tile), F32),
-    ]
-    res = kernel_call(
-        functools.partial(numer_col_kernel, shares),
+    return kernel_call(
+        functools.partial(numer_col_kernel, order),
         "numer_col",
         scal,
-        [r_hi, r_lo, row_factors, mask_ext, *parts, *scales],
-        outs + [piece] * shares,
-        [pltpu.VMEM((ext, factors, tile), F32)],
-    )
-    return *res[:3], res[3:]
+        [r_hi, r_lo, row_factors, u, after],
+        [piece] * len(order),
+        [pltpu.VMEM((u.shape[0], factors, tile), F32)],
+    )
 
 
 def numer_row(scal, r_hi, r_lo, col_ext, u, shares):
@@ -577,42 +602,55 @@
     keep = lax.broadcasted_iota(jnp.int32, (pad, 1), 0) < reach
     mask_ext = jnp.concatenate([mask, jnp.where(keep, mask_next * has_next, 0.0)])
 
+    counts = pltpu.with_memory_space_constraint(counts, pltpu.HBM)
+    inner_v, kept = first_main(scal, counts, mask, rows + pad)
+    col_late, _ = lax.optimization_barrier((col_factors, inner_v))
+    ring_left = [(i, (i - 1) % genome_count) for i in range(genome_count)]
+    col_next = lax.ppermute(col_late[:, : pad * tile], "genome", ring_left)
+    col_next = jnp.where(has_next[:, :1] > 0, col_next, 1.0)
+    col_ext = jnp.concatenate([col_factors, col_next], axis=1)
+
     scales = []
-    ratios = []
-    cut = [0] + [(rows * (3 * t + 3) // (8 * STEP)) * STEP for t in range(ITERS - 1)] + [rows]
+    quarter = rows // (ITERS + 1)
     for t in range(ITERS):
         if t == 0:
             u = mask_ext
-            counts = pltpu.with_memory_space_constraint(counts, pltpu.HBM)
-            edge_v, edge, kept = first_edge(scal, counts, u)
+            v, edge = first_edge(scal, kept, u, inner_v)
         else:
-            edge_v, edge, u = cover_edge(scal, kept, mask_ext, parts, ratios[0])
+            v, edge, u = cover_edge(scal, kept, mask_ext, parts, ratios[0])
         scales.append(u)
         after, before = both_sides(edge, even)
-        if t == 0:
-            v, kept = first_main(scal, counts, u, edge_v, kept)
-            col_late, _ = lax.optimization_barrier((col_factors, v))
-            ring_left = [(i, (i - 1) % genome_count) for i in range(genome_count)]
-            col_next = lax.ppermute(col_late[:, : pad * tile], "genome", ring_left)
-            col_next = jnp.where(has_next[:, :1] > 0, col_next, 1.0)
-            col_ext = jnp.concatenate([col_factors, col_next], axis=1)
+        if t > 0:
+            v = cover_main(scal, kept, u, v)
         else:
-            v = cover_main(scal, kept, u, edge_v)
+            *ratios, v = ratio(scal, kept, row_factors, col_factors, v, [], 0, quarter)
         front = v[:pad] + before[pad:] * has_prev
         back = v[rows:] + after[:pad] * has_next
         x = jnp.concatenate([front, v[pad:rows], back])
-        parts = [x] + [xor_exchange(x, "offset", k) for k in range(1, offset_count)]
-        ratios = ratio(
-            scal, kept, row_factors, col_ext, x, ratios, cut[t], cut[t + 1] - cut[t]
-        )
+        others = {k: xor_exchange(x, "offset", k) for k in reversed(range(1, offset_count))}
+        parts = [x, *others.values()]
+        start = (t + 1) * quarter
+        ratios = ratio(scal, kept, row_factors, col_ext, x, ratios, start, quarter)
 
     r_hi, r_lo = ratios
-    u, tail, sums, h_parts = numer_col(scal, r_hi, r_lo, row_factors, mask_ext, parts, scales)
+    u, tail, sums, early = numer_first(
+        scal, r_hi, r_lo, row_factors, mask_ext, parts, scales, EARLY
+    )
     w_parts = numer_row(scal, r_hi, r_lo, col_ext, u, offset_count)
-    per = rows // offset_count
-
     right = [(i, (i + 1) % genome_count) for i in range(genome_count)]
     arrived = lax.ppermute(tail, "genome", right)
+    row_terms = coefficient(
+        row_coefficient_kernel, scal, offset_count, row_factors, mask_ext, col_ext
+    )
+    col_terms = coefficient(
+        col_coefficient_kernel, scal, offset_count, col_factors, mask_ext, row_factors, arrived[pad]
+    )
+    order = [k for k in (3, 1, 0, *range(4, offset_count))]
+    rest = numer_col(scal, r_hi, r_lo, row_factors, u, col_terms[0], order, offset_count)
+    h_parts = dict(zip(order, rest)) | {EARLY: early}
+    h_parts = [h_parts[k] for k in range(offset_count)]
+    per = rows // offset_count
+
     if offset_count == 4 and pad <= per:
         diagonal = [
             (i * 4 + j, (i + 1) % genome_count * 4 + (j ^ 1))
@@ -636,12 +674,6 @@
     sums = jnp.sum(lax.all_gather(sums, "genome"), axis=0)
     bias = (u[:rows] * mean_scale(sums)).reshape(-1)
 
-    row_terms = coefficient(
-        row_coefficient_kernel, scal, offset_count, row_factors, mask_ext, col_ext
-    )
-    col_terms = coefficient(
-        col_coefficient_kernel, scal, offset_count, col_factors, mask_ext, row_factors, arrived[pad]
-    )
     col_update = update(scal, sums, *col_terms, h_terms)
     row_update = update(scal, sums, *row_terms, w_terms)
     return bias, row_update, col_update

time: 106 us -> 97.7 us (0.922)
  waiting for transfers between devices: 23.3 us -> 12.7 us
  Pallas kernels: 37.7 us -> 39.1 us
    ppermute x15, waiting for transfers between devices: 20.2 us -> 11.6 us  [xor_exchange(): lax.ppermute(x, axis, [(i, i ^ k) for i in range(lax.axis_size(axis))])]
    ppermute x15, starting transfers between devices: 17.8 us -> 21.8 us  [xor_exchange(): lax.ppermute(x, axis, [(i, i ^ k) for i in range(lax.axis_size(axis))])]
    ppermute x4, starting transfers between devices: 3.62 us -> 1.11 us  [both_sides(): a = lax.ppermute(x, 'genome', [(i, i ^ 1) for i in range(size)])]
    ppermute x1, starting transfers between devices: 0.14 us -> 2.6 us  [per_device(): col_next = lax.ppermute(col_late[:, :pad * tile], 'genome', ring_left)]
    ppermute x4, starting transfers between devices: 6.33 us -> 4.29 us  [both_sides(): lax.ppermute(x, 'genome', [(i, ((i + 1 ^ 1) - 1) % size) for i in range(s...]
    ppermute x1, waiting for transfers between devices: 1.73 us -> 0.01 us  [per_device(): across = lax.ppermute(tail[:pad], ('genome', 'offset'), diagonal)]
    pallas_call x15 -> x17, Pallas kernels: 37.7 us -> 39.1 us  [kernel_call(): pl.pallas_call(body, grid_spec=pltpu.PrefetchScalarGridSpec(num_scalar_pr...]
    ppermute x1, starting transfers between devices: 2.42 us -> 1.25 us  [per_device(): across = lax.ppermute(tail[:pad], ('genome', 'offset'), diagonal)]
  transfers between devices with their start and end apart: 26 -> 26, of which waited for: 7 -> 6; matrix products, arithmetic and copies ran while one was open for 1% -> 2% of each run, Pallas kernels for 25% -> 32%
where the time goes in v5:
time: 97.7 us; the launch traced here: 97.3 us
  Pallas kernels  39.1 us (40%)
  starting transfers between devices  31 us (32%)
  waiting for transfers between devices  12.7 us (13%)
  blocking collectives  9.53 us (10%)
  other arithmetic  2.79 us (3%)
  between operations  1.66 us (2%)
    pallas_call x17, Pallas kernels, kernel_call(): pl.pallas_call(body, grid_spec=pltpu.PrefetchScalarGridSpec(num_scalar_pr...  39.1 us
    ppermute x15, starting transfers between devices, xor_exchange(): lax.ppermute(x, axis, [(i, i ^ k) for i in range(lax.axis_size(axis))])  21.8 us
    ppermute x15, waiting for transfers between devices, xor_exchange(): lax.ppermute(x, axis, [(i, i ^ k) for i in range(lax.axis_size(axis))])  11.6 us
    all_gather x1, blocking collectives, per_device(): sums = jnp.sum(lax.all_gather(sums, 'genome'), axis=0)  9.53 us
    ppermute x4, starting transfers between devices, both_sides(): lax.ppermute(x, 'genome', [(i, ((i + 1 ^ 1) - 1) % size) for i in range(s...  4.29 us
    ppermute x1, starting transfers between devices, per_device(): col_next = lax.ppermute(col_late[:, :pad * tile], 'genome', ring_left)  2.6 us
  transfers between devices with their start and end apart: 26, of which 6 were waited for; matrix products, arithmetic and copies ran while one was open for 2% of the time, Pallas kernels for 32%

profile of v5, /device:TPU:0, one launch (start us, length us, event | category | flops | bytes accessed | tf_op | source)
XLA Modules:
  0.0 97.3 jit_solution(4930579170296939598)
XLA Ops:
  0.9 0.7 pad_add_fusion.scal
  1.7 0.8 fusion.14
  2.4 0.5 collective-permute-start.1
  2.9 3.6 %collective-permute-start.2 = (f32[8,128]{1,0:T(8,128)S(1)}, f32[8,128]{1,0:T(8,128)S(1)}, u32[]{:S(2)}, u32[]{:S(2)}) collective-permute-start(f32[8,128]{1,0:T(8,128)S(1)} %slice_bitcast_fusion.1), channel_id=1, source_target_pairs={{0,28},{4,8},{8,4},{12,16},{16,12},{20,24},{24,20},{28,0},{1,29},{... | collective-permute-start | bytes 12296 | tf_op jit(solution)/shard_map/ppermute | solution.py:552
  6.5 4.8 %first_main.1 = (f32[72,128]{1,0:T(8,128)S(1)}, f32[64,2,128,128]{3,2,1,0:T(8,128)S(1)}) custom-call(s32[4]{0:T(128)S(1)} %pad_add_fusion.scal, s32[64,2,128,128]{3,2,1,0:T(8,128)} %hbm.1, f32[64,128]{1,0:T(8,128)S(1)} %get-tuple-element.127.mask), custom_call_target="tpu_custom_call" | custom-call | tf_op jit(solution)/shard_map/first_main/pallas_call | solution.py:47
  11.3 1.4 %first_edge.1 = (f32[72,128]{1,0:T(8,128)S(1)}, f32[16,128]{1,0:T(8,128)S(1)}) custom-call(s32[4]{0:T(128)S(1)} %pad_add_fusion.scal, f32[64,2,128,128]{3,2,1,0:T(8,128)S(1)} %get-tuple-element.80.kept, f32[72,128]{1,0:T(8,128)S(1)} %pad_maximum_fusion.1.u_ref.mask.refs_4_, f32[72,128]{1,0:T(8,128)S(1)} %get-tuple-element.82.inner_v), custom_call_target="tpu_custom_call" | custom-call | tf_op jit(solution)/shard_map/first_edge/pallas_call | solution.py:47
  12.9 2.6 %collective-permute-start = (f32[32,1024]{1,0:T(8,128)S(1)}, f32[32,1024]{1,0:T(8,128)S(1)}, u32[]{:S(2)}, u32[]{:S(2)}) collective-permute-start(f32[32,1024]{1,0:T(8,128)S(1)} %slice.190), channel_id=1, source_target_pairs={{0,28},{4,0},{8,4},{12,8},{16,12},{20,16},{24,20},{28,24},{1,29},{... | collective-permute-start | bytes 393224 | tf_op jit(solution)/shard_map/ppermute | solution.py:609
  15.5 0.5 slice.189
  16.6 2.0 %ratio.4 = (bf16[64,128,256]{2,1,0:T(8,128)(2,1)S(1)}, bf16[64,128,256]{2,1,0:T(8,128)(2,1)S(1)}, f32[72,128]{1,0:T(8,128)S(1)}) custom-call(s32[4]{0:T(128)S(1)} %pad_add_fusion.scal, f32[64,2,128,128]{3,2,1,0:T(8,128)S(1)} %get-tuple-element.80.kept, f32[32,8192]{1,0:T(8,128)S(1)} %copy-done, f32[32,8192]{1,0:T(8,128)S(1)} %copy-done.1, ...), custom_call_target="tpu_custom_call" | custom-call | tf_op jit(solution)/shard_map/ratio/pallas_call | solution.py:47
  18.7 3.7 %collective-permute-start.5 = (f32[72,128]{1,0:T(8,128)S(1)}, f32[72,128]{1,0:T(8,128)S(1)}, u32[]{:S(2)}, u32[]{:S(2)}) collective-permute-start(f32[72,128]{1,0:T(8,128)S(1)} %pad_maximum_fusion.2.after.refs_0_), channel_id=1, source_target_pairs={{0,3},{1,2},{2,1},{3,0},{4,7},{5,6},{6,5},{7,4},{8,11},{9,10},{10,... | collective-permute-start | bytes 110600 | tf_op jit(solution)/shard_map/ppermute | solution.py:546
  22.4 0.8 collective-permute-start.7
  23.3 2.2 %ratio.5 = (bf16[64,128,256]{2,1,0:T(8,128)(2,1)S(1)}, bf16[64,128,256]{2,1,0:T(8,128)(2,1)S(1)}) custom-call(s32[4]{0:T(128)S(1)} %pad_add_fusion.scal, f32[64,2,128,128]{3,2,1,0:T(8,128)S(1)} %get-tuple-element.80.kept, f32[32,8192]{1,0:T(8,128)S(1)} %copy-done, ...), custom_call_target="tpu_custom_call", output_to_operand_aliasing={{0}: (5, {}), {1}: (6, {})} | custom-call | tf_op jit(solution)/shard_map/ratio/pallas_call | solution.py:47
  25.5 1.8 %collective-permute-done.6.refs_2_ = f32[72,128]{1,0:T(8,128)S(1)} collective-permute-done((f32[72,128]{1,0:T(8,128)S(1)}, f32[72,128]{1,0:T(8,128)S(1)}, u32[]{:S(2)}, u32[]{:S(2)}) %collective-permute-start.6) | collective-permute-done | bytes 36896 | tf_op jit(solution)/shard_map/ppermute | solution.py:546
  27.2 1.4 %cover_edge.2 = (f32[72,128]{1,0:T(8,128)S(1)}, f32[16,128]{1,0:T(8,128)S(1)}, f32[72,128]{1,0:T(8,128)S(1)}) custom-call(s32[4]{0:T(128)S(1)} %pad_add_fusion.scal, f32[64,2,128,128]{3,2,1,0:T(8,128)S(1)} %get-tuple-element.80.kept, f32[72,128]{1,0:T(8,128)S(1)} %pad_maximum_fusion.1.u_ref.mask.refs_4_, f32[72,128]{1,0:T(8,128)S(1)} %pad_maximum_fusion.2.after.refs_0_, ...), custom_call_target="tpu_custom_call" | custom-call | tf_op jit(solution)/shard_map/cover_edge/pallas_call | solution.py:47
  28.8 2.8 %cover_main.2 = f32[72,128]{1,0:T(8,128)S(1)} custom-call(s32[4]{0:T(128)S(1)} %pad_add_fusion.scal, f32[64,2,128,128]{3,2,1,0:T(8,128)S(1)} %get-tuple-element.80.kept, f32[72,128]{1,0:T(8,128)S(1)} %get-tuple-element.90.u_ref.refs_5_, f32[72,128]{1,0:T(8,128)S(1)} %get-tuple-element.91.edge_v), custom_call_target="tpu_custom_call" | custom-call | tf_op jit(solution)/shard_map/cover_main/pallas_call | solution.py:47
  31.6 1.0 %collective-permute-done.8 = f32[16,128]{1,0:T(8,128)S(1)} collective-permute-done((f32[16,128]{1,0:T(8,128)S(1)}, f32[16,128]{1,0:T(8,128)S(1)}, u32[]{:S(2)}, u32[]{:S(2)}) %collective-permute-start.8) | collective-permute-done | bytes 8224 | tf_op jit(solution)/shard_map/ppermute | solution.py:552
  32.7 1.9 %collective-permute-start.10 = (f32[72,128]{1,0:T(8,128)S(1)}, f32[72,128]{1,0:T(8,128)S(1)}, u32[]{:S(2)}, u32[]{:S(2)}) collective-permute-start(f32[72,128]{1,0:T(8,128)S(1)} %pad_maximum_fusion.3.after.refs_0_), channel_id=1, source_target_pairs={{0,3},{1,2},{2,1},{3,0},{4,7},{5,6},{6,5},{7,4},{8,11},{9,10},{10,... | collective-permute-start | bytes 110600 | tf_op jit(solution)/shard_map/ppermute | solution.py:546
  34.6 0.3 collective-permute-start.11
  34.8 2.3 %collective-permute-start.12 = (f32[72,128]{1,0:T(8,128)S(1)}, f32[72,128]{1,0:T(8,128)S(1)}, u32[]{:S(2)}, u32[]{:S(2)}) collective-permute-start(f32[72,128]{1,0:T(8,128)S(1)} %pad_maximum_fusion.3.after.refs_0_), channel_id=1, source_target_pairs={{0,1},{1,0},{2,3},{3,2},{4,5},{5,4},{6,7},{7,6},{8,9},{9,8},{10,11... | collective-permute-start | bytes 110600 | tf_op jit(solution)/shard_map/ppermute | solution.py:546
  37.1 2.0 %ratio.6 = (bf16[64,128,256]{2,1,0:T(8,128)(2,1)S(1)}, bf16[64,128,256]{2,1,0:T(8,128)(2,1)S(1)}) custom-call(s32[4]{0:T(128)S(1)} %pad_add_fusion.scal, f32[64,2,128,128]{3,2,1,0:T(8,128)S(1)} %get-tuple-element.80.kept, f32[32,8192]{1,0:T(8,128)S(1)} %copy-done, ...), custom_call_target="tpu_custom_call", output_to_operand_aliasing={{0}: (5, {}), {1}: (6, {})} | custom-call | tf_op jit(solution)/shard_map/ratio/pallas_call | solution.py:47
  39.1 0.7 collective-permute-done.11.refs_2_
  39.8 1.4 %cover_edge.3 = (f32[72,128]{1,0:T(8,128)S(1)}, f32[16,128]{1,0:T(8,128)S(1)}, f32[72,128]{1,0:T(8,128)S(1)}) custom-call(s32[4]{0:T(128)S(1)} %pad_add_fusion.scal, f32[64,2,128,128]{3,2,1,0:T(8,128)S(1)} %get-tuple-element.80.kept, f32[72,128]{1,0:T(8,128)S(1)} %pad_maximum_fusion.1.u_ref.mask.refs_4_, f32[72,128]{1,0:T(8,128)S(1)} %pad_maximum_fusion.3.after.refs_0_, ...), custom_call_target="tpu_custom_call" | custom-call | tf_op jit(solution)/shard_map/cover_edge/pallas_call | solution.py:47
  41.2 0.6 collective-permute-start.13
  41.9 0.5 collective-permute-start.14
  42.4 2.8 %cover_main.3 = f32[72,128]{1,0:T(8,128)S(1)} custom-call(s32[4]{0:T(128)S(1)} %pad_add_fusion.scal, f32[64,2,128,128]{3,2,1,0:T(8,128)S(1)} %get-tuple-element.80.kept, f32[72,128]{1,0:T(8,128)S(1)} %get-tuple-element.95.u_ref.refs_6_, f32[72,128]{1,0:T(8,128)S(1)} %get-tuple-element.96.edge_v), custom_call_target="tpu_custom_call" | custom-call | tf_op jit(solution)/shard_map/cover_main/pallas_call | solution.py:47
  45.3 2.3 %collective-permute-start.15 = (f32[72,128]{1,0:T(8,128)S(1)}, f32[72,128]{1,0:T(8,128)S(1)}, u32[]{:S(2)}, u32[]{:S(2)}) collective-permute-start(f32[72,128]{1,0:T(8,128)S(1)} %pad_maximum_fusion.4.after.refs_0_), channel_id=1, source_target_pairs={{0,3},{1,2},{2,1},{3,0},{4,7},{5,6},{6,5},{7,4},{8,11},{9,10},{10,... | collective-permute-start | bytes 110600 | tf_op jit(solution)/shard_map/ppermute | solution.py:546
  47.6 0.4 collective-permute-start.16
  48.1 1.7 %collective-permute-start.17 = (f32[72,128]{1,0:T(8,128)S(1)}, f32[72,128]{1,0:T(8,128)S(1)}, u32[]{:S(2)}, u32[]{:S(2)}) collective-permute-start(f32[72,128]{1,0:T(8,128)S(1)} %pad_maximum_fusion.4.after.refs_0_), channel_id=1, source_target_pairs={{0,1},{1,0},{2,3},{3,2},{4,5},{5,4},{6,7},{7,6},{8,9},{9,8},{10,11... | collective-permute-start | bytes 110600 | tf_op jit(solution)/shard_map/ppermute | solution.py:546
  49.7 2.0 %ratio.7 = (bf16[64,128,256]{2,1,0:T(8,128)(2,1)S(1)}, bf16[64,128,256]{2,1,0:T(8,128)(2,1)S(1)}) custom-call(s32[4]{0:T(128)S(1)} %pad_add_fusion.scal, f32[64,2,128,128]{3,2,1,0:T(8,128)S(1)} %get-tuple-element.80.kept, f32[32,8192]{1,0:T(8,128)S(1)} %copy-done, ...), custom_call_target="tpu_custom_call", output_to_operand_aliasing={{0}: (5, {}), {1}: (6, {})} | custom-call | tf_op jit(solution)/shard_map/ratio/pallas_call | solution.py:47
  51.7 0.8 collective-permute-done.16.refs_2_
  52.5 2.5 %numer_first.1 = (f32[72,128]{1,0:T(8,128)S(1)}, f32[9,32,128]{2,1,0:T(8,128)S(1)}, f32[8,128]{1,0:T(8,128)S(1)}, f32[16,32,128]{2,1,0:T(8,128)S(1)}) custom-call(s32[4]{0:T(128)S(1)} %pad_add_fusion.scal, bf16[64,128,256]{2,1,0:T(8,128)(2,1)S(1)} %get-tuple-element.99.hi_ref, bf16[64,128,256]{2,1,0:T(8,128)(2,1)S(1)} %get-tuple-element.100.lo_ref, ...), custom_call_target="tpu_custom_call" | custom-call | tf_op jit(solution)/shard_map/numer_first/pallas_call | solution.py:47
  55.0 1.2 %collective-permute-start.23 = (f32[16,32,128]{2,1,0:T(8,128)S(1)}, f32[16,32,128]{2,1,0:T(8,128)S(1)}, u32[]{:S(2)}, u32[]{:S(2)}) collective-permute-start(f32[16,32,128]{2,1,0:T(8,128)S(1)} %get-tuple-element.116), channel_id=1, source_target_pairs={{0,1},{1,0},{2,3},{3,2},{4,5},{5,4},{6,7},{7,6},{8,9},{9,8},{10,11... | collective-permute-start | bytes 786440 | tf_op jit(solution)/shard_map/ppermute | solution.py:546
  56.3 0.7 coefficient.2
  57.0 1.3 %collective-permute-start.24 = (f32[8,32,128]{2,1,0:T(8,128)S(1)}, f32[8,32,128]{2,1,0:T(8,128)S(1)}, u32[]{:S(2)}, u32[]{:S(2)}) collective-permute-start(f32[8,32,128]{2,1,0:T(8,128)S(1)} %slice.224), channel_id=1, source_target_pairs={{0,5},{1,4},{2,7},{3,6},{4,9},{5,8},{6,11},{7,10},{8,13},{9,12},{1... | collective-permute-start | bytes 393224 | tf_op jit(solution)/shard_map/ppermute | solution.py:660
  58.3 5.4 %numer_row.1 = (f32[16,32,128]{2,1,0:T(8,128)S(1)}, f32[16,32,128]{2,1,0:T(8,128)S(1)}, f32[16,32,128]{2,1,0:T(8,128)S(1)}, f32[16,32,128]{2,1,0:T(8,128)S(1)}) custom-call(s32[4]{0:T(128)S(1)} %pad_add_fusion.scal, bf16[64,128,256]{2,1,0:T(8,128)(2,1)S(1)} %get-tuple-element.99.hi_ref, bf16[64,128,256]{2,1,0:T(8,128)(2,1)S(1)} %get-tuple-element.100.lo_ref, ...), custom_call_target="tpu_custom_call" | custom-call | tf_op jit(solution)/shard_map/numer_row/pallas_call | solution.py:47
  63.7 1.2 %collective-permute-start.18 = (f32[16,32,128]{2,1,0:T(8,128)S(1)}, f32[16,32,128]{2,1,0:T(8,128)S(1)}, u32[]{:S(2)}, u32[]{:S(2)}) collective-permute-start(f32[16,32,128]{2,1,0:T(8,128)S(1)} %get-tuple-element.104), channel_id=1, source_target_pairs={{0,1},{1,0},{2,3},{3,2},{4,5},{5,4},{6,7},{7,6},{8,9},{9,8},{10,11... | collective-permute-start | bytes 786440 | tf_op jit(solution)/shard_map/ppermute | solution.py:546
  64.9 0.9 collective-permute-start.19
  65.7 0.9 coefficient.3
  66.6 4.2 %numer_col.1 = (f32[16,32,128]{2,1,0:T(8,128)S(1)}, f32[16,32,128]{2,1,0:T(8,128)S(1)}, f32[16,32,128]{2,1,0:T(8,128)S(1)}) custom-call(s32[4]{0:T(128)S(1)} %pad_add_fusion.scal, bf16[64,128,256]{2,1,0:T(8,128)(2,1)S(1)} %get-tuple-element.99.hi_ref, bf16[64,128,256]{2,1,0:T(8,128)(2,1)S(1)} %get-tuple-element.100.lo_ref, f32[32,8192]{1,0:T(8,128)S(1)} %copy-done, ...), custom_call_target="tpu_custom_call" | custom-call | tf_op jit(solution)/shard_map/numer_col/pallas_call | solution.py:47
  71.0 1.2 %collective-permute-start.22 = (f32[16,32,128]{2,1,0:T(8,128)S(1)}, f32[16,32,128]{2,1,0:T(8,128)S(1)}, u32[]{:S(2)}, u32[]{:S(2)}) collective-permute-start(f32[16,32,128]{2,1,0:T(8,128)S(1)} %get-tuple-element.118), channel_id=1, source_target_pairs={{0,1},{1,0},{2,3},{3,2},{4,5},{5,4},{6,7},{7,6},{8,9},{9,8},{10,11... | collective-permute-start | bytes 786440 | tf_op jit(solution)/shard_map/ppermute | solution.py:546
  72.3 1.5 %collective-permute-start.25 = (f32[16,32,128]{2,1,0:T(8,128)S(1)}, f32[16,32,128]{2,1,0:T(8,128)S(1)}, u32[]{:S(2)}, u32[]{:S(2)}) collective-permute-start(f32[16,32,128]{2,1,0:T(8,128)S(1)} %get-tuple-element.117), channel_id=1, source_target_pairs={{0,3},{1,2},{2,1},{3,0},{4,7},{5,6},{6,5},{7,4},{8,11},{9,10},{10,... | collective-permute-start | bytes 786440 | tf_op jit(solution)/shard_map/ppermute | solution.py:546
  73.9 2.3 %collective-permute-start.20 = (f32[16,32,128]{2,1,0:T(8,128)S(1)}, f32[16,32,128]{2,1,0:T(8,128)S(1)}, u32[]{:S(2)}, u32[]{:S(2)}) collective-permute-start(f32[16,32,128]{2,1,0:T(8,128)S(1)} %add.72), channel_id=1, source_target_pairs={{0,3},{1,2},{2,1},{3,0},{4,7},{5,6},{6,5},{7,4},{8,11},{9,10},{10,... | collective-permute-start | bytes 786440 | tf_op jit(solution)/shard_map/ppermute | solution.py:546
  76.2 9.5 %all-gather = f32[64,128]{1,0:T(8,128)S(1)} all-gather(f32[8,128]{1,0:T(8,128)S(1)} %get-tuple-element.105), channel_id=2, replica_groups=mesh['genome'=8,'offset'=4] {'genome'}, dimensions={0}, use_global_device_ids=true | all-gather | bytes 36864 | tf_op jit(solution)/shard_map/all_gather | solution.py:674
  85.8 0.6 multiply_bitcast_fusion
  86.4 4.2 %collective-permute-done.25.refs_2_ = f32[16,32,128]{2,1,0:T(8,128)S(1)} collective-permute-done((f32[16,32,128]{2,1,0:T(8,128)S(1)}, f32[16,32,128]{2,1,0:T(8,128)S(1)}, u32[]{:S(2)}, u32[]{:S(2)}) %collective-permute-start.25) | collective-permute-done | bytes 262176 | tf_op jit(solution)/shard_map/ppermute | solution.py:546
  90.6 1.3 %update.3 = f32[32,2048]{1,0:T(8,128)} custom-call(s32[4]{0:T(128)S(1)} %pad_add_fusion.scal, f32[8,128]{1,0:T(8,128)S(1)} %bitcast_reduce_fusion.sums, f32[16,32,128]{2,1,0:T(8,128)S(1)} %get-tuple-element.111.after.times, f32[16,32,128]{2,1,0:T(8,128)S(1)} %get-tuple-element.112.plus, f32[16,32,128]{2,1,0:T(8,128)S(1)} %get-tuple-element.119.refs_0_, ...), custom_call_target="tpu_custom_call" | custom-call | tf_op jit(solution)/shard_map/update/pallas_call | solution.py:47
  91.9 4.1 %collective-permute-done.20.refs_2_ = f32[16,32,128]{2,1,0:T(8,128)S(1)} collective-permute-done((f32[16,32,128]{2,1,0:T(8,128)S(1)}, f32[16,32,128]{2,1,0:T(8,128)S(1)}, u32[]{:S(2)}, u32[]{:S(2)}) %collective-permute-start.20) | collective-permute-done | bytes 262176 | tf_op jit(solution)/shard_map/ppermute | solution.py:546
  96.0 1.3 %update.2 = f32[32,2048]{1,0:T(8,128)} custom-call(s32[4]{0:T(128)S(1)} %pad_add_fusion.scal, f32[8,128]{1,0:T(8,128)S(1)} %bitcast_reduce_fusion.sums, f32[16,32,128]{2,1,0:T(8,128)S(1)} %get-tuple-element.106.times, f32[16,32,128]{2,1,0:T(8,128)S(1)} %get-tuple-element.107.plus, f32[16,32,128]{2,1,0:T(8,128)S(1)} %get-tuple-element.108.refs_0_, ...), custom_call_target="tpu_custom_call" | custom-call | tf_op jit(solution)/shard_map/update/pallas_call | solution.py:47
  (61 shorter events, 1.1 us)
Async XLA Ops:
  2.4 8.8 %collective-permute-start.1 = (f32[8,128]{1,0:T(8,128)S(1)}, f32[8,128]{1,0:T(8,128)S(1)}, u32[]{:S(2)}, u32[]{:S(2)}) collective-permute-start(f32[8,128]{1,0:T(8,128)S(1)} %slice_bitcast_fusion.1), channel_id=1, source_target_pairs={{0,4},{4,0},{8,12},{12,8},{16,20},{20,16},{24,28},{28,24},{1,5},{5... | collective-permute-start | bytes 12296 | tf_op jit(solution)/shard_map/ppermute | solution.py:551
  2.9 8.4 %collective-permute-start.2 = (f32[8,128]{1,0:T(8,128)S(1)}, f32[8,128]{1,0:T(8,128)S(1)}, u32[]{:S(2)}, u32[]{:S(2)}) collective-permute-start(f32[8,128]{1,0:T(8,128)S(1)} %slice_bitcast_fusion.1), channel_id=1, source_target_pairs={{0,28},{4,8},{8,4},{12,16},{16,12},{20,24},{24,20},{28,0},{1,29},{... | collective-permute-start | bytes 12296 | tf_op jit(solution)/shard_map/ppermute | solution.py:552
  11.3 1.5 %copy-start.1 = (f32[32,8192]{1,0:T(8,128)S(1)}, f32[32,8192]{1,0:T(8,128)}, u32[]{:S(2)}) copy-start(f32[32,8192]{1,0:T(8,128)} %old_ref.3) | copy-start | bytes 3145732
  11.3 5.3 %copy-start = (f32[32,8192]{1,0:T(8,128)S(1)}, f32[32,8192]{1,0:T(8,128)}, u32[]{:S(2)}) copy-start(f32[32,8192]{1,0:T(8,128)} %w_ref.11) | copy-start | bytes 3145732
  12.7 5.9 %collective-permute-start.3 = (f32[16,128]{1,0:T(8,128)S(1)}, f32[16,128]{1,0:T(8,128)S(1)}, u32[]{:S(2)}, u32[]{:S(2)}) collective-permute-start(f32[16,128]{1,0:T(8,128)S(1)} %get-tuple-element.86), channel_id=1, source_target_pairs={{0,28},{4,8},{8,4},{12,16},{16,12},{20,24},{24,20},{28,0},{1,29},{... | collective-permute-start | bytes 24584 | tf_op jit(solution)/shard_map/ppermute | solution.py:552
  12.8 5.9 %collective-permute-start.4 = (f32[16,128]{1,0:T(8,128)S(1)}, f32[16,128]{1,0:T(8,128)S(1)}, u32[]{:S(2)}, u32[]{:S(2)}) collective-permute-start(f32[16,128]{1,0:T(8,128)S(1)} %get-tuple-element.86), channel_id=1, source_target_pairs={{0,4},{4,0},{8,12},{12,8},{16,20},{20,16},{24,28},{28,24},{1,5},{5... | collective-permute-start | bytes 24584 | tf_op jit(solution)/shard_map/ppermute | solution.py:551
  12.9 10.3 %collective-permute-start = (f32[32,1024]{1,0:T(8,128)S(1)}, f32[32,1024]{1,0:T(8,128)S(1)}, u32[]{:S(2)}, u32[]{:S(2)}) collective-permute-start(f32[32,1024]{1,0:T(8,128)S(1)} %slice.190), channel_id=1, source_target_pairs={{0,28},{4,0},{8,4},{12,8},{16,12},{20,16},{24,20},{28,24},{1,29},{... | collective-permute-start | bytes 393224 | tf_op jit(solution)/shard_map/ppermute | solution.py:609
  18.7 6.7 %collective-permute-start.5 = (f32[72,128]{1,0:T(8,128)S(1)}, f32[72,128]{1,0:T(8,128)S(1)}, u32[]{:S(2)}, u32[]{:S(2)}) collective-permute-start(f32[72,128]{1,0:T(8,128)S(1)} %pad_maximum_fusion.2.after.refs_0_), channel_id=1, source_target_pairs={{0,3},{1,2},{2,1},{3,0},{4,7},{5,6},{6,5},{7,4},{8,11},{9,10},{10,... | collective-permute-start | bytes 110600 | tf_op jit(solution)/shard_map/ppermute | solution.py:546
  22.4 4.9 %collective-permute-start.6 = (f32[72,128]{1,0:T(8,128)S(1)}, f32[72,128]{1,0:T(8,128)S(1)}, u32[]{:S(2)}, u32[]{:S(2)}) collective-permute-start(f32[72,128]{1,0:T(8,128)S(1)} %pad_maximum_fusion.2.after.refs_0_), channel_id=1, source_target_pairs={{0,2},{1,3},{2,0},{3,1},{4,6},{5,7},{6,4},{7,5},{8,10},{9,11},{10,... | collective-permute-start | bytes 110600 | tf_op jit(solution)/shard_map/ppermute | solution.py:546
  22.4 4.9 %collective-permute-start.7 = (f32[72,128]{1,0:T(8,128)S(1)}, f32[72,128]{1,0:T(8,128)S(1)}, u32[]{:S(2)}, u32[]{:S(2)}) collective-permute-start(f32[72,128]{1,0:T(8,128)S(1)} %pad_maximum_fusion.2.after.refs_0_), channel_id=1, source_target_pairs={{0,1},{1,0},{2,3},{3,2},{4,5},{5,4},{6,7},{7,6},{8,9},{9,8},{10,11... | collective-permute-start | bytes 110600 | tf_op jit(solution)/shard_map/ppermute | solution.py:546
  28.6 4.0 %collective-permute-start.8 = (f32[16,128]{1,0:T(8,128)S(1)}, f32[16,128]{1,0:T(8,128)S(1)}, u32[]{:S(2)}, u32[]{:S(2)}) collective-permute-start(f32[16,128]{1,0:T(8,128)S(1)} %get-tuple-element.92), channel_id=1, source_target_pairs={{0,28},{4,8},{8,4},{12,16},{16,12},{20,24},{24,20},{28,0},{1,29},{... | collective-permute-start | bytes 24584 | tf_op jit(solution)/shard_map/ppermute | solution.py:552
  28.7 4.0 %collective-permute-start.9 = (f32[16,128]{1,0:T(8,128)S(1)}, f32[16,128]{1,0:T(8,128)S(1)}, u32[]{:S(2)}, u32[]{:S(2)}) collective-permute-start(f32[16,128]{1,0:T(8,128)S(1)} %get-tuple-element.92), channel_id=1, source_target_pairs={{0,4},{4,0},{8,12},{12,8},{16,20},{20,16},{24,28},{28,24},{1,5},{5... | collective-permute-start | bytes 24584 | tf_op jit(solution)/shard_map/ppermute | solution.py:551
  32.7 6.4 %collective-permute-start.10 = (f32[72,128]{1,0:T(8,128)S(1)}, f32[72,128]{1,0:T(8,128)S(1)}, u32[]{:S(2)}, u32[]{:S(2)}) collective-permute-start(f32[72,128]{1,0:T(8,128)S(1)} %pad_maximum_fusion.3.after.refs_0_), channel_id=1, source_target_pairs={{0,3},{1,2},{2,1},{3,0},{4,7},{5,6},{6,5},{7,4},{8,11},{9,10},{10,... | collective-permute-start | bytes 110600 | tf_op jit(solution)/shard_map/ppermute | solution.py:546
  34.6 5.3 %collective-permute-start.11 = (f32[72,128]{1,0:T(8,128)S(1)}, f32[72,128]{1,0:T(8,128)S(1)}, u32[]{:S(2)}, u32[]{:S(2)}) collective-permute-start(f32[72,128]{1,0:T(8,128)S(1)} %pad_maximum_fusion.3.after.refs_0_), channel_id=1, source_target_pairs={{0,2},{1,3},{2,0},{3,1},{4,6},{5,7},{6,4},{7,5},{8,10},{9,11},{10,... | collective-permute-start | bytes 110600 | tf_op jit(solution)/shard_map/ppermute | solution.py:546
  34.8 5.0 %collective-permute-start.12 = (f32[72,128]{1,0:T(8,128)S(1)}, f32[72,128]{1,0:T(8,128)S(1)}, u32[]{:S(2)}, u32[]{:S(2)}) collective-permute-start(f32[72,128]{1,0:T(8,128)S(1)} %pad_maximum_fusion.3.after.refs_0_), channel_id=1, source_target_pairs={{0,1},{1,0},{2,3},{3,2},{4,5},{5,4},{6,7},{7,6},{8,9},{9,8},{10,11... | collective-permute-start | bytes 110600 | tf_op jit(solution)/shard_map/ppermute | solution.py:546
  41.2 4.0 %collective-permute-start.13 = (f32[16,128]{1,0:T(8,128)S(1)}, f32[16,128]{1,0:T(8,128)S(1)}, u32[]{:S(2)}, u32[]{:S(2)}) collective-permute-start(f32[16,128]{1,0:T(8,128)S(1)} %get-tuple-element.97), channel_id=1, source_target_pairs={{0,28},{4,8},{8,4},{12,16},{16,12},{20,24},{24,20},{28,0},{1,29},{... | collective-permute-start | bytes 24584 | tf_op jit(solution)/shard_map/ppermute | solution.py:552
  41.9 3.4 %collective-permute-start.14 = (f32[16,128]{1,0:T(8,128)S(1)}, f32[16,128]{1,0:T(8,128)S(1)}, u32[]{:S(2)}, u32[]{:S(2)}) collective-permute-start(f32[16,128]{1,0:T(8,128)S(1)} %get-tuple-element.97), channel_id=1, source_target_pairs={{0,4},{4,0},{8,12},{12,8},{16,20},{20,16},{24,28},{28,24},{1,5},{5... | collective-permute-start | bytes 24584 | tf_op jit(solution)/shard_map/ppermute | solution.py:551
  45.3 6.4 %collective-permute-start.15 = (f32[72,128]{1,0:T(8,128)S(1)}, f32[72,128]{1,0:T(8,128)S(1)}, u32[]{:S(2)}, u32[]{:S(2)}) collective-permute-start(f32[72,128]{1,0:T(8,128)S(1)} %pad_maximum_fusion.4.after.refs_0_), channel_id=1, source_target_pairs={{0,3},{1,2},{2,1},{3,0},{4,7},{5,6},{6,5},{7,4},{8,11},{9,10},{10,... | collective-permute-start | bytes 110600 | tf_op jit(solution)/shard_map/ppermute | solution.py:546
  47.6 4.9 %collective-permute-start.16 = (f32[72,128]{1,0:T(8,128)S(1)}, f32[72,128]{1,0:T(8,128)S(1)}, u32[]{:S(2)}, u32[]{:S(2)}) collective-permute-start(f32[72,128]{1,0:T(8,128)S(1)} %pad_maximum_fusion.4.after.refs_0_), channel_id=1, source_target_pairs={{0,2},{1,3},{2,0},{3,1},{4,6},{5,7},{6,4},{7,5},{8,10},{9,11},{10,... | collective-permute-start | bytes 110600 | tf_op jit(solution)/shard_map/ppermute | solution.py:546
  48.1 4.5 %collective-permute-start.17 = (f32[72,128]{1,0:T(8,128)S(1)}, f32[72,128]{1,0:T(8,128)S(1)}, u32[]{:S(2)}, u32[]{:S(2)}) collective-permute-start(f32[72,128]{1,0:T(8,128)S(1)} %pad_maximum_fusion.4.after.refs_0_), channel_id=1, source_target_pairs={{0,1},{1,0},{2,3},{3,2},{4,5},{5,4},{6,7},{7,6},{8,9},{9,8},{10,11... | collective-permute-start | bytes 110600 | tf_op jit(solution)/shard_map/ppermute | solution.py:546
  55.0 10.7 %collective-permute-start.21 = (f32[9,32,128]{2,1,0:T(8,128)S(1)}, f32[9,32,128]{2,1,0:T(8,128)S(1)}, u32[]{:S(2)}, u32[]{:S(2)}) collective-permute-start(f32[9,32,128]{2,1,0:T(8,128)S(1)} %get-tuple-element.110), channel_id=1, source_target_pairs={{0,4},{4,8},{8,12},{12,16},{16,20},{20,24},{24,28},{28,0},{1,5},{5... | collective-permute-start | bytes 442376 | tf_op jit(solution)/shard_map/ppermute | solution.py:641
  55.0 15.8 %collective-permute-start.23 = (f32[16,32,128]{2,1,0:T(8,128)S(1)}, f32[16,32,128]{2,1,0:T(8,128)S(1)}, u32[]{:S(2)}, u32[]{:S(2)}) collective-permute-start(f32[16,32,128]{2,1,0:T(8,128)S(1)} %get-tuple-element.116), channel_id=1, source_target_pairs={{0,1},{1,0},{2,3},{3,2},{4,5},{5,4},{6,7},{7,6},{8,9},{9,8},{10,11... | collective-permute-start | bytes 786440 | tf_op jit(solution)/shard_map/ppermute | solution.py:546
  57.0 13.9 %collective-permute-start.24 = (f32[8,32,128]{2,1,0:T(8,128)S(1)}, f32[8,32,128]{2,1,0:T(8,128)S(1)}, u32[]{:S(2)}, u32[]{:S(2)}) collective-permute-start(f32[8,32,128]{2,1,0:T(8,128)S(1)} %slice.224), channel_id=1, source_target_pairs={{0,5},{1,4},{2,7},{3,6},{4,9},{5,8},{6,11},{7,10},{8,13},{9,12},{1... | collective-permute-start | bytes 393224 | tf_op jit(solution)/shard_map/ppermute | solution.py:660
  63.7 10.2 %collective-permute-start.18 = (f32[16,32,128]{2,1,0:T(8,128)S(1)}, f32[16,32,128]{2,1,0:T(8,128)S(1)}, u32[]{:S(2)}, u32[]{:S(2)}) collective-permute-start(f32[16,32,128]{2,1,0:T(8,128)S(1)} %get-tuple-element.104), channel_id=1, source_target_pairs={{0,1},{1,0},{2,3},{3,2},{4,5},{5,4},{6,7},{7,6},{8,9},{9,8},{10,11... | collective-permute-start | bytes 786440 | tf_op jit(solution)/shard_map/ppermute | solution.py:546
  64.9 27.1 %collective-permute-start.19 = (f32[16,32,128]{2,1,0:T(8,128)S(1)}, f32[16,32,128]{2,1,0:T(8,128)S(1)}, u32[]{:S(2)}, u32[]{:S(2)}) collective-permute-start(f32[16,32,128]{2,1,0:T(8,128)S(1)} %get-tuple-element.109), channel_id=1, source_target_pairs={{0,1},{1,0},{2,3},{3,2},{4,5},{5,4},{6,7},{7,6},{8,9},{9,8},{10,11... | collective-permute-start | bytes 786440 | tf_op jit(solution)/shard_map/ppermute | solution.py:546
  71.0 15.4 %collective-permute-start.22 = (f32[16,32,128]{2,1,0:T(8,128)S(1)}, f32[16,32,128]{2,1,0:T(8,128)S(1)}, u32[]{:S(2)}, u32[]{:S(2)}) collective-permute-start(f32[16,32,128]{2,1,0:T(8,128)S(1)} %get-tuple-element.118), channel_id=1, source_target_pairs={{0,1},{1,0},{2,3},{3,2},{4,5},{5,4},{6,7},{7,6},{8,9},{9,8},{10,11... | collective-permute-start | bytes 786440 | tf_op jit(solution)/shard_map/ppermute | solution.py:546
  72.3 18.3 %collective-permute-start.25 = (f32[16,32,128]{2,1,0:T(8,128)S(1)}, f32[16,32,128]{2,1,0:T(8,128)S(1)}, u32[]{:S(2)}, u32[]{:S(2)}) collective-permute-start(f32[16,32,128]{2,1,0:T(8,128)S(1)} %get-tuple-element.117), channel_id=1, source_target_pairs={{0,3},{1,2},{2,1},{3,0},{4,7},{5,6},{6,5},{7,4},{8,11},{9,10},{10,... | collective-permute-start | bytes 786440 | tf_op jit(solution)/shard_map/ppermute | solution.py:546
  73.9 22.1 %collective-permute-start.20 = (f32[16,32,128]{2,1,0:T(8,128)S(1)}, f32[16,32,128]{2,1,0:T(8,128)S(1)}, u32[]{:S(2)}, u32[]{:S(2)}) collective-permute-start(f32[16,32,128]{2,1,0:T(8,128)S(1)} %add.72), channel_id=1, source_target_pairs={{0,3},{1,2},{2,1},{3,0},{4,7},{5,6},{6,5},{7,4},{8,11},{9,10},{10,... | collective-permute-start | bytes 786440 | tf_op jit(solution)/shard_map/ppermute | solution.py:546

commit v6 on v5

--- a/solution.py
+++ b/solution.py
@@ -397,12 +397,17 @@
         sums_out[t : t + 1, :] = jnp.broadcast_to(line, (1, mask.shape[1]))
 
 
-def numer_row_kernel(scal, hi_ref, lo_ref, h_ref, u_ref, *refs):
+def numer_row_kernel(order, scal, hi_ref, lo_ref, h_ref, u_ref, after, *refs):
     outs, terms = refs[:-1], refs[-1]
     ext, tile = u_ref.shape
     offs = offsets(scal, hi_ref.shape[2] // tile)
-    scaled_terms(h_ref, u_ref, terms, 0, ext)
-    row_pieces(scal, offs, terms, hi_ref, lo_ref, u_ref, range(len(outs)), outs)
+    rows, per = hi_ref.shape[0], outs[0].shape[0]
+    if len(outs) > 1:
+        scaled_terms(h_ref, u_ref, terms, 0, ext)
+    else:
+        first = jnp.bitwise_xor(scal[0], order[0]) * per
+        scaled_terms(h_ref, u_ref, terms, first, per + ext - rows)
+    row_pieces(scal, offs, terms, hi_ref, lo_ref, u_ref, order, outs)
 
 
 def numer_first(scal, r_hi, r_lo, row_factors, mask_ext, parts, scales, k):
@@ -441,16 +446,16 @@
     )
 
 
-def numer_row(scal, r_hi, r_lo, col_ext, u, shares):
+def numer_row(scal, r_hi, r_lo, col_ext, u, after, order, shares):
     rows, tile = r_hi.shape[:2]
     factors = col_ext.shape[0]
     piece = jax.ShapeDtypeStruct((rows // shares, factors, tile), F32)
     return kernel_call(
-        numer_row_kernel,
+        functools.partial(numer_row_kernel, order),
         "numer_row",
         scal,
-        [r_hi, r_lo, col_ext, u],
-        [piece] * shares,
+        [r_hi, r_lo, col_ext, u, after],
+        [piece] * len(order),
         [pltpu.VMEM((u.shape[0], 2 * factors, tile), BF16)],
     )
 
@@ -636,7 +641,7 @@
     u, tail, sums, early = numer_first(
         scal, r_hi, r_lo, row_factors, mask_ext, parts, scales, EARLY
     )
-    w_parts = numer_row(scal, r_hi, r_lo, col_ext, u, offset_count)
+    (w_early,) = numer_row(scal, r_hi, r_lo, col_ext, u, sums, [EARLY], offset_count)
     right = [(i, (i + 1) % genome_count) for i in range(genome_count)]
     arrived = lax.ppermute(tail, "genome", right)
     row_terms = coefficient(
@@ -668,9 +673,11 @@
                 at = s * offset_count + k
                 h_parts[k] = h_parts[k].at[: piece.shape[0]].add(piece * mine[at : at + 1])
         h_terms, half_way = scatter_terms(h_parts)
-    w_terms, half_way_too = scatter_terms(w_parts)
-
-    sums, _ = lax.optimization_barrier((sums, half_way_too))
+    w_rest = numer_row(scal, r_hi, r_lo, col_ext, u, half_way, order, offset_count)
+    w_parts = dict(zip(order, w_rest)) | {EARLY: w_early}
+    w_terms, _ = scatter_terms([w_parts[k] for k in range(offset_count)])
+
+    sums, _ = lax.optimization_barrier((sums, h_terms[2]))
     sums = jnp.sum(lax.all_gather(sums, "genome"), axis=0)
     bias = (u[:rows] * mean_scale(sums)).reshape(-1)
 

time: 97.7 us -> 97.6 us (level)
    ppermute x1, waiting for transfers between devices: 0.01 us -> 2.82 us  [per_device(): across = lax.ppermute(tail[:pad], ('genome', 'offset'), diagonal)]
    ppermute x15, waiting for transfers between devices: 11.6 us -> 9.5 us  [xor_exchange(): lax.ppermute(x, axis, [(i, i ^ k) for i in range(lax.axis_size(axis))])]
    pallas_call x17 -> x18, Pallas kernels: 39.1 us -> 39.8 us  [kernel_call(): pl.pallas_call(body, grid_spec=pltpu.PrefetchScalarGridSpec(num_scalar_pr...]
  transfers between devices with their start and end apart: 26 -> 26, of which waited for: 6 -> 8; matrix products, arithmetic and copies ran while one was open for 2% -> 2% of each run, Pallas kernels for 32% -> 33%
where the time goes in v6:
time: 97.6 us; the launch traced here: 97.4 us
  Pallas kernels  39.8 us (41%)
  starting transfers between devices  30.1 us (31%)
  waiting for transfers between devices  13.4 us (14%)
  blocking collectives  9.06 us (9%)
  other arithmetic  2.76 us (3%)
  between operations  1.67 us (2%)
    pallas_call x18, Pallas kernels, kernel_call(): pl.pallas_call(body, grid_spec=pltpu.PrefetchScalarGridSpec(num_scalar_pr...  39.8 us
    ppermute x15, starting transfers between devices, xor_exchange(): lax.ppermute(x, axis, [(i, i ^ k) for i in range(lax.axis_size(axis))])  20.8 us
    ppermute x15, waiting for transfers between devices, xor_exchange(): lax.ppermute(x, axis, [(i, i ^ k) for i in range(lax.axis_size(axis))])  9.5 us
    all_gather x1, blocking collectives, per_device(): sums = jnp.sum(lax.all_gather(sums, 'genome'), axis=0)  9.06 us
    ppermute x4, starting transfers between devices, both_sides(): lax.ppermute(x, 'genome', [(i, ((i + 1 ^ 1) - 1) % size) for i in range(s...  4.29 us
    ppermute x1, waiting for transfers between devices, per_device(): across = lax.ppermute(tail[:pad], ('genome', 'offset'), diagonal)  2.82 us
    ppermute x1, starting transfers between devices, per_device(): col_next = lax.ppermute(col_late[:, :pad * tile], 'genome', ring_left)  2.6 us
  transfers between devices with their start and end apart: 26, of which 8 were waited for; matrix products, arithmetic and copies ran while one was open for 2% of the time, Pallas kernels for 33%

profile of v6, /device:TPU:0, one launch (start us, length us, event | category | flops | bytes accessed | tf_op | source)
XLA Modules:
  0.0 97.4 jit_solution(2302922223557123889)
XLA Ops:
  0.9 0.7 pad_add_fusion.scal
  1.7 0.8 fusion.14
  2.9 3.6 %collective-permute-start.2 = (f32[8,128]{1,0:T(8,128)S(1)}, f32[8,128]{1,0:T(8,128)S(1)}, u32[]{:S(2)}, u32[]{:S(2)}) collective-permute-start(f32[8,128]{1,0:T(8,128)S(1)} %slice_bitcast_fusion.1), channel_id=1, source_target_pairs={{0,28},{4,8},{8,4},{12,16},{16,12},{20,24},{24,20},{28,0},{1,29},{... | collective-permute-start | bytes 12296 | tf_op jit(solution)/shard_map/ppermute | solution.py:557
  6.5 4.8 %first_main.1 = (f32[72,128]{1,0:T(8,128)S(1)}, f32[64,2,128,128]{3,2,1,0:T(8,128)S(1)}) custom-call(s32[4]{0:T(128)S(1)} %pad_add_fusion.scal, s32[64,2,128,128]{3,2,1,0:T(8,128)} %hbm.1, f32[64,128]{1,0:T(8,128)S(1)} %get-tuple-element.125.mask), custom_call_target="tpu_custom_call" | custom-call | tf_op jit(solution)/shard_map/first_main/pallas_call | solution.py:47
  11.3 1.4 %first_edge.1 = (f32[72,128]{1,0:T(8,128)S(1)}, f32[16,128]{1,0:T(8,128)S(1)}) custom-call(s32[4]{0:T(128)S(1)} %pad_add_fusion.scal, f32[64,2,128,128]{3,2,1,0:T(8,128)S(1)} %get-tuple-element.79.kept, f32[72,128]{1,0:T(8,128)S(1)} %pad_maximum_fusion.1.u_ref.mask.refs_4_, f32[72,128]{1,0:T(8,128)S(1)} %get-tuple-element.81.inner_v), custom_call_target="tpu_custom_call" | custom-call | tf_op jit(solution)/shard_map/first_edge/pallas_call | solution.py:47
  12.9 2.6 %collective-permute-start = (f32[32,1024]{1,0:T(8,128)S(1)}, f32[32,1024]{1,0:T(8,128)S(1)}, u32[]{:S(2)}, u32[]{:S(2)}) collective-permute-start(f32[32,1024]{1,0:T(8,128)S(1)} %slice.190), channel_id=1, source_target_pairs={{0,28},{4,0},{8,4},{12,8},{16,12},{20,16},{24,20},{28,24},{1,29},{... | collective-permute-start | bytes 393224 | tf_op jit(solution)/shard_map/ppermute | solution.py:614
  15.5 0.5 slice.189
  16.6 2.0 %ratio.4 = (bf16[64,128,256]{2,1,0:T(8,128)(2,1)S(1)}, bf16[64,128,256]{2,1,0:T(8,128)(2,1)S(1)}, f32[72,128]{1,0:T(8,128)S(1)}) custom-call(s32[4]{0:T(128)S(1)} %pad_add_fusion.scal, f32[64,2,128,128]{3,2,1,0:T(8,128)S(1)} %get-tuple-element.79.kept, f32[32,8192]{1,0:T(8,128)S(1)} %copy-done, f32[32,8192]{1,0:T(8,128)S(1)} %copy-done.1, ...), custom_call_target="tpu_custom_call" | custom-call | tf_op jit(solution)/shard_map/ratio/pallas_call | solution.py:47
  18.7 3.7 %collective-permute-start.5 = (f32[72,128]{1,0:T(8,128)S(1)}, f32[72,128]{1,0:T(8,128)S(1)}, u32[]{:S(2)}, u32[]{:S(2)}) collective-permute-start(f32[72,128]{1,0:T(8,128)S(1)} %pad_maximum_fusion.2.after.refs_0_), channel_id=1, source_target_pairs={{0,3},{1,2},{2,1},{3,0},{4,7},{5,6},{6,5},{7,4},{8,11},{9,10},{10,... | collective-permute-start | bytes 110600 | tf_op jit(solution)/shard_map/ppermute | solution.py:551
  22.4 0.8 collective-permute-start.7
  23.3 2.2 %ratio.5 = (bf16[64,128,256]{2,1,0:T(8,128)(2,1)S(1)}, bf16[64,128,256]{2,1,0:T(8,128)(2,1)S(1)}) custom-call(s32[4]{0:T(128)S(1)} %pad_add_fusion.scal, f32[64,2,128,128]{3,2,1,0:T(8,128)S(1)} %get-tuple-element.79.kept, f32[32,8192]{1,0:T(8,128)S(1)} %copy-done, ...), custom_call_target="tpu_custom_call", output_to_operand_aliasing={{0}: (5, {}), {1}: (6, {})} | custom-call | tf_op jit(solution)/shard_map/ratio/pallas_call | solution.py:47
  25.5 1.8 %collective-permute-done.6.refs_2_ = f32[72,128]{1,0:T(8,128)S(1)} collective-permute-done((f32[72,128]{1,0:T(8,128)S(1)}, f32[72,128]{1,0:T(8,128)S(1)}, u32[]{:S(2)}, u32[]{:S(2)}) %collective-permute-start.6) | collective-permute-done | bytes 36896 | tf_op jit(solution)/shard_map/ppermute | solution.py:551
  27.2 1.4 %cover_edge.2 = (f32[72,128]{1,0:T(8,128)S(1)}, f32[16,128]{1,0:T(8,128)S(1)}, f32[72,128]{1,0:T(8,128)S(1)}) custom-call(s32[4]{0:T(128)S(1)} %pad_add_fusion.scal, f32[64,2,128,128]{3,2,1,0:T(8,128)S(1)} %get-tuple-element.79.kept, f32[72,128]{1,0:T(8,128)S(1)} %pad_maximum_fusion.1.u_ref.mask.refs_4_, f32[72,128]{1,0:T(8,128)S(1)} %pad_maximum_fusion.2.after.refs_0_, ...), custom_call_target="tpu_custom_call" | custom-call | tf_op jit(solution)/shard_map/cover_edge/pallas_call | solution.py:47
  28.8 2.8 %cover_main.2 = f32[72,128]{1,0:T(8,128)S(1)} custom-call(s32[4]{0:T(128)S(1)} %pad_add_fusion.scal, f32[64,2,128,128]{3,2,1,0:T(8,128)S(1)} %get-tuple-element.79.kept, f32[72,128]{1,0:T(8,128)S(1)} %get-tuple-element.89.u_ref.refs_5_, f32[72,128]{1,0:T(8,128)S(1)} %get-tuple-element.90.edge_v), custom_call_target="tpu_custom_call" | custom-call | tf_op jit(solution)/shard_map/cover_main/pallas_call | solution.py:47
  31.6 1.0 %collective-permute-done.8 = f32[16,128]{1,0:T(8,128)S(1)} collective-permute-done((f32[16,128]{1,0:T(8,128)S(1)}, f32[16,128]{1,0:T(8,128)S(1)}, u32[]{:S(2)}, u32[]{:S(2)}) %collective-permute-start.8) | collective-permute-done | bytes 8224 | tf_op jit(solution)/shard_map/ppermute | solution.py:557
  32.7 1.9 %collective-permute-start.10 = (f32[72,128]{1,0:T(8,128)S(1)}, f32[72,128]{1,0:T(8,128)S(1)}, u32[]{:S(2)}, u32[]{:S(2)}) collective-permute-start(f32[72,128]{1,0:T(8,128)S(1)} %pad_maximum_fusion.3.after.refs_0_), channel_id=1, source_target_pairs={{0,3},{1,2},{2,1},{3,0},{4,7},{5,6},{6,5},{7,4},{8,11},{9,10},{10,... | collective-permute-start | bytes 110600 | tf_op jit(solution)/shard_map/ppermute | solution.py:551
  34.8 2.3 %collective-permute-start.12 = (f32[72,128]{1,0:T(8,128)S(1)}, f32[72,128]{1,0:T(8,128)S(1)}, u32[]{:S(2)}, u32[]{:S(2)}) collective-permute-start(f32[72,128]{1,0:T(8,128)S(1)} %pad_maximum_fusion.3.after.refs_0_), channel_id=1, source_target_pairs={{0,1},{1,0},{2,3},{3,2},{4,5},{5,4},{6,7},{7,6},{8,9},{9,8},{10,11... | collective-permute-start | bytes 110600 | tf_op jit(solution)/shard_map/ppermute | solution.py:551
  37.1 2.0 %ratio.6 = (bf16[64,128,256]{2,1,0:T(8,128)(2,1)S(1)}, bf16[64,128,256]{2,1,0:T(8,128)(2,1)S(1)}) custom-call(s32[4]{0:T(128)S(1)} %pad_add_fusion.scal, f32[64,2,128,128]{3,2,1,0:T(8,128)S(1)} %get-tuple-element.79.kept, f32[32,8192]{1,0:T(8,128)S(1)} %copy-done, ...), custom_call_target="tpu_custom_call", output_to_operand_aliasing={{0}: (5, {}), {1}: (6, {})} | custom-call | tf_op jit(solution)/shard_map/ratio/pallas_call | solution.py:47
  39.1 0.7 collective-permute-done.11.refs_2_
  39.8 1.4 %cover_edge.3 = (f32[72,128]{1,0:T(8,128)S(1)}, f32[16,128]{1,0:T(8,128)S(1)}, f32[72,128]{1,0:T(8,128)S(1)}) custom-call(s32[4]{0:T(128)S(1)} %pad_add_fusion.scal, f32[64,2,128,128]{3,2,1,0:T(8,128)S(1)} %get-tuple-element.79.kept, f32[72,128]{1,0:T(8,128)S(1)} %pad_maximum_fusion.1.u_ref.mask.refs_4_, f32[72,128]{1,0:T(8,128)S(1)} %pad_maximum_fusion.3.after.refs_0_, ...), custom_call_target="tpu_custom_call" | custom-call | tf_op jit(solution)/shard_map/cover_edge/pallas_call | solution.py:47
  41.2 0.6 collective-permute-start.13
  41.9 0.5 collective-permute-start.14
  42.4 2.8 %cover_main.3 = f32[72,128]{1,0:T(8,128)S(1)} custom-call(s32[4]{0:T(128)S(1)} %pad_add_fusion.scal, f32[64,2,128,128]{3,2,1,0:T(8,128)S(1)} %get-tuple-element.79.kept, f32[72,128]{1,0:T(8,128)S(1)} %get-tuple-element.94.u_ref.refs_6_, f32[72,128]{1,0:T(8,128)S(1)} %get-tuple-element.95.edge_v), custom_call_target="tpu_custom_call" | custom-call | tf_op jit(solution)/shard_map/cover_main/pallas_call | solution.py:47
  45.3 2.3 %collective-permute-start.15 = (f32[72,128]{1,0:T(8,128)S(1)}, f32[72,128]{1,0:T(8,128)S(1)}, u32[]{:S(2)}, u32[]{:S(2)}) collective-permute-start(f32[72,128]{1,0:T(8,128)S(1)} %pad_maximum_fusion.4.after.refs_0_), channel_id=1, source_target_pairs={{0,3},{1,2},{2,1},{3,0},{4,7},{5,6},{6,5},{7,4},{8,11},{9,10},{10,... | collective-permute-start | bytes 110600 | tf_op jit(solution)/shard_map/ppermute | solution.py:551
  47.6 0.5 collective-permute-start.16
  48.1 1.7 %collective-permute-start.17 = (f32[72,128]{1,0:T(8,128)S(1)}, f32[72,128]{1,0:T(8,128)S(1)}, u32[]{:S(2)}, u32[]{:S(2)}) collective-permute-start(f32[72,128]{1,0:T(8,128)S(1)} %pad_maximum_fusion.4.after.refs_0_), channel_id=1, source_target_pairs={{0,1},{1,0},{2,3},{3,2},{4,5},{5,4},{6,7},{7,6},{8,9},{9,8},{10,11... | collective-permute-start | bytes 110600 | tf_op jit(solution)/shard_map/ppermute | solution.py:551
  49.7 2.0 %ratio.7 = (bf16[64,128,256]{2,1,0:T(8,128)(2,1)S(1)}, bf16[64,128,256]{2,1,0:T(8,128)(2,1)S(1)}) custom-call(s32[4]{0:T(128)S(1)} %pad_add_fusion.scal, f32[64,2,128,128]{3,2,1,0:T(8,128)S(1)} %get-tuple-element.79.kept, f32[32,8192]{1,0:T(8,128)S(1)} %copy-done, ...), custom_call_target="tpu_custom_call", output_to_operand_aliasing={{0}: (5, {}), {1}: (6, {})} | custom-call | tf_op jit(solution)/shard_map/ratio/pallas_call | solution.py:47
  51.7 0.8 collective-permute-done.16.refs_2_
  52.5 2.5 %numer_first.1 = (f32[72,128]{1,0:T(8,128)S(1)}, f32[9,32,128]{2,1,0:T(8,128)S(1)}, f32[8,128]{1,0:T(8,128)S(1)}, f32[16,32,128]{2,1,0:T(8,128)S(1)}) custom-call(s32[4]{0:T(128)S(1)} %pad_add_fusion.scal, bf16[64,128,256]{2,1,0:T(8,128)(2,1)S(1)} %get-tuple-element.98.hi_ref, bf16[64,128,256]{2,1,0:T(8,128)(2,1)S(1)} %get-tuple-element.99.lo_ref, ...), custom_call_target="tpu_custom_call" | custom-call | tf_op jit(solution)/shard_map/numer_first/pallas_call | solution.py:47
  55.0 1.2 %collective-permute-start.19 = (f32[16,32,128]{2,1,0:T(8,128)S(1)}, f32[16,32,128]{2,1,0:T(8,128)S(1)}, u32[]{:S(2)}, u32[]{:S(2)}) collective-permute-start(f32[16,32,128]{2,1,0:T(8,128)S(1)} %get-tuple-element.105), channel_id=1, source_target_pairs={{0,1},{1,0},{2,3},{3,2},{4,5},{5,4},{6,7},{7,6},{8,9},{9,8},{10,11... | collective-permute-start | bytes 786440 | tf_op jit(solution)/shard_map/ppermute | solution.py:551
  56.3 1.3 %collective-permute-start.20 = (f32[8,32,128]{2,1,0:T(8,128)S(1)}, f32[8,32,128]{2,1,0:T(8,128)S(1)}, u32[]{:S(2)}, u32[]{:S(2)}) collective-permute-start(f32[8,32,128]{2,1,0:T(8,128)S(1)} %slice.216), channel_id=1, source_target_pairs={{0,5},{1,4},{2,7},{3,6},{4,9},{5,8},{6,11},{7,10},{8,13},{9,12},{1... | collective-permute-start | bytes 393224 | tf_op jit(solution)/shard_map/ppermute | solution.py:665
  57.5 1.8 %numer_row.3 = f32[16,32,128]{2,1,0:T(8,128)S(1)} custom-call(s32[4]{0:T(128)S(1)} %pad_add_fusion.scal, bf16[64,128,256]{2,1,0:T(8,128)(2,1)S(1)} %get-tuple-element.98.hi_ref, bf16[64,128,256]{2,1,0:T(8,128)(2,1)S(1)} %get-tuple-element.99.lo_ref, f32[32,9216]{1,0:T(8,128)S(1)} %pad_maximum_fusion.h_ref.other, f32[72,128]{1,0:T(8,128)S(1)} %get-tuple-element.100.u_ref, ...), custom_call_target="tpu_custom_call" | custom-call | tf_op jit(solution)/shard_map/numer_row/pallas_call | solution.py:47
  59.3 1.2 %collective-permute-start.23 = (f32[16,32,128]{2,1,0:T(8,128)S(1)}, f32[16,32,128]{2,1,0:T(8,128)S(1)}, u32[]{:S(2)}, u32[]{:S(2)}) collective-permute-start(f32[16,32,128]{2,1,0:T(8,128)S(1)} %numer_row.3), channel_id=1, source_target_pairs={{0,1},{1,0},{2,3},{3,2},{4,5},{5,4},{6,7},{7,6},{8,9},{9,8},{10,11... | collective-permute-start | bytes 786440 | tf_op jit(solution)/shard_map/ppermute | solution.py:551
  60.5 0.9 coefficient.2
  61.4 4.2 %numer_col.1 = (f32[16,32,128]{2,1,0:T(8,128)S(1)}, f32[16,32,128]{2,1,0:T(8,128)S(1)}, f32[16,32,128]{2,1,0:T(8,128)S(1)}) custom-call(s32[4]{0:T(128)S(1)} %pad_add_fusion.scal, bf16[64,128,256]{2,1,0:T(8,128)(2,1)S(1)} %get-tuple-element.98.hi_ref, bf16[64,128,256]{2,1,0:T(8,128)(2,1)S(1)} %get-tuple-element.99.lo_ref, f32[32,8192]{1,0:T(8,128)S(1)} %copy-done, ...), custom_call_target="tpu_custom_call" | custom-call | tf_op jit(solution)/shard_map/numer_col/pallas_call | solution.py:47
  65.7 2.8 %collective-permute-done.20 = f32[8,32,128]{2,1,0:T(8,128)S(1)} collective-permute-done((f32[8,32,128]{2,1,0:T(8,128)S(1)}, f32[8,32,128]{2,1,0:T(8,128)S(1)}, u32[]{:S(2)}, u32[]{:S(2)}) %collective-permute-start.20) | collective-permute-done | bytes 131104 | tf_op jit(solution)/shard_map/ppermute | solution.py:665
  68.6 2.2 %collective-permute-start.21 = (f32[16,32,128]{2,1,0:T(8,128)S(1)}, f32[16,32,128]{2,1,0:T(8,128)S(1)}, u32[]{:S(2)}, u32[]{:S(2)}) collective-permute-start(f32[16,32,128]{2,1,0:T(8,128)S(1)} %get-tuple-element.117.after), channel_id=1, source_target_pairs={{0,3},{1,2},{2,1},{3,0},{4,7},{5,6},{6,5},{7,4},{8,11},{9,10},{10,... | collective-permute-start | bytes 786440 | tf_op jit(solution)/shard_map/ppermute | solution.py:551
  70.8 0.7 coefficient.3
  71.5 4.3 %numer_row.2 = (f32[16,32,128]{2,1,0:T(8,128)S(1)}, f32[16,32,128]{2,1,0:T(8,128)S(1)}, f32[16,32,128]{2,1,0:T(8,128)S(1)}) custom-call(s32[4]{0:T(128)S(1)} %pad_add_fusion.scal, bf16[64,128,256]{2,1,0:T(8,128)(2,1)S(1)} %get-tuple-element.98.hi_ref, bf16[64,128,256]{2,1,0:T(8,128)(2,1)S(1)} %get-tuple-element.99.lo_ref, ...), custom_call_target="tpu_custom_call" | custom-call | tf_op jit(solution)/shard_map/numer_row/pallas_call | solution.py:47
  75.9 2.0 %collective-permute-start.24 = (f32[16,32,128]{2,1,0:T(8,128)S(1)}, f32[16,32,128]{2,1,0:T(8,128)S(1)}, u32[]{:S(2)}, u32[]{:S(2)}) collective-permute-start(f32[16,32,128]{2,1,0:T(8,128)S(1)} %add.75), channel_id=1, source_target_pairs={{0,3},{1,2},{2,1},{3,0},{4,7},{5,6},{6,5},{7,4},{8,11},{9,10},{10,... | collective-permute-start | bytes 786440 | tf_op jit(solution)/shard_map/ppermute | solution.py:551
  77.9 0.9 collective-permute-start.22
  78.8 1.0 %collective-permute-done.21.refs_2_ = f32[16,32,128]{2,1,0:T(8,128)S(1)} collective-permute-done((f32[16,32,128]{2,1,0:T(8,128)S(1)}, f32[16,32,128]{2,1,0:T(8,128)S(1)}, u32[]{:S(2)}, u32[]{:S(2)}) %collective-permute-start.21) | collective-permute-done | bytes 262176 | tf_op jit(solution)/shard_map/ppermute | solution.py:551
  79.8 9.1 %all-gather = f32[64,128]{1,0:T(8,128)S(1)} all-gather(f32[8,128]{1,0:T(8,128)S(1)} %get-tuple-element.106.after), channel_id=2, replica_groups=mesh['genome'=8,'offset'=4] {'genome'}, dimensions={0}, use_global_device_ids=true | all-gather | bytes 36864 | tf_op jit(solution)/shard_map/all_gather | solution.py:681
  88.9 1.9 %collective-permute-done.25.refs_1_ = f32[16,32,128]{2,1,0:T(8,128)S(1)} collective-permute-done((f32[16,32,128]{2,1,0:T(8,128)S(1)}, f32[16,32,128]{2,1,0:T(8,128)S(1)}, u32[]{:S(2)}, u32[]{:S(2)}) %collective-permute-start.25) | collective-permute-done | bytes 262176 | tf_op jit(solution)/shard_map/ppermute | solution.py:551
  90.7 1.3 %update.3 = f32[32,2048]{1,0:T(8,128)} custom-call(s32[4]{0:T(128)S(1)} %pad_add_fusion.scal, f32[8,128]{1,0:T(8,128)S(1)} %bitcast_reduce_fusion.sums, f32[16,32,128]{2,1,0:T(8,128)S(1)} %get-tuple-element.103.after.times, f32[16,32,128]{2,1,0:T(8,128)S(1)} %get-tuple-element.112.plus, f32[16,32,128]{2,1,0:T(8,128)S(1)} %get-tuple-element.116.refs_0_, ...), custom_call_target="tpu_custom_call" | custom-call | tf_op jit(solution)/shard_map/update/pallas_call | solution.py:47
  92.0 0.6 multiply_bitcast_fusion
  92.7 3.4 %collective-permute-done.22.refs_1_ = f32[16,32,128]{2,1,0:T(8,128)S(1)} collective-permute-done((f32[16,32,128]{2,1,0:T(8,128)S(1)}, f32[16,32,128]{2,1,0:T(8,128)S(1)}, u32[]{:S(2)}, u32[]{:S(2)}) %collective-permute-start.22) | collective-permute-done | bytes 262176 | tf_op jit(solution)/shard_map/ppermute | solution.py:551
  96.0 1.3 %update.2 = f32[32,2048]{1,0:T(8,128)} custom-call(s32[4]{0:T(128)S(1)} %pad_add_fusion.scal, f32[8,128]{1,0:T(8,128)S(1)} %bitcast_reduce_fusion.sums, f32[16,32,128]{2,1,0:T(8,128)S(1)} %get-tuple-element.107.times, f32[16,32,128]{2,1,0:T(8,128)S(1)} %get-tuple-element.108.plus, f32[16,32,128]{2,1,0:T(8,128)S(1)} %get-tuple-element.109.refs_0_, ...), custom_call_target="tpu_custom_call" | custom-call | tf_op jit(solution)/shard_map/update/pallas_call | solution.py:47
  (62 shorter events, 1.8 us)
Async XLA Ops:
  2.4 8.8 %collective-permute-start.1 = (f32[8,128]{1,0:T(8,128)S(1)}, f32[8,128]{1,0:T(8,128)S(1)}, u32[]{:S(2)}, u32[]{:S(2)}) collective-permute-start(f32[8,128]{1,0:T(8,128)S(1)} %slice_bitcast_fusion.1), channel_id=1, source_target_pairs={{0,4},{4,0},{8,12},{12,8},{16,20},{20,16},{24,28},{28,24},{1,5},{5... | collective-permute-start | bytes 12296 | tf_op jit(solution)/shard_map/ppermute | solution.py:556
  2.9 8.4 %collective-permute-start.2 = (f32[8,128]{1,0:T(8,128)S(1)}, f32[8,128]{1,0:T(8,128)S(1)}, u32[]{:S(2)}, u32[]{:S(2)}) collective-permute-start(f32[8,128]{1,0:T(8,128)S(1)} %slice_bitcast_fusion.1), channel_id=1, source_target_pairs={{0,28},{4,8},{8,4},{12,16},{16,12},{20,24},{24,20},{28,0},{1,29},{... | collective-permute-start | bytes 12296 | tf_op jit(solution)/shard_map/ppermute | solution.py:557
  11.3 1.5 %copy-start.1 = (f32[32,8192]{1,0:T(8,128)S(1)}, f32[32,8192]{1,0:T(8,128)}, u32[]{:S(2)}) copy-start(f32[32,8192]{1,0:T(8,128)} %old_ref.2) | copy-start | bytes 3145732
  11.3 5.3 %copy-start = (f32[32,8192]{1,0:T(8,128)S(1)}, f32[32,8192]{1,0:T(8,128)}, u32[]{:S(2)}) copy-start(f32[32,8192]{1,0:T(8,128)} %old_ref.3) | copy-start | bytes 3145732
  12.7 5.9 %collective-permute-start.3 = (f32[16,128]{1,0:T(8,128)S(1)}, f32[16,128]{1,0:T(8,128)S(1)}, u32[]{:S(2)}, u32[]{:S(2)}) collective-permute-start(f32[16,128]{1,0:T(8,128)S(1)} %get-tuple-element.85), channel_id=1, source_target_pairs={{0,28},{4,8},{8,4},{12,16},{16,12},{20,24},{24,20},{28,0},{1,29},{... | collective-permute-start | bytes 24584 | tf_op jit(solution)/shard_map/ppermute | solution.py:557
  12.8 5.9 %collective-permute-start.4 = (f32[16,128]{1,0:T(8,128)S(1)}, f32[16,128]{1,0:T(8,128)S(1)}, u32[]{:S(2)}, u32[]{:S(2)}) collective-permute-start(f32[16,128]{1,0:T(8,128)S(1)} %get-tuple-element.85), channel_id=1, source_target_pairs={{0,4},{4,0},{8,12},{12,8},{16,20},{20,16},{24,28},{28,24},{1,5},{5... | collective-permute-start | bytes 24584 | tf_op jit(solution)/shard_map/ppermute | solution.py:556
  12.9 10.3 %collective-permute-start = (f32[32,1024]{1,0:T(8,128)S(1)}, f32[32,1024]{1,0:T(8,128)S(1)}, u32[]{:S(2)}, u32[]{:S(2)}) collective-permute-start(f32[32,1024]{1,0:T(8,128)S(1)} %slice.190), channel_id=1, source_target_pairs={{0,28},{4,0},{8,4},{12,8},{16,12},{20,16},{24,20},{28,24},{1,29},{... | collective-permute-start | bytes 393224 | tf_op jit(solution)/shard_map/ppermute | solution.py:614
  18.7 6.7 %collective-permute-start.5 = (f32[72,128]{1,0:T(8,128)S(1)}, f32[72,128]{1,0:T(8,128)S(1)}, u32[]{:S(2)}, u32[]{:S(2)}) collective-permute-start(f32[72,128]{1,0:T(8,128)S(1)} %pad_maximum_fusion.2.after.refs_0_), channel_id=1, source_target_pairs={{0,3},{1,2},{2,1},{3,0},{4,7},{5,6},{6,5},{7,4},{8,11},{9,10},{10,... | collective-permute-start | bytes 110600 | tf_op jit(solution)/shard_map/ppermute | solution.py:551
  22.4 4.9 %collective-permute-start.6 = (f32[72,128]{1,0:T(8,128)S(1)}, f32[72,128]{1,0:T(8,128)S(1)}, u32[]{:S(2)}, u32[]{:S(2)}) collective-permute-start(f32[72,128]{1,0:T(8,128)S(1)} %pad_maximum_fusion.2.after.refs_0_), channel_id=1, source_target_pairs={{0,2},{1,3},{2,0},{3,1},{4,6},{5,7},{6,4},{7,5},{8,10},{9,11},{10,... | collective-permute-start | bytes 110600 | tf_op jit(solution)/shard_map/ppermute | solution.py:551
  22.4 4.9 %collective-permute-start.7 = (f32[72,128]{1,0:T(8,128)S(1)}, f32[72,128]{1,0:T(8,128)S(1)}, u32[]{:S(2)}, u32[]{:S(2)}) collective-permute-start(f32[72,128]{1,0:T(8,128)S(1)} %pad_maximum_fusion.2.after.refs_0_), channel_id=1, source_target_pairs={{0,1},{1,0},{2,3},{3,2},{4,5},{5,4},{6,7},{7,6},{8,9},{9,8},{10,11... | collective-permute-start | bytes 110600 | tf_op jit(solution)/shard_map/ppermute | solution.py:551
  28.6 4.0 %collective-permute-start.8 = (f32[16,128]{1,0:T(8,128)S(1)}, f32[16,128]{1,0:T(8,128)S(1)}, u32[]{:S(2)}, u32[]{:S(2)}) collective-permute-start(f32[16,128]{1,0:T(8,128)S(1)} %get-tuple-element.91), channel_id=1, source_target_pairs={{0,28},{4,8},{8,4},{12,16},{16,12},{20,24},{24,20},{28,0},{1,29},{... | collective-permute-start | bytes 24584 | tf_op jit(solution)/shard_map/ppermute | solution.py:557
  28.7 4.0 %collective-permute-start.9 = (f32[16,128]{1,0:T(8,128)S(1)}, f32[16,128]{1,0:T(8,128)S(1)}, u32[]{:S(2)}, u32[]{:S(2)}) collective-permute-start(f32[16,128]{1,0:T(8,128)S(1)} %get-tuple-element.91), channel_id=1, source_target_pairs={{0,4},{4,0},{8,12},{12,8},{16,20},{20,16},{24,28},{28,24},{1,5},{5... | collective-permute-start | bytes 24584 | tf_op jit(solution)/shard_map/ppermute | solution.py:556
  32.7 6.4 %collective-permute-start.10 = (f32[72,128]{1,0:T(8,128)S(1)}, f32[72,128]{1,0:T(8,128)S(1)}, u32[]{:S(2)}, u32[]{:S(2)}) collective-permute-start(f32[72,128]{1,0:T(8,128)S(1)} %pad_maximum_fusion.3.after.refs_0_), channel_id=1, source_target_pairs={{0,3},{1,2},{2,1},{3,0},{4,7},{5,6},{6,5},{7,4},{8,11},{9,10},{10,... | collective-permute-start | bytes 110600 | tf_op jit(solution)/shard_map/ppermute | solution.py:551
  34.6 5.3 %collective-permute-start.11 = (f32[72,128]{1,0:T(8,128)S(1)}, f32[72,128]{1,0:T(8,128)S(1)}, u32[]{:S(2)}, u32[]{:S(2)}) collective-permute-start(f32[72,128]{1,0:T(8,128)S(1)} %pad_maximum_fusion.3.after.refs_0_), channel_id=1, source_target_pairs={{0,2},{1,3},{2,0},{3,1},{4,6},{5,7},{6,4},{7,5},{8,10},{9,11},{10,... | collective-permute-start | bytes 110600 | tf_op jit(solution)/shard_map/ppermute | solution.py:551
  34.8 5.0 %collective-permute-start.12 = (f32[72,128]{1,0:T(8,128)S(1)}, f32[72,128]{1,0:T(8,128)S(1)}, u32[]{:S(2)}, u32[]{:S(2)}) collective-permute-start(f32[72,128]{1,0:T(8,128)S(1)} %pad_maximum_fusion.3.after.refs_0_), channel_id=1, source_target_pairs={{0,1},{1,0},{2,3},{3,2},{4,5},{5,4},{6,7},{7,6},{8,9},{9,8},{10,11... | collective-permute-start | bytes 110600 | tf_op jit(solution)/shard_map/ppermute | solution.py:551
  41.2 4.0 %collective-permute-start.13 = (f32[16,128]{1,0:T(8,128)S(1)}, f32[16,128]{1,0:T(8,128)S(1)}, u32[]{:S(2)}, u32[]{:S(2)}) collective-permute-start(f32[16,128]{1,0:T(8,128)S(1)} %get-tuple-element.96), channel_id=1, source_target_pairs={{0,28},{4,8},{8,4},{12,16},{16,12},{20,24},{24,20},{28,0},{1,29},{... | collective-permute-start | bytes 24584 | tf_op jit(solution)/shard_map/ppermute | solution.py:557
  41.9 3.4 %collective-permute-start.14 = (f32[16,128]{1,0:T(8,128)S(1)}, f32[16,128]{1,0:T(8,128)S(1)}, u32[]{:S(2)}, u32[]{:S(2)}) collective-permute-start(f32[16,128]{1,0:T(8,128)S(1)} %get-tuple-element.96), channel_id=1, source_target_pairs={{0,4},{4,0},{8,12},{12,8},{16,20},{20,16},{24,28},{28,24},{1,5},{5... | collective-permute-start | bytes 24584 | tf_op jit(solution)/shard_map/ppermute | solution.py:556
  45.3 6.4 %collective-permute-start.15 = (f32[72,128]{1,0:T(8,128)S(1)}, f32[72,128]{1,0:T(8,128)S(1)}, u32[]{:S(2)}, u32[]{:S(2)}) collective-permute-start(f32[72,128]{1,0:T(8,128)S(1)} %pad_maximum_fusion.4.after.refs_0_), channel_id=1, source_target_pairs={{0,3},{1,2},{2,1},{3,0},{4,7},{5,6},{6,5},{7,4},{8,11},{9,10},{10,... | collective-permute-start | bytes 110600 | tf_op jit(solution)/shard_map/ppermute | solution.py:551
  47.6 4.9 %collective-permute-start.16 = (f32[72,128]{1,0:T(8,128)S(1)}, f32[72,128]{1,0:T(8,128)S(1)}, u32[]{:S(2)}, u32[]{:S(2)}) collective-permute-start(f32[72,128]{1,0:T(8,128)S(1)} %pad_maximum_fusion.4.after.refs_0_), channel_id=1, source_target_pairs={{0,2},{1,3},{2,0},{3,1},{4,6},{5,7},{6,4},{7,5},{8,10},{9,11},{10,... | collective-permute-start | bytes 110600 | tf_op jit(solution)/shard_map/ppermute | solution.py:551
  48.1 4.5 %collective-permute-start.17 = (f32[72,128]{1,0:T(8,128)S(1)}, f32[72,128]{1,0:T(8,128)S(1)}, u32[]{:S(2)}, u32[]{:S(2)}) collective-permute-start(f32[72,128]{1,0:T(8,128)S(1)} %pad_maximum_fusion.4.after.refs_0_), channel_id=1, source_target_pairs={{0,1},{1,0},{2,3},{3,2},{4,5},{5,4},{6,7},{7,6},{8,9},{9,8},{10,11... | collective-permute-start | bytes 110600 | tf_op jit(solution)/shard_map/ppermute | solution.py:551
  55.0 5.5 %collective-permute-start.18 = (f32[9,32,128]{2,1,0:T(8,128)S(1)}, f32[9,32,128]{2,1,0:T(8,128)S(1)}, u32[]{:S(2)}, u32[]{:S(2)}) collective-permute-start(f32[9,32,128]{2,1,0:T(8,128)S(1)} %get-tuple-element.102), channel_id=1, source_target_pairs={{0,4},{4,8},{8,12},{12,16},{16,20},{20,24},{24,28},{28,0},{1,5},{5... | collective-permute-start | bytes 442376 | tf_op jit(solution)/shard_map/ppermute | solution.py:646
  55.0 10.6 %collective-permute-start.19 = (f32[16,32,128]{2,1,0:T(8,128)S(1)}, f32[16,32,128]{2,1,0:T(8,128)S(1)}, u32[]{:S(2)}, u32[]{:S(2)}) collective-permute-start(f32[16,32,128]{2,1,0:T(8,128)S(1)} %get-tuple-element.105), channel_id=1, source_target_pairs={{0,1},{1,0},{2,3},{3,2},{4,5},{5,4},{6,7},{7,6},{8,9},{9,8},{10,11... | collective-permute-start | bytes 786440 | tf_op jit(solution)/shard_map/ppermute | solution.py:551
  56.3 12.3 %collective-permute-start.20 = (f32[8,32,128]{2,1,0:T(8,128)S(1)}, f32[8,32,128]{2,1,0:T(8,128)S(1)}, u32[]{:S(2)}, u32[]{:S(2)}) collective-permute-start(f32[8,32,128]{2,1,0:T(8,128)S(1)} %slice.216), channel_id=1, source_target_pairs={{0,5},{1,4},{2,7},{3,6},{4,9},{5,8},{6,11},{7,10},{8,13},{9,12},{1... | collective-permute-start | bytes 393224 | tf_op jit(solution)/shard_map/ppermute | solution.py:665
  59.3 16.5 %collective-permute-start.23 = (f32[16,32,128]{2,1,0:T(8,128)S(1)}, f32[16,32,128]{2,1,0:T(8,128)S(1)}, u32[]{:S(2)}, u32[]{:S(2)}) collective-permute-start(f32[16,32,128]{2,1,0:T(8,128)S(1)} %numer_row.3), channel_id=1, source_target_pairs={{0,1},{1,0},{2,3},{3,2},{4,5},{5,4},{6,7},{7,6},{8,9},{9,8},{10,11... | collective-permute-start | bytes 786440 | tf_op jit(solution)/shard_map/ppermute | solution.py:551
  68.6 11.2 %collective-permute-start.21 = (f32[16,32,128]{2,1,0:T(8,128)S(1)}, f32[16,32,128]{2,1,0:T(8,128)S(1)}, u32[]{:S(2)}, u32[]{:S(2)}) collective-permute-start(f32[16,32,128]{2,1,0:T(8,128)S(1)} %get-tuple-element.117.after), channel_id=1, source_target_pairs={{0,3},{1,2},{2,1},{3,0},{4,7},{5,6},{6,5},{7,4},{8,11},{9,10},{10,... | collective-permute-start | bytes 786440 | tf_op jit(solution)/shard_map/ppermute | solution.py:551
  75.8 14.9 %collective-permute-start.25 = (f32[16,32,128]{2,1,0:T(8,128)S(1)}, f32[16,32,128]{2,1,0:T(8,128)S(1)}, u32[]{:S(2)}, u32[]{:S(2)}) collective-permute-start(f32[16,32,128]{2,1,0:T(8,128)S(1)} %get-tuple-element.115), channel_id=1, source_target_pairs={{0,1},{1,0},{2,3},{3,2},{4,5},{5,4},{6,7},{7,6},{8,9},{9,8},{10,11... | collective-permute-start | bytes 786440 | tf_op jit(solution)/shard_map/ppermute | solution.py:551
  75.9 16.8 %collective-permute-start.24 = (f32[16,32,128]{2,1,0:T(8,128)S(1)}, f32[16,32,128]{2,1,0:T(8,128)S(1)}, u32[]{:S(2)}, u32[]{:S(2)}) collective-permute-start(f32[16,32,128]{2,1,0:T(8,128)S(1)} %add.75), channel_id=1, source_target_pairs={{0,3},{1,2},{2,1},{3,0},{4,7},{5,6},{6,5},{7,4},{8,11},{9,10},{10,... | collective-permute-start | bytes 786440 | tf_op jit(solution)/shard_map/ppermute | solution.py:551
  77.9 18.1 %collective-permute-start.22 = (f32[16,32,128]{2,1,0:T(8,128)S(1)}, f32[16,32,128]{2,1,0:T(8,128)S(1)}, u32[]{:S(2)}, u32[]{:S(2)}) collective-permute-start(f32[16,32,128]{2,1,0:T(8,128)S(1)} %get-tuple-element.110), channel_id=1, source_target_pairs={{0,1},{1,0},{2,3},{3,2},{4,5},{5,4},{6,7},{7,6},{8,9},{9,8},{10,11... | collective-permute-start | bytes 786440 | tf_op jit(solution)/shard_map/ppermute | solution.py:551

commit v7 on v6

--- a/solution.py
+++ b/solution.py
@@ -331,9 +331,9 @@
     lax.fori_loop(0, count, fill, 0, unroll=4)
 
 
-def numer_first_kernel(k, shares, scal, hi_ref, lo_ref, w_ref, mask, *refs):
+def numer_first_kernel(k, shares, scal, hi_ref, lo_ref, w_ref, h_ref, mask, *refs):
     parts, scales = refs[:shares], refs[shares : shares + ITERS]
-    u_out, tail_out, sums_out, out, acc = refs[shares + ITERS :]
+    u_out, tail_out, sums_out, out, acc, terms = refs[shares + ITERS :]
     rows = hi_ref.shape[0]
     ext, tile = mask.shape
     offs = offsets(scal, hi_ref.shape[2] // tile)
@@ -352,18 +352,8 @@
     tail_out[pad] = ends
 
     first = jnp.bitwise_xor(scal[0], k) * per
-    acc[...] = jnp.zeros_like(acc)
-    block = min(per, pad)
-    col_loop(offs, w_ref, hi_ref, lo_ref, u_out, acc, first, per, first - pad)
-    for q in range(1, pad // block + 1):
-
-        @pl.when(first >= q * block)
-        def _():
-            start = first - q * block
-            col_loop(offs, w_ref, hi_ref, lo_ref, u_out, acc, start, block, first - pad)
-
-    for t in range(per):
-        out[t] = acc[pad + t] * u_out[pl.ds(first + t, 1), :]
+    scaled_terms(h_ref, u_out, terms, first, per + pad)
+    row_pieces(scal, offs, terms, hi_ref, lo_ref, u_out, [k], [out])
     write_sums(sums_out, [*scales, u_out], rows)
 
 
@@ -401,16 +391,11 @@
     outs, terms = refs[:-1], refs[-1]
     ext, tile = u_ref.shape
     offs = offsets(scal, hi_ref.shape[2] // tile)
-    rows, per = hi_ref.shape[0], outs[0].shape[0]
-    if len(outs) > 1:
-        scaled_terms(h_ref, u_ref, terms, 0, ext)
-    else:
-        first = jnp.bitwise_xor(scal[0], order[0]) * per
-        scaled_terms(h_ref, u_ref, terms, first, per + ext - rows)
+    scaled_terms(h_ref, u_ref, terms, 0, ext)
     row_pieces(scal, offs, terms, hi_ref, lo_ref, u_ref, order, outs)
 
 
-def numer_first(scal, r_hi, r_lo, row_factors, mask_ext, parts, scales, k):
+def numer_first(scal, r_hi, r_lo, row_factors, col_ext, mask_ext, parts, scales, k):
     shares = len(parts)
     rows, tile = r_hi.shape[:2]
     factors = row_factors.shape[0]
@@ -421,14 +406,17 @@
         functools.partial(numer_first_kernel, k, shares),
         "numer_first",
         scal,
-        [r_hi, r_lo, row_factors, mask_ext, *parts, *scales],
+        [r_hi, r_lo, row_factors, col_ext, mask_ext, *parts, *scales],
         [
             jax.ShapeDtypeStruct((ext, tile), F32),
             jax.ShapeDtypeStruct((pad + 1, factors, tile), F32),
             jax.ShapeDtypeStruct((8, tile), F32),
             jax.ShapeDtypeStruct((per, factors, tile), F32),
         ],
-        [pltpu.VMEM((per + 2 * pad, factors, tile), F32)],
+        [
+            pltpu.VMEM((2 * pad, factors, tile), F32),
+            pltpu.VMEM((ext, 2 * factors, tile), BF16),
+        ],
     )
 
 
@@ -558,23 +546,13 @@
     return jnp.where(even > 0, a, b), jnp.where(even > 0, b, a)
 
 
-def scatter_terms(pieces, extra=None, across=None):
+def scatter_terms(pieces):
     size = lax.axis_size("offset")
-
-    def piece(k):
-        return pieces[k] if extra is None else put(pieces[k], extra[k])
-
-    def put(x, y):
-        return x.at[: y.shape[0]].add(y)
-
     if size == 4:
         far = pieces[3] + xor_exchange(pieces[2], "offset", 1)
-        if extra is not None:
-            far = put(far, extra[3] + across)
-        moved = xor_exchange(far, "offset", 3)
-        return [piece(0), xor_exchange(piece(1), "offset", 1), moved], far
-    moved = [xor_exchange(piece(k), "offset", k) for k in range(1, size)]
-    return [piece(0), *moved], moved[0]
+        far = xor_exchange(far, "offset", 3)
+        return [pieces[0], xor_exchange(pieces[1], "offset", 1), far]
+    return [pieces[0]] + [xor_exchange(pieces[k], "offset", k) for k in range(1, size)]
 
 
 def per_device(counts, band_offset, bin_mask, row_factors, col_factors):
@@ -638,12 +616,22 @@
         ratios = ratio(scal, kept, row_factors, col_ext, x, ratios, start, quarter)
 
     r_hi, r_lo = ratios
+    per = rows // offset_count
     u, tail, sums, early = numer_first(
-        scal, r_hi, r_lo, row_factors, mask_ext, parts, scales, EARLY
-    )
-    (w_early,) = numer_row(scal, r_hi, r_lo, col_ext, u, sums, [EARLY], offset_count)
+        scal, r_hi, r_lo, row_factors, col_ext, mask_ext, parts, scales, EARLY
+    )
+    order = [EARLY, *(k for k in range(offset_count) if k != EARLY)]
+    pieces = numer_col(scal, r_hi, r_lo, row_factors, u, sums, order, offset_count)
+    h_parts = dict(zip(order, pieces))
+
     right = [(i, (i + 1) % genome_count) for i in range(genome_count)]
     arrived = lax.ppermute(tail, "genome", right)
+    for s in range(-(-pad // per)):
+        piece = arrived[s * per : min(pad, (s + 1) * per)]
+        for k in range(offset_count):
+            at = s * offset_count + k
+            h_parts[k] = h_parts[k].at[: piece.shape[0]].add(piece * mine[at : at + 1])
+
     row_terms = coefficient(
         row_coefficient_kernel, scal, offset_count, row_factors, mask_ext, col_ext
     )
@@ -651,33 +639,12 @@
         col_coefficient_kernel, scal, offset_count, col_factors, mask_ext, row_factors, arrived[pad]
     )
     order = [k for k in (3, 1, 0, *range(4, offset_count))]
-    rest = numer_col(scal, r_hi, r_lo, row_factors, u, col_terms[0], order, offset_count)
-    h_parts = dict(zip(order, rest)) | {EARLY: early}
-    h_parts = [h_parts[k] for k in range(offset_count)]
-    per = rows // offset_count
-
-    if offset_count == 4 and pad <= per:
-        diagonal = [
-            (i * 4 + j, (i + 1) % genome_count * 4 + (j ^ 1))
-            for i in range(genome_count)
-            for j in range(4)
-        ]
-        across = lax.ppermute(tail[:pad], ("genome", "offset"), diagonal)
-        extra = [arrived[:pad] * mine[k : k + 1] for k in range(4)]
-        h_terms, half_way = scatter_terms(h_parts, extra, across * mine[3:4])
-    else:
-        h_parts = list(h_parts)
-        for s in range(-(-pad // per)):
-            piece = arrived[s * per : min(pad, (s + 1) * per)]
-            for k in range(offset_count):
-                at = s * offset_count + k
-                h_parts[k] = h_parts[k].at[: piece.shape[0]].add(piece * mine[at : at + 1])
-        h_terms, half_way = scatter_terms(h_parts)
-    w_rest = numer_row(scal, r_hi, r_lo, col_ext, u, half_way, order, offset_count)
-    w_parts = dict(zip(order, w_rest)) | {EARLY: w_early}
-    w_terms, _ = scatter_terms([w_parts[k] for k in range(offset_count)])
-
-    sums, _ = lax.optimization_barrier((sums, h_terms[2]))
+    pieces = numer_row(scal, r_hi, r_lo, col_ext, u, h_parts[EARLY], order, offset_count)
+    w_parts = dict(zip(order, pieces)) | {EARLY: early}
+    w_terms = scatter_terms([w_parts[k] for k in range(offset_count)])
+    h_terms = scatter_terms([h_parts[k] for k in range(offset_count)])
+
+    sums, _ = lax.optimization_barrier((sums, w_terms[2]))
     sums = jnp.sum(lax.all_gather(sums, "genome"), axis=0)
     bias = (u[:rows] * mean_scale(sums)).reshape(-1)
 

time: 97.6 us -> 95.1 us (0.974)
  Pallas kernels: 39.8 us -> 37.9 us
    ppermute x1 -> x0, waiting for transfers between devices: 2.82 us -> none  [per_device(): across = lax.ppermute(tail[:pad], ('genome', 'offset'), diagonal)]
    ppermute x15, waiting for transfers between devices: 9.5 us -> 11.9 us  [xor_exchange(): lax.ppermute(x, axis, [(i, i ^ k) for i in range(lax.axis_size(axis))])]
    pallas_call x18 -> x17, Pallas kernels: 39.8 us -> 37.9 us  [kernel_call(): pl.pallas_call(body, grid_spec=pltpu.PrefetchScalarGridSpec(num_scalar_pr...]
    ppermute x1 -> x0, starting transfers between devices: 1.26 us -> none  [per_device(): across = lax.ppermute(tail[:pad], ('genome', 'offset'), diagonal)]
    ppermute x15, starting transfers between devices: 20.8 us -> 21.9 us  [xor_exchange(): lax.ppermute(x, axis, [(i, i ^ k) for i in range(lax.axis_size(axis))])]
  transfers between devices with their start and end apart: 26 -> 25, of which waited for: 8 -> 7; matrix products, arithmetic and copies ran while one was open for 2% -> 2% of each run, Pallas kernels for 33% -> 32%
where the time goes in v7:
time: 95.1 us; the launch traced here: 94.9 us
  Pallas kernels  37.9 us (40%)
  starting transfers between devices  29.9 us (31%)
  waiting for transfers between devices  13 us (14%)
  blocking collectives  9.1 us (10%)
  other arithmetic  2.77 us (3%)
  between operations  1.67 us (2%)
    pallas_call x17, Pallas kernels, kernel_call(): pl.pallas_call(body, grid_spec=pltpu.PrefetchScalarGridSpec(num_scalar_pr...  37.9 us
    ppermute x15, starting transfers between devices, xor_exchange(): lax.ppermute(x, axis, [(i, i ^ k) for i in range(lax.axis_size(axis))])  21.9 us
    ppermute x15, waiting for transfers between devices, xor_exchange(): lax.ppermute(x, axis, [(i, i ^ k) for i in range(lax.axis_size(axis))])  11.9 us
    all_gather x1, blocking collectives, per_device(): sums = jnp.sum(lax.all_gather(sums, 'genome'), axis=0)  9.1 us
    ppermute x4, starting transfers between devices, both_sides(): lax.ppermute(x, 'genome', [(i, ((i + 1 ^ 1) - 1) % size) for i in range(s...  4.29 us
    ppermute x1, starting transfers between devices, per_device(): col_next = lax.ppermute(col_late[:, :pad * tile], 'genome', ring_left)  2.6 us
  transfers between devices with their start and end apart: 25, of which 7 were waited for; matrix products, arithmetic and copies ran while one was open for 2% of the time, Pallas kernels for 32%

profile of v7, /device:TPU:0, one launch (start us, length us, event | category | flops | bytes accessed | tf_op | source)
XLA Modules:
  0.0 94.9 jit_solution(3767158870647800788)
XLA Ops:
  0.9 0.7 pad_add_fusion.scal
  1.7 0.8 fusion.13
  2.4 0.5 collective-permute-start.1
  2.9 3.6 %collective-permute-start.2 = (f32[8,128]{1,0:T(8,128)S(1)}, f32[8,128]{1,0:T(8,128)S(1)}, u32[]{:S(2)}, u32[]{:S(2)}) collective-permute-start(f32[8,128]{1,0:T(8,128)S(1)} %slice_bitcast_fusion.1), channel_id=1, source_target_pairs={{0,28},{4,8},{8,4},{12,16},{16,12},{20,24},{24,20},{28,0},{1,29},{... | collective-permute-start | bytes 12296 | tf_op jit(solution)/shard_map/ppermute | solution.py:545
  6.5 4.8 %first_main.1 = (f32[72,128]{1,0:T(8,128)S(1)}, f32[64,2,128,128]{3,2,1,0:T(8,128)S(1)}) custom-call(s32[4]{0:T(128)S(1)} %pad_add_fusion.scal, s32[64,2,128,128]{3,2,1,0:T(8,128)} %hbm.1, f32[64,128]{1,0:T(8,128)S(1)} %get-tuple-element.140.mask), custom_call_target="tpu_custom_call" | custom-call | tf_op jit(solution)/shard_map/first_main/pallas_call | solution.py:47
  11.3 1.4 %first_edge.1 = (f32[72,128]{1,0:T(8,128)S(1)}, f32[16,128]{1,0:T(8,128)S(1)}) custom-call(s32[4]{0:T(128)S(1)} %pad_add_fusion.scal, f32[64,2,128,128]{3,2,1,0:T(8,128)S(1)} %get-tuple-element.92.kept, f32[72,128]{1,0:T(8,128)S(1)} %pad_maximum_fusion.1.u_ref.mask.refs_4_, f32[72,128]{1,0:T(8,128)S(1)} %get-tuple-element.94.inner_v), custom_call_target="tpu_custom_call" | custom-call | tf_op jit(solution)/shard_map/first_edge/pallas_call | solution.py:47
  12.9 2.6 %collective-permute-start = (f32[32,1024]{1,0:T(8,128)S(1)}, f32[32,1024]{1,0:T(8,128)S(1)}, u32[]{:S(2)}, u32[]{:S(2)}) collective-permute-start(f32[32,1024]{1,0:T(8,128)S(1)} %slice.212), channel_id=1, source_target_pairs={{0,28},{4,0},{8,4},{12,8},{16,12},{20,16},{24,20},{28,24},{1,29},{... | collective-permute-start | bytes 393224 | tf_op jit(solution)/shard_map/ppermute | solution.py:592
  15.5 0.5 slice.211
  16.6 2.0 %ratio.4 = (bf16[64,128,256]{2,1,0:T(8,128)(2,1)S(1)}, bf16[64,128,256]{2,1,0:T(8,128)(2,1)S(1)}, f32[72,128]{1,0:T(8,128)S(1)}) custom-call(s32[4]{0:T(128)S(1)} %pad_add_fusion.scal, f32[64,2,128,128]{3,2,1,0:T(8,128)S(1)} %get-tuple-element.92.kept, f32[32,8192]{1,0:T(8,128)S(1)} %copy-done, f32[32,8192]{1,0:T(8,128)S(1)} %copy-done.1, ...), custom_call_target="tpu_custom_call" | custom-call | tf_op jit(solution)/shard_map/ratio/pallas_call | solution.py:47
  18.7 3.7 %collective-permute-start.5 = (f32[72,128]{1,0:T(8,128)S(1)}, f32[72,128]{1,0:T(8,128)S(1)}, u32[]{:S(2)}, u32[]{:S(2)}) collective-permute-start(f32[72,128]{1,0:T(8,128)S(1)} %pad_maximum_fusion.2.after.refs_0_), channel_id=1, source_target_pairs={{0,3},{1,2},{2,1},{3,0},{4,7},{5,6},{6,5},{7,4},{8,11},{9,10},{10,... | collective-permute-start | bytes 110600 | tf_op jit(solution)/shard_map/ppermute | solution.py:539
  22.4 0.8 collective-permute-start.7
  23.3 2.2 %ratio.5 = (bf16[64,128,256]{2,1,0:T(8,128)(2,1)S(1)}, bf16[64,128,256]{2,1,0:T(8,128)(2,1)S(1)}) custom-call(s32[4]{0:T(128)S(1)} %pad_add_fusion.scal, f32[64,2,128,128]{3,2,1,0:T(8,128)S(1)} %get-tuple-element.92.kept, f32[32,8192]{1,0:T(8,128)S(1)} %copy-done, ...), custom_call_target="tpu_custom_call", output_to_operand_aliasing={{0}: (5, {}), {1}: (6, {})} | custom-call | tf_op jit(solution)/shard_map/ratio/pallas_call | solution.py:47
  25.4 1.8 %collective-permute-done.6.refs_2_ = f32[72,128]{1,0:T(8,128)S(1)} collective-permute-done((f32[72,128]{1,0:T(8,128)S(1)}, f32[72,128]{1,0:T(8,128)S(1)}, u32[]{:S(2)}, u32[]{:S(2)}) %collective-permute-start.6) | collective-permute-done | bytes 36896 | tf_op jit(solution)/shard_map/ppermute | solution.py:539
  27.2 1.4 %cover_edge.2 = (f32[72,128]{1,0:T(8,128)S(1)}, f32[16,128]{1,0:T(8,128)S(1)}, f32[72,128]{1,0:T(8,128)S(1)}) custom-call(s32[4]{0:T(128)S(1)} %pad_add_fusion.scal, f32[64,2,128,128]{3,2,1,0:T(8,128)S(1)} %get-tuple-element.92.kept, f32[72,128]{1,0:T(8,128)S(1)} %pad_maximum_fusion.1.u_ref.mask.refs_4_, f32[72,128]{1,0:T(8,128)S(1)} %pad_maximum_fusion.2.after.refs_0_, ...), custom_call_target="tpu_custom_call" | custom-call | tf_op jit(solution)/shard_map/cover_edge/pallas_call | solution.py:47
  28.8 2.8 %cover_main.2 = f32[72,128]{1,0:T(8,128)S(1)} custom-call(s32[4]{0:T(128)S(1)} %pad_add_fusion.scal, f32[64,2,128,128]{3,2,1,0:T(8,128)S(1)} %get-tuple-element.92.kept, f32[72,128]{1,0:T(8,128)S(1)} %get-tuple-element.102.u_ref.refs_5_, f32[72,128]{1,0:T(8,128)S(1)} %get-tuple-element.103.edge_v), custom_call_target="tpu_custom_call" | custom-call | tf_op jit(solution)/shard_map/cover_main/pallas_call | solution.py:47
  31.6 1.0 %collective-permute-done.8 = f32[16,128]{1,0:T(8,128)S(1)} collective-permute-done((f32[16,128]{1,0:T(8,128)S(1)}, f32[16,128]{1,0:T(8,128)S(1)}, u32[]{:S(2)}, u32[]{:S(2)}) %collective-permute-start.8) | collective-permute-done | bytes 8224 | tf_op jit(solution)/shard_map/ppermute | solution.py:545
  32.7 1.9 %collective-permute-start.10 = (f32[72,128]{1,0:T(8,128)S(1)}, f32[72,128]{1,0:T(8,128)S(1)}, u32[]{:S(2)}, u32[]{:S(2)}) collective-permute-start(f32[72,128]{1,0:T(8,128)S(1)} %pad_maximum_fusion.3.after.refs_0_), channel_id=1, source_target_pairs={{0,3},{1,2},{2,1},{3,0},{4,7},{5,6},{6,5},{7,4},{8,11},{9,10},{10,... | collective-permute-start | bytes 110600 | tf_op jit(solution)/shard_map/ppermute | solution.py:539
  34.6 0.3 collective-permute-start.11
  34.8 2.3 %collective-permute-start.12 = (f32[72,128]{1,0:T(8,128)S(1)}, f32[72,128]{1,0:T(8,128)S(1)}, u32[]{:S(2)}, u32[]{:S(2)}) collective-permute-start(f32[72,128]{1,0:T(8,128)S(1)} %pad_maximum_fusion.3.after.refs_0_), channel_id=1, source_target_pairs={{0,1},{1,0},{2,3},{3,2},{4,5},{5,4},{6,7},{7,6},{8,9},{9,8},{10,11... | collective-permute-start | bytes 110600 | tf_op jit(solution)/shard_map/ppermute | solution.py:539
  37.1 2.0 %ratio.6 = (bf16[64,128,256]{2,1,0:T(8,128)(2,1)S(1)}, bf16[64,128,256]{2,1,0:T(8,128)(2,1)S(1)}) custom-call(s32[4]{0:T(128)S(1)} %pad_add_fusion.scal, f32[64,2,128,128]{3,2,1,0:T(8,128)S(1)} %get-tuple-element.92.kept, f32[32,8192]{1,0:T(8,128)S(1)} %copy-done, ...), custom_call_target="tpu_custom_call", output_to_operand_aliasing={{0}: (5, {}), {1}: (6, {})} | custom-call | tf_op jit(solution)/shard_map/ratio/pallas_call | solution.py:47
  39.1 0.7 collective-permute-done.11.refs_2_
  39.8 1.4 %cover_edge.3 = (f32[72,128]{1,0:T(8,128)S(1)}, f32[16,128]{1,0:T(8,128)S(1)}, f32[72,128]{1,0:T(8,128)S(1)}) custom-call(s32[4]{0:T(128)S(1)} %pad_add_fusion.scal, f32[64,2,128,128]{3,2,1,0:T(8,128)S(1)} %get-tuple-element.92.kept, f32[72,128]{1,0:T(8,128)S(1)} %pad_maximum_fusion.1.u_ref.mask.refs_4_, f32[72,128]{1,0:T(8,128)S(1)} %pad_maximum_fusion.3.after.refs_0_, ...), custom_call_target="tpu_custom_call" | custom-call | tf_op jit(solution)/shard_map/cover_edge/pallas_call | solution.py:47
  41.2 0.6 collective-permute-start.13
  41.9 0.5 collective-permute-start.14
  42.4 2.8 %cover_main.3 = f32[72,128]{1,0:T(8,128)S(1)} custom-call(s32[4]{0:T(128)S(1)} %pad_add_fusion.scal, f32[64,2,128,128]{3,2,1,0:T(8,128)S(1)} %get-tuple-element.92.kept, f32[72,128]{1,0:T(8,128)S(1)} %get-tuple-element.107.u_ref.refs_6_, f32[72,128]{1,0:T(8,128)S(1)} %get-tuple-element.108.edge_v), custom_call_target="tpu_custom_call" | custom-call | tf_op jit(solution)/shard_map/cover_main/pallas_call | solution.py:47
  45.3 2.3 %collective-permute-start.15 = (f32[72,128]{1,0:T(8,128)S(1)}, f32[72,128]{1,0:T(8,128)S(1)}, u32[]{:S(2)}, u32[]{:S(2)}) collective-permute-start(f32[72,128]{1,0:T(8,128)S(1)} %pad_maximum_fusion.4.after.refs_0_), channel_id=1, source_target_pairs={{0,3},{1,2},{2,1},{3,0},{4,7},{5,6},{6,5},{7,4},{8,11},{9,10},{10,... | collective-permute-start | bytes 110600 | tf_op jit(solution)/shard_map/ppermute | solution.py:539
  47.6 0.4 collective-permute-start.16
  48.1 1.7 %collective-permute-start.17 = (f32[72,128]{1,0:T(8,128)S(1)}, f32[72,128]{1,0:T(8,128)S(1)}, u32[]{:S(2)}, u32[]{:S(2)}) collective-permute-start(f32[72,128]{1,0:T(8,128)S(1)} %pad_maximum_fusion.4.after.refs_0_), channel_id=1, source_target_pairs={{0,1},{1,0},{2,3},{3,2},{4,5},{5,4},{6,7},{7,6},{8,9},{9,8},{10,11... | collective-permute-start | bytes 110600 | tf_op jit(solution)/shard_map/ppermute | solution.py:539
  49.7 2.0 %ratio.7 = (bf16[64,128,256]{2,1,0:T(8,128)(2,1)S(1)}, bf16[64,128,256]{2,1,0:T(8,128)(2,1)S(1)}) custom-call(s32[4]{0:T(128)S(1)} %pad_add_fusion.scal, f32[64,2,128,128]{3,2,1,0:T(8,128)S(1)} %get-tuple-element.92.kept, f32[32,8192]{1,0:T(8,128)S(1)} %copy-done, ...), custom_call_target="tpu_custom_call", output_to_operand_aliasing={{0}: (5, {}), {1}: (6, {})} | custom-call | tf_op jit(solution)/shard_map/ratio/pallas_call | solution.py:47
  51.7 0.8 collective-permute-done.16.refs_2_
  52.5 2.4 %numer_first.1 = (f32[72,128]{1,0:T(8,128)S(1)}, f32[9,32,128]{2,1,0:T(8,128)S(1)}, f32[8,128]{1,0:T(8,128)S(1)}, f32[16,32,128]{2,1,0:T(8,128)S(1)}) custom-call(s32[4]{0:T(128)S(1)} %pad_add_fusion.scal, bf16[64,128,256]{2,1,0:T(8,128)(2,1)S(1)} %get-tuple-element.111.hi_ref, bf16[64,128,256]{2,1,0:T(8,128)(2,1)S(1)} %get-tuple-element.112.lo_ref, ...), custom_call_target="tpu_custom_call" | custom-call | tf_op jit(solution)/shard_map/numer_first/pallas_call | solution.py:47
  55.0 1.2 %collective-permute-start.19 = (f32[16,32,128]{2,1,0:T(8,128)S(1)}, f32[16,32,128]{2,1,0:T(8,128)S(1)}, u32[]{:S(2)}, u32[]{:S(2)}) collective-permute-start(f32[16,32,128]{2,1,0:T(8,128)S(1)} %get-tuple-element.118), channel_id=1, source_target_pairs={{0,1},{1,0},{2,3},{3,2},{4,5},{5,4},{6,7},{7,6},{8,9},{9,8},{10,11... | collective-permute-start | bytes 786440 | tf_op jit(solution)/shard_map/ppermute | solution.py:539
  56.2 4.2 %numer_col.1 = (f32[16,32,128]{2,1,0:T(8,128)S(1)}, f32[16,32,128]{2,1,0:T(8,128)S(1)}, f32[16,32,128]{2,1,0:T(8,128)S(1)}, f32[16,32,128]{2,1,0:T(8,128)S(1)}) custom-call(s32[4]{0:T(128)S(1)} %pad_add_fusion.scal, bf16[64,128,256]{2,1,0:T(8,128)(2,1)S(1)} %get-tuple-element.111.hi_ref, bf16[64,128,256]{2,1,0:T(8,128)(2,1)S(1)} %get-tuple-element.112.lo_ref, ...), custom_call_target="tpu_custom_call" | custom-call | tf_op jit(solution)/shard_map/numer_col/pallas_call | solution.py:47
  60.5 0.1 add_dynamic-update-slice_fusion
  60.6 1.2 %collective-permute-start.23 = (f32[16,32,128]{2,1,0:T(8,128)S(1)}, f32[16,32,128]{2,1,0:T(8,128)S(1)}, u32[]{:S(2)}, u32[]{:S(2)}) collective-permute-start(f32[16,32,128]{2,1,0:T(8,128)S(1)} %get-tuple-element.132.after), channel_id=1, source_target_pairs={{0,1},{1,0},{2,3},{3,2},{4,5},{5,4},{6,7},{7,6},{8,9},{9,8},{10,11... | collective-permute-start | bytes 786440 | tf_op jit(solution)/shard_map/ppermute | solution.py:539
  61.8 4.3 %numer_row.1 = (f32[16,32,128]{2,1,0:T(8,128)S(1)}, f32[16,32,128]{2,1,0:T(8,128)S(1)}, f32[16,32,128]{2,1,0:T(8,128)S(1)}) custom-call(s32[4]{0:T(128)S(1)} %pad_add_fusion.scal, bf16[64,128,256]{2,1,0:T(8,128)(2,1)S(1)} %get-tuple-element.111.hi_ref, bf16[64,128,256]{2,1,0:T(8,128)(2,1)S(1)} %get-tuple-element.112.lo_ref, ...), custom_call_target="tpu_custom_call" | custom-call | tf_op jit(solution)/shard_map/numer_row/pallas_call | solution.py:47
  66.1 2.3 %collective-permute-start.20 = (f32[16,32,128]{2,1,0:T(8,128)S(1)}, f32[16,32,128]{2,1,0:T(8,128)S(1)}, u32[]{:S(2)}, u32[]{:S(2)}) collective-permute-start(f32[16,32,128]{2,1,0:T(8,128)S(1)} %add.77), channel_id=1, source_target_pairs={{0,3},{1,2},{2,1},{3,0},{4,7},{5,6},{6,5},{7,4},{8,11},{9,10},{10,... | collective-permute-start | bytes 786440 | tf_op jit(solution)/shard_map/ppermute | solution.py:539
  68.4 0.7 coefficient.2
  69.3 0.9 coefficient.3
  70.2 2.1 %collective-permute-start.21 = (f32[16,32,128]{2,1,0:T(8,128)S(1)}, f32[16,32,128]{2,1,0:T(8,128)S(1)}, u32[]{:S(2)}, u32[]{:S(2)}) collective-permute-start(f32[16,32,128]{2,1,0:T(8,128)S(1)} %get-tuple-element.123), channel_id=1, source_target_pairs={{0,1},{1,0},{2,3},{3,2},{4,5},{5,4},{6,7},{7,6},{8,9},{9,8},{10,11... | collective-permute-start | bytes 786440 | tf_op jit(solution)/shard_map/ppermute | solution.py:539
  72.3 1.6 %collective-permute-start.24 = (f32[16,32,128]{2,1,0:T(8,128)S(1)}, f32[16,32,128]{2,1,0:T(8,128)S(1)}, u32[]{:S(2)}, u32[]{:S(2)}) collective-permute-start(f32[16,32,128]{2,1,0:T(8,128)S(1)} %add.81), channel_id=1, source_target_pairs={{0,3},{1,2},{2,1},{3,0},{4,7},{5,6},{6,5},{7,4},{8,11},{9,10},{10,... | collective-permute-start | bytes 786440 | tf_op jit(solution)/shard_map/ppermute | solution.py:539
  73.9 3.3 %collective-permute-done.20.refs_2_ = f32[16,32,128]{2,1,0:T(8,128)S(1)} collective-permute-done((f32[16,32,128]{2,1,0:T(8,128)S(1)}, f32[16,32,128]{2,1,0:T(8,128)S(1)}, u32[]{:S(2)}, u32[]{:S(2)}) %collective-permute-start.20) | collective-permute-done | bytes 262176 | tf_op jit(solution)/shard_map/ppermute | solution.py:539
  77.2 9.1 %all-gather = f32[64,128]{1,0:T(8,128)S(1)} all-gather(f32[8,128]{1,0:T(8,128)S(1)} %get-tuple-element.119.after), channel_id=2, replica_groups=mesh['genome'=8,'offset'=4] {'genome'}, dimensions={0}, use_global_device_ids=true | all-gather | bytes 36864 | tf_op jit(solution)/shard_map/all_gather | solution.py:648
  86.3 1.9 %collective-permute-done.21.refs_1_ = f32[16,32,128]{2,1,0:T(8,128)S(1)} collective-permute-done((f32[16,32,128]{2,1,0:T(8,128)S(1)}, f32[16,32,128]{2,1,0:T(8,128)S(1)}, u32[]{:S(2)}, u32[]{:S(2)}) %collective-permute-start.21) | collective-permute-done | bytes 262176 | tf_op jit(solution)/shard_map/ppermute | solution.py:539
  88.3 1.3 %update.2 = f32[32,2048]{1,0:T(8,128)} custom-call(s32[4]{0:T(128)S(1)} %pad_add_fusion.scal, f32[8,128]{1,0:T(8,128)S(1)} %bitcast_reduce_fusion.sums, f32[16,32,128]{2,1,0:T(8,128)S(1)} %get-tuple-element.120.times, f32[16,32,128]{2,1,0:T(8,128)S(1)} %get-tuple-element.121.plus, f32[16,32,128]{2,1,0:T(8,128)S(1)} %get-tuple-element.122.refs_0_, ...), custom_call_target="tpu_custom_call" | custom-call | tf_op jit(solution)/shard_map/update/pallas_call | solution.py:47
  89.6 0.6 multiply_bitcast_fusion
  90.2 3.3 %collective-permute-done.24.refs_2_ = f32[16,32,128]{2,1,0:T(8,128)S(1)} collective-permute-done((f32[16,32,128]{2,1,0:T(8,128)S(1)}, f32[16,32,128]{2,1,0:T(8,128)S(1)}, u32[]{:S(2)}, u32[]{:S(2)}) %collective-permute-start.24) | collective-permute-done | bytes 262176 | tf_op jit(solution)/shard_map/ppermute | solution.py:539
  93.6 1.3 %update.3 = f32[32,2048]{1,0:T(8,128)} custom-call(s32[4]{0:T(128)S(1)} %pad_add_fusion.scal, f32[8,128]{1,0:T(8,128)S(1)} %bitcast_reduce_fusion.sums, f32[16,32,128]{2,1,0:T(8,128)S(1)} %get-tuple-element.124.times, f32[16,32,128]{2,1,0:T(8,128)S(1)} %get-tuple-element.125.plus, f32[16,32,128]{2,1,0:T(8,128)S(1)} %get-tuple-element.130.refs_0_, ...), custom_call_target="tpu_custom_call" | custom-call | tf_op jit(solution)/shard_map/update/pallas_call | solution.py:47
  (58 shorter events, 1.0 us)
Async XLA Ops:
  2.4 8.8 %collective-permute-start.1 = (f32[8,128]{1,0:T(8,128)S(1)}, f32[8,128]{1,0:T(8,128)S(1)}, u32[]{:S(2)}, u32[]{:S(2)}) collective-permute-start(f32[8,128]{1,0:T(8,128)S(1)} %slice_bitcast_fusion.1), channel_id=1, source_target_pairs={{0,4},{4,0},{8,12},{12,8},{16,20},{20,16},{24,28},{28,24},{1,5},{5... | collective-permute-start | bytes 12296 | tf_op jit(solution)/shard_map/ppermute | solution.py:544
  2.9 8.4 %collective-permute-start.2 = (f32[8,128]{1,0:T(8,128)S(1)}, f32[8,128]{1,0:T(8,128)S(1)}, u32[]{:S(2)}, u32[]{:S(2)}) collective-permute-start(f32[8,128]{1,0:T(8,128)S(1)} %slice_bitcast_fusion.1), channel_id=1, source_target_pairs={{0,28},{4,8},{8,4},{12,16},{16,12},{20,24},{24,20},{28,0},{1,29},{... | collective-permute-start | bytes 12296 | tf_op jit(solution)/shard_map/ppermute | solution.py:545
  11.3 1.5 %copy-start.1 = (f32[32,8192]{1,0:T(8,128)S(1)}, f32[32,8192]{1,0:T(8,128)}, u32[]{:S(2)}) copy-start(f32[32,8192]{1,0:T(8,128)} %old_ref.3) | copy-start | bytes 3145732
  11.3 5.3 %copy-start = (f32[32,8192]{1,0:T(8,128)S(1)}, f32[32,8192]{1,0:T(8,128)}, u32[]{:S(2)}) copy-start(f32[32,8192]{1,0:T(8,128)} %other.1) | copy-start | bytes 3145732
  12.7 5.9 %collective-permute-start.3 = (f32[16,128]{1,0:T(8,128)S(1)}, f32[16,128]{1,0:T(8,128)S(1)}, u32[]{:S(2)}, u32[]{:S(2)}) collective-permute-start(f32[16,128]{1,0:T(8,128)S(1)} %get-tuple-element.98), channel_id=1, source_target_pairs={{0,28},{4,8},{8,4},{12,16},{16,12},{20,24},{24,20},{28,0},{1,29},{... | collective-permute-start | bytes 24584 | tf_op jit(solution)/shard_map/ppermute | solution.py:545
  12.8 5.9 %collective-permute-start.4 = (f32[16,128]{1,0:T(8,128)S(1)}, f32[16,128]{1,0:T(8,128)S(1)}, u32[]{:S(2)}, u32[]{:S(2)}) collective-permute-start(f32[16,128]{1,0:T(8,128)S(1)} %get-tuple-element.98), channel_id=1, source_target_pairs={{0,4},{4,0},{8,12},{12,8},{16,20},{20,16},{24,28},{28,24},{1,5},{5... | collective-permute-start | bytes 24584 | tf_op jit(solution)/shard_map/ppermute | solution.py:544
  12.9 10.3 %collective-permute-start = (f32[32,1024]{1,0:T(8,128)S(1)}, f32[32,1024]{1,0:T(8,128)S(1)}, u32[]{:S(2)}, u32[]{:S(2)}) collective-permute-start(f32[32,1024]{1,0:T(8,128)S(1)} %slice.212), channel_id=1, source_target_pairs={{0,28},{4,0},{8,4},{12,8},{16,12},{20,16},{24,20},{28,24},{1,29},{... | collective-permute-start | bytes 393224 | tf_op jit(solution)/shard_map/ppermute | solution.py:592
  18.7 6.7 %collective-permute-start.5 = (f32[72,128]{1,0:T(8,128)S(1)}, f32[72,128]{1,0:T(8,128)S(1)}, u32[]{:S(2)}, u32[]{:S(2)}) collective-permute-start(f32[72,128]{1,0:T(8,128)S(1)} %pad_maximum_fusion.2.after.refs_0_), channel_id=1, source_target_pairs={{0,3},{1,2},{2,1},{3,0},{4,7},{5,6},{6,5},{7,4},{8,11},{9,10},{10,... | collective-permute-start | bytes 110600 | tf_op jit(solution)/shard_map/ppermute | solution.py:539
  22.4 4.9 %collective-permute-start.6 = (f32[72,128]{1,0:T(8,128)S(1)}, f32[72,128]{1,0:T(8,128)S(1)}, u32[]{:S(2)}, u32[]{:S(2)}) collective-permute-start(f32[72,128]{1,0:T(8,128)S(1)} %pad_maximum_fusion.2.after.refs_0_), channel_id=1, source_target_pairs={{0,2},{1,3},{2,0},{3,1},{4,6},{5,7},{6,4},{7,5},{8,10},{9,11},{10,... | collective-permute-start | bytes 110600 | tf_op jit(solution)/shard_map/ppermute | solution.py:539
  22.4 4.9 %collective-permute-start.7 = (f32[72,128]{1,0:T(8,128)S(1)}, f32[72,128]{1,0:T(8,128)S(1)}, u32[]{:S(2)}, u32[]{:S(2)}) collective-permute-start(f32[72,128]{1,0:T(8,128)S(1)} %pad_maximum_fusion.2.after.refs_0_), channel_id=1, source_target_pairs={{0,1},{1,0},{2,3},{3,2},{4,5},{5,4},{6,7},{7,6},{8,9},{9,8},{10,11... | collective-permute-start | bytes 110600 | tf_op jit(solution)/shard_map/ppermute | solution.py:539
  28.6 4.0 %collective-permute-start.8 = (f32[16,128]{1,0:T(8,128)S(1)}, f32[16,128]{1,0:T(8,128)S(1)}, u32[]{:S(2)}, u32[]{:S(2)}) collective-permute-start(f32[16,128]{1,0:T(8,128)S(1)} %get-tuple-element.104), channel_id=1, source_target_pairs={{0,28},{4,8},{8,4},{12,16},{16,12},{20,24},{24,20},{28,0},{1,29},{... | collective-permute-start | bytes 24584 | tf_op jit(solution)/shard_map/ppermute | solution.py:545
  28.7 4.0 %collective-permute-start.9 = (f32[16,128]{1,0:T(8,128)S(1)}, f32[16,128]{1,0:T(8,128)S(1)}, u32[]{:S(2)}, u32[]{:S(2)}) collective-permute-start(f32[16,128]{1,0:T(8,128)S(1)} %get-tuple-element.104), channel_id=1, source_target_pairs={{0,4},{4,0},{8,12},{12,8},{16,20},{20,16},{24,28},{28,24},{1,5},{5... | collective-permute-start | bytes 24584 | tf_op jit(solution)/shard_map/ppermute | solution.py:544
  32.7 6.4 %collective-permute-start.10 = (f32[72,128]{1,0:T(8,128)S(1)}, f32[72,128]{1,0:T(8,128)S(1)}, u32[]{:S(2)}, u32[]{:S(2)}) collective-permute-start(f32[72,128]{1,0:T(8,128)S(1)} %pad_maximum_fusion.3.after.refs_0_), channel_id=1, source_target_pairs={{0,3},{1,2},{2,1},{3,0},{4,7},{5,6},{6,5},{7,4},{8,11},{9,10},{10,... | collective-permute-start | bytes 110600 | tf_op jit(solution)/shard_map/ppermute | solution.py:539
  34.6 5.3 %collective-permute-start.11 = (f32[72,128]{1,0:T(8,128)S(1)}, f32[72,128]{1,0:T(8,128)S(1)}, u32[]{:S(2)}, u32[]{:S(2)}) collective-permute-start(f32[72,128]{1,0:T(8,128)S(1)} %pad_maximum_fusion.3.after.refs_0_), channel_id=1, source_target_pairs={{0,2},{1,3},{2,0},{3,1},{4,6},{5,7},{6,4},{7,5},{8,10},{9,11},{10,... | collective-permute-start | bytes 110600 | tf_op jit(solution)/shard_map/ppermute | solution.py:539
  34.8 5.0 %collective-permute-start.12 = (f32[72,128]{1,0:T(8,128)S(1)}, f32[72,128]{1,0:T(8,128)S(1)}, u32[]{:S(2)}, u32[]{:S(2)}) collective-permute-start(f32[72,128]{1,0:T(8,128)S(1)} %pad_maximum_fusion.3.after.refs_0_), channel_id=1, source_target_pairs={{0,1},{1,0},{2,3},{3,2},{4,5},{5,4},{6,7},{7,6},{8,9},{9,8},{10,11... | collective-permute-start | bytes 110600 | tf_op jit(solution)/shard_map/ppermute | solution.py:539
  41.2 4.0 %collective-permute-start.13 = (f32[16,128]{1,0:T(8,128)S(1)}, f32[16,128]{1,0:T(8,128)S(1)}, u32[]{:S(2)}, u32[]{:S(2)}) collective-permute-start(f32[16,128]{1,0:T(8,128)S(1)} %get-tuple-element.109), channel_id=1, source_target_pairs={{0,28},{4,8},{8,4},{12,16},{16,12},{20,24},{24,20},{28,0},{1,29},{... | collective-permute-start | bytes 24584 | tf_op jit(solution)/shard_map/ppermute | solution.py:545
  41.9 3.4 %collective-permute-start.14 = (f32[16,128]{1,0:T(8,128)S(1)}, f32[16,128]{1,0:T(8,128)S(1)}, u32[]{:S(2)}, u32[]{:S(2)}) collective-permute-start(f32[16,128]{1,0:T(8,128)S(1)} %get-tuple-element.109), channel_id=1, source_target_pairs={{0,4},{4,0},{8,12},{12,8},{16,20},{20,16},{24,28},{28,24},{1,5},{5... | collective-permute-start | bytes 24584 | tf_op jit(solution)/shard_map/ppermute | solution.py:544
  45.3 6.5 %collective-permute-start.15 = (f32[72,128]{1,0:T(8,128)S(1)}, f32[72,128]{1,0:T(8,128)S(1)}, u32[]{:S(2)}, u32[]{:S(2)}) collective-permute-start(f32[72,128]{1,0:T(8,128)S(1)} %pad_maximum_fusion.4.after.refs_0_), channel_id=1, source_target_pairs={{0,3},{1,2},{2,1},{3,0},{4,7},{5,6},{6,5},{7,4},{8,11},{9,10},{10,... | collective-permute-start | bytes 110600 | tf_op jit(solution)/shard_map/ppermute | solution.py:539
  47.6 4.9 %collective-permute-start.16 = (f32[72,128]{1,0:T(8,128)S(1)}, f32[72,128]{1,0:T(8,128)S(1)}, u32[]{:S(2)}, u32[]{:S(2)}) collective-permute-start(f32[72,128]{1,0:T(8,128)S(1)} %pad_maximum_fusion.4.after.refs_0_), channel_id=1, source_target_pairs={{0,2},{1,3},{2,0},{3,1},{4,6},{5,7},{6,4},{7,5},{8,10},{9,11},{10,... | collective-permute-start | bytes 110600 | tf_op jit(solution)/shard_map/ppermute | solution.py:539
  48.1 4.5 %collective-permute-start.17 = (f32[72,128]{1,0:T(8,128)S(1)}, f32[72,128]{1,0:T(8,128)S(1)}, u32[]{:S(2)}, u32[]{:S(2)}) collective-permute-start(f32[72,128]{1,0:T(8,128)S(1)} %pad_maximum_fusion.4.after.refs_0_), channel_id=1, source_target_pairs={{0,1},{1,0},{2,3},{3,2},{4,5},{5,4},{6,7},{7,6},{8,9},{9,8},{10,11... | collective-permute-start | bytes 110600 | tf_op jit(solution)/shard_map/ppermute | solution.py:539
  55.0 5.5 %collective-permute-start.18 = (f32[9,32,128]{2,1,0:T(8,128)S(1)}, f32[9,32,128]{2,1,0:T(8,128)S(1)}, u32[]{:S(2)}, u32[]{:S(2)}) collective-permute-start(f32[9,32,128]{2,1,0:T(8,128)S(1)} %get-tuple-element.116), channel_id=1, source_target_pairs={{0,4},{4,8},{8,12},{12,16},{16,20},{20,24},{24,28},{28,0},{1,5},{5... | collective-permute-start | bytes 442376 | tf_op jit(solution)/shard_map/ppermute | solution.py:628
  55.0 11.1 %collective-permute-start.19 = (f32[16,32,128]{2,1,0:T(8,128)S(1)}, f32[16,32,128]{2,1,0:T(8,128)S(1)}, u32[]{:S(2)}, u32[]{:S(2)}) collective-permute-start(f32[16,32,128]{2,1,0:T(8,128)S(1)} %get-tuple-element.118), channel_id=1, source_target_pairs={{0,1},{1,0},{2,3},{3,2},{4,5},{5,4},{6,7},{7,6},{8,9},{9,8},{10,11... | collective-permute-start | bytes 786440 | tf_op jit(solution)/shard_map/ppermute | solution.py:539
  60.6 11.7 %collective-permute-start.23 = (f32[16,32,128]{2,1,0:T(8,128)S(1)}, f32[16,32,128]{2,1,0:T(8,128)S(1)}, u32[]{:S(2)}, u32[]{:S(2)}) collective-permute-start(f32[16,32,128]{2,1,0:T(8,128)S(1)} %get-tuple-element.132.after), channel_id=1, source_target_pairs={{0,1},{1,0},{2,3},{3,2},{4,5},{5,4},{6,7},{7,6},{8,9},{9,8},{10,11... | collective-permute-start | bytes 786440 | tf_op jit(solution)/shard_map/ppermute | solution.py:539
  66.1 11.1 %collective-permute-start.20 = (f32[16,32,128]{2,1,0:T(8,128)S(1)}, f32[16,32,128]{2,1,0:T(8,128)S(1)}, u32[]{:S(2)}, u32[]{:S(2)}) collective-permute-start(f32[16,32,128]{2,1,0:T(8,128)S(1)} %add.77), channel_id=1, source_target_pairs={{0,3},{1,2},{2,1},{3,0},{4,7},{5,6},{6,5},{7,4},{8,11},{9,10},{10,... | collective-permute-start | bytes 786440 | tf_op jit(solution)/shard_map/ppermute | solution.py:539
  69.2 21.0 %collective-permute-start.22 = (f32[16,32,128]{2,1,0:T(8,128)S(1)}, f32[16,32,128]{2,1,0:T(8,128)S(1)}, u32[]{:S(2)}, u32[]{:S(2)}) collective-permute-start(f32[16,32,128]{2,1,0:T(8,128)S(1)} %get-tuple-element.131), channel_id=1, source_target_pairs={{0,1},{1,0},{2,3},{3,2},{4,5},{5,4},{6,7},{7,6},{8,9},{9,8},{10,11... | collective-permute-start | bytes 786440 | tf_op jit(solution)/shard_map/ppermute | solution.py:539
  70.2 18.1 %collective-permute-start.21 = (f32[16,32,128]{2,1,0:T(8,128)S(1)}, f32[16,32,128]{2,1,0:T(8,128)S(1)}, u32[]{:S(2)}, u32[]{:S(2)}) collective-permute-start(f32[16,32,128]{2,1,0:T(8,128)S(1)} %get-tuple-element.123), channel_id=1, source_target_pairs={{0,1},{1,0},{2,3},{3,2},{4,5},{5,4},{6,7},{7,6},{8,9},{9,8},{10,11... | collective-permute-start | bytes 786440 | tf_op jit(solution)/shard_map/ppermute | solution.py:539
  72.3 21.3 %collective-permute-start.24 = (f32[16,32,128]{2,1,0:T(8,128)S(1)}, f32[16,32,128]{2,1,0:T(8,128)S(1)}, u32[]{:S(2)}, u32[]{:S(2)}) collective-permute-start(f32[16,32,128]{2,1,0:T(8,128)S(1)} %add.81), channel_id=1, source_target_pairs={{0,3},{1,2},{2,1},{3,0},{4,7},{5,6},{6,5},{7,4},{8,11},{9,10},{10,... | collective-permute-start | bytes 786440 | tf_op jit(solution)/shard_map/ppermute | solution.py:539

commit v8 on v7

--- a/solution.py
+++ b/solution.py
@@ -332,8 +332,8 @@
 
 
 def numer_first_kernel(k, shares, scal, hi_ref, lo_ref, w_ref, h_ref, mask, *refs):
-    parts, scales = refs[:shares], refs[shares : shares + ITERS]
-    u_out, tail_out, sums_out, out, acc, terms = refs[shares + ITERS :]
+    parts = refs[:shares]
+    u_out, tail_out, out, acc, terms = refs[shares:]
     rows = hi_ref.shape[0]
     ext, tile = mask.shape
     offs = offsets(scal, hi_ref.shape[2] // tile)
@@ -354,11 +354,12 @@
     first = jnp.bitwise_xor(scal[0], k) * per
     scaled_terms(h_ref, u_out, terms, first, per + pad)
     row_pieces(scal, offs, terms, hi_ref, lo_ref, u_out, [k], [out])
-    write_sums(sums_out, [*scales, u_out], rows)
-
-
-def numer_col_kernel(order, scal, hi_ref, lo_ref, w_ref, u_ref, after, *refs):
-    outs, acc = refs[:-1], refs[-1]
+
+
+def numer_col_kernel(order, scal, hi_ref, lo_ref, w_ref, *refs):
+    scales, refs = refs[: ITERS + 1], refs[ITERS + 1 :]
+    sums_out, outs, acc = refs[0], refs[1:-1], refs[-1]
+    u_ref = scales[-1]
     rows = hi_ref.shape[0]
     tile = u_ref.shape[1]
     offs = offsets(scal, hi_ref.shape[2] // tile)
@@ -373,6 +374,7 @@
             return carry
 
         lax.fori_loop(0, per, body, 0, unroll=4)
+    write_sums(sums_out, scales, rows)
 
 
 def write_sums(sums_out, scales, rows):
@@ -395,7 +397,7 @@
     row_pieces(scal, offs, terms, hi_ref, lo_ref, u_ref, order, outs)
 
 
-def numer_first(scal, r_hi, r_lo, row_factors, col_ext, mask_ext, parts, scales, k):
+def numer_first(scal, r_hi, r_lo, row_factors, col_ext, mask_ext, parts, k):
     shares = len(parts)
     rows, tile = r_hi.shape[:2]
     factors = row_factors.shape[0]
@@ -406,11 +408,10 @@
         functools.partial(numer_first_kernel, k, shares),
         "numer_first",
         scal,
-        [r_hi, r_lo, row_factors, col_ext, mask_ext, *parts, *scales],
+        [r_hi, r_lo, row_factors, col_ext, mask_ext, *parts],
         [
             jax.ShapeDtypeStruct((ext, tile), F32),
             jax.ShapeDtypeStruct((pad + 1, factors, tile), F32),
-            jax.ShapeDtypeStruct((8, tile), F32),
             jax.ShapeDtypeStruct((per, factors, tile), F32),
         ],
         [
@@ -420,18 +421,19 @@
     )
 
 
-def numer_col(scal, r_hi, r_lo, row_factors, u, after, order, shares):
+def numer_col(scal, r_hi, r_lo, row_factors, scales, order, shares):
     rows, tile = r_hi.shape[:2]
     factors = row_factors.shape[0]
     piece = jax.ShapeDtypeStruct((rows // shares, factors, tile), F32)
-    return kernel_call(
+    res = kernel_call(
         functools.partial(numer_col_kernel, order),
         "numer_col",
         scal,
-        [r_hi, r_lo, row_factors, u, after],
-        [piece] * len(order),
-        [pltpu.VMEM((u.shape[0], factors, tile), F32)],
-    )
+        [r_hi, r_lo, row_factors, *scales],
+        [jax.ShapeDtypeStruct((8, tile), F32)] + [piece] * len(order),
+        [pltpu.VMEM((scales[0].shape[0], factors, tile), F32)],
+    )
+    return res[0], res[1:]
 
 
 def numer_row(scal, r_hi, r_lo, col_ext, u, after, order, shares):
@@ -587,11 +589,6 @@
 
     counts = pltpu.with_memory_space_constraint(counts, pltpu.HBM)
     inner_v, kept = first_main(scal, counts, mask, rows + pad)
-    col_late, _ = lax.optimization_barrier((col_factors, inner_v))
-    ring_left = [(i, (i - 1) % genome_count) for i in range(genome_count)]
-    col_next = lax.ppermute(col_late[:, : pad * tile], "genome", ring_left)
-    col_next = jnp.where(has_next[:, :1] > 0, col_next, 1.0)
-    col_ext = jnp.concatenate([col_factors, col_next], axis=1)
 
     scales = []
     quarter = rows // (ITERS + 1)
@@ -606,22 +603,31 @@
         if t > 0:
             v = cover_main(scal, kept, u, v)
         else:
-            *ratios, v = ratio(scal, kept, row_factors, col_factors, v, [], 0, quarter)
+            *ratios, v = ratio(scal, kept, row_factors, col_factors, v, [], 0, 2 * quarter)
         front = v[:pad] + before[pad:] * has_prev
         back = v[rows:] + after[:pad] * has_next
         x = jnp.concatenate([front, v[pad:rows], back])
         others = {k: xor_exchange(x, "offset", k) for k in reversed(range(1, offset_count))}
         parts = [x, *others.values()]
-        start = (t + 1) * quarter
-        ratios = ratio(scal, kept, row_factors, col_ext, x, ratios, start, quarter)
+        if t == 0:
+            col_late, _ = lax.optimization_barrier((col_factors, x))
+            ring_left = [(i, (i - 1) % genome_count) for i in range(genome_count)]
+            col_next = lax.ppermute(col_late[:, : pad * tile], "genome", ring_left)
+            col_next = jnp.where(has_next[:, :1] > 0, col_next, 1.0)
+            col_ext = jnp.concatenate([col_factors, col_next], axis=1)
+        else:
+            columns = col_ext if t == ITERS - 1 else col_factors
+            start = (t + 1) * quarter
+            ratios = ratio(scal, kept, row_factors, columns, x, ratios, start, quarter)
 
     r_hi, r_lo = ratios
     per = rows // offset_count
-    u, tail, sums, early = numer_first(
-        scal, r_hi, r_lo, row_factors, col_ext, mask_ext, parts, scales, EARLY
-    )
+    u, tail, early = numer_first(
+        scal, r_hi, r_lo, row_factors, col_ext, mask_ext, parts, EARLY
+    )
+    scales.append(u)
     order = [EARLY, *(k for k in range(offset_count) if k != EARLY)]
-    pieces = numer_col(scal, r_hi, r_lo, row_factors, u, sums, order, offset_count)
+    sums, pieces = numer_col(scal, r_hi, r_lo, row_factors, scales, order, offset_count)
     h_parts = dict(zip(order, pieces))
 
     right = [(i, (i + 1) % genome_count) for i in range(genome_count)]

time: 95.1 us -> 96.6 us (1.016)
  waiting for transfers between devices: 13 us -> 14.3 us
    ppermute x15, waiting for transfers between devices: 11.9 us -> 14 us  [xor_exchange(): lax.ppermute(x, axis, [(i, i ^ k) for i in range(lax.axis_size(axis))])]
    ppermute x4, starting transfers between devices: 4.29 us -> 5.96 us  [both_sides(): lax.ppermute(x, 'genome', [(i, ((i + 1 ^ 1) - 1) % size) for i in range(s...]
    ppermute x1, starting transfers between devices: 2.6 us -> 1.44 us  [per_device(): col_next = lax.ppermute(col_late[:, :pad * tile], 'genome', ring_left)]
    pallas_call x17 -> x16, Pallas kernels: 37.9 us -> 37.3 us  [kernel_call(): pl.pallas_call(body, grid_spec=pltpu.PrefetchScalarGridSpec(num_scalar_pr...]
  transfers between devices with their start and end apart: 25 -> 25, of which waited for: 7 -> 10; matrix products, arithmetic and copies ran while one was open for 2% -> 2% of each run, Pallas kernels for 32% -> 31%
where the time goes in v8:
time: 96.6 us; the launch traced here: 96.4 us
  Pallas kernels  37.3 us (39%)
  starting transfers between devices  30.6 us (32%)
  waiting for transfers between devices  14.3 us (15%)
  blocking collectives  9.13 us (9%)
  other arithmetic  2.78 us (3%)
  between operations  1.61 us (2%)
    pallas_call x16, Pallas kernels, kernel_call(): pl.pallas_call(body, grid_spec=pltpu.PrefetchScalarGridSpec(num_scalar_pr...  37.3 us
    ppermute x15, starting transfers between devices, xor_exchange(): lax.ppermute(x, axis, [(i, i ^ k) for i in range(lax.axis_size(axis))])  21.7 us
    ppermute x15, waiting for transfers between devices, xor_exchange(): lax.ppermute(x, axis, [(i, i ^ k) for i in range(lax.axis_size(axis))])  14 us
    all_gather x1, blocking collectives, per_device(): sums = jnp.sum(lax.all_gather(sums, 'genome'), axis=0)  9.13 us
    ppermute x4, starting transfers between devices, both_sides(): lax.ppermute(x, 'genome', [(i, ((i + 1 ^ 1) - 1) % size) for i in range(s...  5.96 us
  transfers between devices with their start and end apart: 25, of which 10 were waited for; matrix products, arithmetic and copies ran while one was open for 2% of the time, Pallas kernels for 31%

profile of v8, /device:TPU:0, one launch (start us, length us, event | category | flops | bytes accessed | tf_op | source)
XLA Modules:
  0.0 96.4 jit_solution(3538974654285736004)
XLA Ops:
  0.9 0.7 pad_add_fusion.scal
  1.7 0.8 fusion.13
  2.4 0.5 collective-permute-start
  2.9 3.6 %collective-permute-start.1 = (f32[8,128]{1,0:T(8,128)S(1)}, f32[8,128]{1,0:T(8,128)S(1)}, u32[]{:S(2)}, u32[]{:S(2)}) collective-permute-start(f32[8,128]{1,0:T(8,128)S(1)} %slice_bitcast_fusion.1), channel_id=1, source_target_pairs={{0,28},{4,8},{8,4},{12,16},{16,12},{20,24},{24,20},{28,0},{1,29},{... | collective-permute-start | bytes 12296 | tf_op jit(solution)/shard_map/ppermute | solution.py:547
  6.5 4.8 %first_main.1 = (f32[72,128]{1,0:T(8,128)S(1)}, f32[64,2,128,128]{3,2,1,0:T(8,128)S(1)}) custom-call(s32[4]{0:T(128)S(1)} %pad_add_fusion.scal, s32[64,2,128,128]{3,2,1,0:T(8,128)} %hbm.1, f32[64,128]{1,0:T(8,128)S(1)} %get-tuple-element.136.mask), custom_call_target="tpu_custom_call" | custom-call | tf_op jit(solution)/shard_map/first_main/pallas_call | solution.py:47
  11.3 1.4 %first_edge.1 = (f32[72,128]{1,0:T(8,128)S(1)}, f32[16,128]{1,0:T(8,128)S(1)}) custom-call(s32[4]{0:T(128)S(1)} %pad_add_fusion.scal, f32[64,2,128,128]{3,2,1,0:T(8,128)S(1)} %get-tuple-element.90.kept, f32[72,128]{1,0:T(8,128)S(1)} %pad_maximum_fusion.1.u_ref.mask.refs_0_, f32[72,128]{1,0:T(8,128)S(1)} %get-tuple-element.92.inner_v), custom_call_target="tpu_custom_call" | custom-call | tf_op jit(solution)/shard_map/first_edge/pallas_call | solution.py:47
  12.9 3.6 %ratio.3 = (bf16[64,128,256]{2,1,0:T(8,128)(2,1)S(1)}, bf16[64,128,256]{2,1,0:T(8,128)(2,1)S(1)}, f32[72,128]{1,0:T(8,128)S(1)}) custom-call(s32[4]{0:T(128)S(1)} %pad_add_fusion.scal, f32[64,2,128,128]{3,2,1,0:T(8,128)S(1)} %get-tuple-element.90.kept, f32[32,8192]{1,0:T(8,128)S(1)} %copy-done, f32[32,8192]{1,0:T(8,128)S(1)} %copy-done.1, ...), custom_call_target="tpu_custom_call" | custom-call | tf_op jit(solution)/shard_map/ratio/pallas_call | solution.py:47
  16.8 3.9 %collective-permute-start.5 = (f32[72,128]{1,0:T(8,128)S(1)}, f32[72,128]{1,0:T(8,128)S(1)}, u32[]{:S(2)}, u32[]{:S(2)}) collective-permute-start(f32[72,128]{1,0:T(8,128)S(1)} %pad_maximum_fusion.2.refs_0_), channel_id=1, source_target_pairs={{0,3},{1,2},{2,1},{3,0},{4,7},{5,6},{6,5},{7,4},{8,11},{9,10},{10,... | collective-permute-start | bytes 110600 | tf_op jit(solution)/shard_map/ppermute | solution.py:541
  20.6 0.6 collective-permute-start.7
  21.3 1.4 %collective-permute-done.5.refs_1_ = f32[72,128]{1,0:T(8,128)S(1)} collective-permute-done((f32[72,128]{1,0:T(8,128)S(1)}, f32[72,128]{1,0:T(8,128)S(1)}, u32[]{:S(2)}, u32[]{:S(2)}) %collective-permute-start.5) | collective-permute-done | bytes 36896 | tf_op jit(solution)/shard_map/ppermute | solution.py:541
  22.7 2.8 %collective-permute-done.6.refs_2_ = f32[72,128]{1,0:T(8,128)S(1)} collective-permute-done((f32[72,128]{1,0:T(8,128)S(1)}, f32[72,128]{1,0:T(8,128)S(1)}, u32[]{:S(2)}, u32[]{:S(2)}) %collective-permute-start.6) | collective-permute-done | bytes 36896 | tf_op jit(solution)/shard_map/ppermute | solution.py:541
  25.5 1.4 %cover_edge.2 = (f32[72,128]{1,0:T(8,128)S(1)}, f32[16,128]{1,0:T(8,128)S(1)}, f32[72,128]{1,0:T(8,128)S(1)}) custom-call(s32[4]{0:T(128)S(1)} %pad_add_fusion.scal, f32[64,2,128,128]{3,2,1,0:T(8,128)S(1)} %get-tuple-element.90.kept, f32[72,128]{1,0:T(8,128)S(1)} %pad_maximum_fusion.1.u_ref.mask.refs_0_, f32[72,128]{1,0:T(8,128)S(1)} %pad_maximum_fusion.2.refs_0_, ...), custom_call_target="tpu_custom_call" | custom-call | tf_op jit(solution)/shard_map/cover_edge/pallas_call | solution.py:47
  26.9 1.5 %collective-permute-start.8 = (f32[16,128]{1,0:T(8,128)S(1)}, f32[16,128]{1,0:T(8,128)S(1)}, u32[]{:S(2)}, u32[]{:S(2)}) collective-permute-start(f32[16,128]{1,0:T(8,128)S(1)} %get-tuple-element.100), channel_id=1, source_target_pairs={{0,28},{4,8},{8,4},{12,16},{16,12},{20,24},{24,20},{28,0},{1,29},{... | collective-permute-start | bytes 24584 | tf_op jit(solution)/shard_map/ppermute | solution.py:547
  28.3 0.5 collective-permute-start.9
  28.9 2.8 %cover_main.2 = f32[72,128]{1,0:T(8,128)S(1)} custom-call(s32[4]{0:T(128)S(1)} %pad_add_fusion.scal, f32[64,2,128,128]{3,2,1,0:T(8,128)S(1)} %get-tuple-element.90.kept, f32[72,128]{1,0:T(8,128)S(1)} %get-tuple-element.98.u_ref.refs_1_, f32[72,128]{1,0:T(8,128)S(1)} %get-tuple-element.99.edge_v), custom_call_target="tpu_custom_call" | custom-call | tf_op jit(solution)/shard_map/cover_main/pallas_call | solution.py:47
  31.8 1.6 %collective-permute-start.10 = (f32[72,128]{1,0:T(8,128)S(1)}, f32[72,128]{1,0:T(8,128)S(1)}, u32[]{:S(2)}, u32[]{:S(2)}) collective-permute-start(f32[72,128]{1,0:T(8,128)S(1)} %pad_maximum_fusion.3.after.refs_0_), channel_id=1, source_target_pairs={{0,3},{1,2},{2,1},{3,0},{4,7},{5,6},{6,5},{7,4},{8,11},{9,10},{10,... | collective-permute-start | bytes 110600 | tf_op jit(solution)/shard_map/ppermute | solution.py:541
  33.4 0.6 collective-permute-start.11
  33.9 2.3 %collective-permute-start.12 = (f32[72,128]{1,0:T(8,128)S(1)}, f32[72,128]{1,0:T(8,128)S(1)}, u32[]{:S(2)}, u32[]{:S(2)}) collective-permute-start(f32[72,128]{1,0:T(8,128)S(1)} %pad_maximum_fusion.3.after.refs_0_), channel_id=1, source_target_pairs={{0,1},{1,0},{2,3},{3,2},{4,5},{5,4},{6,7},{7,6},{8,9},{9,8},{10,11... | collective-permute-start | bytes 110600 | tf_op jit(solution)/shard_map/ppermute | solution.py:541
  36.2 2.0 %ratio.4 = (bf16[64,128,256]{2,1,0:T(8,128)(2,1)S(1)}, bf16[64,128,256]{2,1,0:T(8,128)(2,1)S(1)}) custom-call(s32[4]{0:T(128)S(1)} %pad_add_fusion.scal, f32[64,2,128,128]{3,2,1,0:T(8,128)S(1)} %get-tuple-element.90.kept, f32[32,8192]{1,0:T(8,128)S(1)} %copy-done, f32[32,8192]{1,0:T(8,128)S(1)} %copy-done.1, ...), custom_call_target="tpu_custom_call", output_to_operand_aliasing={{0}: (5, {}), {1}: (6, {})} | custom-call | tf_op jit(solution)/shard_map/ratio/pallas_call | solution.py:47
  38.4 0.3 collective-permute-done.12.refs_3_
  38.7 1.4 %cover_edge.3 = (f32[72,128]{1,0:T(8,128)S(1)}, f32[16,128]{1,0:T(8,128)S(1)}, f32[72,128]{1,0:T(8,128)S(1)}) custom-call(s32[4]{0:T(128)S(1)} %pad_add_fusion.scal, f32[64,2,128,128]{3,2,1,0:T(8,128)S(1)} %get-tuple-element.90.kept, f32[72,128]{1,0:T(8,128)S(1)} %pad_maximum_fusion.1.u_ref.mask.refs_0_, f32[72,128]{1,0:T(8,128)S(1)} %pad_maximum_fusion.3.after.refs_0_, ...), custom_call_target="tpu_custom_call" | custom-call | tf_op jit(solution)/shard_map/cover_edge/pallas_call | solution.py:47
  40.1 0.9 collective-permute-start.13
  41.0 0.4 collective-permute-start.14
  41.4 0.5 slice.211
  42.6 1.4 %collective-permute-start.4 = (f32[32,1024]{1,0:T(8,128)S(1)}, f32[32,1024]{1,0:T(8,128)S(1)}, u32[]{:S(2)}, u32[]{:S(2)}) collective-permute-start(f32[32,1024]{1,0:T(8,128)S(1)} %slice.222), channel_id=1, source_target_pairs={{0,28},{4,0},{8,4},{12,8},{16,12},{20,16},{24,20},{28,24},{1,29},{... | collective-permute-start | bytes 393224 | tf_op jit(solution)/shard_map/ppermute | solution.py:615
  44.0 2.8 %cover_main.3 = f32[72,128]{1,0:T(8,128)S(1)} custom-call(s32[4]{0:T(128)S(1)} %pad_add_fusion.scal, f32[64,2,128,128]{3,2,1,0:T(8,128)S(1)} %get-tuple-element.90.kept, f32[72,128]{1,0:T(8,128)S(1)} %get-tuple-element.103.u_ref.refs_2_, f32[72,128]{1,0:T(8,128)S(1)} %get-tuple-element.104.edge_v), custom_call_target="tpu_custom_call" | custom-call | tf_op jit(solution)/shard_map/cover_main/pallas_call | solution.py:47
  46.9 2.5 %collective-permute-start.15 = (f32[72,128]{1,0:T(8,128)S(1)}, f32[72,128]{1,0:T(8,128)S(1)}, u32[]{:S(2)}, u32[]{:S(2)}) collective-permute-start(f32[72,128]{1,0:T(8,128)S(1)} %pad_maximum_fusion.4.after.refs_0_), channel_id=1, source_target_pairs={{0,3},{1,2},{2,1},{3,0},{4,7},{5,6},{6,5},{7,4},{8,11},{9,10},{10,... | collective-permute-start | bytes 110600 | tf_op jit(solution)/shard_map/ppermute | solution.py:541
  49.4 0.6 collective-permute-start.16
  49.9 1.4 %collective-permute-start.17 = (f32[72,128]{1,0:T(8,128)S(1)}, f32[72,128]{1,0:T(8,128)S(1)}, u32[]{:S(2)}, u32[]{:S(2)}) collective-permute-start(f32[72,128]{1,0:T(8,128)S(1)} %pad_maximum_fusion.4.after.refs_0_), channel_id=1, source_target_pairs={{0,1},{1,0},{2,3},{3,2},{4,5},{5,4},{6,7},{7,6},{8,9},{9,8},{10,11... | collective-permute-start | bytes 110600 | tf_op jit(solution)/shard_map/ppermute | solution.py:541
  51.4 2.0 %ratio.5 = (bf16[64,128,256]{2,1,0:T(8,128)(2,1)S(1)}, bf16[64,128,256]{2,1,0:T(8,128)(2,1)S(1)}) custom-call(s32[4]{0:T(128)S(1)} %pad_add_fusion.scal, f32[64,2,128,128]{3,2,1,0:T(8,128)S(1)} %get-tuple-element.90.kept, f32[32,8192]{1,0:T(8,128)S(1)} %copy-done, ...), custom_call_target="tpu_custom_call", output_to_operand_aliasing={{0}: (5, {}), {1}: (6, {})} | custom-call | tf_op jit(solution)/shard_map/ratio/pallas_call | solution.py:47
  53.4 0.8 collective-permute-done.16.refs_2_
  54.3 2.3 %numer_first.1 = (f32[72,128]{1,0:T(8,128)S(1)}, f32[9,32,128]{2,1,0:T(8,128)S(1)}, f32[16,32,128]{2,1,0:T(8,128)S(1)}) custom-call(s32[4]{0:T(128)S(1)} %pad_add_fusion.scal, bf16[64,128,256]{2,1,0:T(8,128)(2,1)S(1)} %get-tuple-element.107.hi_ref, bf16[64,128,256]{2,1,0:T(8,128)(2,1)S(1)} %get-tuple-element.108.lo_ref, f32[32,8192]{1,0:T(8,128)S(1)} %copy-done, ...), custom_call_target="tpu_custom_call" | custom-call | tf_op jit(solution)/shard_map/numer_first/pallas_call | solution.py:47
  56.6 1.1 %collective-permute-start.19 = (f32[16,32,128]{2,1,0:T(8,128)S(1)}, f32[16,32,128]{2,1,0:T(8,128)S(1)}, u32[]{:S(2)}, u32[]{:S(2)}) collective-permute-start(f32[16,32,128]{2,1,0:T(8,128)S(1)} %get-tuple-element.114), channel_id=1, source_target_pairs={{0,1},{1,0},{2,3},{3,2},{4,5},{5,4},{6,7},{7,6},{8,9},{9,8},{10,11... | collective-permute-start | bytes 786440 | tf_op jit(solution)/shard_map/ppermute | solution.py:541
  57.7 4.3 %numer_col.1 = (f32[8,128]{1,0:T(8,128)S(1)}, f32[16,32,128]{2,1,0:T(8,128)S(1)}, f32[16,32,128]{2,1,0:T(8,128)S(1)}, f32[16,32,128]{2,1,0:T(8,128)S(1)}, f32[16,32,128]{2,1,0:T(8,128)S(1)}) custom-call(s32[4]{0:T(128)S(1)} %pad_add_fusion.scal, bf16[64,128,256]{2,1,0:T(8,128)(2,1)S(1)} %get-tuple-element.107.hi_ref, ...), custom_call_target="tpu_custom_call" | custom-call | tf_op jit(solution)/shard_map/numer_col/pallas_call | solution.py:47
  62.2 1.1 %collective-permute-start.23 = (f32[16,32,128]{2,1,0:T(8,128)S(1)}, f32[16,32,128]{2,1,0:T(8,128)S(1)}, u32[]{:S(2)}, u32[]{:S(2)}) collective-permute-start(f32[16,32,128]{2,1,0:T(8,128)S(1)} %get-tuple-element.128.after), channel_id=1, source_target_pairs={{0,1},{1,0},{2,3},{3,2},{4,5},{5,4},{6,7},{7,6},{8,9},{9,8},{10,11... | collective-permute-start | bytes 786440 | tf_op jit(solution)/shard_map/ppermute | solution.py:541
  63.3 4.3 %numer_row.1 = (f32[16,32,128]{2,1,0:T(8,128)S(1)}, f32[16,32,128]{2,1,0:T(8,128)S(1)}, f32[16,32,128]{2,1,0:T(8,128)S(1)}) custom-call(s32[4]{0:T(128)S(1)} %pad_add_fusion.scal, bf16[64,128,256]{2,1,0:T(8,128)(2,1)S(1)} %get-tuple-element.107.hi_ref, bf16[64,128,256]{2,1,0:T(8,128)(2,1)S(1)} %get-tuple-element.108.lo_ref, ...), custom_call_target="tpu_custom_call" | custom-call | tf_op jit(solution)/shard_map/numer_row/pallas_call | solution.py:47
  67.6 2.5 %collective-permute-start.20 = (f32[16,32,128]{2,1,0:T(8,128)S(1)}, f32[16,32,128]{2,1,0:T(8,128)S(1)}, u32[]{:S(2)}, u32[]{:S(2)}) collective-permute-start(f32[16,32,128]{2,1,0:T(8,128)S(1)} %add.77), channel_id=1, source_target_pairs={{0,3},{1,2},{2,1},{3,0},{4,7},{5,6},{6,5},{7,4},{8,11},{9,10},{10,... | collective-permute-start | bytes 786440 | tf_op jit(solution)/shard_map/ppermute | solution.py:541
  70.1 0.7 coefficient.2
  71.0 0.9 coefficient.3
  71.9 2.0 %collective-permute-start.21 = (f32[16,32,128]{2,1,0:T(8,128)S(1)}, f32[16,32,128]{2,1,0:T(8,128)S(1)}, u32[]{:S(2)}, u32[]{:S(2)}) collective-permute-start(f32[16,32,128]{2,1,0:T(8,128)S(1)} %get-tuple-element.119), channel_id=1, source_target_pairs={{0,1},{1,0},{2,3},{3,2},{4,5},{5,4},{6,7},{7,6},{8,9},{9,8},{10,11... | collective-permute-start | bytes 786440 | tf_op jit(solution)/shard_map/ppermute | solution.py:541
  74.0 1.5 %collective-permute-start.24 = (f32[16,32,128]{2,1,0:T(8,128)S(1)}, f32[16,32,128]{2,1,0:T(8,128)S(1)}, u32[]{:S(2)}, u32[]{:S(2)}) collective-permute-start(f32[16,32,128]{2,1,0:T(8,128)S(1)} %add.81), channel_id=1, source_target_pairs={{0,3},{1,2},{2,1},{3,0},{4,7},{5,6},{6,5},{7,4},{8,11},{9,10},{10,... | collective-permute-start | bytes 786440 | tf_op jit(solution)/shard_map/ppermute | solution.py:541
  75.4 3.3 %collective-permute-done.20.refs_2_ = f32[16,32,128]{2,1,0:T(8,128)S(1)} collective-permute-done((f32[16,32,128]{2,1,0:T(8,128)S(1)}, f32[16,32,128]{2,1,0:T(8,128)S(1)}, u32[]{:S(2)}, u32[]{:S(2)}) %collective-permute-start.20) | collective-permute-done | bytes 262176 | tf_op jit(solution)/shard_map/ppermute | solution.py:541
  78.7 9.1 %all-gather = f32[64,128]{1,0:T(8,128)S(1)} all-gather(f32[8,128]{1,0:T(8,128)S(1)} %get-tuple-element.115), channel_id=2, replica_groups=mesh['genome'=8,'offset'=4] {'genome'}, dimensions={0}, use_global_device_ids=true | all-gather | bytes 36864 | tf_op jit(solution)/shard_map/all_gather | solution.py:654
  87.9 2.1 %collective-permute-done.21.refs_1_ = f32[16,32,128]{2,1,0:T(8,128)S(1)} collective-permute-done((f32[16,32,128]{2,1,0:T(8,128)S(1)}, f32[16,32,128]{2,1,0:T(8,128)S(1)}, u32[]{:S(2)}, u32[]{:S(2)}) %collective-permute-start.21) | collective-permute-done | bytes 262176 | tf_op jit(solution)/shard_map/ppermute | solution.py:541
  90.0 1.3 %update.2 = f32[32,2048]{1,0:T(8,128)} custom-call(s32[4]{0:T(128)S(1)} %pad_add_fusion.scal, f32[8,128]{1,0:T(8,128)S(1)} %bitcast_reduce_fusion.sums, f32[16,32,128]{2,1,0:T(8,128)S(1)} %get-tuple-element.116.times, f32[16,32,128]{2,1,0:T(8,128)S(1)} %get-tuple-element.117.plus, f32[16,32,128]{2,1,0:T(8,128)S(1)} %get-tuple-element.118.refs_0_, ...), custom_call_target="tpu_custom_call" | custom-call | tf_op jit(solution)/shard_map/update/pallas_call | solution.py:47
  91.3 0.6 multiply_bitcast_fusion
  91.9 3.1 %collective-permute-done.24.refs_2_ = f32[16,32,128]{2,1,0:T(8,128)S(1)} collective-permute-done((f32[16,32,128]{2,1,0:T(8,128)S(1)}, f32[16,32,128]{2,1,0:T(8,128)S(1)}, u32[]{:S(2)}, u32[]{:S(2)}) %collective-permute-start.24) | collective-permute-done | bytes 262176 | tf_op jit(solution)/shard_map/ppermute | solution.py:541
  95.0 1.3 %update.3 = f32[32,2048]{1,0:T(8,128)} custom-call(s32[4]{0:T(128)S(1)} %pad_add_fusion.scal, f32[8,128]{1,0:T(8,128)S(1)} %bitcast_reduce_fusion.sums, f32[16,32,128]{2,1,0:T(8,128)S(1)} %get-tuple-element.120.times, f32[16,32,128]{2,1,0:T(8,128)S(1)} %get-tuple-element.121.plus, f32[16,32,128]{2,1,0:T(8,128)S(1)} %get-tuple-element.126.refs_0_, ...), custom_call_target="tpu_custom_call" | custom-call | tf_op jit(solution)/shard_map/update/pallas_call | solution.py:47
  (57 shorter events, 1.5 us)
Async XLA Ops:
  2.4 8.8 %collective-permute-start = (f32[8,128]{1,0:T(8,128)S(1)}, f32[8,128]{1,0:T(8,128)S(1)}, u32[]{:S(2)}, u32[]{:S(2)}) collective-permute-start(f32[8,128]{1,0:T(8,128)S(1)} %slice_bitcast_fusion.1), channel_id=1, source_target_pairs={{0,4},{4,0},{8,12},{12,8},{16,20},{20,16},{24,28},{28,24},{1,5},{5... | collective-permute-start | bytes 12296 | tf_op jit(solution)/shard_map/ppermute | solution.py:546
  2.9 8.4 %collective-permute-start.1 = (f32[8,128]{1,0:T(8,128)S(1)}, f32[8,128]{1,0:T(8,128)S(1)}, u32[]{:S(2)}, u32[]{:S(2)}) collective-permute-start(f32[8,128]{1,0:T(8,128)S(1)} %slice_bitcast_fusion.1), channel_id=1, source_target_pairs={{0,28},{4,8},{8,4},{12,16},{16,12},{20,24},{24,20},{28,0},{1,29},{... | collective-permute-start | bytes 12296 | tf_op jit(solution)/shard_map/ppermute | solution.py:547
  11.3 1.5 %copy-start = (f32[32,8192]{1,0:T(8,128)S(1)}, f32[32,8192]{1,0:T(8,128)}, u32[]{:S(2)}) copy-start(f32[32,8192]{1,0:T(8,128)} %other.1) | copy-start | bytes 3145732
  11.3 1.5 %copy-start.1 = (f32[32,8192]{1,0:T(8,128)S(1)}, f32[32,8192]{1,0:T(8,128)}, u32[]{:S(2)}) copy-start(f32[32,8192]{1,0:T(8,128)} %old_ref.3) | copy-start | bytes 3145732
  12.7 4.0 %collective-permute-start.2 = (f32[16,128]{1,0:T(8,128)S(1)}, f32[16,128]{1,0:T(8,128)S(1)}, u32[]{:S(2)}, u32[]{:S(2)}) collective-permute-start(f32[16,128]{1,0:T(8,128)S(1)} %get-tuple-element.95), channel_id=1, source_target_pairs={{0,28},{4,8},{8,4},{12,16},{16,12},{20,24},{24,20},{28,0},{1,29},{... | collective-permute-start | bytes 24584 | tf_op jit(solution)/shard_map/ppermute | solution.py:547
  12.8 4.0 %collective-permute-start.3 = (f32[16,128]{1,0:T(8,128)S(1)}, f32[16,128]{1,0:T(8,128)S(1)}, u32[]{:S(2)}, u32[]{:S(2)}) collective-permute-start(f32[16,128]{1,0:T(8,128)S(1)} %get-tuple-element.95), channel_id=1, source_target_pairs={{0,4},{4,0},{8,12},{12,8},{16,20},{20,16},{24,28},{28,24},{1,5},{5... | collective-permute-start | bytes 24584 | tf_op jit(solution)/shard_map/ppermute | solution.py:546
  16.8 5.9 %collective-permute-start.5 = (f32[72,128]{1,0:T(8,128)S(1)}, f32[72,128]{1,0:T(8,128)S(1)}, u32[]{:S(2)}, u32[]{:S(2)}) collective-permute-start(f32[72,128]{1,0:T(8,128)S(1)} %pad_maximum_fusion.2.refs_0_), channel_id=1, source_target_pairs={{0,3},{1,2},{2,1},{3,0},{4,7},{5,6},{6,5},{7,4},{8,11},{9,10},{10,... | collective-permute-start | bytes 110600 | tf_op jit(solution)/shard_map/ppermute | solution.py:541
  20.6 4.9 %collective-permute-start.6 = (f32[72,128]{1,0:T(8,128)S(1)}, f32[72,128]{1,0:T(8,128)S(1)}, u32[]{:S(2)}, u32[]{:S(2)}) collective-permute-start(f32[72,128]{1,0:T(8,128)S(1)} %pad_maximum_fusion.2.refs_0_), channel_id=1, source_target_pairs={{0,2},{1,3},{2,0},{3,1},{4,6},{5,7},{6,4},{7,5},{8,10},{9,11},{10,... | collective-permute-start | bytes 110600 | tf_op jit(solution)/shard_map/ppermute | solution.py:541
  20.6 4.9 %collective-permute-start.7 = (f32[72,128]{1,0:T(8,128)S(1)}, f32[72,128]{1,0:T(8,128)S(1)}, u32[]{:S(2)}, u32[]{:S(2)}) collective-permute-start(f32[72,128]{1,0:T(8,128)S(1)} %pad_maximum_fusion.2.refs_0_), channel_id=1, source_target_pairs={{0,1},{1,0},{2,3},{3,2},{4,5},{5,4},{6,7},{7,6},{8,9},{9,8},{10,11... | collective-permute-start | bytes 110600 | tf_op jit(solution)/shard_map/ppermute | solution.py:541
  26.9 4.9 %collective-permute-start.8 = (f32[16,128]{1,0:T(8,128)S(1)}, f32[16,128]{1,0:T(8,128)S(1)}, u32[]{:S(2)}, u32[]{:S(2)}) collective-permute-start(f32[16,128]{1,0:T(8,128)S(1)} %get-tuple-element.100), channel_id=1, source_target_pairs={{0,28},{4,8},{8,4},{12,16},{16,12},{20,24},{24,20},{28,0},{1,29},{... | collective-permute-start | bytes 24584 | tf_op jit(solution)/shard_map/ppermute | solution.py:547
  28.3 3.4 %collective-permute-start.9 = (f32[16,128]{1,0:T(8,128)S(1)}, f32[16,128]{1,0:T(8,128)S(1)}, u32[]{:S(2)}, u32[]{:S(2)}) collective-permute-start(f32[16,128]{1,0:T(8,128)S(1)} %get-tuple-element.100), channel_id=1, source_target_pairs={{0,4},{4,0},{8,12},{12,8},{16,20},{20,16},{24,28},{28,24},{1,5},{5... | collective-permute-start | bytes 24584 | tf_op jit(solution)/shard_map/ppermute | solution.py:546
  31.8 6.4 %collective-permute-start.10 = (f32[72,128]{1,0:T(8,128)S(1)}, f32[72,128]{1,0:T(8,128)S(1)}, u32[]{:S(2)}, u32[]{:S(2)}) collective-permute-start(f32[72,128]{1,0:T(8,128)S(1)} %pad_maximum_fusion.3.after.refs_0_), channel_id=1, source_target_pairs={{0,3},{1,2},{2,1},{3,0},{4,7},{5,6},{6,5},{7,4},{8,11},{9,10},{10,... | collective-permute-start | bytes 110600 | tf_op jit(solution)/shard_map/ppermute | solution.py:541
  33.4 5.0 %collective-permute-start.11 = (f32[72,128]{1,0:T(8,128)S(1)}, f32[72,128]{1,0:T(8,128)S(1)}, u32[]{:S(2)}, u32[]{:S(2)}) collective-permute-start(f32[72,128]{1,0:T(8,128)S(1)} %pad_maximum_fusion.3.after.refs_0_), channel_id=1, source_target_pairs={{0,2},{1,3},{2,0},{3,1},{4,6},{5,7},{6,4},{7,5},{8,10},{9,11},{10,... | collective-permute-start | bytes 110600 | tf_op jit(solution)/shard_map/ppermute | solution.py:541
  33.9 4.7 %collective-permute-start.12 = (f32[72,128]{1,0:T(8,128)S(1)}, f32[72,128]{1,0:T(8,128)S(1)}, u32[]{:S(2)}, u32[]{:S(2)}) collective-permute-start(f32[72,128]{1,0:T(8,128)S(1)} %pad_maximum_fusion.3.after.refs_0_), channel_id=1, source_target_pairs={{0,1},{1,0},{2,3},{3,2},{4,5},{5,4},{6,7},{7,6},{8,9},{9,8},{10,11... | collective-permute-start | bytes 110600 | tf_op jit(solution)/shard_map/ppermute | solution.py:541
  40.1 6.8 %collective-permute-start.13 = (f32[16,128]{1,0:T(8,128)S(1)}, f32[16,128]{1,0:T(8,128)S(1)}, u32[]{:S(2)}, u32[]{:S(2)}) collective-permute-start(f32[16,128]{1,0:T(8,128)S(1)} %get-tuple-element.105), channel_id=1, source_target_pairs={{0,28},{4,8},{8,4},{12,16},{16,12},{20,24},{24,20},{28,0},{1,29},{... | collective-permute-start | bytes 24584 | tf_op jit(solution)/shard_map/ppermute | solution.py:547
  41.0 5.9 %collective-permute-start.14 = (f32[16,128]{1,0:T(8,128)S(1)}, f32[16,128]{1,0:T(8,128)S(1)}, u32[]{:S(2)}, u32[]{:S(2)}) collective-permute-start(f32[16,128]{1,0:T(8,128)S(1)} %get-tuple-element.105), channel_id=1, source_target_pairs={{0,4},{4,0},{8,12},{12,8},{16,20},{20,16},{24,28},{28,24},{1,5},{5... | collective-permute-start | bytes 24584 | tf_op jit(solution)/shard_map/ppermute | solution.py:546
  42.6 8.8 %collective-permute-start.4 = (f32[32,1024]{1,0:T(8,128)S(1)}, f32[32,1024]{1,0:T(8,128)S(1)}, u32[]{:S(2)}, u32[]{:S(2)}) collective-permute-start(f32[32,1024]{1,0:T(8,128)S(1)} %slice.222), channel_id=1, source_target_pairs={{0,28},{4,0},{8,4},{12,8},{16,12},{20,16},{24,20},{28,24},{1,29},{... | collective-permute-start | bytes 393224 | tf_op jit(solution)/shard_map/ppermute | solution.py:615
  46.9 6.6 %collective-permute-start.15 = (f32[72,128]{1,0:T(8,128)S(1)}, f32[72,128]{1,0:T(8,128)S(1)}, u32[]{:S(2)}, u32[]{:S(2)}) collective-permute-start(f32[72,128]{1,0:T(8,128)S(1)} %pad_maximum_fusion.4.after.refs_0_), channel_id=1, source_target_pairs={{0,3},{1,2},{2,1},{3,0},{4,7},{5,6},{6,5},{7,4},{8,11},{9,10},{10,... | collective-permute-start | bytes 110600 | tf_op jit(solution)/shard_map/ppermute | solution.py:541
  49.4 4.9 %collective-permute-start.16 = (f32[72,128]{1,0:T(8,128)S(1)}, f32[72,128]{1,0:T(8,128)S(1)}, u32[]{:S(2)}, u32[]{:S(2)}) collective-permute-start(f32[72,128]{1,0:T(8,128)S(1)} %pad_maximum_fusion.4.after.refs_0_), channel_id=1, source_target_pairs={{0,2},{1,3},{2,0},{3,1},{4,6},{5,7},{6,4},{7,5},{8,10},{9,11},{10,... | collective-permute-start | bytes 110600 | tf_op jit(solution)/shard_map/ppermute | solution.py:541
  49.9 4.4 %collective-permute-start.17 = (f32[72,128]{1,0:T(8,128)S(1)}, f32[72,128]{1,0:T(8,128)S(1)}, u32[]{:S(2)}, u32[]{:S(2)}) collective-permute-start(f32[72,128]{1,0:T(8,128)S(1)} %pad_maximum_fusion.4.after.refs_0_), channel_id=1, source_target_pairs={{0,1},{1,0},{2,3},{3,2},{4,5},{5,4},{6,7},{7,6},{8,9},{9,8},{10,11... | collective-permute-start | bytes 110600 | tf_op jit(solution)/shard_map/ppermute | solution.py:541
  56.6 5.5 %collective-permute-start.18 = (f32[9,32,128]{2,1,0:T(8,128)S(1)}, f32[9,32,128]{2,1,0:T(8,128)S(1)}, u32[]{:S(2)}, u32[]{:S(2)}) collective-permute-start(f32[9,32,128]{2,1,0:T(8,128)S(1)} %get-tuple-element.112), channel_id=1, source_target_pairs={{0,4},{4,8},{8,12},{12,16},{16,20},{20,24},{24,28},{28,0},{1,5},{5... | collective-permute-start | bytes 442376 | tf_op jit(solution)/shard_map/ppermute | solution.py:634
  56.6 10.9 %collective-permute-start.19 = (f32[16,32,128]{2,1,0:T(8,128)S(1)}, f32[16,32,128]{2,1,0:T(8,128)S(1)}, u32[]{:S(2)}, u32[]{:S(2)}) collective-permute-start(f32[16,32,128]{2,1,0:T(8,128)S(1)} %get-tuple-element.114), channel_id=1, source_target_pairs={{0,1},{1,0},{2,3},{3,2},{4,5},{5,4},{6,7},{7,6},{8,9},{9,8},{10,11... | collective-permute-start | bytes 786440 | tf_op jit(solution)/shard_map/ppermute | solution.py:541
  62.2 11.7 %collective-permute-start.23 = (f32[16,32,128]{2,1,0:T(8,128)S(1)}, f32[16,32,128]{2,1,0:T(8,128)S(1)}, u32[]{:S(2)}, u32[]{:S(2)}) collective-permute-start(f32[16,32,128]{2,1,0:T(8,128)S(1)} %get-tuple-element.128.after), channel_id=1, source_target_pairs={{0,1},{1,0},{2,3},{3,2},{4,5},{5,4},{6,7},{7,6},{8,9},{9,8},{10,11... | collective-permute-start | bytes 786440 | tf_op jit(solution)/shard_map/ppermute | solution.py:541
  67.6 11.1 %collective-permute-start.20 = (f32[16,32,128]{2,1,0:T(8,128)S(1)}, f32[16,32,128]{2,1,0:T(8,128)S(1)}, u32[]{:S(2)}, u32[]{:S(2)}) collective-permute-start(f32[16,32,128]{2,1,0:T(8,128)S(1)} %add.77), channel_id=1, source_target_pairs={{0,3},{1,2},{2,1},{3,0},{4,7},{5,6},{6,5},{7,4},{8,11},{9,10},{10,... | collective-permute-start | bytes 786440 | tf_op jit(solution)/shard_map/ppermute | solution.py:541
  70.8 21.1 %collective-permute-start.22 = (f32[16,32,128]{2,1,0:T(8,128)S(1)}, f32[16,32,128]{2,1,0:T(8,128)S(1)}, u32[]{:S(2)}, u32[]{:S(2)}) collective-permute-start(f32[16,32,128]{2,1,0:T(8,128)S(1)} %get-tuple-element.127), channel_id=1, source_target_pairs={{0,1},{1,0},{2,3},{3,2},{4,5},{5,4},{6,7},{7,6},{8,9},{9,8},{10,11... | collective-permute-start | bytes 786440 | tf_op jit(solution)/shard_map/ppermute | solution.py:541
  71.9 18.1 %collective-permute-start.21 = (f32[16,32,128]{2,1,0:T(8,128)S(1)}, f32[16,32,128]{2,1,0:T(8,128)S(1)}, u32[]{:S(2)}, u32[]{:S(2)}) collective-permute-start(f32[16,32,128]{2,1,0:T(8,128)S(1)} %get-tuple-element.119), channel_id=1, source_target_pairs={{0,1},{1,0},{2,3},{3,2},{4,5},{5,4},{6,7},{7,6},{8,9},{9,8},{10,11... | collective-permute-start | bytes 786440 | tf_op jit(solution)/shard_map/ppermute | solution.py:541
  74.0 21.1 %collective-permute-start.24 = (f32[16,32,128]{2,1,0:T(8,128)S(1)}, f32[16,32,128]{2,1,0:T(8,128)S(1)}, u32[]{:S(2)}, u32[]{:S(2)}) collective-permute-start(f32[16,32,128]{2,1,0:T(8,128)S(1)} %add.81), channel_id=1, source_target_pairs={{0,3},{1,2},{2,1},{3,0},{4,7},{5,6},{6,5},{7,4},{8,11},{9,10},{10,... | collective-permute-start | bytes 786440 | tf_op jit(solution)/shard_map/ppermute | solution.py:541

commit v9 on v8

--- a/solution.py
+++ b/solution.py
@@ -589,6 +589,10 @@
 
     counts = pltpu.with_memory_space_constraint(counts, pltpu.HBM)
     inner_v, kept = first_main(scal, counts, mask, rows + pad)
+    col_late, _ = lax.optimization_barrier((col_factors, inner_v))
+    ring_left = [(i, (i - 1) % genome_count) for i in range(genome_count)]
+    col_next = lax.ppermute(col_late[:, : pad * tile], "genome", ring_left)
+    col_ext = jnp.concatenate([col_factors, col_next], axis=1)
 
     scales = []
     quarter = rows // (ITERS + 1)
@@ -610,15 +614,9 @@
         others = {k: xor_exchange(x, "offset", k) for k in reversed(range(1, offset_count))}
         parts = [x, *others.values()]
         if t == 0:
-            col_late, _ = lax.optimization_barrier((col_factors, x))
-            ring_left = [(i, (i - 1) % genome_count) for i in range(genome_count)]
-            col_next = lax.ppermute(col_late[:, : pad * tile], "genome", ring_left)
-            col_next = jnp.where(has_next[:, :1] > 0, col_next, 1.0)
-            col_ext = jnp.concatenate([col_factors, col_next], axis=1)
-        else:
-            columns = col_ext if t == ITERS - 1 else col_factors
-            start = (t + 1) * quarter
-            ratios = ratio(scal, kept, row_factors, columns, x, ratios, start, quarter)
+            ratios = ratio(scal, kept, row_factors, col_factors, x, ratios, 2 * quarter, quarter)
+        elif t == ITERS - 1:
+            ratios = ratio(scal, kept, row_factors, col_ext, x, ratios, 3 * quarter, quarter)
 
     r_hi, r_lo = ratios
     per = rows // offset_count

time: 96.6 us -> 94 us (0.973)
  starting transfers between devices: 30.6 us -> 29 us
    ppermute x4, starting transfers between devices: 5.96 us -> 4.56 us  [both_sides(): lax.ppermute(x, 'genome', [(i, ((i + 1 ^ 1) - 1) % size) for i in range(s...]
    ppermute x1, starting transfers between devices: 1.44 us -> 0.25 us  [per_device(): col_next = lax.ppermute(col_late[:, :pad * tile], 'genome', ring_left)]
    ppermute x4, starting transfers between devices: 1.48 us -> 2.57 us  [both_sides(): a = lax.ppermute(x, 'genome', [(i, i ^ 1) for i in range(size)])]
  transfers between devices with their start and end apart: 25 -> 25, of which waited for: 10 -> 11; matrix products, arithmetic and copies ran while one was open for 2% -> 1% of each run, Pallas kernels for 31% -> 33%
where the time goes in v9:
time: 94 us; the launch traced here: 93.8 us
  Pallas kernels  37.4 us (40%)
  starting transfers between devices  29 us (31%)
  waiting for transfers between devices  13.9 us (15%)
  blocking collectives  9.68 us (10%)
  other arithmetic  2.7 us (3%)
  between operations  0.95 us (1%)
    pallas_call x16, Pallas kernels, kernel_call(): pl.pallas_call(body, grid_spec=pltpu.PrefetchScalarGridSpec(num_scalar_pr...  37.4 us
    ppermute x15, starting transfers between devices, xor_exchange(): lax.ppermute(x, axis, [(i, i ^ k) for i in range(lax.axis_size(axis))])  21.6 us
    ppermute x15, waiting for transfers between devices, xor_exchange(): lax.ppermute(x, axis, [(i, i ^ k) for i in range(lax.axis_size(axis))])  13.4 us
    all_gather x1, blocking collectives, per_device(): sums = jnp.sum(lax.all_gather(sums, 'genome'), axis=0)  9.68 us
    ppermute x4, starting transfers between devices, both_sides(): lax.ppermute(x, 'genome', [(i, ((i + 1 ^ 1) - 1) % size) for i in range(s...  4.56 us
    ppermute x4, starting transfers between devices, both_sides(): a = lax.ppermute(x, 'genome', [(i, i ^ 1) for i in range(size)])  2.57 us
  transfers between devices with their start and end apart: 25, of which 11 were waited for; matrix products, arithmetic and copies ran while one was open for 1% of the time, Pallas kernels for 33%

profile of v9, /device:TPU:0, one launch (start us, length us, event | category | flops | bytes accessed | tf_op | source)
XLA Modules:
  0.0 93.8 jit_solution(9416923254400652)
XLA Ops:
  0.9 0.7 pad_add_fusion.scal
  1.7 0.8 fusion.13
  2.4 0.5 collective-permute-start.1
  2.9 3.6 %collective-permute-start.2 = (f32[8,128]{1,0:T(8,128)S(1)}, f32[8,128]{1,0:T(8,128)S(1)}, u32[]{:S(2)}, u32[]{:S(2)}) collective-permute-start(f32[8,128]{1,0:T(8,128)S(1)} %slice_bitcast_fusion.1), channel_id=1, source_target_pairs={{0,28},{4,8},{8,4},{12,16},{16,12},{20,24},{24,20},{28,0},{1,29},{... | collective-permute-start | bytes 12296 | tf_op jit(solution)/shard_map/ppermute | solution.py:547
  6.5 4.8 %first_main.1 = (f32[72,128]{1,0:T(8,128)S(1)}, f32[64,2,128,128]{3,2,1,0:T(8,128)S(1)}) custom-call(s32[4]{0:T(128)S(1)} %pad_add_fusion.scal, s32[64,2,128,128]{3,2,1,0:T(8,128)} %hbm.1, f32[64,128]{1,0:T(8,128)S(1)} %get-tuple-element.136.mask), custom_call_target="tpu_custom_call" | custom-call | tf_op jit(solution)/shard_map/first_main/pallas_call | solution.py:47
  11.3 1.4 %first_edge.1 = (f32[72,128]{1,0:T(8,128)S(1)}, f32[16,128]{1,0:T(8,128)S(1)}) custom-call(s32[4]{0:T(128)S(1)} %pad_add_fusion.scal, f32[64,2,128,128]{3,2,1,0:T(8,128)S(1)} %get-tuple-element.90.kept, f32[72,128]{1,0:T(8,128)S(1)} %pad_maximum_fusion.u_ref.mask.refs_0_, f32[72,128]{1,0:T(8,128)S(1)} %get-tuple-element.91.inner_v), custom_call_target="tpu_custom_call" | custom-call | tf_op jit(solution)/shard_map/first_edge/pallas_call | solution.py:47
  12.9 3.4 %ratio.3 = (bf16[64,128,256]{2,1,0:T(8,128)(2,1)S(1)}, bf16[64,128,256]{2,1,0:T(8,128)(2,1)S(1)}, f32[72,128]{1,0:T(8,128)S(1)}) custom-call(s32[4]{0:T(128)S(1)} %pad_add_fusion.scal, f32[64,2,128,128]{3,2,1,0:T(8,128)S(1)} %get-tuple-element.90.kept, f32[32,8192]{1,0:T(8,128)S(1)} %copy-done, f32[32,8192]{1,0:T(8,128)S(1)} %copy-done.1, ...), custom_call_target="tpu_custom_call" | custom-call | tf_op jit(solution)/shard_map/ratio/pallas_call | solution.py:47
  16.3 0.4 collective-permute-done.3
  16.8 3.7 %collective-permute-start.5 = (f32[72,128]{1,0:T(8,128)S(1)}, f32[72,128]{1,0:T(8,128)S(1)}, u32[]{:S(2)}, u32[]{:S(2)}) collective-permute-start(f32[72,128]{1,0:T(8,128)S(1)} %pad_maximum_fusion.1.after.refs_0_), channel_id=1, source_target_pairs={{0,3},{1,2},{2,1},{3,0},{4,7},{5,6},{6,5},{7,4},{8,11},{9,10},{10,... | collective-permute-start | bytes 110600 | tf_op jit(solution)/shard_map/ppermute | solution.py:541
  20.4 0.8 collective-permute-start.7
  21.2 2.2 %ratio.4 = (bf16[64,128,256]{2,1,0:T(8,128)(2,1)S(1)}, bf16[64,128,256]{2,1,0:T(8,128)(2,1)S(1)}) custom-call(s32[4]{0:T(128)S(1)} %pad_add_fusion.scal, f32[64,2,128,128]{3,2,1,0:T(8,128)S(1)} %get-tuple-element.90.kept, f32[32,8192]{1,0:T(8,128)S(1)} %copy-done, f32[32,8192]{1,0:T(8,128)S(1)} %copy-done.1, ...), custom_call_target="tpu_custom_call", output_to_operand_aliasing={{0}: (5, {}), {1}: (6, {})} | custom-call | tf_op jit(solution)/shard_map/ratio/pallas_call | solution.py:47
  23.4 1.9 %collective-permute-done.6.refs_2_ = f32[72,128]{1,0:T(8,128)S(1)} collective-permute-done((f32[72,128]{1,0:T(8,128)S(1)}, f32[72,128]{1,0:T(8,128)S(1)}, u32[]{:S(2)}, u32[]{:S(2)}) %collective-permute-start.6) | collective-permute-done | bytes 36896 | tf_op jit(solution)/shard_map/ppermute | solution.py:541
  25.3 1.4 %cover_edge.2 = (f32[72,128]{1,0:T(8,128)S(1)}, f32[16,128]{1,0:T(8,128)S(1)}, f32[72,128]{1,0:T(8,128)S(1)}) custom-call(s32[4]{0:T(128)S(1)} %pad_add_fusion.scal, f32[64,2,128,128]{3,2,1,0:T(8,128)S(1)} %get-tuple-element.90.kept, f32[72,128]{1,0:T(8,128)S(1)} %pad_maximum_fusion.u_ref.mask.refs_0_, f32[72,128]{1,0:T(8,128)S(1)} %pad_maximum_fusion.1.after.refs_0_, ...), custom_call_target="tpu_custom_call" | custom-call | tf_op jit(solution)/shard_map/cover_edge/pallas_call | solution.py:47
  26.7 0.7 collective-permute-start.8
  27.4 1.0 %collective-permute-start.9 = (f32[16,128]{1,0:T(8,128)S(1)}, f32[16,128]{1,0:T(8,128)S(1)}, u32[]{:S(2)}, u32[]{:S(2)}) collective-permute-start(f32[16,128]{1,0:T(8,128)S(1)} %get-tuple-element.102), channel_id=1, source_target_pairs={{0,4},{4,0},{8,12},{12,8},{16,20},{20,16},{24,28},{28,24},{1,5},{5... | collective-permute-start | bytes 24584 | tf_op jit(solution)/shard_map/ppermute | solution.py:546
  28.4 2.8 %cover_main.2 = f32[72,128]{1,0:T(8,128)S(1)} custom-call(s32[4]{0:T(128)S(1)} %pad_add_fusion.scal, f32[64,2,128,128]{3,2,1,0:T(8,128)S(1)} %get-tuple-element.90.kept, f32[72,128]{1,0:T(8,128)S(1)} %get-tuple-element.100.u_ref.refs_1_, f32[72,128]{1,0:T(8,128)S(1)} %get-tuple-element.101.edge_v), custom_call_target="tpu_custom_call" | custom-call | tf_op jit(solution)/shard_map/cover_main/pallas_call | solution.py:47
  31.3 1.8 %collective-permute-start.10 = (f32[72,128]{1,0:T(8,128)S(1)}, f32[72,128]{1,0:T(8,128)S(1)}, u32[]{:S(2)}, u32[]{:S(2)}) collective-permute-start(f32[72,128]{1,0:T(8,128)S(1)} %pad_maximum_fusion.2.refs_0_), channel_id=1, source_target_pairs={{0,3},{1,2},{2,1},{3,0},{4,7},{5,6},{6,5},{7,4},{8,11},{9,10},{10,... | collective-permute-start | bytes 110600 | tf_op jit(solution)/shard_map/ppermute | solution.py:541
  33.1 0.4 collective-permute-start.11
  33.5 2.3 %collective-permute-start.12 = (f32[72,128]{1,0:T(8,128)S(1)}, f32[72,128]{1,0:T(8,128)S(1)}, u32[]{:S(2)}, u32[]{:S(2)}) collective-permute-start(f32[72,128]{1,0:T(8,128)S(1)} %pad_maximum_fusion.2.refs_0_), channel_id=1, source_target_pairs={{0,1},{1,0},{2,3},{3,2},{4,5},{5,4},{6,7},{7,6},{8,9},{9,8},{10,11... | collective-permute-start | bytes 110600 | tf_op jit(solution)/shard_map/ppermute | solution.py:541
  35.8 0.3 collective-permute-start
  36.0 1.5 %collective-permute-done.10.refs_1_ = f32[72,128]{1,0:T(8,128)S(1)} collective-permute-done((f32[72,128]{1,0:T(8,128)S(1)}, f32[72,128]{1,0:T(8,128)S(1)}, u32[]{:S(2)}, u32[]{:S(2)}) %collective-permute-start.10) | collective-permute-done | bytes 36896 | tf_op jit(solution)/shard_map/ppermute | solution.py:541
  37.5 0.7 collective-permute-done.11.refs_2_
  38.4 1.4 %cover_edge.3 = (f32[72,128]{1,0:T(8,128)S(1)}, f32[16,128]{1,0:T(8,128)S(1)}, f32[72,128]{1,0:T(8,128)S(1)}) custom-call(s32[4]{0:T(128)S(1)} %pad_add_fusion.scal, f32[64,2,128,128]{3,2,1,0:T(8,128)S(1)} %get-tuple-element.90.kept, f32[72,128]{1,0:T(8,128)S(1)} %pad_maximum_fusion.u_ref.mask.refs_0_, f32[72,128]{1,0:T(8,128)S(1)} %pad_maximum_fusion.2.refs_0_, ...), custom_call_target="tpu_custom_call" | custom-call | tf_op jit(solution)/shard_map/cover_edge/pallas_call | solution.py:47
  39.8 0.2 collective-permute-start.13
  40.0 1.1 %collective-permute-start.14 = (f32[16,128]{1,0:T(8,128)S(1)}, f32[16,128]{1,0:T(8,128)S(1)}, u32[]{:S(2)}, u32[]{:S(2)}) collective-permute-start(f32[16,128]{1,0:T(8,128)S(1)} %get-tuple-element.105), channel_id=1, source_target_pairs={{0,4},{4,0},{8,12},{12,8},{16,20},{20,16},{24,28},{28,24},{1,5},{5... | collective-permute-start | bytes 24584 | tf_op jit(solution)/shard_map/ppermute | solution.py:546
  41.1 2.8 %cover_main.3 = f32[72,128]{1,0:T(8,128)S(1)} custom-call(s32[4]{0:T(128)S(1)} %pad_add_fusion.scal, f32[64,2,128,128]{3,2,1,0:T(8,128)S(1)} %get-tuple-element.90.kept, f32[72,128]{1,0:T(8,128)S(1)} %get-tuple-element.103.u_ref.refs_2_, f32[72,128]{1,0:T(8,128)S(1)} %get-tuple-element.104.edge_v), custom_call_target="tpu_custom_call" | custom-call | tf_op jit(solution)/shard_map/cover_main/pallas_call | solution.py:47
  44.0 2.4 %collective-permute-start.15 = (f32[72,128]{1,0:T(8,128)S(1)}, f32[72,128]{1,0:T(8,128)S(1)}, u32[]{:S(2)}, u32[]{:S(2)}) collective-permute-start(f32[72,128]{1,0:T(8,128)S(1)} %pad_maximum_fusion.3.after.refs_0_), channel_id=1, source_target_pairs={{0,3},{1,2},{2,1},{3,0},{4,7},{5,6},{6,5},{7,4},{8,11},{9,10},{10,... | collective-permute-start | bytes 110600 | tf_op jit(solution)/shard_map/ppermute | solution.py:541
  46.4 0.5 collective-permute-start.16
  46.9 1.6 %collective-permute-start.17 = (f32[72,128]{1,0:T(8,128)S(1)}, f32[72,128]{1,0:T(8,128)S(1)}, u32[]{:S(2)}, u32[]{:S(2)}) collective-permute-start(f32[72,128]{1,0:T(8,128)S(1)} %pad_maximum_fusion.3.after.refs_0_), channel_id=1, source_target_pairs={{0,1},{1,0},{2,3},{3,2},{4,5},{5,4},{6,7},{7,6},{8,9},{9,8},{10,11... | collective-permute-start | bytes 110600 | tf_op jit(solution)/shard_map/ppermute | solution.py:541
  48.5 2.0 %ratio.5 = (bf16[64,128,256]{2,1,0:T(8,128)(2,1)S(1)}, bf16[64,128,256]{2,1,0:T(8,128)(2,1)S(1)}) custom-call(s32[4]{0:T(128)S(1)} %pad_add_fusion.scal, f32[64,2,128,128]{3,2,1,0:T(8,128)S(1)} %get-tuple-element.90.kept, f32[32,8192]{1,0:T(8,128)S(1)} %copy-done, ...), custom_call_target="tpu_custom_call", output_to_operand_aliasing={{0}: (5, {}), {1}: (6, {})} | custom-call | tf_op jit(solution)/shard_map/ratio/pallas_call | solution.py:47
  50.5 0.8 collective-permute-done.16.refs_2_
  51.4 2.3 %numer_first.1 = (f32[72,128]{1,0:T(8,128)S(1)}, f32[9,32,128]{2,1,0:T(8,128)S(1)}, f32[16,32,128]{2,1,0:T(8,128)S(1)}) custom-call(s32[4]{0:T(128)S(1)} %pad_add_fusion.scal, bf16[64,128,256]{2,1,0:T(8,128)(2,1)S(1)} %get-tuple-element.107.hi_ref, bf16[64,128,256]{2,1,0:T(8,128)(2,1)S(1)} %get-tuple-element.108.lo_ref, f32[32,8192]{1,0:T(8,128)S(1)} %copy-done, ...), custom_call_target="tpu_custom_call" | custom-call | tf_op jit(solution)/shard_map/numer_first/pallas_call | solution.py:47
  53.8 1.1 %collective-permute-start.19 = (f32[16,32,128]{2,1,0:T(8,128)S(1)}, f32[16,32,128]{2,1,0:T(8,128)S(1)}, u32[]{:S(2)}, u32[]{:S(2)}) collective-permute-start(f32[16,32,128]{2,1,0:T(8,128)S(1)} %get-tuple-element.114), channel_id=1, source_target_pairs={{0,1},{1,0},{2,3},{3,2},{4,5},{5,4},{6,7},{7,6},{8,9},{9,8},{10,11... | collective-permute-start | bytes 786440 | tf_op jit(solution)/shard_map/ppermute | solution.py:541
  54.9 4.3 %numer_col.1 = (f32[8,128]{1,0:T(8,128)S(1)}, f32[16,32,128]{2,1,0:T(8,128)S(1)}, f32[16,32,128]{2,1,0:T(8,128)S(1)}, f32[16,32,128]{2,1,0:T(8,128)S(1)}, f32[16,32,128]{2,1,0:T(8,128)S(1)}) custom-call(s32[4]{0:T(128)S(1)} %pad_add_fusion.scal, bf16[64,128,256]{2,1,0:T(8,128)(2,1)S(1)} %get-tuple-element.107.hi_ref, ...), custom_call_target="tpu_custom_call" | custom-call | tf_op jit(solution)/shard_map/numer_col/pallas_call | solution.py:47
  59.4 1.1 %collective-permute-start.23 = (f32[16,32,128]{2,1,0:T(8,128)S(1)}, f32[16,32,128]{2,1,0:T(8,128)S(1)}, u32[]{:S(2)}, u32[]{:S(2)}) collective-permute-start(f32[16,32,128]{2,1,0:T(8,128)S(1)} %get-tuple-element.128.after), channel_id=1, source_target_pairs={{0,1},{1,0},{2,3},{3,2},{4,5},{5,4},{6,7},{7,6},{8,9},{9,8},{10,11... | collective-permute-start | bytes 786440 | tf_op jit(solution)/shard_map/ppermute | solution.py:541
  60.4 4.3 %numer_row.1 = (f32[16,32,128]{2,1,0:T(8,128)S(1)}, f32[16,32,128]{2,1,0:T(8,128)S(1)}, f32[16,32,128]{2,1,0:T(8,128)S(1)}) custom-call(s32[4]{0:T(128)S(1)} %pad_add_fusion.scal, bf16[64,128,256]{2,1,0:T(8,128)(2,1)S(1)} %get-tuple-element.107.hi_ref, bf16[64,128,256]{2,1,0:T(8,128)(2,1)S(1)} %get-tuple-element.108.lo_ref, ...), custom_call_target="tpu_custom_call" | custom-call | tf_op jit(solution)/shard_map/numer_row/pallas_call | solution.py:47
  64.8 2.4 %collective-permute-start.20 = (f32[16,32,128]{2,1,0:T(8,128)S(1)}, f32[16,32,128]{2,1,0:T(8,128)S(1)}, u32[]{:S(2)}, u32[]{:S(2)}) collective-permute-start(f32[16,32,128]{2,1,0:T(8,128)S(1)} %add.77), channel_id=1, source_target_pairs={{0,3},{1,2},{2,1},{3,0},{4,7},{5,6},{6,5},{7,4},{8,11},{9,10},{10,... | collective-permute-start | bytes 786440 | tf_op jit(solution)/shard_map/ppermute | solution.py:541
  67.1 0.7 coefficient.2
  68.0 0.9 coefficient.3
  68.9 2.0 %collective-permute-start.21 = (f32[16,32,128]{2,1,0:T(8,128)S(1)}, f32[16,32,128]{2,1,0:T(8,128)S(1)}, u32[]{:S(2)}, u32[]{:S(2)}) collective-permute-start(f32[16,32,128]{2,1,0:T(8,128)S(1)} %get-tuple-element.119), channel_id=1, source_target_pairs={{0,1},{1,0},{2,3},{3,2},{4,5},{5,4},{6,7},{7,6},{8,9},{9,8},{10,11... | collective-permute-start | bytes 786440 | tf_op jit(solution)/shard_map/ppermute | solution.py:541
  71.0 1.6 %collective-permute-start.24 = (f32[16,32,128]{2,1,0:T(8,128)S(1)}, f32[16,32,128]{2,1,0:T(8,128)S(1)}, u32[]{:S(2)}, u32[]{:S(2)}) collective-permute-start(f32[16,32,128]{2,1,0:T(8,128)S(1)} %add.81), channel_id=1, source_target_pairs={{0,3},{1,2},{2,1},{3,0},{4,7},{5,6},{6,5},{7,4},{8,11},{9,10},{10,... | collective-permute-start | bytes 786440 | tf_op jit(solution)/shard_map/ppermute | solution.py:541
  72.6 3.1 %collective-permute-done.20.refs_2_ = f32[16,32,128]{2,1,0:T(8,128)S(1)} collective-permute-done((f32[16,32,128]{2,1,0:T(8,128)S(1)}, f32[16,32,128]{2,1,0:T(8,128)S(1)}, u32[]{:S(2)}, u32[]{:S(2)}) %collective-permute-start.20) | collective-permute-done | bytes 262176 | tf_op jit(solution)/shard_map/ppermute | solution.py:541
  75.7 9.7 %all-gather = f32[64,128]{1,0:T(8,128)S(1)} all-gather(f32[8,128]{1,0:T(8,128)S(1)} %get-tuple-element.115), channel_id=2, replica_groups=mesh['genome'=8,'offset'=4] {'genome'}, dimensions={0}, use_global_device_ids=true | all-gather | bytes 36864 | tf_op jit(solution)/shard_map/all_gather | solution.py:652
  85.4 2.1 %collective-permute-done.21.refs_1_ = f32[16,32,128]{2,1,0:T(8,128)S(1)} collective-permute-done((f32[16,32,128]{2,1,0:T(8,128)S(1)}, f32[16,32,128]{2,1,0:T(8,128)S(1)}, u32[]{:S(2)}, u32[]{:S(2)}) %collective-permute-start.21) | collective-permute-done | bytes 262176 | tf_op jit(solution)/shard_map/ppermute | solution.py:541
  87.5 1.3 %update.2 = f32[32,2048]{1,0:T(8,128)} custom-call(s32[4]{0:T(128)S(1)} %pad_add_fusion.scal, f32[8,128]{1,0:T(8,128)S(1)} %bitcast_reduce_fusion.sums, f32[16,32,128]{2,1,0:T(8,128)S(1)} %get-tuple-element.116.times, f32[16,32,128]{2,1,0:T(8,128)S(1)} %get-tuple-element.117.plus, f32[16,32,128]{2,1,0:T(8,128)S(1)} %get-tuple-element.118.refs_0_, ...), custom_call_target="tpu_custom_call" | custom-call | tf_op jit(solution)/shard_map/update/pallas_call | solution.py:47
  88.8 0.6 multiply_bitcast_fusion
  89.4 3.0 %collective-permute-done.24.refs_2_ = f32[16,32,128]{2,1,0:T(8,128)S(1)} collective-permute-done((f32[16,32,128]{2,1,0:T(8,128)S(1)}, f32[16,32,128]{2,1,0:T(8,128)S(1)}, u32[]{:S(2)}, u32[]{:S(2)}) %collective-permute-start.24) | collective-permute-done | bytes 262176 | tf_op jit(solution)/shard_map/ppermute | solution.py:541
  92.4 1.3 %update.3 = f32[32,2048]{1,0:T(8,128)} custom-call(s32[4]{0:T(128)S(1)} %pad_add_fusion.scal, f32[8,128]{1,0:T(8,128)S(1)} %bitcast_reduce_fusion.sums, f32[16,32,128]{2,1,0:T(8,128)S(1)} %get-tuple-element.120.times, f32[16,32,128]{2,1,0:T(8,128)S(1)} %get-tuple-element.121.plus, f32[16,32,128]{2,1,0:T(8,128)S(1)} %get-tuple-element.126.refs_0_, ...), custom_call_target="tpu_custom_call" | custom-call | tf_op jit(solution)/shard_map/update/pallas_call | solution.py:47
  (56 shorter events, 1.5 us)
Async XLA Ops:
  2.4 8.8 %collective-permute-start.1 = (f32[8,128]{1,0:T(8,128)S(1)}, f32[8,128]{1,0:T(8,128)S(1)}, u32[]{:S(2)}, u32[]{:S(2)}) collective-permute-start(f32[8,128]{1,0:T(8,128)S(1)} %slice_bitcast_fusion.1), channel_id=1, source_target_pairs={{0,4},{4,0},{8,12},{12,8},{16,20},{20,16},{24,28},{28,24},{1,5},{5... | collective-permute-start | bytes 12296 | tf_op jit(solution)/shard_map/ppermute | solution.py:546
  2.9 8.4 %collective-permute-start.2 = (f32[8,128]{1,0:T(8,128)S(1)}, f32[8,128]{1,0:T(8,128)S(1)}, u32[]{:S(2)}, u32[]{:S(2)}) collective-permute-start(f32[8,128]{1,0:T(8,128)S(1)} %slice_bitcast_fusion.1), channel_id=1, source_target_pairs={{0,28},{4,8},{8,4},{12,16},{16,12},{20,24},{24,20},{28,0},{1,29},{... | collective-permute-start | bytes 12296 | tf_op jit(solution)/shard_map/ppermute | solution.py:547
  11.3 1.5 %copy-start = (f32[32,8192]{1,0:T(8,128)S(1)}, f32[32,8192]{1,0:T(8,128)}, u32[]{:S(2)}) copy-start(f32[32,8192]{1,0:T(8,128)} %other.1) | copy-start | bytes 3145732
  11.3 1.5 %copy-start.1 = (f32[32,8192]{1,0:T(8,128)S(1)}, f32[32,8192]{1,0:T(8,128)}, u32[]{:S(2)}) copy-start(f32[32,8192]{1,0:T(8,128)} %old_ref.3) | copy-start | bytes 3145732
  12.7 4.0 %collective-permute-start.3 = (f32[16,128]{1,0:T(8,128)S(1)}, f32[16,128]{1,0:T(8,128)S(1)}, u32[]{:S(2)}, u32[]{:S(2)}) collective-permute-start(f32[16,128]{1,0:T(8,128)S(1)} %get-tuple-element.96), channel_id=1, source_target_pairs={{0,28},{4,8},{8,4},{12,16},{16,12},{20,24},{24,20},{28,0},{1,29},{... | collective-permute-start | bytes 24584 | tf_op jit(solution)/shard_map/ppermute | solution.py:547
  12.8 4.0 %collective-permute-start.4 = (f32[16,128]{1,0:T(8,128)S(1)}, f32[16,128]{1,0:T(8,128)S(1)}, u32[]{:S(2)}, u32[]{:S(2)}) collective-permute-start(f32[16,128]{1,0:T(8,128)S(1)} %get-tuple-element.96), channel_id=1, source_target_pairs={{0,4},{4,0},{8,12},{12,8},{16,20},{20,16},{24,28},{28,24},{1,5},{5... | collective-permute-start | bytes 24584 | tf_op jit(solution)/shard_map/ppermute | solution.py:546
  16.8 6.6 %collective-permute-start.5 = (f32[72,128]{1,0:T(8,128)S(1)}, f32[72,128]{1,0:T(8,128)S(1)}, u32[]{:S(2)}, u32[]{:S(2)}) collective-permute-start(f32[72,128]{1,0:T(8,128)S(1)} %pad_maximum_fusion.1.after.refs_0_), channel_id=1, source_target_pairs={{0,3},{1,2},{2,1},{3,0},{4,7},{5,6},{6,5},{7,4},{8,11},{9,10},{10,... | collective-permute-start | bytes 110600 | tf_op jit(solution)/shard_map/ppermute | solution.py:541
  20.4 4.9 %collective-permute-start.6 = (f32[72,128]{1,0:T(8,128)S(1)}, f32[72,128]{1,0:T(8,128)S(1)}, u32[]{:S(2)}, u32[]{:S(2)}) collective-permute-start(f32[72,128]{1,0:T(8,128)S(1)} %pad_maximum_fusion.1.after.refs_0_), channel_id=1, source_target_pairs={{0,2},{1,3},{2,0},{3,1},{4,6},{5,7},{6,4},{7,5},{8,10},{9,11},{10,... | collective-permute-start | bytes 110600 | tf_op jit(solution)/shard_map/ppermute | solution.py:541
  20.4 4.9 %collective-permute-start.7 = (f32[72,128]{1,0:T(8,128)S(1)}, f32[72,128]{1,0:T(8,128)S(1)}, u32[]{:S(2)}, u32[]{:S(2)}) collective-permute-start(f32[72,128]{1,0:T(8,128)S(1)} %pad_maximum_fusion.1.after.refs_0_), channel_id=1, source_target_pairs={{0,1},{1,0},{2,3},{3,2},{4,5},{5,4},{6,7},{7,6},{8,9},{9,8},{10,11... | collective-permute-start | bytes 110600 | tf_op jit(solution)/shard_map/ppermute | solution.py:541
  26.7 4.6 %collective-permute-start.8 = (f32[16,128]{1,0:T(8,128)S(1)}, f32[16,128]{1,0:T(8,128)S(1)}, u32[]{:S(2)}, u32[]{:S(2)}) collective-permute-start(f32[16,128]{1,0:T(8,128)S(1)} %get-tuple-element.102), channel_id=1, source_target_pairs={{0,28},{4,8},{8,4},{12,16},{16,12},{20,24},{24,20},{28,0},{1,29},{... | collective-permute-start | bytes 24584 | tf_op jit(solution)/shard_map/ppermute | solution.py:547
  27.4 3.8 %collective-permute-start.9 = (f32[16,128]{1,0:T(8,128)S(1)}, f32[16,128]{1,0:T(8,128)S(1)}, u32[]{:S(2)}, u32[]{:S(2)}) collective-permute-start(f32[16,128]{1,0:T(8,128)S(1)} %get-tuple-element.102), channel_id=1, source_target_pairs={{0,4},{4,0},{8,12},{12,8},{16,20},{20,16},{24,28},{28,24},{1,5},{5... | collective-permute-start | bytes 24584 | tf_op jit(solution)/shard_map/ppermute | solution.py:546
  31.3 6.2 %collective-permute-start.10 = (f32[72,128]{1,0:T(8,128)S(1)}, f32[72,128]{1,0:T(8,128)S(1)}, u32[]{:S(2)}, u32[]{:S(2)}) collective-permute-start(f32[72,128]{1,0:T(8,128)S(1)} %pad_maximum_fusion.2.refs_0_), channel_id=1, source_target_pairs={{0,3},{1,2},{2,1},{3,0},{4,7},{5,6},{6,5},{7,4},{8,11},{9,10},{10,... | collective-permute-start | bytes 110600 | tf_op jit(solution)/shard_map/ppermute | solution.py:541
  33.1 5.1 %collective-permute-start.11 = (f32[72,128]{1,0:T(8,128)S(1)}, f32[72,128]{1,0:T(8,128)S(1)}, u32[]{:S(2)}, u32[]{:S(2)}) collective-permute-start(f32[72,128]{1,0:T(8,128)S(1)} %pad_maximum_fusion.2.refs_0_), channel_id=1, source_target_pairs={{0,2},{1,3},{2,0},{3,1},{4,6},{5,7},{6,4},{7,5},{8,10},{9,11},{10,... | collective-permute-start | bytes 110600 | tf_op jit(solution)/shard_map/ppermute | solution.py:541
  33.5 4.9 %collective-permute-start.12 = (f32[72,128]{1,0:T(8,128)S(1)}, f32[72,128]{1,0:T(8,128)S(1)}, u32[]{:S(2)}, u32[]{:S(2)}) collective-permute-start(f32[72,128]{1,0:T(8,128)S(1)} %pad_maximum_fusion.2.refs_0_), channel_id=1, source_target_pairs={{0,1},{1,0},{2,3},{3,2},{4,5},{5,4},{6,7},{7,6},{8,9},{9,8},{10,11... | collective-permute-start | bytes 110600 | tf_op jit(solution)/shard_map/ppermute | solution.py:541
  35.8 12.7 %collective-permute-start = (f32[32,1024]{1,0:T(8,128)S(1)}, f32[32,1024]{1,0:T(8,128)S(1)}, u32[]{:S(2)}, u32[]{:S(2)}) collective-permute-start(f32[32,1024]{1,0:T(8,128)S(1)} %slice.207), channel_id=1, source_target_pairs={{0,28},{4,0},{8,4},{12,8},{16,12},{20,16},{24,20},{28,24},{1,29},{... | collective-permute-start | bytes 393224 | tf_op jit(solution)/shard_map/ppermute | solution.py:594
  39.8 4.2 %collective-permute-start.13 = (f32[16,128]{1,0:T(8,128)S(1)}, f32[16,128]{1,0:T(8,128)S(1)}, u32[]{:S(2)}, u32[]{:S(2)}) collective-permute-start(f32[16,128]{1,0:T(8,128)S(1)} %get-tuple-element.105), channel_id=1, source_target_pairs={{0,28},{4,8},{8,4},{12,16},{16,12},{20,24},{24,20},{28,0},{1,29},{... | collective-permute-start | bytes 24584 | tf_op jit(solution)/shard_map/ppermute | solution.py:547
  40.0 4.0 %collective-permute-start.14 = (f32[16,128]{1,0:T(8,128)S(1)}, f32[16,128]{1,0:T(8,128)S(1)}, u32[]{:S(2)}, u32[]{:S(2)}) collective-permute-start(f32[16,128]{1,0:T(8,128)S(1)} %get-tuple-element.105), channel_id=1, source_target_pairs={{0,4},{4,0},{8,12},{12,8},{16,20},{20,16},{24,28},{28,24},{1,5},{5... | collective-permute-start | bytes 24584 | tf_op jit(solution)/shard_map/ppermute | solution.py:546
  44.0 6.5 %collective-permute-start.15 = (f32[72,128]{1,0:T(8,128)S(1)}, f32[72,128]{1,0:T(8,128)S(1)}, u32[]{:S(2)}, u32[]{:S(2)}) collective-permute-start(f32[72,128]{1,0:T(8,128)S(1)} %pad_maximum_fusion.3.after.refs_0_), channel_id=1, source_target_pairs={{0,3},{1,2},{2,1},{3,0},{4,7},{5,6},{6,5},{7,4},{8,11},{9,10},{10,... | collective-permute-start | bytes 110600 | tf_op jit(solution)/shard_map/ppermute | solution.py:541
  46.4 4.9 %collective-permute-start.16 = (f32[72,128]{1,0:T(8,128)S(1)}, f32[72,128]{1,0:T(8,128)S(1)}, u32[]{:S(2)}, u32[]{:S(2)}) collective-permute-start(f32[72,128]{1,0:T(8,128)S(1)} %pad_maximum_fusion.3.after.refs_0_), channel_id=1, source_target_pairs={{0,2},{1,3},{2,0},{3,1},{4,6},{5,7},{6,4},{7,5},{8,10},{9,11},{10,... | collective-permute-start | bytes 110600 | tf_op jit(solution)/shard_map/ppermute | solution.py:541
  46.9 4.6 %collective-permute-start.17 = (f32[72,128]{1,0:T(8,128)S(1)}, f32[72,128]{1,0:T(8,128)S(1)}, u32[]{:S(2)}, u32[]{:S(2)}) collective-permute-start(f32[72,128]{1,0:T(8,128)S(1)} %pad_maximum_fusion.3.after.refs_0_), channel_id=1, source_target_pairs={{0,1},{1,0},{2,3},{3,2},{4,5},{5,4},{6,7},{7,6},{8,9},{9,8},{10,11... | collective-permute-start | bytes 110600 | tf_op jit(solution)/shard_map/ppermute | solution.py:541
  53.8 5.5 %collective-permute-start.18 = (f32[9,32,128]{2,1,0:T(8,128)S(1)}, f32[9,32,128]{2,1,0:T(8,128)S(1)}, u32[]{:S(2)}, u32[]{:S(2)}) collective-permute-start(f32[9,32,128]{2,1,0:T(8,128)S(1)} %get-tuple-element.112), channel_id=1, source_target_pairs={{0,4},{4,8},{8,12},{12,16},{16,20},{20,24},{24,28},{28,0},{1,5},{5... | collective-permute-start | bytes 442376 | tf_op jit(solution)/shard_map/ppermute | solution.py:632
  53.8 10.9 %collective-permute-start.19 = (f32[16,32,128]{2,1,0:T(8,128)S(1)}, f32[16,32,128]{2,1,0:T(8,128)S(1)}, u32[]{:S(2)}, u32[]{:S(2)}) collective-permute-start(f32[16,32,128]{2,1,0:T(8,128)S(1)} %get-tuple-element.114), channel_id=1, source_target_pairs={{0,1},{1,0},{2,3},{3,2},{4,5},{5,4},{6,7},{7,6},{8,9},{9,8},{10,11... | collective-permute-start | bytes 786440 | tf_op jit(solution)/shard_map/ppermute | solution.py:541
  59.4 11.6 %collective-permute-start.23 = (f32[16,32,128]{2,1,0:T(8,128)S(1)}, f32[16,32,128]{2,1,0:T(8,128)S(1)}, u32[]{:S(2)}, u32[]{:S(2)}) collective-permute-start(f32[16,32,128]{2,1,0:T(8,128)S(1)} %get-tuple-element.128.after), channel_id=1, source_target_pairs={{0,1},{1,0},{2,3},{3,2},{4,5},{5,4},{6,7},{7,6},{8,9},{9,8},{10,11... | collective-permute-start | bytes 786440 | tf_op jit(solution)/shard_map/ppermute | solution.py:541
  64.8 10.9 %collective-permute-start.20 = (f32[16,32,128]{2,1,0:T(8,128)S(1)}, f32[16,32,128]{2,1,0:T(8,128)S(1)}, u32[]{:S(2)}, u32[]{:S(2)}) collective-permute-start(f32[16,32,128]{2,1,0:T(8,128)S(1)} %add.77), channel_id=1, source_target_pairs={{0,3},{1,2},{2,1},{3,0},{4,7},{5,6},{6,5},{7,4},{8,11},{9,10},{10,... | collective-permute-start | bytes 786440 | tf_op jit(solution)/shard_map/ppermute | solution.py:541
  67.9 21.6 %collective-permute-start.22 = (f32[16,32,128]{2,1,0:T(8,128)S(1)}, f32[16,32,128]{2,1,0:T(8,128)S(1)}, u32[]{:S(2)}, u32[]{:S(2)}) collective-permute-start(f32[16,32,128]{2,1,0:T(8,128)S(1)} %get-tuple-element.127), channel_id=1, source_target_pairs={{0,1},{1,0},{2,3},{3,2},{4,5},{5,4},{6,7},{7,6},{8,9},{9,8},{10,11... | collective-permute-start | bytes 786440 | tf_op jit(solution)/shard_map/ppermute | solution.py:541
  68.9 18.5 %collective-permute-start.21 = (f32[16,32,128]{2,1,0:T(8,128)S(1)}, f32[16,32,128]{2,1,0:T(8,128)S(1)}, u32[]{:S(2)}, u32[]{:S(2)}) collective-permute-start(f32[16,32,128]{2,1,0:T(8,128)S(1)} %get-tuple-element.119), channel_id=1, source_target_pairs={{0,1},{1,0},{2,3},{3,2},{4,5},{5,4},{6,7},{7,6},{8,9},{9,8},{10,11... | collective-permute-start | bytes 786440 | tf_op jit(solution)/shard_map/ppermute | solution.py:541
  71.0 21.5 %collective-permute-start.24 = (f32[16,32,128]{2,1,0:T(8,128)S(1)}, f32[16,32,128]{2,1,0:T(8,128)S(1)}, u32[]{:S(2)}, u32[]{:S(2)}) collective-permute-start(f32[16,32,128]{2,1,0:T(8,128)S(1)} %add.81), channel_id=1, source_target_pairs={{0,3},{1,2},{2,1},{3,0},{4,7},{5,6},{6,5},{7,4},{8,11},{9,10},{10,... | collective-permute-start | bytes 786440 | tf_op jit(solution)/shard_map/ppermute | solution.py:541

commit v10 on v9

--- a/solution.py
+++ b/solution.py
@@ -357,7 +357,7 @@
 
 
 def numer_col_kernel(order, scal, hi_ref, lo_ref, w_ref, *refs):
-    scales, refs = refs[: ITERS + 1], refs[ITERS + 1 :]
+    scales, refs = refs[: ITERS + 1], refs[ITERS + 2 :]
     sums_out, outs, acc = refs[0], refs[1:-1], refs[-1]
     u_ref = scales[-1]
     rows = hi_ref.shape[0]
@@ -393,7 +393,12 @@
     outs, terms = refs[:-1], refs[-1]
     ext, tile = u_ref.shape
     offs = offsets(scal, hi_ref.shape[2] // tile)
-    scaled_terms(h_ref, u_ref, terms, 0, ext)
+    rows, per = hi_ref.shape[0], outs[0].shape[0]
+    if len(order) > 1:
+        scaled_terms(h_ref, u_ref, terms, 0, ext)
+    else:
+        first = jnp.bitwise_xor(scal[0], order[0]) * per
+        scaled_terms(h_ref, u_ref, terms, first, per + ext - rows)
     row_pieces(scal, offs, terms, hi_ref, lo_ref, u_ref, order, outs)
 
 
@@ -421,7 +426,7 @@
     )
 
 
-def numer_col(scal, r_hi, r_lo, row_factors, scales, order, shares):
+def numer_col(scal, r_hi, r_lo, row_factors, scales, after, order, shares):
     rows, tile = r_hi.shape[:2]
     factors = row_factors.shape[0]
     piece = jax.ShapeDtypeStruct((rows // shares, factors, tile), F32)
@@ -429,7 +434,7 @@
         functools.partial(numer_col_kernel, order),
         "numer_col",
         scal,
-        [r_hi, r_lo, row_factors, *scales],
+        [r_hi, r_lo, row_factors, *scales, after],
         [jax.ShapeDtypeStruct((8, tile), F32)] + [piece] * len(order),
         [pltpu.VMEM((scales[0].shape[0], factors, tile), F32)],
     )
@@ -548,11 +553,12 @@
     return jnp.where(even > 0, a, b), jnp.where(even > 0, b, a)
 
 
-def scatter_terms(pieces):
+def scatter_terms(pieces, far=None):
     size = lax.axis_size("offset")
     if size == 4:
-        far = pieces[3] + xor_exchange(pieces[2], "offset", 1)
-        far = xor_exchange(far, "offset", 3)
+        if far is None:
+            far = pieces[3] + xor_exchange(pieces[2], "offset", 1)
+            far = xor_exchange(far, "offset", 3)
         return [pieces[0], xor_exchange(pieces[1], "offset", 1), far]
     return [pieces[0]] + [xor_exchange(pieces[k], "offset", k) for k in range(1, size)]
 
@@ -625,7 +631,10 @@
     )
     scales.append(u)
     order = [EARLY, *(k for k in range(offset_count) if k != EARLY)]
-    sums, pieces = numer_col(scal, r_hi, r_lo, row_factors, scales, order, offset_count)
+    (second,) = numer_row(scal, r_hi, r_lo, col_ext, u, early, [3], offset_count)
+    sums, pieces = numer_col(
+        scal, r_hi, r_lo, row_factors, scales, second, order, offset_count
+    )
     h_parts = dict(zip(order, pieces))
 
     right = [(i, (i + 1) % genome_count) for i in range(genome_count)]
@@ -642,10 +651,17 @@
     col_terms = coefficient(
         col_coefficient_kernel, scal, offset_count, col_factors, mask_ext, row_factors, arrived[pad]
     )
-    order = [k for k in (3, 1, 0, *range(4, offset_count))]
-    pieces = numer_row(scal, r_hi, r_lo, col_ext, u, h_parts[EARLY], order, offset_count)
-    w_parts = dict(zip(order, pieces)) | {EARLY: early}
-    w_terms = scatter_terms([w_parts[k] for k in range(offset_count)])
+    w_parts = {EARLY: early, 3: second}
+    hop = None
+    if offset_count == 4:
+        half_way = second + xor_exchange(early, "offset", 1)
+        hop = xor_exchange(half_way, "offset", 3)
+    else:
+        half_way = h_parts[EARLY]
+    order = [k for k in range(offset_count) if k not in w_parts]
+    pieces = numer_row(scal, r_hi, r_lo, col_ext, u, half_way, order, offset_count)
+    w_parts |= dict(zip(order, pieces))
+    w_terms = scatter_terms([w_parts[k] for k in range(offset_count)], hop)
     h_terms = scatter_terms([h_parts[k] for k in range(offset_count)])
 
     sums, _ = lax.optimization_barrier((sums, w_terms[2]))

time: 94 us -> 94.7 us (level)
    pallas_call x16 -> x17, Pallas kernels: 37.4 us -> 38.1 us  [kernel_call(): pl.pallas_call(body, grid_spec=pltpu.PrefetchScalarGridSpec(num_scalar_pr...]
  transfers between devices with their start and end apart: 25 -> 25, of which waited for: 11 -> 10; matrix products, arithmetic and copies ran while one was open for 1% -> 1% of each run, Pallas kernels for 33% -> 34%
where the time goes in v10:
time: 94.7 us; the launch traced here: 94.4 us
  Pallas kernels  38.1 us (40%)
  starting transfers between devices  28.9 us (31%)
  waiting for transfers between devices  13.9 us (15%)
  blocking collectives  9.79 us (10%)
  other arithmetic  2.7 us (3%)
  between operations  0.95 us (1%)
    pallas_call x17, Pallas kernels, kernel_call(): pl.pallas_call(body, grid_spec=pltpu.PrefetchScalarGridSpec(num_scalar_pr...  38.1 us
    ppermute x15, starting transfers between devices, xor_exchange(): lax.ppermute(x, axis, [(i, i ^ k) for i in range(lax.axis_size(axis))])  21.5 us
    ppermute x15, waiting for transfers between devices, xor_exchange(): lax.ppermute(x, axis, [(i, i ^ k) for i in range(lax.axis_size(axis))])  13.4 us
    all_gather x1, blocking collectives, per_device(): sums = jnp.sum(lax.all_gather(sums, 'genome'), axis=0)  9.79 us
    ppermute x4, starting transfers between devices, both_sides(): lax.ppermute(x, 'genome', [(i, ((i + 1 ^ 1) - 1) % size) for i in range(s...  4.56 us
    ppermute x4, starting transfers between devices, both_sides(): a = lax.ppermute(x, 'genome', [(i, i ^ 1) for i in range(size)])  2.57 us
  transfers between devices with their start and end apart: 25, of which 10 were waited for; matrix products, arithmetic and copies ran while one was open for 1% of the time, Pallas kernels for 34%

profile of v10, /device:TPU:0, one launch (start us, length us, event | category | flops | bytes accessed | tf_op | source)
XLA Modules:
  0.0 94.4 jit_solution(12470065030679267686)
XLA Ops:
  0.9 0.7 pad_add_fusion.scal
  1.7 0.8 fusion.13
  2.4 0.5 collective-permute-start.1
  2.9 3.6 %collective-permute-start.2 = (f32[8,128]{1,0:T(8,128)S(1)}, f32[8,128]{1,0:T(8,128)S(1)}, u32[]{:S(2)}, u32[]{:S(2)}) collective-permute-start(f32[8,128]{1,0:T(8,128)S(1)} %slice_bitcast_fusion.1), channel_id=1, source_target_pairs={{0,28},{4,8},{8,4},{12,16},{16,12},{20,24},{24,20},{28,0},{1,29},{... | collective-permute-start | bytes 12296 | tf_op jit(solution)/shard_map/ppermute | solution.py:552
  6.5 4.8 %first_main.1 = (f32[72,128]{1,0:T(8,128)S(1)}, f32[64,2,128,128]{3,2,1,0:T(8,128)S(1)}) custom-call(s32[4]{0:T(128)S(1)} %pad_add_fusion.scal, s32[64,2,128,128]{3,2,1,0:T(8,128)} %hbm.1, f32[64,128]{1,0:T(8,128)S(1)} %get-tuple-element.134.mask), custom_call_target="tpu_custom_call" | custom-call | tf_op jit(solution)/shard_map/first_main/pallas_call | solution.py:47
  11.3 1.4 %first_edge.1 = (f32[72,128]{1,0:T(8,128)S(1)}, f32[16,128]{1,0:T(8,128)S(1)}) custom-call(s32[4]{0:T(128)S(1)} %pad_add_fusion.scal, f32[64,2,128,128]{3,2,1,0:T(8,128)S(1)} %get-tuple-element.89.kept, f32[72,128]{1,0:T(8,128)S(1)} %pad_maximum_fusion.u_ref.mask.refs_0_, f32[72,128]{1,0:T(8,128)S(1)} %get-tuple-element.90.inner_v), custom_call_target="tpu_custom_call" | custom-call | tf_op jit(solution)/shard_map/first_edge/pallas_call | solution.py:47
  12.9 3.4 %ratio.3 = (bf16[64,128,256]{2,1,0:T(8,128)(2,1)S(1)}, bf16[64,128,256]{2,1,0:T(8,128)(2,1)S(1)}, f32[72,128]{1,0:T(8,128)S(1)}) custom-call(s32[4]{0:T(128)S(1)} %pad_add_fusion.scal, f32[64,2,128,128]{3,2,1,0:T(8,128)S(1)} %get-tuple-element.89.kept, f32[32,8192]{1,0:T(8,128)S(1)} %copy-done, f32[32,8192]{1,0:T(8,128)S(1)} %copy-done.1, ...), custom_call_target="tpu_custom_call" | custom-call | tf_op jit(solution)/shard_map/ratio/pallas_call | solution.py:47
  16.3 0.4 collective-permute-done.3
  16.8 3.7 %collective-permute-start.5 = (f32[72,128]{1,0:T(8,128)S(1)}, f32[72,128]{1,0:T(8,128)S(1)}, u32[]{:S(2)}, u32[]{:S(2)}) collective-permute-start(f32[72,128]{1,0:T(8,128)S(1)} %pad_maximum_fusion.1.after.refs_0_), channel_id=1, source_target_pairs={{0,3},{1,2},{2,1},{3,0},{4,7},{5,6},{6,5},{7,4},{8,11},{9,10},{10,... | collective-permute-start | bytes 110600 | tf_op jit(solution)/shard_map/ppermute | solution.py:546
  20.4 0.8 collective-permute-start.7
  21.2 2.2 %ratio.4 = (bf16[64,128,256]{2,1,0:T(8,128)(2,1)S(1)}, bf16[64,128,256]{2,1,0:T(8,128)(2,1)S(1)}) custom-call(s32[4]{0:T(128)S(1)} %pad_add_fusion.scal, f32[64,2,128,128]{3,2,1,0:T(8,128)S(1)} %get-tuple-element.89.kept, f32[32,8192]{1,0:T(8,128)S(1)} %copy-done, f32[32,8192]{1,0:T(8,128)S(1)} %copy-done.1, ...), custom_call_target="tpu_custom_call", output_to_operand_aliasing={{0}: (5, {}), {1}: (6, {})} | custom-call | tf_op jit(solution)/shard_map/ratio/pallas_call | solution.py:47
  23.4 1.9 %collective-permute-done.6.refs_2_ = f32[72,128]{1,0:T(8,128)S(1)} collective-permute-done((f32[72,128]{1,0:T(8,128)S(1)}, f32[72,128]{1,0:T(8,128)S(1)}, u32[]{:S(2)}, u32[]{:S(2)}) %collective-permute-start.6) | collective-permute-done | bytes 36896 | tf_op jit(solution)/shard_map/ppermute | solution.py:546
  25.3 1.4 %cover_edge.2 = (f32[72,128]{1,0:T(8,128)S(1)}, f32[16,128]{1,0:T(8,128)S(1)}, f32[72,128]{1,0:T(8,128)S(1)}) custom-call(s32[4]{0:T(128)S(1)} %pad_add_fusion.scal, f32[64,2,128,128]{3,2,1,0:T(8,128)S(1)} %get-tuple-element.89.kept, f32[72,128]{1,0:T(8,128)S(1)} %pad_maximum_fusion.u_ref.mask.refs_0_, f32[72,128]{1,0:T(8,128)S(1)} %pad_maximum_fusion.1.after.refs_0_, ...), custom_call_target="tpu_custom_call" | custom-call | tf_op jit(solution)/shard_map/cover_edge/pallas_call | solution.py:47
  26.7 0.7 collective-permute-start.8
  27.4 1.0 %collective-permute-start.9 = (f32[16,128]{1,0:T(8,128)S(1)}, f32[16,128]{1,0:T(8,128)S(1)}, u32[]{:S(2)}, u32[]{:S(2)}) collective-permute-start(f32[16,128]{1,0:T(8,128)S(1)} %get-tuple-element.101), channel_id=1, source_target_pairs={{0,4},{4,0},{8,12},{12,8},{16,20},{20,16},{24,28},{28,24},{1,5},{5... | collective-permute-start | bytes 24584 | tf_op jit(solution)/shard_map/ppermute | solution.py:551
  28.4 2.8 %cover_main.2 = f32[72,128]{1,0:T(8,128)S(1)} custom-call(s32[4]{0:T(128)S(1)} %pad_add_fusion.scal, f32[64,2,128,128]{3,2,1,0:T(8,128)S(1)} %get-tuple-element.89.kept, f32[72,128]{1,0:T(8,128)S(1)} %get-tuple-element.99.u_ref.refs_1_, f32[72,128]{1,0:T(8,128)S(1)} %get-tuple-element.100.edge_v), custom_call_target="tpu_custom_call" | custom-call | tf_op jit(solution)/shard_map/cover_main/pallas_call | solution.py:47
  31.3 1.8 %collective-permute-start.10 = (f32[72,128]{1,0:T(8,128)S(1)}, f32[72,128]{1,0:T(8,128)S(1)}, u32[]{:S(2)}, u32[]{:S(2)}) collective-permute-start(f32[72,128]{1,0:T(8,128)S(1)} %pad_maximum_fusion.2.refs_0_), channel_id=1, source_target_pairs={{0,3},{1,2},{2,1},{3,0},{4,7},{5,6},{6,5},{7,4},{8,11},{9,10},{10,... | collective-permute-start | bytes 110600 | tf_op jit(solution)/shard_map/ppermute | solution.py:546
  33.1 0.4 collective-permute-start.11
  33.5 2.3 %collective-permute-start.12 = (f32[72,128]{1,0:T(8,128)S(1)}, f32[72,128]{1,0:T(8,128)S(1)}, u32[]{:S(2)}, u32[]{:S(2)}) collective-permute-start(f32[72,128]{1,0:T(8,128)S(1)} %pad_maximum_fusion.2.refs_0_), channel_id=1, source_target_pairs={{0,1},{1,0},{2,3},{3,2},{4,5},{5,4},{6,7},{7,6},{8,9},{9,8},{10,11... | collective-permute-start | bytes 110600 | tf_op jit(solution)/shard_map/ppermute | solution.py:546
  36.0 1.5 %collective-permute-done.10.refs_1_ = f32[72,128]{1,0:T(8,128)S(1)} collective-permute-done((f32[72,128]{1,0:T(8,128)S(1)}, f32[72,128]{1,0:T(8,128)S(1)}, u32[]{:S(2)}, u32[]{:S(2)}) %collective-permute-start.10) | collective-permute-done | bytes 36896 | tf_op jit(solution)/shard_map/ppermute | solution.py:546
  37.5 0.7 collective-permute-done.11.refs_2_
  38.4 1.4 %cover_edge.3 = (f32[72,128]{1,0:T(8,128)S(1)}, f32[16,128]{1,0:T(8,128)S(1)}, f32[72,128]{1,0:T(8,128)S(1)}) custom-call(s32[4]{0:T(128)S(1)} %pad_add_fusion.scal, f32[64,2,128,128]{3,2,1,0:T(8,128)S(1)} %get-tuple-element.89.kept, f32[72,128]{1,0:T(8,128)S(1)} %pad_maximum_fusion.u_ref.mask.refs_0_, f32[72,128]{1,0:T(8,128)S(1)} %pad_maximum_fusion.2.refs_0_, ...), custom_call_target="tpu_custom_call" | custom-call | tf_op jit(solution)/shard_map/cover_edge/pallas_call | solution.py:47
  40.0 1.1 %collective-permute-start.14 = (f32[16,128]{1,0:T(8,128)S(1)}, f32[16,128]{1,0:T(8,128)S(1)}, u32[]{:S(2)}, u32[]{:S(2)}) collective-permute-start(f32[16,128]{1,0:T(8,128)S(1)} %get-tuple-element.104), channel_id=1, source_target_pairs={{0,4},{4,0},{8,12},{12,8},{16,20},{20,16},{24,28},{28,24},{1,5},{5... | collective-permute-start | bytes 24584 | tf_op jit(solution)/shard_map/ppermute | solution.py:551
  41.1 2.8 %cover_main.3 = f32[72,128]{1,0:T(8,128)S(1)} custom-call(s32[4]{0:T(128)S(1)} %pad_add_fusion.scal, f32[64,2,128,128]{3,2,1,0:T(8,128)S(1)} %get-tuple-element.89.kept, f32[72,128]{1,0:T(8,128)S(1)} %get-tuple-element.102.u_ref.refs_2_, f32[72,128]{1,0:T(8,128)S(1)} %get-tuple-element.103.edge_v), custom_call_target="tpu_custom_call" | custom-call | tf_op jit(solution)/shard_map/cover_main/pallas_call | solution.py:47
  44.0 2.4 %collective-permute-start.15 = (f32[72,128]{1,0:T(8,128)S(1)}, f32[72,128]{1,0:T(8,128)S(1)}, u32[]{:S(2)}, u32[]{:S(2)}) collective-permute-start(f32[72,128]{1,0:T(8,128)S(1)} %pad_maximum_fusion.3.after.refs_0_), channel_id=1, source_target_pairs={{0,3},{1,2},{2,1},{3,0},{4,7},{5,6},{6,5},{7,4},{8,11},{9,10},{10,... | collective-permute-start | bytes 110600 | tf_op jit(solution)/shard_map/ppermute | solution.py:546
  46.4 0.5 collective-permute-start.16
  46.9 1.6 %collective-permute-start.17 = (f32[72,128]{1,0:T(8,128)S(1)}, f32[72,128]{1,0:T(8,128)S(1)}, u32[]{:S(2)}, u32[]{:S(2)}) collective-permute-start(f32[72,128]{1,0:T(8,128)S(1)} %pad_maximum_fusion.3.after.refs_0_), channel_id=1, source_target_pairs={{0,1},{1,0},{2,3},{3,2},{4,5},{5,4},{6,7},{7,6},{8,9},{9,8},{10,11... | collective-permute-start | bytes 110600 | tf_op jit(solution)/shard_map/ppermute | solution.py:546
  48.5 2.0 %ratio.5 = (bf16[64,128,256]{2,1,0:T(8,128)(2,1)S(1)}, bf16[64,128,256]{2,1,0:T(8,128)(2,1)S(1)}) custom-call(s32[4]{0:T(128)S(1)} %pad_add_fusion.scal, f32[64,2,128,128]{3,2,1,0:T(8,128)S(1)} %get-tuple-element.89.kept, f32[32,8192]{1,0:T(8,128)S(1)} %copy-done, ...), custom_call_target="tpu_custom_call", output_to_operand_aliasing={{0}: (5, {}), {1}: (6, {})} | custom-call | tf_op jit(solution)/shard_map/ratio/pallas_call | solution.py:47
  50.5 0.8 collective-permute-done.16.refs_2_
  51.4 2.3 %numer_first.1 = (f32[72,128]{1,0:T(8,128)S(1)}, f32[9,32,128]{2,1,0:T(8,128)S(1)}, f32[16,32,128]{2,1,0:T(8,128)S(1)}) custom-call(s32[4]{0:T(128)S(1)} %pad_add_fusion.scal, bf16[64,128,256]{2,1,0:T(8,128)(2,1)S(1)} %get-tuple-element.106.hi_ref, bf16[64,128,256]{2,1,0:T(8,128)(2,1)S(1)} %get-tuple-element.107.lo_ref, f32[32,8192]{1,0:T(8,128)S(1)} %copy-done, ...), custom_call_target="tpu_custom_call" | custom-call | tf_op jit(solution)/shard_map/numer_first/pallas_call | solution.py:47
  53.8 1.1 %collective-permute-start.18 = (f32[16,32,128]{2,1,0:T(8,128)S(1)}, f32[16,32,128]{2,1,0:T(8,128)S(1)}, u32[]{:S(2)}, u32[]{:S(2)}) collective-permute-start(f32[16,32,128]{2,1,0:T(8,128)S(1)} %get-tuple-element.109.after), channel_id=1, source_target_pairs={{0,1},{1,0},{2,3},{3,2},{4,5},{5,4},{6,7},{7,6},{8,9},{9,8},{10,11... | collective-permute-start | bytes 786440 | tf_op jit(solution)/shard_map/ppermute | solution.py:546
  54.9 1.8 %numer_row.2.refs_4_ = f32[16,32,128]{2,1,0:T(8,128)S(1)} custom-call(s32[4]{0:T(128)S(1)} %pad_add_fusion.scal, bf16[64,128,256]{2,1,0:T(8,128)(2,1)S(1)} %get-tuple-element.106.hi_ref, bf16[64,128,256]{2,1,0:T(8,128)(2,1)S(1)} %get-tuple-element.107.lo_ref, f32[32,9216]{1,0:T(8,128)S(1)} %constant_dynamic-update-slice_fusion.h_ref.other, ...), custom_call_target="tpu_custom_call" | custom-call | tf_op jit(solution)/shard_map/numer_row/pallas_call | solution.py:47
  56.6 4.4 %numer_col.1 = (f32[8,128]{1,0:T(8,128)S(1)}, f32[16,32,128]{2,1,0:T(8,128)S(1)}, f32[16,32,128]{2,1,0:T(8,128)S(1)}, f32[16,32,128]{2,1,0:T(8,128)S(1)}, f32[16,32,128]{2,1,0:T(8,128)S(1)}) custom-call(s32[4]{0:T(128)S(1)} %pad_add_fusion.scal, bf16[64,128,256]{2,1,0:T(8,128)(2,1)S(1)} %get-tuple-element.106.hi_ref, ...), custom_call_target="tpu_custom_call" | custom-call | tf_op jit(solution)/shard_map/numer_col/pallas_call | solution.py:47
  61.1 1.0 %collective-permute-start.23 = (f32[16,32,128]{2,1,0:T(8,128)S(1)}, f32[16,32,128]{2,1,0:T(8,128)S(1)}, u32[]{:S(2)}, u32[]{:S(2)}) collective-permute-start(f32[16,32,128]{2,1,0:T(8,128)S(1)} %get-tuple-element.123), channel_id=1, source_target_pairs={{0,1},{1,0},{2,3},{3,2},{4,5},{5,4},{6,7},{7,6},{8,9},{9,8},{10,11... | collective-permute-start | bytes 786440 | tf_op jit(solution)/shard_map/ppermute | solution.py:546
  62.2 1.9 %collective-permute-start.19 = (f32[16,32,128]{2,1,0:T(8,128)S(1)}, f32[16,32,128]{2,1,0:T(8,128)S(1)}, u32[]{:S(2)}, u32[]{:S(2)}) collective-permute-start(f32[16,32,128]{2,1,0:T(8,128)S(1)} %add.76.after), channel_id=1, source_target_pairs={{0,3},{1,2},{2,1},{3,0},{4,7},{5,6},{6,5},{7,4},{8,11},{9,10},{10,... | collective-permute-start | bytes 786440 | tf_op jit(solution)/shard_map/ppermute | solution.py:546
  64.1 0.7 coefficient.2
  64.8 0.7 collective-permute-start.22
  65.5 0.9 coefficient.3
  66.5 3.1 %numer_row.3 = (f32[16,32,128]{2,1,0:T(8,128)S(1)}, f32[16,32,128]{2,1,0:T(8,128)S(1)}) custom-call(s32[4]{0:T(128)S(1)} %pad_add_fusion.scal, bf16[64,128,256]{2,1,0:T(8,128)(2,1)S(1)} %get-tuple-element.106.hi_ref, bf16[64,128,256]{2,1,0:T(8,128)(2,1)S(1)} %get-tuple-element.107.lo_ref, f32[32,9216]{1,0:T(8,128)S(1)} %constant_dynamic-update-slice_fusion.h_ref.other, ...), custom_call_target="tpu_custom_call" | custom-call | tf_op jit(solution)/shard_map/numer_row/pallas_call | solution.py:47
  69.6 1.4 %collective-permute-start.20 = (f32[16,32,128]{2,1,0:T(8,128)S(1)}, f32[16,32,128]{2,1,0:T(8,128)S(1)}, u32[]{:S(2)}, u32[]{:S(2)}) collective-permute-start(f32[16,32,128]{2,1,0:T(8,128)S(1)} %get-tuple-element.115), channel_id=1, source_target_pairs={{0,1},{1,0},{2,3},{3,2},{4,5},{5,4},{6,7},{7,6},{8,9},{9,8},{10,11... | collective-permute-start | bytes 786440 | tf_op jit(solution)/shard_map/ppermute | solution.py:546
  71.0 2.1 %collective-permute-start.24 = (f32[16,32,128]{2,1,0:T(8,128)S(1)}, f32[16,32,128]{2,1,0:T(8,128)S(1)}, u32[]{:S(2)}, u32[]{:S(2)}) collective-permute-start(f32[16,32,128]{2,1,0:T(8,128)S(1)} %add.81), channel_id=1, source_target_pairs={{0,3},{1,2},{2,1},{3,0},{4,7},{5,6},{6,5},{7,4},{8,11},{9,10},{10,... | collective-permute-start | bytes 786440 | tf_op jit(solution)/shard_map/ppermute | solution.py:546
  73.1 3.2 %collective-permute-done.19.refs_2_ = f32[16,32,128]{2,1,0:T(8,128)S(1)} collective-permute-done((f32[16,32,128]{2,1,0:T(8,128)S(1)}, f32[16,32,128]{2,1,0:T(8,128)S(1)}, u32[]{:S(2)}, u32[]{:S(2)}) %collective-permute-start.19) | collective-permute-done | bytes 262176 | tf_op jit(solution)/shard_map/ppermute | solution.py:546
  76.4 9.8 %all-gather = f32[64,128]{1,0:T(8,128)S(1)} all-gather(f32[8,128]{1,0:T(8,128)S(1)} %get-tuple-element.111), channel_id=2, replica_groups=mesh['genome'=8,'offset'=4] {'genome'}, dimensions={0}, use_global_device_ids=true | all-gather | bytes 36864 | tf_op jit(solution)/shard_map/all_gather | solution.py:668
  86.2 0.4 collective-permute-done.20.refs_1_
  86.6 1.3 %update.2 = f32[32,2048]{1,0:T(8,128)} custom-call(s32[4]{0:T(128)S(1)} %pad_add_fusion.scal, f32[8,128]{1,0:T(8,128)S(1)} %bitcast_reduce_fusion.sums, f32[16,32,128]{2,1,0:T(8,128)S(1)} %get-tuple-element.112.times, f32[16,32,128]{2,1,0:T(8,128)S(1)} %get-tuple-element.113.plus, f32[16,32,128]{2,1,0:T(8,128)S(1)} %get-tuple-element.114.refs_0_, ...), custom_call_target="tpu_custom_call" | custom-call | tf_op jit(solution)/shard_map/update/pallas_call | solution.py:47
  88.0 0.6 multiply_bitcast_fusion
  88.6 4.5 %collective-permute-done.24.refs_2_ = f32[16,32,128]{2,1,0:T(8,128)S(1)} collective-permute-done((f32[16,32,128]{2,1,0:T(8,128)S(1)}, f32[16,32,128]{2,1,0:T(8,128)S(1)}, u32[]{:S(2)}, u32[]{:S(2)}) %collective-permute-start.24) | collective-permute-done | bytes 262176 | tf_op jit(solution)/shard_map/ppermute | solution.py:546
  93.1 1.3 %update.3 = f32[32,2048]{1,0:T(8,128)} custom-call(s32[4]{0:T(128)S(1)} %pad_add_fusion.scal, f32[8,128]{1,0:T(8,128)S(1)} %bitcast_reduce_fusion.sums, f32[16,32,128]{2,1,0:T(8,128)S(1)} %get-tuple-element.117.times, f32[16,32,128]{2,1,0:T(8,128)S(1)} %get-tuple-element.118.plus, f32[16,32,128]{2,1,0:T(8,128)S(1)} %get-tuple-element.126.refs_0_, ...), custom_call_target="tpu_custom_call" | custom-call | tf_op jit(solution)/shard_map/update/pallas_call | solution.py:47
  (57 shorter events, 1.7 us)
Async XLA Ops:
  2.4 8.8 %collective-permute-start.1 = (f32[8,128]{1,0:T(8,128)S(1)}, f32[8,128]{1,0:T(8,128)S(1)}, u32[]{:S(2)}, u32[]{:S(2)}) collective-permute-start(f32[8,128]{1,0:T(8,128)S(1)} %slice_bitcast_fusion.1), channel_id=1, source_target_pairs={{0,4},{4,0},{8,12},{12,8},{16,20},{20,16},{24,28},{28,24},{1,5},{5... | collective-permute-start | bytes 12296 | tf_op jit(solution)/shard_map/ppermute | solution.py:551
  2.9 8.4 %collective-permute-start.2 = (f32[8,128]{1,0:T(8,128)S(1)}, f32[8,128]{1,0:T(8,128)S(1)}, u32[]{:S(2)}, u32[]{:S(2)}) collective-permute-start(f32[8,128]{1,0:T(8,128)S(1)} %slice_bitcast_fusion.1), channel_id=1, source_target_pairs={{0,28},{4,8},{8,4},{12,16},{16,12},{20,24},{24,20},{28,0},{1,29},{... | collective-permute-start | bytes 12296 | tf_op jit(solution)/shard_map/ppermute | solution.py:552
  11.3 1.5 %copy-start = (f32[32,8192]{1,0:T(8,128)S(1)}, f32[32,8192]{1,0:T(8,128)}, u32[]{:S(2)}) copy-start(f32[32,8192]{1,0:T(8,128)} %other.1) | copy-start | bytes 3145732
  11.3 1.5 %copy-start.1 = (f32[32,8192]{1,0:T(8,128)S(1)}, f32[32,8192]{1,0:T(8,128)}, u32[]{:S(2)}) copy-start(f32[32,8192]{1,0:T(8,128)} %old_ref.3) | copy-start | bytes 3145732
  12.7 4.0 %collective-permute-start.3 = (f32[16,128]{1,0:T(8,128)S(1)}, f32[16,128]{1,0:T(8,128)S(1)}, u32[]{:S(2)}, u32[]{:S(2)}) collective-permute-start(f32[16,128]{1,0:T(8,128)S(1)} %get-tuple-element.95), channel_id=1, source_target_pairs={{0,28},{4,8},{8,4},{12,16},{16,12},{20,24},{24,20},{28,0},{1,29},{... | collective-permute-start | bytes 24584 | tf_op jit(solution)/shard_map/ppermute | solution.py:552
  12.8 4.0 %collective-permute-start.4 = (f32[16,128]{1,0:T(8,128)S(1)}, f32[16,128]{1,0:T(8,128)S(1)}, u32[]{:S(2)}, u32[]{:S(2)}) collective-permute-start(f32[16,128]{1,0:T(8,128)S(1)} %get-tuple-element.95), channel_id=1, source_target_pairs={{0,4},{4,0},{8,12},{12,8},{16,20},{20,16},{24,28},{28,24},{1,5},{5... | collective-permute-start | bytes 24584 | tf_op jit(solution)/shard_map/ppermute | solution.py:551
  16.8 6.6 %collective-permute-start.5 = (f32[72,128]{1,0:T(8,128)S(1)}, f32[72,128]{1,0:T(8,128)S(1)}, u32[]{:S(2)}, u32[]{:S(2)}) collective-permute-start(f32[72,128]{1,0:T(8,128)S(1)} %pad_maximum_fusion.1.after.refs_0_), channel_id=1, source_target_pairs={{0,3},{1,2},{2,1},{3,0},{4,7},{5,6},{6,5},{7,4},{8,11},{9,10},{10,... | collective-permute-start | bytes 110600 | tf_op jit(solution)/shard_map/ppermute | solution.py:546
  20.4 4.9 %collective-permute-start.6 = (f32[72,128]{1,0:T(8,128)S(1)}, f32[72,128]{1,0:T(8,128)S(1)}, u32[]{:S(2)}, u32[]{:S(2)}) collective-permute-start(f32[72,128]{1,0:T(8,128)S(1)} %pad_maximum_fusion.1.after.refs_0_), channel_id=1, source_target_pairs={{0,2},{1,3},{2,0},{3,1},{4,6},{5,7},{6,4},{7,5},{8,10},{9,11},{10,... | collective-permute-start | bytes 110600 | tf_op jit(solution)/shard_map/ppermute | solution.py:546
  20.4 4.9 %collective-permute-start.7 = (f32[72,128]{1,0:T(8,128)S(1)}, f32[72,128]{1,0:T(8,128)S(1)}, u32[]{:S(2)}, u32[]{:S(2)}) collective-permute-start(f32[72,128]{1,0:T(8,128)S(1)} %pad_maximum_fusion.1.after.refs_0_), channel_id=1, source_target_pairs={{0,1},{1,0},{2,3},{3,2},{4,5},{5,4},{6,7},{7,6},{8,9},{9,8},{10,11... | collective-permute-start | bytes 110600 | tf_op jit(solution)/shard_map/ppermute | solution.py:546
  26.7 4.6 %collective-permute-start.8 = (f32[16,128]{1,0:T(8,128)S(1)}, f32[16,128]{1,0:T(8,128)S(1)}, u32[]{:S(2)}, u32[]{:S(2)}) collective-permute-start(f32[16,128]{1,0:T(8,128)S(1)} %get-tuple-element.101), channel_id=1, source_target_pairs={{0,28},{4,8},{8,4},{12,16},{16,12},{20,24},{24,20},{28,0},{1,29},{... | collective-permute-start | bytes 24584 | tf_op jit(solution)/shard_map/ppermute | solution.py:552
  27.4 3.8 %collective-permute-start.9 = (f32[16,128]{1,0:T(8,128)S(1)}, f32[16,128]{1,0:T(8,128)S(1)}, u32[]{:S(2)}, u32[]{:S(2)}) collective-permute-start(f32[16,128]{1,0:T(8,128)S(1)} %get-tuple-element.101), channel_id=1, source_target_pairs={{0,4},{4,0},{8,12},{12,8},{16,20},{20,16},{24,28},{28,24},{1,5},{5... | collective-permute-start | bytes 24584 | tf_op jit(solution)/shard_map/ppermute | solution.py:551
  31.3 6.2 %collective-permute-start.10 = (f32[72,128]{1,0:T(8,128)S(1)}, f32[72,128]{1,0:T(8,128)S(1)}, u32[]{:S(2)}, u32[]{:S(2)}) collective-permute-start(f32[72,128]{1,0:T(8,128)S(1)} %pad_maximum_fusion.2.refs_0_), channel_id=1, source_target_pairs={{0,3},{1,2},{2,1},{3,0},{4,7},{5,6},{6,5},{7,4},{8,11},{9,10},{10,... | collective-permute-start | bytes 110600 | tf_op jit(solution)/shard_map/ppermute | solution.py:546
  33.1 5.1 %collective-permute-start.11 = (f32[72,128]{1,0:T(8,128)S(1)}, f32[72,128]{1,0:T(8,128)S(1)}, u32[]{:S(2)}, u32[]{:S(2)}) collective-permute-start(f32[72,128]{1,0:T(8,128)S(1)} %pad_maximum_fusion.2.refs_0_), channel_id=1, source_target_pairs={{0,2},{1,3},{2,0},{3,1},{4,6},{5,7},{6,4},{7,5},{8,10},{9,11},{10,... | collective-permute-start | bytes 110600 | tf_op jit(solution)/shard_map/ppermute | solution.py:546
  33.5 4.9 %collective-permute-start.12 = (f32[72,128]{1,0:T(8,128)S(1)}, f32[72,128]{1,0:T(8,128)S(1)}, u32[]{:S(2)}, u32[]{:S(2)}) collective-permute-start(f32[72,128]{1,0:T(8,128)S(1)} %pad_maximum_fusion.2.refs_0_), channel_id=1, source_target_pairs={{0,1},{1,0},{2,3},{3,2},{4,5},{5,4},{6,7},{7,6},{8,9},{9,8},{10,11... | collective-permute-start | bytes 110600 | tf_op jit(solution)/shard_map/ppermute | solution.py:546
  35.8 12.7 %collective-permute-start = (f32[32,1024]{1,0:T(8,128)S(1)}, f32[32,1024]{1,0:T(8,128)S(1)}, u32[]{:S(2)}, u32[]{:S(2)}) collective-permute-start(f32[32,1024]{1,0:T(8,128)S(1)} %slice.207), channel_id=1, source_target_pairs={{0,28},{4,0},{8,4},{12,8},{16,12},{20,16},{24,20},{28,24},{1,29},{... | collective-permute-start | bytes 393224 | tf_op jit(solution)/shard_map/ppermute | solution.py:600
  39.8 4.2 %collective-permute-start.13 = (f32[16,128]{1,0:T(8,128)S(1)}, f32[16,128]{1,0:T(8,128)S(1)}, u32[]{:S(2)}, u32[]{:S(2)}) collective-permute-start(f32[16,128]{1,0:T(8,128)S(1)} %get-tuple-element.104), channel_id=1, source_target_pairs={{0,28},{4,8},{8,4},{12,16},{16,12},{20,24},{24,20},{28,0},{1,29},{... | collective-permute-start | bytes 24584 | tf_op jit(solution)/shard_map/ppermute | solution.py:552
  40.0 4.0 %collective-permute-start.14 = (f32[16,128]{1,0:T(8,128)S(1)}, f32[16,128]{1,0:T(8,128)S(1)}, u32[]{:S(2)}, u32[]{:S(2)}) collective-permute-start(f32[16,128]{1,0:T(8,128)S(1)} %get-tuple-element.104), channel_id=1, source_target_pairs={{0,4},{4,0},{8,12},{12,8},{16,20},{20,16},{24,28},{28,24},{1,5},{5... | collective-permute-start | bytes 24584 | tf_op jit(solution)/shard_map/ppermute | solution.py:551
  44.0 6.5 %collective-permute-start.15 = (f32[72,128]{1,0:T(8,128)S(1)}, f32[72,128]{1,0:T(8,128)S(1)}, u32[]{:S(2)}, u32[]{:S(2)}) collective-permute-start(f32[72,128]{1,0:T(8,128)S(1)} %pad_maximum_fusion.3.after.refs_0_), channel_id=1, source_target_pairs={{0,3},{1,2},{2,1},{3,0},{4,7},{5,6},{6,5},{7,4},{8,11},{9,10},{10,... | collective-permute-start | bytes 110600 | tf_op jit(solution)/shard_map/ppermute | solution.py:546
  46.4 4.9 %collective-permute-start.16 = (f32[72,128]{1,0:T(8,128)S(1)}, f32[72,128]{1,0:T(8,128)S(1)}, u32[]{:S(2)}, u32[]{:S(2)}) collective-permute-start(f32[72,128]{1,0:T(8,128)S(1)} %pad_maximum_fusion.3.after.refs_0_), channel_id=1, source_target_pairs={{0,2},{1,3},{2,0},{3,1},{4,6},{5,7},{6,4},{7,5},{8,10},{9,11},{10,... | collective-permute-start | bytes 110600 | tf_op jit(solution)/shard_map/ppermute | solution.py:546
  46.9 4.6 %collective-permute-start.17 = (f32[72,128]{1,0:T(8,128)S(1)}, f32[72,128]{1,0:T(8,128)S(1)}, u32[]{:S(2)}, u32[]{:S(2)}) collective-permute-start(f32[72,128]{1,0:T(8,128)S(1)} %pad_maximum_fusion.3.after.refs_0_), channel_id=1, source_target_pairs={{0,1},{1,0},{2,3},{3,2},{4,5},{5,4},{6,7},{7,6},{8,9},{9,8},{10,11... | collective-permute-start | bytes 110600 | tf_op jit(solution)/shard_map/ppermute | solution.py:546
  53.8 7.3 %collective-permute-start.21 = (f32[9,32,128]{2,1,0:T(8,128)S(1)}, f32[9,32,128]{2,1,0:T(8,128)S(1)}, u32[]{:S(2)}, u32[]{:S(2)}) collective-permute-start(f32[9,32,128]{2,1,0:T(8,128)S(1)} %get-tuple-element.116), channel_id=1, source_target_pairs={{0,4},{4,8},{8,12},{12,16},{16,20},{20,24},{24,28},{28,0},{1,5},{5... | collective-permute-start | bytes 442376 | tf_op jit(solution)/shard_map/ppermute | solution.py:641
  53.8 8.4 %collective-permute-start.18 = (f32[16,32,128]{2,1,0:T(8,128)S(1)}, f32[16,32,128]{2,1,0:T(8,128)S(1)}, u32[]{:S(2)}, u32[]{:S(2)}) collective-permute-start(f32[16,32,128]{2,1,0:T(8,128)S(1)} %get-tuple-element.109.after), channel_id=1, source_target_pairs={{0,1},{1,0},{2,3},{3,2},{4,5},{5,4},{6,7},{7,6},{8,9},{9,8},{10,11... | collective-permute-start | bytes 786440 | tf_op jit(solution)/shard_map/ppermute | solution.py:546
  61.1 9.9 %collective-permute-start.23 = (f32[16,32,128]{2,1,0:T(8,128)S(1)}, f32[16,32,128]{2,1,0:T(8,128)S(1)}, u32[]{:S(2)}, u32[]{:S(2)}) collective-permute-start(f32[16,32,128]{2,1,0:T(8,128)S(1)} %get-tuple-element.123), channel_id=1, source_target_pairs={{0,1},{1,0},{2,3},{3,2},{4,5},{5,4},{6,7},{7,6},{8,9},{9,8},{10,11... | collective-permute-start | bytes 786440 | tf_op jit(solution)/shard_map/ppermute | solution.py:546
  62.2 14.1 %collective-permute-start.19 = (f32[16,32,128]{2,1,0:T(8,128)S(1)}, f32[16,32,128]{2,1,0:T(8,128)S(1)}, u32[]{:S(2)}, u32[]{:S(2)}) collective-permute-start(f32[16,32,128]{2,1,0:T(8,128)S(1)} %add.76.after), channel_id=1, source_target_pairs={{0,3},{1,2},{2,1},{3,0},{4,7},{5,6},{6,5},{7,4},{8,11},{9,10},{10,... | collective-permute-start | bytes 786440 | tf_op jit(solution)/shard_map/ppermute | solution.py:546
  64.8 23.7 %collective-permute-start.22 = (f32[16,32,128]{2,1,0:T(8,128)S(1)}, f32[16,32,128]{2,1,0:T(8,128)S(1)}, u32[]{:S(2)}, u32[]{:S(2)}) collective-permute-start(f32[16,32,128]{2,1,0:T(8,128)S(1)} %get-tuple-element.124), channel_id=1, source_target_pairs={{0,1},{1,0},{2,3},{3,2},{4,5},{5,4},{6,7},{7,6},{8,9},{9,8},{10,11... | collective-permute-start | bytes 786440 | tf_op jit(solution)/shard_map/ppermute | solution.py:546
  69.6 17.0 %collective-permute-start.20 = (f32[16,32,128]{2,1,0:T(8,128)S(1)}, f32[16,32,128]{2,1,0:T(8,128)S(1)}, u32[]{:S(2)}, u32[]{:S(2)}) collective-permute-start(f32[16,32,128]{2,1,0:T(8,128)S(1)} %get-tuple-element.115), channel_id=1, source_target_pairs={{0,1},{1,0},{2,3},{3,2},{4,5},{5,4},{6,7},{7,6},{8,9},{9,8},{10,11... | collective-permute-start | bytes 786440 | tf_op jit(solution)/shard_map/ppermute | solution.py:546
  71.0 22.1 %collective-permute-start.24 = (f32[16,32,128]{2,1,0:T(8,128)S(1)}, f32[16,32,128]{2,1,0:T(8,128)S(1)}, u32[]{:S(2)}, u32[]{:S(2)}) collective-permute-start(f32[16,32,128]{2,1,0:T(8,128)S(1)} %add.81), channel_id=1, source_target_pairs={{0,3},{1,2},{2,1},{3,0},{4,7},{5,6},{6,5},{7,4},{8,11},{9,10},{10,... | collective-permute-start | bytes 786440 | tf_op jit(solution)/shard_map/ppermute | solution.py:546

commit v11 on v9

--- a/solution.py
+++ b/solution.py
@@ -34,7 +34,7 @@
 
 
 def scale_from(mask, parts):
-    cover = tree_sum([p[...] for p in parts[:1] + parts[:0:-1]])
+    cover = tree_sum([p[...] for p in parts])
     live = mask[...] > 0
     return jnp.where(live, 1.0 / jnp.where(live, cover, 1.0), 0.0)
 
@@ -611,7 +611,7 @@
         front = v[:pad] + before[pad:] * has_prev
         back = v[rows:] + after[:pad] * has_next
         x = jnp.concatenate([front, v[pad:rows], back])
-        others = {k: xor_exchange(x, "offset", k) for k in reversed(range(1, offset_count))}
+        others = {k: xor_exchange(x, "offset", k) for k in range(1, offset_count)}
         parts = [x, *others.values()]
         if t == 0:
             ratios = ratio(scal, kept, row_factors, col_factors, x, ratios, 2 * quarter, quarter)

time: 94 us -> 97.5 us (1.037)
  waiting for transfers between devices: 13.9 us -> 18.5 us
    ppermute x15, waiting for transfers between devices: 13.4 us -> 17 us  [xor_exchange(): lax.ppermute(x, axis, [(i, i ^ k) for i in range(lax.axis_size(axis))])]
    ppermute x15, starting transfers between devices: 21.6 us -> 20.6 us  [xor_exchange(): lax.ppermute(x, axis, [(i, i ^ k) for i in range(lax.axis_size(axis))])]
  transfers between devices with their start and end apart: 25 -> 25, of which waited for: 11 -> 10; matrix products, arithmetic and copies ran while one was open for 1% -> 1% of each run, Pallas kernels for 33% -> 32%
where the time goes in v11:
time: 97.5 us; the launch traced here: 97.4 us
  Pallas kernels  37.4 us (38%)
  starting transfers between devices  28.1 us (29%)
  waiting for transfers between devices  18.5 us (19%)
  blocking collectives  9.64 us (10%)
  other arithmetic  2.7 us (3%)
  between operations  0.98 us (1%)
    pallas_call x16, Pallas kernels, kernel_call(): pl.pallas_call(body, grid_spec=pltpu.PrefetchScalarGridSpec(num_scalar_pr...  37.4 us
    ppermute x15, starting transfers between devices, xor_exchange(): lax.ppermute(x, axis, [(i, i ^ k) for i in range(lax.axis_size(axis))])  20.6 us
    ppermute x15, waiting for transfers between devices, xor_exchange(): lax.ppermute(x, axis, [(i, i ^ k) for i in range(lax.axis_size(axis))])  17 us
    all_gather x1, blocking collectives, per_device(): sums = jnp.sum(lax.all_gather(sums, 'genome'), axis=0)  9.64 us
    ppermute x4, starting transfers between devices, both_sides(): lax.ppermute(x, 'genome', [(i, ((i + 1 ^ 1) - 1) % size) for i in range(s...  4.23 us
    ppermute x4, starting transfers between devices, both_sides(): a = lax.ppermute(x, 'genome', [(i, i ^ 1) for i in range(size)])  3.03 us
  transfers between devices with their start and end apart: 25, of which 10 were waited for; matrix products, arithmetic and copies ran while one was open for 1% of the time, Pallas kernels for 32%

profile of v11, /device:TPU:0, one launch (start us, length us, event | category | flops | bytes accessed | tf_op | source)
XLA Modules:
  0.0 97.4 jit_solution(3198539267846377722)
XLA Ops:
  0.9 0.7 pad_add_fusion.scal
  1.7 0.8 fusion.13
  2.4 0.5 collective-permute-start.1
  2.9 3.6 %collective-permute-start.2 = (f32[8,128]{1,0:T(8,128)S(1)}, f32[8,128]{1,0:T(8,128)S(1)}, u32[]{:S(2)}, u32[]{:S(2)}) collective-permute-start(f32[8,128]{1,0:T(8,128)S(1)} %slice_bitcast_fusion.1), channel_id=1, source_target_pairs={{0,28},{4,8},{8,4},{12,16},{16,12},{20,24},{24,20},{28,0},{1,29},{... | collective-permute-start | bytes 12296 | tf_op jit(solution)/shard_map/ppermute | solution.py:547
  6.5 4.8 %first_main.1 = (f32[72,128]{1,0:T(8,128)S(1)}, f32[64,2,128,128]{3,2,1,0:T(8,128)S(1)}) custom-call(s32[4]{0:T(128)S(1)} %pad_add_fusion.scal, s32[64,2,128,128]{3,2,1,0:T(8,128)} %hbm.1, f32[64,128]{1,0:T(8,128)S(1)} %get-tuple-element.136.mask), custom_call_target="tpu_custom_call" | custom-call | tf_op jit(solution)/shard_map/first_main/pallas_call | solution.py:47
  11.3 1.4 %first_edge.1 = (f32[72,128]{1,0:T(8,128)S(1)}, f32[16,128]{1,0:T(8,128)S(1)}) custom-call(s32[4]{0:T(128)S(1)} %pad_add_fusion.scal, f32[64,2,128,128]{3,2,1,0:T(8,128)S(1)} %get-tuple-element.90.kept, f32[72,128]{1,0:T(8,128)S(1)} %pad_maximum_fusion.u_ref.mask.refs_0_, f32[72,128]{1,0:T(8,128)S(1)} %get-tuple-element.91.inner_v), custom_call_target="tpu_custom_call" | custom-call | tf_op jit(solution)/shard_map/first_edge/pallas_call | solution.py:47
  12.9 3.4 %ratio.3 = (bf16[64,128,256]{2,1,0:T(8,128)(2,1)S(1)}, bf16[64,128,256]{2,1,0:T(8,128)(2,1)S(1)}, f32[72,128]{1,0:T(8,128)S(1)}) custom-call(s32[4]{0:T(128)S(1)} %pad_add_fusion.scal, f32[64,2,128,128]{3,2,1,0:T(8,128)S(1)} %get-tuple-element.90.kept, f32[32,8192]{1,0:T(8,128)S(1)} %copy-done, f32[32,8192]{1,0:T(8,128)S(1)} %copy-done.1, ...), custom_call_target="tpu_custom_call" | custom-call | tf_op jit(solution)/shard_map/ratio/pallas_call | solution.py:47
  16.3 0.4 collective-permute-done.3
  16.8 1.6 %collective-permute-start.5 = (f32[72,128]{1,0:T(8,128)S(1)}, f32[72,128]{1,0:T(8,128)S(1)}, u32[]{:S(2)}, u32[]{:S(2)}) collective-permute-start(f32[72,128]{1,0:T(8,128)S(1)} %pad_maximum_fusion.1.after.refs_0_), channel_id=1, source_target_pairs={{0,1},{1,0},{2,3},{3,2},{4,5},{5,4},{6,7},{7,6},{8,9},{9,8},{10,11... | collective-permute-start | bytes 110600 | tf_op jit(solution)/shard_map/ppermute | solution.py:541
  18.4 2.8 %collective-permute-start.6 = (f32[72,128]{1,0:T(8,128)S(1)}, f32[72,128]{1,0:T(8,128)S(1)}, u32[]{:S(2)}, u32[]{:S(2)}) collective-permute-start(f32[72,128]{1,0:T(8,128)S(1)} %pad_maximum_fusion.1.after.refs_0_), channel_id=1, source_target_pairs={{0,2},{1,3},{2,0},{3,1},{4,6},{5,7},{6,4},{7,5},{8,10},{9,11},{10,... | collective-permute-start | bytes 110600 | tf_op jit(solution)/shard_map/ppermute | solution.py:541
  21.2 2.2 %ratio.4 = (bf16[64,128,256]{2,1,0:T(8,128)(2,1)S(1)}, bf16[64,128,256]{2,1,0:T(8,128)(2,1)S(1)}) custom-call(s32[4]{0:T(128)S(1)} %pad_add_fusion.scal, f32[64,2,128,128]{3,2,1,0:T(8,128)S(1)} %get-tuple-element.90.kept, f32[32,8192]{1,0:T(8,128)S(1)} %copy-done, f32[32,8192]{1,0:T(8,128)S(1)} %copy-done.1, ...), custom_call_target="tpu_custom_call", output_to_operand_aliasing={{0}: (5, {}), {1}: (6, {})} | custom-call | tf_op jit(solution)/shard_map/ratio/pallas_call | solution.py:47
  23.4 0.6 collective-permute-done.6.refs_2_
  24.0 2.9 %collective-permute-done.7.refs_3_ = f32[72,128]{1,0:T(8,128)S(1)} collective-permute-done((f32[72,128]{1,0:T(8,128)S(1)}, f32[72,128]{1,0:T(8,128)S(1)}, u32[]{:S(2)}, u32[]{:S(2)}) %collective-permute-start.7) | collective-permute-done | bytes 36896 | tf_op jit(solution)/shard_map/ppermute | solution.py:541
  26.9 1.4 %cover_edge.2 = (f32[72,128]{1,0:T(8,128)S(1)}, f32[16,128]{1,0:T(8,128)S(1)}, f32[72,128]{1,0:T(8,128)S(1)}) custom-call(s32[4]{0:T(128)S(1)} %pad_add_fusion.scal, f32[64,2,128,128]{3,2,1,0:T(8,128)S(1)} %get-tuple-element.90.kept, f32[72,128]{1,0:T(8,128)S(1)} %pad_maximum_fusion.u_ref.mask.refs_0_, f32[72,128]{1,0:T(8,128)S(1)} %pad_maximum_fusion.1.after.refs_0_, ...), custom_call_target="tpu_custom_call" | custom-call | tf_op jit(solution)/shard_map/cover_edge/pallas_call | solution.py:47
  28.3 0.6 collective-permute-start.8
  28.9 1.3 %collective-permute-start.9 = (f32[16,128]{1,0:T(8,128)S(1)}, f32[16,128]{1,0:T(8,128)S(1)}, u32[]{:S(2)}, u32[]{:S(2)}) collective-permute-start(f32[16,128]{1,0:T(8,128)S(1)} %get-tuple-element.102), channel_id=1, source_target_pairs={{0,4},{4,0},{8,12},{12,8},{16,20},{20,16},{24,28},{28,24},{1,5},{5... | collective-permute-start | bytes 24584 | tf_op jit(solution)/shard_map/ppermute | solution.py:546
  30.2 2.8 %cover_main.2 = f32[72,128]{1,0:T(8,128)S(1)} custom-call(s32[4]{0:T(128)S(1)} %pad_add_fusion.scal, f32[64,2,128,128]{3,2,1,0:T(8,128)S(1)} %get-tuple-element.90.kept, f32[72,128]{1,0:T(8,128)S(1)} %get-tuple-element.100.u_ref.refs_1_, f32[72,128]{1,0:T(8,128)S(1)} %get-tuple-element.101.edge_v), custom_call_target="tpu_custom_call" | custom-call | tf_op jit(solution)/shard_map/cover_main/pallas_call | solution.py:47
  33.1 1.0 %collective-permute-start.11 = (f32[72,128]{1,0:T(8,128)S(1)}, f32[72,128]{1,0:T(8,128)S(1)}, u32[]{:S(2)}, u32[]{:S(2)}) collective-permute-start(f32[72,128]{1,0:T(8,128)S(1)} %pad_maximum_fusion.2.refs_0_), channel_id=1, source_target_pairs={{0,2},{1,3},{2,0},{3,1},{4,6},{5,7},{6,4},{7,5},{8,10},{9,11},{10,... | collective-permute-start | bytes 110600 | tf_op jit(solution)/shard_map/ppermute | solution.py:541
  34.1 3.4 %collective-permute-start.12 = (f32[72,128]{1,0:T(8,128)S(1)}, f32[72,128]{1,0:T(8,128)S(1)}, u32[]{:S(2)}, u32[]{:S(2)}) collective-permute-start(f32[72,128]{1,0:T(8,128)S(1)} %pad_maximum_fusion.2.refs_0_), channel_id=1, source_target_pairs={{0,3},{1,2},{2,1},{3,0},{4,7},{5,6},{6,5},{7,4},{8,11},{9,10},{10,... | collective-permute-start | bytes 110600 | tf_op jit(solution)/shard_map/ppermute | solution.py:541
  37.5 0.2 collective-permute-start
  37.8 1.1 %collective-permute-done.11.refs_2_ = f32[72,128]{1,0:T(8,128)S(1)} collective-permute-done((f32[72,128]{1,0:T(8,128)S(1)}, f32[72,128]{1,0:T(8,128)S(1)}, u32[]{:S(2)}, u32[]{:S(2)}) %collective-permute-start.11) | collective-permute-done | bytes 36896 | tf_op jit(solution)/shard_map/ppermute | solution.py:541
  38.9 1.1 %collective-permute-done.12.refs_3_ = f32[72,128]{1,0:T(8,128)S(1)} collective-permute-done((f32[72,128]{1,0:T(8,128)S(1)}, f32[72,128]{1,0:T(8,128)S(1)}, u32[]{:S(2)}, u32[]{:S(2)}) %collective-permute-start.12) | collective-permute-done | bytes 36896 | tf_op jit(solution)/shard_map/ppermute | solution.py:541
  39.9 1.4 %cover_edge.3 = (f32[72,128]{1,0:T(8,128)S(1)}, f32[16,128]{1,0:T(8,128)S(1)}, f32[72,128]{1,0:T(8,128)S(1)}) custom-call(s32[4]{0:T(128)S(1)} %pad_add_fusion.scal, f32[64,2,128,128]{3,2,1,0:T(8,128)S(1)} %get-tuple-element.90.kept, f32[72,128]{1,0:T(8,128)S(1)} %pad_maximum_fusion.u_ref.mask.refs_0_, f32[72,128]{1,0:T(8,128)S(1)} %pad_maximum_fusion.2.refs_0_, ...), custom_call_target="tpu_custom_call" | custom-call | tf_op jit(solution)/shard_map/cover_edge/pallas_call | solution.py:47
  41.4 1.3 %collective-permute-start.14 = (f32[16,128]{1,0:T(8,128)S(1)}, f32[16,128]{1,0:T(8,128)S(1)}, u32[]{:S(2)}, u32[]{:S(2)}) collective-permute-start(f32[16,128]{1,0:T(8,128)S(1)} %get-tuple-element.105), channel_id=1, source_target_pairs={{0,4},{4,0},{8,12},{12,8},{16,20},{20,16},{24,28},{28,24},{1,5},{5... | collective-permute-start | bytes 24584 | tf_op jit(solution)/shard_map/ppermute | solution.py:546
  42.7 2.8 %cover_main.3 = f32[72,128]{1,0:T(8,128)S(1)} custom-call(s32[4]{0:T(128)S(1)} %pad_add_fusion.scal, f32[64,2,128,128]{3,2,1,0:T(8,128)S(1)} %get-tuple-element.90.kept, f32[72,128]{1,0:T(8,128)S(1)} %get-tuple-element.103.u_ref.refs_2_, f32[72,128]{1,0:T(8,128)S(1)} %get-tuple-element.104.edge_v), custom_call_target="tpu_custom_call" | custom-call | tf_op jit(solution)/shard_map/cover_main/pallas_call | solution.py:47
  45.6 0.6 collective-permute-start.15
  46.2 3.2 %collective-permute-start.16 = (f32[72,128]{1,0:T(8,128)S(1)}, f32[72,128]{1,0:T(8,128)S(1)}, u32[]{:S(2)}, u32[]{:S(2)}) collective-permute-start(f32[72,128]{1,0:T(8,128)S(1)} %pad_maximum_fusion.3.after.refs_0_), channel_id=1, source_target_pairs={{0,2},{1,3},{2,0},{3,1},{4,6},{5,7},{6,4},{7,5},{8,10},{9,11},{10,... | collective-permute-start | bytes 110600 | tf_op jit(solution)/shard_map/ppermute | solution.py:541
  49.5 0.6 collective-permute-start.17
  50.1 2.0 %ratio.5 = (bf16[64,128,256]{2,1,0:T(8,128)(2,1)S(1)}, bf16[64,128,256]{2,1,0:T(8,128)(2,1)S(1)}) custom-call(s32[4]{0:T(128)S(1)} %pad_add_fusion.scal, f32[64,2,128,128]{3,2,1,0:T(8,128)S(1)} %get-tuple-element.90.kept, f32[32,8192]{1,0:T(8,128)S(1)} %copy-done, ...), custom_call_target="tpu_custom_call", output_to_operand_aliasing={{0}: (5, {}), {1}: (6, {})} | custom-call | tf_op jit(solution)/shard_map/ratio/pallas_call | solution.py:47
  52.1 3.1 %collective-permute-done.17.refs_3_ = f32[72,128]{1,0:T(8,128)S(1)} collective-permute-done((f32[72,128]{1,0:T(8,128)S(1)}, f32[72,128]{1,0:T(8,128)S(1)}, u32[]{:S(2)}, u32[]{:S(2)}) %collective-permute-start.17) | collective-permute-done | bytes 36896 | tf_op jit(solution)/shard_map/ppermute | solution.py:541
  55.2 2.3 %numer_first.1 = (f32[72,128]{1,0:T(8,128)S(1)}, f32[9,32,128]{2,1,0:T(8,128)S(1)}, f32[16,32,128]{2,1,0:T(8,128)S(1)}) custom-call(s32[4]{0:T(128)S(1)} %pad_add_fusion.scal, bf16[64,128,256]{2,1,0:T(8,128)(2,1)S(1)} %get-tuple-element.107.hi_ref, bf16[64,128,256]{2,1,0:T(8,128)(2,1)S(1)} %get-tuple-element.108.lo_ref, f32[32,8192]{1,0:T(8,128)S(1)} %copy-done, ...), custom_call_target="tpu_custom_call" | custom-call | tf_op jit(solution)/shard_map/numer_first/pallas_call | solution.py:47
  57.7 4.3 %numer_col.1 = (f32[8,128]{1,0:T(8,128)S(1)}, f32[16,32,128]{2,1,0:T(8,128)S(1)}, f32[16,32,128]{2,1,0:T(8,128)S(1)}, f32[16,32,128]{2,1,0:T(8,128)S(1)}, f32[16,32,128]{2,1,0:T(8,128)S(1)}) custom-call(s32[4]{0:T(128)S(1)} %pad_add_fusion.scal, bf16[64,128,256]{2,1,0:T(8,128)(2,1)S(1)} %get-tuple-element.107.hi_ref, ...), custom_call_target="tpu_custom_call" | custom-call | tf_op jit(solution)/shard_map/numer_col/pallas_call | solution.py:47
  62.0 1.0 %collective-permute-done.18 = f32[9,32,128]{2,1,0:T(8,128)S(1)} collective-permute-done((f32[9,32,128]{2,1,0:T(8,128)S(1)}, f32[9,32,128]{2,1,0:T(8,128)S(1)}, u32[]{:S(2)}, u32[]{:S(2)}) %collective-permute-start.18) | collective-permute-done | bytes 147488 | tf_op jit(solution)/shard_map/ppermute | solution.py:632
  63.2 1.0 %collective-permute-start.23 = (f32[16,32,128]{2,1,0:T(8,128)S(1)}, f32[16,32,128]{2,1,0:T(8,128)S(1)}, u32[]{:S(2)}, u32[]{:S(2)}) collective-permute-start(f32[16,32,128]{2,1,0:T(8,128)S(1)} %get-tuple-element.128.after), channel_id=1, source_target_pairs={{0,1},{1,0},{2,3},{3,2},{4,5},{5,4},{6,7},{7,6},{8,9},{9,8},{10,11... | collective-permute-start | bytes 786440 | tf_op jit(solution)/shard_map/ppermute | solution.py:541
  64.2 4.3 %numer_row.1 = (f32[16,32,128]{2,1,0:T(8,128)S(1)}, f32[16,32,128]{2,1,0:T(8,128)S(1)}, f32[16,32,128]{2,1,0:T(8,128)S(1)}) custom-call(s32[4]{0:T(128)S(1)} %pad_add_fusion.scal, bf16[64,128,256]{2,1,0:T(8,128)(2,1)S(1)} %get-tuple-element.107.hi_ref, bf16[64,128,256]{2,1,0:T(8,128)(2,1)S(1)} %get-tuple-element.108.lo_ref, ...), custom_call_target="tpu_custom_call" | custom-call | tf_op jit(solution)/shard_map/numer_row/pallas_call | solution.py:47
  68.5 0.7 collective-permute-start.20
  69.2 0.7 coefficient.2
  69.9 0.6 collective-permute-start.22
  70.5 0.9 coefficient.3
  71.4 1.6 %collective-permute-start.21 = (f32[16,32,128]{2,1,0:T(8,128)S(1)}, f32[16,32,128]{2,1,0:T(8,128)S(1)}, u32[]{:S(2)}, u32[]{:S(2)}) collective-permute-start(f32[16,32,128]{2,1,0:T(8,128)S(1)} %get-tuple-element.119), channel_id=1, source_target_pairs={{0,1},{1,0},{2,3},{3,2},{4,5},{5,4},{6,7},{7,6},{8,9},{9,8},{10,11... | collective-permute-start | bytes 786440 | tf_op jit(solution)/shard_map/ppermute | solution.py:541
  73.0 3.3 %collective-permute-start.24 = (f32[16,32,128]{2,1,0:T(8,128)S(1)}, f32[16,32,128]{2,1,0:T(8,128)S(1)}, u32[]{:S(2)}, u32[]{:S(2)}) collective-permute-start(f32[16,32,128]{2,1,0:T(8,128)S(1)} %add.81), channel_id=1, source_target_pairs={{0,3},{1,2},{2,1},{3,0},{4,7},{5,6},{6,5},{7,4},{8,11},{9,10},{10,... | collective-permute-start | bytes 786440 | tf_op jit(solution)/shard_map/ppermute | solution.py:541
  76.3 3.0 %collective-permute-done.20.refs_2_ = f32[16,32,128]{2,1,0:T(8,128)S(1)} collective-permute-done((f32[16,32,128]{2,1,0:T(8,128)S(1)}, f32[16,32,128]{2,1,0:T(8,128)S(1)}, u32[]{:S(2)}, u32[]{:S(2)}) %collective-permute-start.20) | collective-permute-done | bytes 262176 | tf_op jit(solution)/shard_map/ppermute | solution.py:541
  79.4 9.6 %all-gather = f32[64,128]{1,0:T(8,128)S(1)} all-gather(f32[8,128]{1,0:T(8,128)S(1)} %get-tuple-element.115), channel_id=2, replica_groups=mesh['genome'=8,'offset'=4] {'genome'}, dimensions={0}, use_global_device_ids=true | all-gather | bytes 36864 | tf_op jit(solution)/shard_map/all_gather | solution.py:652
  89.0 1.3 %collective-permute-done.21.refs_1_ = f32[16,32,128]{2,1,0:T(8,128)S(1)} collective-permute-done((f32[16,32,128]{2,1,0:T(8,128)S(1)}, f32[16,32,128]{2,1,0:T(8,128)S(1)}, u32[]{:S(2)}, u32[]{:S(2)}) %collective-permute-start.21) | collective-permute-done | bytes 262176 | tf_op jit(solution)/shard_map/ppermute | solution.py:541
  90.3 1.3 %update.2 = f32[32,2048]{1,0:T(8,128)} custom-call(s32[4]{0:T(128)S(1)} %pad_add_fusion.scal, f32[8,128]{1,0:T(8,128)S(1)} %bitcast_reduce_fusion.sums, f32[16,32,128]{2,1,0:T(8,128)S(1)} %get-tuple-element.116.times, f32[16,32,128]{2,1,0:T(8,128)S(1)} %get-tuple-element.117.plus, f32[16,32,128]{2,1,0:T(8,128)S(1)} %get-tuple-element.118.refs_0_, ...), custom_call_target="tpu_custom_call" | custom-call | tf_op jit(solution)/shard_map/update/pallas_call | solution.py:47
  91.6 0.6 multiply_bitcast_fusion
  92.3 3.9 %collective-permute-done.24.refs_2_ = f32[16,32,128]{2,1,0:T(8,128)S(1)} collective-permute-done((f32[16,32,128]{2,1,0:T(8,128)S(1)}, f32[16,32,128]{2,1,0:T(8,128)S(1)}, u32[]{:S(2)}, u32[]{:S(2)}) %collective-permute-start.24) | collective-permute-done | bytes 262176 | tf_op jit(solution)/shard_map/ppermute | solution.py:541
  96.1 1.3 %update.3 = f32[32,2048]{1,0:T(8,128)} custom-call(s32[4]{0:T(128)S(1)} %pad_add_fusion.scal, f32[8,128]{1,0:T(8,128)S(1)} %bitcast_reduce_fusion.sums, f32[16,32,128]{2,1,0:T(8,128)S(1)} %get-tuple-element.120.times, f32[16,32,128]{2,1,0:T(8,128)S(1)} %get-tuple-element.121.plus, f32[16,32,128]{2,1,0:T(8,128)S(1)} %get-tuple-element.126.refs_0_, ...), custom_call_target="tpu_custom_call" | custom-call | tf_op jit(solution)/shard_map/update/pallas_call | solution.py:47
  (56 shorter events, 1.1 us)
Async XLA Ops:
  2.4 8.8 %collective-permute-start.1 = (f32[8,128]{1,0:T(8,128)S(1)}, f32[8,128]{1,0:T(8,128)S(1)}, u32[]{:S(2)}, u32[]{:S(2)}) collective-permute-start(f32[8,128]{1,0:T(8,128)S(1)} %slice_bitcast_fusion.1), channel_id=1, source_target_pairs={{0,4},{4,0},{8,12},{12,8},{16,20},{20,16},{24,28},{28,24},{1,5},{5... | collective-permute-start | bytes 12296 | tf_op jit(solution)/shard_map/ppermute | solution.py:546
  2.9 8.4 %collective-permute-start.2 = (f32[8,128]{1,0:T(8,128)S(1)}, f32[8,128]{1,0:T(8,128)S(1)}, u32[]{:S(2)}, u32[]{:S(2)}) collective-permute-start(f32[8,128]{1,0:T(8,128)S(1)} %slice_bitcast_fusion.1), channel_id=1, source_target_pairs={{0,28},{4,8},{8,4},{12,16},{16,12},{20,24},{24,20},{28,0},{1,29},{... | collective-permute-start | bytes 12296 | tf_op jit(solution)/shard_map/ppermute | solution.py:547
  11.3 1.5 %copy-start = (f32[32,8192]{1,0:T(8,128)S(1)}, f32[32,8192]{1,0:T(8,128)}, u32[]{:S(2)}) copy-start(f32[32,8192]{1,0:T(8,128)} %other.1) | copy-start | bytes 3145732
  11.3 1.5 %copy-start.1 = (f32[32,8192]{1,0:T(8,128)S(1)}, f32[32,8192]{1,0:T(8,128)}, u32[]{:S(2)}) copy-start(f32[32,8192]{1,0:T(8,128)} %old_ref.3) | copy-start | bytes 3145732
  12.7 4.0 %collective-permute-start.3 = (f32[16,128]{1,0:T(8,128)S(1)}, f32[16,128]{1,0:T(8,128)S(1)}, u32[]{:S(2)}, u32[]{:S(2)}) collective-permute-start(f32[16,128]{1,0:T(8,128)S(1)} %get-tuple-element.96), channel_id=1, source_target_pairs={{0,28},{4,8},{8,4},{12,16},{16,12},{20,24},{24,20},{28,0},{1,29},{... | collective-permute-start | bytes 24584 | tf_op jit(solution)/shard_map/ppermute | solution.py:547
  12.8 4.0 %collective-permute-start.4 = (f32[16,128]{1,0:T(8,128)S(1)}, f32[16,128]{1,0:T(8,128)S(1)}, u32[]{:S(2)}, u32[]{:S(2)}) collective-permute-start(f32[16,128]{1,0:T(8,128)S(1)} %get-tuple-element.96), channel_id=1, source_target_pairs={{0,4},{4,0},{8,12},{12,8},{16,20},{20,16},{24,28},{28,24},{1,5},{5... | collective-permute-start | bytes 24584 | tf_op jit(solution)/shard_map/ppermute | solution.py:546
  16.8 6.6 %collective-permute-start.5 = (f32[72,128]{1,0:T(8,128)S(1)}, f32[72,128]{1,0:T(8,128)S(1)}, u32[]{:S(2)}, u32[]{:S(2)}) collective-permute-start(f32[72,128]{1,0:T(8,128)S(1)} %pad_maximum_fusion.1.after.refs_0_), channel_id=1, source_target_pairs={{0,1},{1,0},{2,3},{3,2},{4,5},{5,4},{6,7},{7,6},{8,9},{9,8},{10,11... | collective-permute-start | bytes 110600 | tf_op jit(solution)/shard_map/ppermute | solution.py:541
  18.4 5.6 %collective-permute-start.6 = (f32[72,128]{1,0:T(8,128)S(1)}, f32[72,128]{1,0:T(8,128)S(1)}, u32[]{:S(2)}, u32[]{:S(2)}) collective-permute-start(f32[72,128]{1,0:T(8,128)S(1)} %pad_maximum_fusion.1.after.refs_0_), channel_id=1, source_target_pairs={{0,2},{1,3},{2,0},{3,1},{4,6},{5,7},{6,4},{7,5},{8,10},{9,11},{10,... | collective-permute-start | bytes 110600 | tf_op jit(solution)/shard_map/ppermute | solution.py:541
  21.2 5.8 %collective-permute-start.7 = (f32[72,128]{1,0:T(8,128)S(1)}, f32[72,128]{1,0:T(8,128)S(1)}, u32[]{:S(2)}, u32[]{:S(2)}) collective-permute-start(f32[72,128]{1,0:T(8,128)S(1)} %pad_maximum_fusion.1.after.refs_0_), channel_id=1, source_target_pairs={{0,3},{1,2},{2,1},{3,0},{4,7},{5,6},{6,5},{7,4},{8,11},{9,10},{10,... | collective-permute-start | bytes 110600 | tf_op jit(solution)/shard_map/ppermute | solution.py:541
  28.3 4.7 %collective-permute-start.8 = (f32[16,128]{1,0:T(8,128)S(1)}, f32[16,128]{1,0:T(8,128)S(1)}, u32[]{:S(2)}, u32[]{:S(2)}) collective-permute-start(f32[16,128]{1,0:T(8,128)S(1)} %get-tuple-element.102), channel_id=1, source_target_pairs={{0,28},{4,8},{8,4},{12,16},{16,12},{20,24},{24,20},{28,0},{1,29},{... | collective-permute-start | bytes 24584 | tf_op jit(solution)/shard_map/ppermute | solution.py:547
  28.9 4.1 %collective-permute-start.9 = (f32[16,128]{1,0:T(8,128)S(1)}, f32[16,128]{1,0:T(8,128)S(1)}, u32[]{:S(2)}, u32[]{:S(2)}) collective-permute-start(f32[16,128]{1,0:T(8,128)S(1)} %get-tuple-element.102), channel_id=1, source_target_pairs={{0,4},{4,0},{8,12},{12,8},{16,20},{20,16},{24,28},{28,24},{1,5},{5... | collective-permute-start | bytes 24584 | tf_op jit(solution)/shard_map/ppermute | solution.py:546
  33.1 4.7 %collective-permute-start.10 = (f32[72,128]{1,0:T(8,128)S(1)}, f32[72,128]{1,0:T(8,128)S(1)}, u32[]{:S(2)}, u32[]{:S(2)}) collective-permute-start(f32[72,128]{1,0:T(8,128)S(1)} %pad_maximum_fusion.2.refs_0_), channel_id=1, source_target_pairs={{0,1},{1,0},{2,3},{3,2},{4,5},{5,4},{6,7},{7,6},{8,9},{9,8},{10,11... | collective-permute-start | bytes 110600 | tf_op jit(solution)/shard_map/ppermute | solution.py:541
  33.1 5.7 %collective-permute-start.11 = (f32[72,128]{1,0:T(8,128)S(1)}, f32[72,128]{1,0:T(8,128)S(1)}, u32[]{:S(2)}, u32[]{:S(2)}) collective-permute-start(f32[72,128]{1,0:T(8,128)S(1)} %pad_maximum_fusion.2.refs_0_), channel_id=1, source_target_pairs={{0,2},{1,3},{2,0},{3,1},{4,6},{5,7},{6,4},{7,5},{8,10},{9,11},{10,... | collective-permute-start | bytes 110600 | tf_op jit(solution)/shard_map/ppermute | solution.py:541
  34.1 5.8 %collective-permute-start.12 = (f32[72,128]{1,0:T(8,128)S(1)}, f32[72,128]{1,0:T(8,128)S(1)}, u32[]{:S(2)}, u32[]{:S(2)}) collective-permute-start(f32[72,128]{1,0:T(8,128)S(1)} %pad_maximum_fusion.2.refs_0_), channel_id=1, source_target_pairs={{0,3},{1,2},{2,1},{3,0},{4,7},{5,6},{6,5},{7,4},{8,11},{9,10},{10,... | collective-permute-start | bytes 110600 | tf_op jit(solution)/shard_map/ppermute | solution.py:541
  37.5 12.5 %collective-permute-start = (f32[32,1024]{1,0:T(8,128)S(1)}, f32[32,1024]{1,0:T(8,128)S(1)}, u32[]{:S(2)}, u32[]{:S(2)}) collective-permute-start(f32[32,1024]{1,0:T(8,128)S(1)} %slice.207), channel_id=1, source_target_pairs={{0,28},{4,0},{8,4},{12,8},{16,12},{20,16},{24,20},{28,24},{1,29},{... | collective-permute-start | bytes 393224 | tf_op jit(solution)/shard_map/ppermute | solution.py:594
  41.3 4.2 %collective-permute-start.13 = (f32[16,128]{1,0:T(8,128)S(1)}, f32[16,128]{1,0:T(8,128)S(1)}, u32[]{:S(2)}, u32[]{:S(2)}) collective-permute-start(f32[16,128]{1,0:T(8,128)S(1)} %get-tuple-element.105), channel_id=1, source_target_pairs={{0,28},{4,8},{8,4},{12,16},{16,12},{20,24},{24,20},{28,0},{1,29},{... | collective-permute-start | bytes 24584 | tf_op jit(solution)/shard_map/ppermute | solution.py:547
  41.4 4.2 %collective-permute-start.14 = (f32[16,128]{1,0:T(8,128)S(1)}, f32[16,128]{1,0:T(8,128)S(1)}, u32[]{:S(2)}, u32[]{:S(2)}) collective-permute-start(f32[16,128]{1,0:T(8,128)S(1)} %get-tuple-element.105), channel_id=1, source_target_pairs={{0,4},{4,0},{8,12},{12,8},{16,20},{20,16},{24,28},{28,24},{1,5},{5... | collective-permute-start | bytes 24584 | tf_op jit(solution)/shard_map/ppermute | solution.py:546
  45.6 6.5 %collective-permute-start.15 = (f32[72,128]{1,0:T(8,128)S(1)}, f32[72,128]{1,0:T(8,128)S(1)}, u32[]{:S(2)}, u32[]{:S(2)}) collective-permute-start(f32[72,128]{1,0:T(8,128)S(1)} %pad_maximum_fusion.3.after.refs_0_), channel_id=1, source_target_pairs={{0,1},{1,0},{2,3},{3,2},{4,5},{5,4},{6,7},{7,6},{8,9},{9,8},{10,11... | collective-permute-start | bytes 110600 | tf_op jit(solution)/shard_map/ppermute | solution.py:541
  46.2 5.8 %collective-permute-start.16 = (f32[72,128]{1,0:T(8,128)S(1)}, f32[72,128]{1,0:T(8,128)S(1)}, u32[]{:S(2)}, u32[]{:S(2)}) collective-permute-start(f32[72,128]{1,0:T(8,128)S(1)} %pad_maximum_fusion.3.after.refs_0_), channel_id=1, source_target_pairs={{0,2},{1,3},{2,0},{3,1},{4,6},{5,7},{6,4},{7,5},{8,10},{9,11},{10,... | collective-permute-start | bytes 110600 | tf_op jit(solution)/shard_map/ppermute | solution.py:541
  49.5 5.8 %collective-permute-start.17 = (f32[72,128]{1,0:T(8,128)S(1)}, f32[72,128]{1,0:T(8,128)S(1)}, u32[]{:S(2)}, u32[]{:S(2)}) collective-permute-start(f32[72,128]{1,0:T(8,128)S(1)} %pad_maximum_fusion.3.after.refs_0_), channel_id=1, source_target_pairs={{0,3},{1,2},{2,1},{3,0},{4,7},{5,6},{6,5},{7,4},{8,11},{9,10},{10,... | collective-permute-start | bytes 110600 | tf_op jit(solution)/shard_map/ppermute | solution.py:541
  57.6 5.5 %collective-permute-start.18 = (f32[9,32,128]{2,1,0:T(8,128)S(1)}, f32[9,32,128]{2,1,0:T(8,128)S(1)}, u32[]{:S(2)}, u32[]{:S(2)}) collective-permute-start(f32[9,32,128]{2,1,0:T(8,128)S(1)} %get-tuple-element.112), channel_id=1, source_target_pairs={{0,4},{4,8},{8,12},{12,16},{16,20},{20,24},{24,28},{28,0},{1,5},{5... | collective-permute-start | bytes 442376 | tf_op jit(solution)/shard_map/ppermute | solution.py:632
  57.6 10.9 %collective-permute-start.19 = (f32[16,32,128]{2,1,0:T(8,128)S(1)}, f32[16,32,128]{2,1,0:T(8,128)S(1)}, u32[]{:S(2)}, u32[]{:S(2)}) collective-permute-start(f32[16,32,128]{2,1,0:T(8,128)S(1)} %get-tuple-element.114), channel_id=1, source_target_pairs={{0,1},{1,0},{2,3},{3,2},{4,5},{5,4},{6,7},{7,6},{8,9},{9,8},{10,11... | collective-permute-start | bytes 786440 | tf_op jit(solution)/shard_map/ppermute | solution.py:541
  63.2 9.8 %collective-permute-start.23 = (f32[16,32,128]{2,1,0:T(8,128)S(1)}, f32[16,32,128]{2,1,0:T(8,128)S(1)}, u32[]{:S(2)}, u32[]{:S(2)}) collective-permute-start(f32[16,32,128]{2,1,0:T(8,128)S(1)} %get-tuple-element.128.after), channel_id=1, source_target_pairs={{0,1},{1,0},{2,3},{3,2},{4,5},{5,4},{6,7},{7,6},{8,9},{9,8},{10,11... | collective-permute-start | bytes 786440 | tf_op jit(solution)/shard_map/ppermute | solution.py:541
  68.5 10.8 %collective-permute-start.20 = (f32[16,32,128]{2,1,0:T(8,128)S(1)}, f32[16,32,128]{2,1,0:T(8,128)S(1)}, u32[]{:S(2)}, u32[]{:S(2)}) collective-permute-start(f32[16,32,128]{2,1,0:T(8,128)S(1)} %add.77), channel_id=1, source_target_pairs={{0,3},{1,2},{2,1},{3,0},{4,7},{5,6},{6,5},{7,4},{8,11},{9,10},{10,... | collective-permute-start | bytes 786440 | tf_op jit(solution)/shard_map/ppermute | solution.py:541
  69.9 22.3 %collective-permute-start.22 = (f32[16,32,128]{2,1,0:T(8,128)S(1)}, f32[16,32,128]{2,1,0:T(8,128)S(1)}, u32[]{:S(2)}, u32[]{:S(2)}) collective-permute-start(f32[16,32,128]{2,1,0:T(8,128)S(1)} %get-tuple-element.127), channel_id=1, source_target_pairs={{0,1},{1,0},{2,3},{3,2},{4,5},{5,4},{6,7},{7,6},{8,9},{9,8},{10,11... | collective-permute-start | bytes 786440 | tf_op jit(solution)/shard_map/ppermute | solution.py:541
  71.4 18.9 %collective-permute-start.21 = (f32[16,32,128]{2,1,0:T(8,128)S(1)}, f32[16,32,128]{2,1,0:T(8,128)S(1)}, u32[]{:S(2)}, u32[]{:S(2)}) collective-permute-start(f32[16,32,128]{2,1,0:T(8,128)S(1)} %get-tuple-element.119), channel_id=1, source_target_pairs={{0,1},{1,0},{2,3},{3,2},{4,5},{5,4},{6,7},{7,6},{8,9},{9,8},{10,11... | collective-permute-start | bytes 786440 | tf_op jit(solution)/shard_map/ppermute | solution.py:541
  73.0 23.1 %collective-permute-start.24 = (f32[16,32,128]{2,1,0:T(8,128)S(1)}, f32[16,32,128]{2,1,0:T(8,128)S(1)}, u32[]{:S(2)}, u32[]{:S(2)}) collective-permute-start(f32[16,32,128]{2,1,0:T(8,128)S(1)} %add.81), channel_id=1, source_target_pairs={{0,3},{1,2},{2,1},{3,0},{4,7},{5,6},{6,5},{7,4},{8,11},{9,10},{10,... | collective-permute-start | bytes 786440 | tf_op jit(solution)/shard_map/ppermute | solution.py:541

commit v12 on v9

--- a/solution.py
+++ b/solution.py
@@ -251,7 +251,7 @@
                 lo_out[i, :, s * tile : (s + 1) * tile] = r_lo
             return carry
 
-        lax.fori_loop(start, start + count, body, 0, unroll=4)
+        lax.fori_loop(start, start + count, body, 0, unroll=8)
 
     by_diagonal(offs, slots, go)
 
@@ -301,7 +301,7 @@
             acc[i + offs[s] - shift] += cols[:, s * tile : (s + 1) * tile]
         return carry
 
-    lax.fori_loop(0, count, body, 0, unroll=4)
+    lax.fori_loop(0, count, body, 0, unroll=8)
 
 
 def row_pieces(scal, offs, g_ref, hi_ref, lo_ref, u_ref, order, outs):

time: 94 us -> 93.1 us (level)
  Pallas kernels: 37.4 us -> 34.4 us
  waiting for transfers between devices: 13.9 us -> 16.8 us
    pallas_call x16, Pallas kernels: 37.4 us -> 34.4 us  [kernel_call(): pl.pallas_call(body, grid_spec=pltpu.PrefetchScalarGridSpec(num_scalar_pr...]
    ppermute x4, waiting for transfers between devices: 0.43 us -> 1.52 us  [both_sides(): lax.ppermute(x, 'genome', [(i, ((i + 1 ^ 1) - 1) % size) for i in range(s...]
    ppermute x1, waiting for transfers between devices: 0.08 us -> 1.06 us  [per_device(): arrived = lax.ppermute(tail, 'genome', right)]
  transfers between devices with their start and end apart: 25 -> 25, of which waited for: 11 -> 12; matrix products, arithmetic and copies ran while one was open for 1% -> 1% of each run, Pallas kernels for 33% -> 30%
where the time goes in v12:
time: 93.1 us; the launch traced here: 92.8 us
  Pallas kernels  34.4 us (37%)
  starting transfers between devices  29 us (31%)
  waiting for transfers between devices  16.8 us (18%)
  blocking collectives  8.85 us (10%)
  other arithmetic  2.7 us (3%)
  between operations  0.95 us (1%)
    pallas_call x16, Pallas kernels, kernel_call(): pl.pallas_call(body, grid_spec=pltpu.PrefetchScalarGridSpec(num_scalar_pr...  34.4 us
    ppermute x15, starting transfers between devices, xor_exchange(): lax.ppermute(x, axis, [(i, i ^ k) for i in range(lax.axis_size(axis))])  21.7 us
    ppermute x15, waiting for transfers between devices, xor_exchange(): lax.ppermute(x, axis, [(i, i ^ k) for i in range(lax.axis_size(axis))])  14.2 us
    all_gather x1, blocking collectives, per_device(): sums = jnp.sum(lax.all_gather(sums, 'genome'), axis=0)  8.85 us
    ppermute x4, starting transfers between devices, both_sides(): lax.ppermute(x, 'genome', [(i, ((i + 1 ^ 1) - 1) % size) for i in range(s...  4.43 us
    ppermute x4, starting transfers between devices, both_sides(): a = lax.ppermute(x, 'genome', [(i, i ^ 1) for i in range(size)])  2.07 us
  transfers between devices with their start and end apart: 25, of which 12 were waited for; matrix products, arithmetic and copies ran while one was open for 1% of the time, Pallas kernels for 30%

profile of v12, /device:TPU:0, one launch (start us, length us, event | category | flops | bytes accessed | tf_op | source)
XLA Modules:
  0.0 92.8 jit_solution(17800407018597274501)
XLA Ops:
  0.9 0.7 pad_add_fusion.scal
  1.7 0.8 fusion.13
  2.4 0.5 collective-permute-start.1
  2.9 3.6 %collective-permute-start.2 = (f32[8,128]{1,0:T(8,128)S(1)}, f32[8,128]{1,0:T(8,128)S(1)}, u32[]{:S(2)}, u32[]{:S(2)}) collective-permute-start(f32[8,128]{1,0:T(8,128)S(1)} %slice_bitcast_fusion.1), channel_id=1, source_target_pairs={{0,28},{4,8},{8,4},{12,16},{16,12},{20,24},{24,20},{28,0},{1,29},{... | collective-permute-start | bytes 12296 | tf_op jit(solution)/shard_map/ppermute | solution.py:547
  6.5 4.8 %first_main.1 = (f32[72,128]{1,0:T(8,128)S(1)}, f32[64,2,128,128]{3,2,1,0:T(8,128)S(1)}) custom-call(s32[4]{0:T(128)S(1)} %pad_add_fusion.scal, s32[64,2,128,128]{3,2,1,0:T(8,128)} %hbm.1, f32[64,128]{1,0:T(8,128)S(1)} %get-tuple-element.136.mask), custom_call_target="tpu_custom_call" | custom-call | tf_op jit(solution)/shard_map/first_main/pallas_call | solution.py:47
  11.3 1.4 %first_edge.1 = (f32[72,128]{1,0:T(8,128)S(1)}, f32[16,128]{1,0:T(8,128)S(1)}) custom-call(s32[4]{0:T(128)S(1)} %pad_add_fusion.scal, f32[64,2,128,128]{3,2,1,0:T(8,128)S(1)} %get-tuple-element.90.kept, f32[72,128]{1,0:T(8,128)S(1)} %pad_maximum_fusion.u_ref.mask.refs_0_, f32[72,128]{1,0:T(8,128)S(1)} %get-tuple-element.91.inner_v), custom_call_target="tpu_custom_call" | custom-call | tf_op jit(solution)/shard_map/first_edge/pallas_call | solution.py:47
  12.9 2.6 %ratio.3 = (bf16[64,128,256]{2,1,0:T(8,128)(2,1)S(1)}, bf16[64,128,256]{2,1,0:T(8,128)(2,1)S(1)}, f32[72,128]{1,0:T(8,128)S(1)}) custom-call(s32[4]{0:T(128)S(1)} %pad_add_fusion.scal, f32[64,2,128,128]{3,2,1,0:T(8,128)S(1)} %get-tuple-element.90.kept, f32[32,8192]{1,0:T(8,128)S(1)} %copy-done, f32[32,8192]{1,0:T(8,128)S(1)} %copy-done.1, ...), custom_call_target="tpu_custom_call" | custom-call | tf_op jit(solution)/shard_map/ratio/pallas_call | solution.py:47
  15.5 1.2 %collective-permute-done.3 = f32[16,128]{1,0:T(8,128)S(1)} collective-permute-done((f32[16,128]{1,0:T(8,128)S(1)}, f32[16,128]{1,0:T(8,128)S(1)}, u32[]{:S(2)}, u32[]{:S(2)}) %collective-permute-start.3) | collective-permute-done | bytes 8224 | tf_op jit(solution)/shard_map/ppermute | solution.py:547
  16.8 3.7 %collective-permute-start.5 = (f32[72,128]{1,0:T(8,128)S(1)}, f32[72,128]{1,0:T(8,128)S(1)}, u32[]{:S(2)}, u32[]{:S(2)}) collective-permute-start(f32[72,128]{1,0:T(8,128)S(1)} %pad_maximum_fusion.1.after.refs_0_), channel_id=1, source_target_pairs={{0,3},{1,2},{2,1},{3,0},{4,7},{5,6},{6,5},{7,4},{8,11},{9,10},{10,... | collective-permute-start | bytes 110600 | tf_op jit(solution)/shard_map/ppermute | solution.py:541
  20.4 0.8 collective-permute-start.7
  21.2 1.8 %ratio.4 = (bf16[64,128,256]{2,1,0:T(8,128)(2,1)S(1)}, bf16[64,128,256]{2,1,0:T(8,128)(2,1)S(1)}) custom-call(s32[4]{0:T(128)S(1)} %pad_add_fusion.scal, f32[64,2,128,128]{3,2,1,0:T(8,128)S(1)} %get-tuple-element.90.kept, f32[32,8192]{1,0:T(8,128)S(1)} %copy-done, f32[32,8192]{1,0:T(8,128)S(1)} %copy-done.1, ...), custom_call_target="tpu_custom_call", output_to_operand_aliasing={{0}: (5, {}), {1}: (6, {})} | custom-call | tf_op jit(solution)/shard_map/ratio/pallas_call | solution.py:47
  23.0 2.3 %collective-permute-done.6.refs_2_ = f32[72,128]{1,0:T(8,128)S(1)} collective-permute-done((f32[72,128]{1,0:T(8,128)S(1)}, f32[72,128]{1,0:T(8,128)S(1)}, u32[]{:S(2)}, u32[]{:S(2)}) %collective-permute-start.6) | collective-permute-done | bytes 36896 | tf_op jit(solution)/shard_map/ppermute | solution.py:541
  25.3 1.4 %cover_edge.2 = (f32[72,128]{1,0:T(8,128)S(1)}, f32[16,128]{1,0:T(8,128)S(1)}, f32[72,128]{1,0:T(8,128)S(1)}) custom-call(s32[4]{0:T(128)S(1)} %pad_add_fusion.scal, f32[64,2,128,128]{3,2,1,0:T(8,128)S(1)} %get-tuple-element.90.kept, f32[72,128]{1,0:T(8,128)S(1)} %pad_maximum_fusion.u_ref.mask.refs_0_, f32[72,128]{1,0:T(8,128)S(1)} %pad_maximum_fusion.1.after.refs_0_, ...), custom_call_target="tpu_custom_call" | custom-call | tf_op jit(solution)/shard_map/cover_edge/pallas_call | solution.py:47
  26.7 0.8 collective-permute-start.9
  27.6 2.8 %cover_main.2 = f32[72,128]{1,0:T(8,128)S(1)} custom-call(s32[4]{0:T(128)S(1)} %pad_add_fusion.scal, f32[64,2,128,128]{3,2,1,0:T(8,128)S(1)} %get-tuple-element.90.kept, f32[72,128]{1,0:T(8,128)S(1)} %get-tuple-element.100.u_ref.refs_1_, f32[72,128]{1,0:T(8,128)S(1)} %get-tuple-element.101.edge_v), custom_call_target="tpu_custom_call" | custom-call | tf_op jit(solution)/shard_map/cover_main/pallas_call | solution.py:47
  30.7 1.5 %collective-permute-start.10 = (f32[72,128]{1,0:T(8,128)S(1)}, f32[72,128]{1,0:T(8,128)S(1)}, u32[]{:S(2)}, u32[]{:S(2)}) collective-permute-start(f32[72,128]{1,0:T(8,128)S(1)} %pad_maximum_fusion.2.refs_0_), channel_id=1, source_target_pairs={{0,3},{1,2},{2,1},{3,0},{4,7},{5,6},{6,5},{7,4},{8,11},{9,10},{10,... | collective-permute-start | bytes 110600 | tf_op jit(solution)/shard_map/ppermute | solution.py:541
  32.2 0.6 collective-permute-start.11
  32.9 2.3 %collective-permute-start.12 = (f32[72,128]{1,0:T(8,128)S(1)}, f32[72,128]{1,0:T(8,128)S(1)}, u32[]{:S(2)}, u32[]{:S(2)}) collective-permute-start(f32[72,128]{1,0:T(8,128)S(1)} %pad_maximum_fusion.2.refs_0_), channel_id=1, source_target_pairs={{0,1},{1,0},{2,3},{3,2},{4,5},{5,4},{6,7},{7,6},{8,9},{9,8},{10,11... | collective-permute-start | bytes 110600 | tf_op jit(solution)/shard_map/ppermute | solution.py:541
  35.2 0.8 collective-permute-start
  35.9 0.7 collective-permute-done.10.refs_1_
  36.7 0.5 collective-permute-done.11.refs_2_
  37.5 1.4 %cover_edge.3 = (f32[72,128]{1,0:T(8,128)S(1)}, f32[16,128]{1,0:T(8,128)S(1)}, f32[72,128]{1,0:T(8,128)S(1)}) custom-call(s32[4]{0:T(128)S(1)} %pad_add_fusion.scal, f32[64,2,128,128]{3,2,1,0:T(8,128)S(1)} %get-tuple-element.90.kept, f32[72,128]{1,0:T(8,128)S(1)} %pad_maximum_fusion.u_ref.mask.refs_0_, f32[72,128]{1,0:T(8,128)S(1)} %pad_maximum_fusion.2.refs_0_, ...), custom_call_target="tpu_custom_call" | custom-call | tf_op jit(solution)/shard_map/cover_edge/pallas_call | solution.py:47
  38.9 0.8 collective-permute-start.13
  39.7 0.7 collective-permute-start.14
  40.4 2.8 %cover_main.3 = f32[72,128]{1,0:T(8,128)S(1)} custom-call(s32[4]{0:T(128)S(1)} %pad_add_fusion.scal, f32[64,2,128,128]{3,2,1,0:T(8,128)S(1)} %get-tuple-element.90.kept, f32[72,128]{1,0:T(8,128)S(1)} %get-tuple-element.103.u_ref.refs_2_, f32[72,128]{1,0:T(8,128)S(1)} %get-tuple-element.104.edge_v), custom_call_target="tpu_custom_call" | custom-call | tf_op jit(solution)/shard_map/cover_main/pallas_call | solution.py:47
  43.3 2.4 %collective-permute-start.15 = (f32[72,128]{1,0:T(8,128)S(1)}, f32[72,128]{1,0:T(8,128)S(1)}, u32[]{:S(2)}, u32[]{:S(2)}) collective-permute-start(f32[72,128]{1,0:T(8,128)S(1)} %pad_maximum_fusion.3.after.refs_0_), channel_id=1, source_target_pairs={{0,3},{1,2},{2,1},{3,0},{4,7},{5,6},{6,5},{7,4},{8,11},{9,10},{10,... | collective-permute-start | bytes 110600 | tf_op jit(solution)/shard_map/ppermute | solution.py:541
  45.7 0.5 collective-permute-start.16
  46.2 1.6 %collective-permute-start.17 = (f32[72,128]{1,0:T(8,128)S(1)}, f32[72,128]{1,0:T(8,128)S(1)}, u32[]{:S(2)}, u32[]{:S(2)}) collective-permute-start(f32[72,128]{1,0:T(8,128)S(1)} %pad_maximum_fusion.3.after.refs_0_), channel_id=1, source_target_pairs={{0,1},{1,0},{2,3},{3,2},{4,5},{5,4},{6,7},{7,6},{8,9},{9,8},{10,11... | collective-permute-start | bytes 110600 | tf_op jit(solution)/shard_map/ppermute | solution.py:541
  47.8 1.6 %ratio.5 = (bf16[64,128,256]{2,1,0:T(8,128)(2,1)S(1)}, bf16[64,128,256]{2,1,0:T(8,128)(2,1)S(1)}) custom-call(s32[4]{0:T(128)S(1)} %pad_add_fusion.scal, f32[64,2,128,128]{3,2,1,0:T(8,128)S(1)} %get-tuple-element.90.kept, f32[32,8192]{1,0:T(8,128)S(1)} %copy-done, ...), custom_call_target="tpu_custom_call", output_to_operand_aliasing={{0}: (5, {}), {1}: (6, {})} | custom-call | tf_op jit(solution)/shard_map/ratio/pallas_call | solution.py:47
  49.4 1.2 %collective-permute-done.16.refs_2_ = f32[72,128]{1,0:T(8,128)S(1)} collective-permute-done((f32[72,128]{1,0:T(8,128)S(1)}, f32[72,128]{1,0:T(8,128)S(1)}, u32[]{:S(2)}, u32[]{:S(2)}) %collective-permute-start.16) | collective-permute-done | bytes 36896 | tf_op jit(solution)/shard_map/ppermute | solution.py:541
  50.7 2.1 %numer_first.1 = (f32[72,128]{1,0:T(8,128)S(1)}, f32[9,32,128]{2,1,0:T(8,128)S(1)}, f32[16,32,128]{2,1,0:T(8,128)S(1)}) custom-call(s32[4]{0:T(128)S(1)} %pad_add_fusion.scal, bf16[64,128,256]{2,1,0:T(8,128)(2,1)S(1)} %get-tuple-element.107.hi_ref, bf16[64,128,256]{2,1,0:T(8,128)(2,1)S(1)} %get-tuple-element.108.lo_ref, f32[32,8192]{1,0:T(8,128)S(1)} %copy-done, ...), custom_call_target="tpu_custom_call" | custom-call | tf_op jit(solution)/shard_map/numer_first/pallas_call | solution.py:47
  52.8 1.1 %collective-permute-start.19 = (f32[16,32,128]{2,1,0:T(8,128)S(1)}, f32[16,32,128]{2,1,0:T(8,128)S(1)}, u32[]{:S(2)}, u32[]{:S(2)}) collective-permute-start(f32[16,32,128]{2,1,0:T(8,128)S(1)} %get-tuple-element.114), channel_id=1, source_target_pairs={{0,1},{1,0},{2,3},{3,2},{4,5},{5,4},{6,7},{7,6},{8,9},{9,8},{10,11... | collective-permute-start | bytes 786440 | tf_op jit(solution)/shard_map/ppermute | solution.py:541
  53.9 3.3 %numer_col.1 = (f32[8,128]{1,0:T(8,128)S(1)}, f32[16,32,128]{2,1,0:T(8,128)S(1)}, f32[16,32,128]{2,1,0:T(8,128)S(1)}, f32[16,32,128]{2,1,0:T(8,128)S(1)}, f32[16,32,128]{2,1,0:T(8,128)S(1)}) custom-call(s32[4]{0:T(128)S(1)} %pad_add_fusion.scal, bf16[64,128,256]{2,1,0:T(8,128)(2,1)S(1)} %get-tuple-element.107.hi_ref, ...), custom_call_target="tpu_custom_call" | custom-call | tf_op jit(solution)/shard_map/numer_col/pallas_call | solution.py:47
  57.2 1.1 %collective-permute-done.18 = f32[9,32,128]{2,1,0:T(8,128)S(1)} collective-permute-done((f32[9,32,128]{2,1,0:T(8,128)S(1)}, f32[9,32,128]{2,1,0:T(8,128)S(1)}, u32[]{:S(2)}, u32[]{:S(2)}) %collective-permute-start.18) | collective-permute-done | bytes 147488 | tf_op jit(solution)/shard_map/ppermute | solution.py:632
  58.4 1.1 %collective-permute-start.23 = (f32[16,32,128]{2,1,0:T(8,128)S(1)}, f32[16,32,128]{2,1,0:T(8,128)S(1)}, u32[]{:S(2)}, u32[]{:S(2)}) collective-permute-start(f32[16,32,128]{2,1,0:T(8,128)S(1)} %get-tuple-element.128.after), channel_id=1, source_target_pairs={{0,1},{1,0},{2,3},{3,2},{4,5},{5,4},{6,7},{7,6},{8,9},{9,8},{10,11... | collective-permute-start | bytes 786440 | tf_op jit(solution)/shard_map/ppermute | solution.py:541
  59.5 4.3 %numer_row.1 = (f32[16,32,128]{2,1,0:T(8,128)S(1)}, f32[16,32,128]{2,1,0:T(8,128)S(1)}, f32[16,32,128]{2,1,0:T(8,128)S(1)}) custom-call(s32[4]{0:T(128)S(1)} %pad_add_fusion.scal, bf16[64,128,256]{2,1,0:T(8,128)(2,1)S(1)} %get-tuple-element.107.hi_ref, bf16[64,128,256]{2,1,0:T(8,128)(2,1)S(1)} %get-tuple-element.108.lo_ref, ...), custom_call_target="tpu_custom_call" | custom-call | tf_op jit(solution)/shard_map/numer_row/pallas_call | solution.py:47
  63.8 2.4 %collective-permute-start.20 = (f32[16,32,128]{2,1,0:T(8,128)S(1)}, f32[16,32,128]{2,1,0:T(8,128)S(1)}, u32[]{:S(2)}, u32[]{:S(2)}) collective-permute-start(f32[16,32,128]{2,1,0:T(8,128)S(1)} %add.77), channel_id=1, source_target_pairs={{0,3},{1,2},{2,1},{3,0},{4,7},{5,6},{6,5},{7,4},{8,11},{9,10},{10,... | collective-permute-start | bytes 786440 | tf_op jit(solution)/shard_map/ppermute | solution.py:541
  66.2 0.7 coefficient.2
  67.0 0.9 coefficient.3
  67.9 2.1 %collective-permute-start.21 = (f32[16,32,128]{2,1,0:T(8,128)S(1)}, f32[16,32,128]{2,1,0:T(8,128)S(1)}, u32[]{:S(2)}, u32[]{:S(2)}) collective-permute-start(f32[16,32,128]{2,1,0:T(8,128)S(1)} %get-tuple-element.119), channel_id=1, source_target_pairs={{0,1},{1,0},{2,3},{3,2},{4,5},{5,4},{6,7},{7,6},{8,9},{9,8},{10,11... | collective-permute-start | bytes 786440 | tf_op jit(solution)/shard_map/ppermute | solution.py:541
  70.1 1.6 %collective-permute-start.24 = (f32[16,32,128]{2,1,0:T(8,128)S(1)}, f32[16,32,128]{2,1,0:T(8,128)S(1)}, u32[]{:S(2)}, u32[]{:S(2)}) collective-permute-start(f32[16,32,128]{2,1,0:T(8,128)S(1)} %add.81), channel_id=1, source_target_pairs={{0,3},{1,2},{2,1},{3,0},{4,7},{5,6},{6,5},{7,4},{8,11},{9,10},{10,... | collective-permute-start | bytes 786440 | tf_op jit(solution)/shard_map/ppermute | solution.py:541
  71.7 3.3 %collective-permute-done.20.refs_2_ = f32[16,32,128]{2,1,0:T(8,128)S(1)} collective-permute-done((f32[16,32,128]{2,1,0:T(8,128)S(1)}, f32[16,32,128]{2,1,0:T(8,128)S(1)}, u32[]{:S(2)}, u32[]{:S(2)}) %collective-permute-start.20) | collective-permute-done | bytes 262176 | tf_op jit(solution)/shard_map/ppermute | solution.py:541
  75.0 8.8 %all-gather = f32[64,128]{1,0:T(8,128)S(1)} all-gather(f32[8,128]{1,0:T(8,128)S(1)} %get-tuple-element.115), channel_id=2, replica_groups=mesh['genome'=8,'offset'=4] {'genome'}, dimensions={0}, use_global_device_ids=true | all-gather | bytes 36864 | tf_op jit(solution)/shard_map/all_gather | solution.py:652
  83.9 1.8 %collective-permute-done.21.refs_1_ = f32[16,32,128]{2,1,0:T(8,128)S(1)} collective-permute-done((f32[16,32,128]{2,1,0:T(8,128)S(1)}, f32[16,32,128]{2,1,0:T(8,128)S(1)}, u32[]{:S(2)}, u32[]{:S(2)}) %collective-permute-start.21) | collective-permute-done | bytes 262176 | tf_op jit(solution)/shard_map/ppermute | solution.py:541
  85.7 1.3 %update.2 = f32[32,2048]{1,0:T(8,128)} custom-call(s32[4]{0:T(128)S(1)} %pad_add_fusion.scal, f32[8,128]{1,0:T(8,128)S(1)} %bitcast_reduce_fusion.sums, f32[16,32,128]{2,1,0:T(8,128)S(1)} %get-tuple-element.116.times, f32[16,32,128]{2,1,0:T(8,128)S(1)} %get-tuple-element.117.plus, f32[16,32,128]{2,1,0:T(8,128)S(1)} %get-tuple-element.118.refs_0_, ...), custom_call_target="tpu_custom_call" | custom-call | tf_op jit(solution)/shard_map/update/pallas_call | solution.py:47
  87.0 0.6 multiply_bitcast_fusion
  87.7 3.9 %collective-permute-done.24.refs_2_ = f32[16,32,128]{2,1,0:T(8,128)S(1)} collective-permute-done((f32[16,32,128]{2,1,0:T(8,128)S(1)}, f32[16,32,128]{2,1,0:T(8,128)S(1)}, u32[]{:S(2)}, u32[]{:S(2)}) %collective-permute-start.24) | collective-permute-done | bytes 262176 | tf_op jit(solution)/shard_map/ppermute | solution.py:541
  91.5 1.3 %update.3 = f32[32,2048]{1,0:T(8,128)} custom-call(s32[4]{0:T(128)S(1)} %pad_add_fusion.scal, f32[8,128]{1,0:T(8,128)S(1)} %bitcast_reduce_fusion.sums, f32[16,32,128]{2,1,0:T(8,128)S(1)} %get-tuple-element.120.times, f32[16,32,128]{2,1,0:T(8,128)S(1)} %get-tuple-element.121.plus, f32[16,32,128]{2,1,0:T(8,128)S(1)} %get-tuple-element.126.refs_0_, ...), custom_call_target="tpu_custom_call" | custom-call | tf_op jit(solution)/shard_map/update/pallas_call | solution.py:47
  (56 shorter events, 1.7 us)
Async XLA Ops:
  2.4 8.8 %collective-permute-start.1 = (f32[8,128]{1,0:T(8,128)S(1)}, f32[8,128]{1,0:T(8,128)S(1)}, u32[]{:S(2)}, u32[]{:S(2)}) collective-permute-start(f32[8,128]{1,0:T(8,128)S(1)} %slice_bitcast_fusion.1), channel_id=1, source_target_pairs={{0,4},{4,0},{8,12},{12,8},{16,20},{20,16},{24,28},{28,24},{1,5},{5... | collective-permute-start | bytes 12296 | tf_op jit(solution)/shard_map/ppermute | solution.py:546
  2.9 8.4 %collective-permute-start.2 = (f32[8,128]{1,0:T(8,128)S(1)}, f32[8,128]{1,0:T(8,128)S(1)}, u32[]{:S(2)}, u32[]{:S(2)}) collective-permute-start(f32[8,128]{1,0:T(8,128)S(1)} %slice_bitcast_fusion.1), channel_id=1, source_target_pairs={{0,28},{4,8},{8,4},{12,16},{16,12},{20,24},{24,20},{28,0},{1,29},{... | collective-permute-start | bytes 12296 | tf_op jit(solution)/shard_map/ppermute | solution.py:547
  11.3 1.5 %copy-start = (f32[32,8192]{1,0:T(8,128)S(1)}, f32[32,8192]{1,0:T(8,128)}, u32[]{:S(2)}) copy-start(f32[32,8192]{1,0:T(8,128)} %other.1) | copy-start | bytes 3145732
  11.3 1.5 %copy-start.1 = (f32[32,8192]{1,0:T(8,128)S(1)}, f32[32,8192]{1,0:T(8,128)}, u32[]{:S(2)}) copy-start(f32[32,8192]{1,0:T(8,128)} %old_ref.3) | copy-start | bytes 3145732
  12.7 4.0 %collective-permute-start.3 = (f32[16,128]{1,0:T(8,128)S(1)}, f32[16,128]{1,0:T(8,128)S(1)}, u32[]{:S(2)}, u32[]{:S(2)}) collective-permute-start(f32[16,128]{1,0:T(8,128)S(1)} %get-tuple-element.96), channel_id=1, source_target_pairs={{0,28},{4,8},{8,4},{12,16},{16,12},{20,24},{24,20},{28,0},{1,29},{... | collective-permute-start | bytes 24584 | tf_op jit(solution)/shard_map/ppermute | solution.py:547
  12.8 4.0 %collective-permute-start.4 = (f32[16,128]{1,0:T(8,128)S(1)}, f32[16,128]{1,0:T(8,128)S(1)}, u32[]{:S(2)}, u32[]{:S(2)}) collective-permute-start(f32[16,128]{1,0:T(8,128)S(1)} %get-tuple-element.96), channel_id=1, source_target_pairs={{0,4},{4,0},{8,12},{12,8},{16,20},{20,16},{24,28},{28,24},{1,5},{5... | collective-permute-start | bytes 24584 | tf_op jit(solution)/shard_map/ppermute | solution.py:546
  16.8 6.2 %collective-permute-start.5 = (f32[72,128]{1,0:T(8,128)S(1)}, f32[72,128]{1,0:T(8,128)S(1)}, u32[]{:S(2)}, u32[]{:S(2)}) collective-permute-start(f32[72,128]{1,0:T(8,128)S(1)} %pad_maximum_fusion.1.after.refs_0_), channel_id=1, source_target_pairs={{0,3},{1,2},{2,1},{3,0},{4,7},{5,6},{6,5},{7,4},{8,11},{9,10},{10,... | collective-permute-start | bytes 110600 | tf_op jit(solution)/shard_map/ppermute | solution.py:541
  20.4 4.9 %collective-permute-start.6 = (f32[72,128]{1,0:T(8,128)S(1)}, f32[72,128]{1,0:T(8,128)S(1)}, u32[]{:S(2)}, u32[]{:S(2)}) collective-permute-start(f32[72,128]{1,0:T(8,128)S(1)} %pad_maximum_fusion.1.after.refs_0_), channel_id=1, source_target_pairs={{0,2},{1,3},{2,0},{3,1},{4,6},{5,7},{6,4},{7,5},{8,10},{9,11},{10,... | collective-permute-start | bytes 110600 | tf_op jit(solution)/shard_map/ppermute | solution.py:541
  20.4 4.9 %collective-permute-start.7 = (f32[72,128]{1,0:T(8,128)S(1)}, f32[72,128]{1,0:T(8,128)S(1)}, u32[]{:S(2)}, u32[]{:S(2)}) collective-permute-start(f32[72,128]{1,0:T(8,128)S(1)} %pad_maximum_fusion.1.after.refs_0_), channel_id=1, source_target_pairs={{0,1},{1,0},{2,3},{3,2},{4,5},{5,4},{6,7},{7,6},{8,9},{9,8},{10,11... | collective-permute-start | bytes 110600 | tf_op jit(solution)/shard_map/ppermute | solution.py:541
  26.7 4.0 %collective-permute-start.8 = (f32[16,128]{1,0:T(8,128)S(1)}, f32[16,128]{1,0:T(8,128)S(1)}, u32[]{:S(2)}, u32[]{:S(2)}) collective-permute-start(f32[16,128]{1,0:T(8,128)S(1)} %get-tuple-element.102), channel_id=1, source_target_pairs={{0,28},{4,8},{8,4},{12,16},{16,12},{20,24},{24,20},{28,0},{1,29},{... | collective-permute-start | bytes 24584 | tf_op jit(solution)/shard_map/ppermute | solution.py:547
  26.7 4.0 %collective-permute-start.9 = (f32[16,128]{1,0:T(8,128)S(1)}, f32[16,128]{1,0:T(8,128)S(1)}, u32[]{:S(2)}, u32[]{:S(2)}) collective-permute-start(f32[16,128]{1,0:T(8,128)S(1)} %get-tuple-element.102), channel_id=1, source_target_pairs={{0,4},{4,0},{8,12},{12,8},{16,20},{20,16},{24,28},{28,24},{1,5},{5... | collective-permute-start | bytes 24584 | tf_op jit(solution)/shard_map/ppermute | solution.py:546
  30.7 6.0 %collective-permute-start.10 = (f32[72,128]{1,0:T(8,128)S(1)}, f32[72,128]{1,0:T(8,128)S(1)}, u32[]{:S(2)}, u32[]{:S(2)}) collective-permute-start(f32[72,128]{1,0:T(8,128)S(1)} %pad_maximum_fusion.2.refs_0_), channel_id=1, source_target_pairs={{0,3},{1,2},{2,1},{3,0},{4,7},{5,6},{6,5},{7,4},{8,11},{9,10},{10,... | collective-permute-start | bytes 110600 | tf_op jit(solution)/shard_map/ppermute | solution.py:541
  32.2 4.9 %collective-permute-start.11 = (f32[72,128]{1,0:T(8,128)S(1)}, f32[72,128]{1,0:T(8,128)S(1)}, u32[]{:S(2)}, u32[]{:S(2)}) collective-permute-start(f32[72,128]{1,0:T(8,128)S(1)} %pad_maximum_fusion.2.refs_0_), channel_id=1, source_target_pairs={{0,2},{1,3},{2,0},{3,1},{4,6},{5,7},{6,4},{7,5},{8,10},{9,11},{10,... | collective-permute-start | bytes 110600 | tf_op jit(solution)/shard_map/ppermute | solution.py:541
  32.9 4.6 %collective-permute-start.12 = (f32[72,128]{1,0:T(8,128)S(1)}, f32[72,128]{1,0:T(8,128)S(1)}, u32[]{:S(2)}, u32[]{:S(2)}) collective-permute-start(f32[72,128]{1,0:T(8,128)S(1)} %pad_maximum_fusion.2.refs_0_), channel_id=1, source_target_pairs={{0,1},{1,0},{2,3},{3,2},{4,5},{5,4},{6,7},{7,6},{8,9},{9,8},{10,11... | collective-permute-start | bytes 110600 | tf_op jit(solution)/shard_map/ppermute | solution.py:541
  35.2 12.6 %collective-permute-start = (f32[32,1024]{1,0:T(8,128)S(1)}, f32[32,1024]{1,0:T(8,128)S(1)}, u32[]{:S(2)}, u32[]{:S(2)}) collective-permute-start(f32[32,1024]{1,0:T(8,128)S(1)} %slice.207), channel_id=1, source_target_pairs={{0,28},{4,0},{8,4},{12,8},{16,12},{20,16},{24,20},{28,24},{1,29},{... | collective-permute-start | bytes 393224 | tf_op jit(solution)/shard_map/ppermute | solution.py:594
  38.9 4.4 %collective-permute-start.13 = (f32[16,128]{1,0:T(8,128)S(1)}, f32[16,128]{1,0:T(8,128)S(1)}, u32[]{:S(2)}, u32[]{:S(2)}) collective-permute-start(f32[16,128]{1,0:T(8,128)S(1)} %get-tuple-element.105), channel_id=1, source_target_pairs={{0,28},{4,8},{8,4},{12,16},{16,12},{20,24},{24,20},{28,0},{1,29},{... | collective-permute-start | bytes 24584 | tf_op jit(solution)/shard_map/ppermute | solution.py:547
  39.7 3.6 %collective-permute-start.14 = (f32[16,128]{1,0:T(8,128)S(1)}, f32[16,128]{1,0:T(8,128)S(1)}, u32[]{:S(2)}, u32[]{:S(2)}) collective-permute-start(f32[16,128]{1,0:T(8,128)S(1)} %get-tuple-element.105), channel_id=1, source_target_pairs={{0,4},{4,0},{8,12},{12,8},{16,20},{20,16},{24,28},{28,24},{1,5},{5... | collective-permute-start | bytes 24584 | tf_op jit(solution)/shard_map/ppermute | solution.py:546
  43.3 6.1 %collective-permute-start.15 = (f32[72,128]{1,0:T(8,128)S(1)}, f32[72,128]{1,0:T(8,128)S(1)}, u32[]{:S(2)}, u32[]{:S(2)}) collective-permute-start(f32[72,128]{1,0:T(8,128)S(1)} %pad_maximum_fusion.3.after.refs_0_), channel_id=1, source_target_pairs={{0,3},{1,2},{2,1},{3,0},{4,7},{5,6},{6,5},{7,4},{8,11},{9,10},{10,... | collective-permute-start | bytes 110600 | tf_op jit(solution)/shard_map/ppermute | solution.py:541
  45.7 4.9 %collective-permute-start.16 = (f32[72,128]{1,0:T(8,128)S(1)}, f32[72,128]{1,0:T(8,128)S(1)}, u32[]{:S(2)}, u32[]{:S(2)}) collective-permute-start(f32[72,128]{1,0:T(8,128)S(1)} %pad_maximum_fusion.3.after.refs_0_), channel_id=1, source_target_pairs={{0,2},{1,3},{2,0},{3,1},{4,6},{5,7},{6,4},{7,5},{8,10},{9,11},{10,... | collective-permute-start | bytes 110600 | tf_op jit(solution)/shard_map/ppermute | solution.py:541
  46.2 4.5 %collective-permute-start.17 = (f32[72,128]{1,0:T(8,128)S(1)}, f32[72,128]{1,0:T(8,128)S(1)}, u32[]{:S(2)}, u32[]{:S(2)}) collective-permute-start(f32[72,128]{1,0:T(8,128)S(1)} %pad_maximum_fusion.3.after.refs_0_), channel_id=1, source_target_pairs={{0,1},{1,0},{2,3},{3,2},{4,5},{5,4},{6,7},{7,6},{8,9},{9,8},{10,11... | collective-permute-start | bytes 110600 | tf_op jit(solution)/shard_map/ppermute | solution.py:541
  52.8 5.5 %collective-permute-start.18 = (f32[9,32,128]{2,1,0:T(8,128)S(1)}, f32[9,32,128]{2,1,0:T(8,128)S(1)}, u32[]{:S(2)}, u32[]{:S(2)}) collective-permute-start(f32[9,32,128]{2,1,0:T(8,128)S(1)} %get-tuple-element.112), channel_id=1, source_target_pairs={{0,4},{4,8},{8,12},{12,16},{16,20},{20,24},{24,28},{28,0},{1,5},{5... | collective-permute-start | bytes 442376 | tf_op jit(solution)/shard_map/ppermute | solution.py:632
  52.8 11.0 %collective-permute-start.19 = (f32[16,32,128]{2,1,0:T(8,128)S(1)}, f32[16,32,128]{2,1,0:T(8,128)S(1)}, u32[]{:S(2)}, u32[]{:S(2)}) collective-permute-start(f32[16,32,128]{2,1,0:T(8,128)S(1)} %get-tuple-element.114), channel_id=1, source_target_pairs={{0,1},{1,0},{2,3},{3,2},{4,5},{5,4},{6,7},{7,6},{8,9},{9,8},{10,11... | collective-permute-start | bytes 786440 | tf_op jit(solution)/shard_map/ppermute | solution.py:541
  58.4 11.6 %collective-permute-start.23 = (f32[16,32,128]{2,1,0:T(8,128)S(1)}, f32[16,32,128]{2,1,0:T(8,128)S(1)}, u32[]{:S(2)}, u32[]{:S(2)}) collective-permute-start(f32[16,32,128]{2,1,0:T(8,128)S(1)} %get-tuple-element.128.after), channel_id=1, source_target_pairs={{0,1},{1,0},{2,3},{3,2},{4,5},{5,4},{6,7},{7,6},{8,9},{9,8},{10,11... | collective-permute-start | bytes 786440 | tf_op jit(solution)/shard_map/ppermute | solution.py:541
  63.8 11.2 %collective-permute-start.20 = (f32[16,32,128]{2,1,0:T(8,128)S(1)}, f32[16,32,128]{2,1,0:T(8,128)S(1)}, u32[]{:S(2)}, u32[]{:S(2)}) collective-permute-start(f32[16,32,128]{2,1,0:T(8,128)S(1)} %add.77), channel_id=1, source_target_pairs={{0,3},{1,2},{2,1},{3,0},{4,7},{5,6},{6,5},{7,4},{8,11},{9,10},{10,... | collective-permute-start | bytes 786440 | tf_op jit(solution)/shard_map/ppermute | solution.py:541
  66.9 20.7 %collective-permute-start.22 = (f32[16,32,128]{2,1,0:T(8,128)S(1)}, f32[16,32,128]{2,1,0:T(8,128)S(1)}, u32[]{:S(2)}, u32[]{:S(2)}) collective-permute-start(f32[16,32,128]{2,1,0:T(8,128)S(1)} %get-tuple-element.127), channel_id=1, source_target_pairs={{0,1},{1,0},{2,3},{3,2},{4,5},{5,4},{6,7},{7,6},{8,9},{9,8},{10,11... | collective-permute-start | bytes 786440 | tf_op jit(solution)/shard_map/ppermute | solution.py:541
  67.9 17.8 %collective-permute-start.21 = (f32[16,32,128]{2,1,0:T(8,128)S(1)}, f32[16,32,128]{2,1,0:T(8,128)S(1)}, u32[]{:S(2)}, u32[]{:S(2)}) collective-permute-start(f32[16,32,128]{2,1,0:T(8,128)S(1)} %get-tuple-element.119), channel_id=1, source_target_pairs={{0,1},{1,0},{2,3},{3,2},{4,5},{5,4},{6,7},{7,6},{8,9},{9,8},{10,11... | collective-permute-start | bytes 786440 | tf_op jit(solution)/shard_map/ppermute | solution.py:541
  70.1 21.5 %collective-permute-start.24 = (f32[16,32,128]{2,1,0:T(8,128)S(1)}, f32[16,32,128]{2,1,0:T(8,128)S(1)}, u32[]{:S(2)}, u32[]{:S(2)}) collective-permute-start(f32[16,32,128]{2,1,0:T(8,128)S(1)} %add.81), channel_id=1, source_target_pairs={{0,3},{1,2},{2,1},{3,0},{4,7},{5,6},{6,5},{7,4},{8,11},{9,10},{10,... | collective-permute-start | bytes 786440 | tf_op jit(solution)/shard_map/ppermute | solution.py:541

commit v13 on v12

--- a/solution.py
+++ b/solution.py
@@ -313,7 +313,7 @@
             out[t] = row_numer(offs, g_ref, hi_ref, lo_ref, u_ref, first + t)
             return carry
 
-        lax.fori_loop(0, per, body, 0, unroll=4)
+        lax.fori_loop(0, per, body, 0, unroll=8)
 
 
 def scaled_terms(h_ref, u_ref, terms, start, count):

time: 93.1 us -> 92.8 us (level)
    pallas_call x16, Pallas kernels: 34.4 us -> 33.5 us  [kernel_call(): pl.pallas_call(body, grid_spec=pltpu.PrefetchScalarGridSpec(num_scalar_pr...]
where the time goes in v13:
time: 92.8 us; the launch traced here: 92.6 us
  Pallas kernels  33.5 us (36%)
  starting transfers between devices  29 us (31%)
  waiting for transfers between devices  17.5 us (19%)
  blocking collectives  8.89 us (10%)
  other arithmetic  2.7 us (3%)
  between operations  0.95 us (1%)
    pallas_call x16, Pallas kernels, kernel_call(): pl.pallas_call(body, grid_spec=pltpu.PrefetchScalarGridSpec(num_scalar_pr...  33.5 us
    ppermute x15, starting transfers between devices, xor_exchange(): lax.ppermute(x, axis, [(i, i ^ k) for i in range(lax.axis_size(axis))])  21.7 us
    ppermute x15, waiting for transfers between devices, xor_exchange(): lax.ppermute(x, axis, [(i, i ^ k) for i in range(lax.axis_size(axis))])  14.9 us
    all_gather x1, blocking collectives, per_device(): sums = jnp.sum(lax.all_gather(sums, 'genome'), axis=0)  8.89 us
    ppermute x4, starting transfers between devices, both_sides(): lax.ppermute(x, 'genome', [(i, ((i + 1 ^ 1) - 1) % size) for i in range(s...  4.44 us
    ppermute x4, starting transfers between devices, both_sides(): a = lax.ppermute(x, 'genome', [(i, i ^ 1) for i in range(size)])  2.07 us
  transfers between devices with their start and end apart: 25, of which 12 were waited for; matrix products, arithmetic and copies ran while one was open for 1% of the time, Pallas kernels for 30%

profile of v13, /device:TPU:0, one launch (start us, length us, event | category | flops | bytes accessed | tf_op | source)
XLA Modules:
  0.0 92.6 jit_solution(941056172356535139)
XLA Ops:
  0.9 0.7 pad_add_fusion.scal
  1.7 0.8 fusion.13
  2.4 0.5 collective-permute-start.1
  2.9 3.6 %collective-permute-start.2 = (f32[8,128]{1,0:T(8,128)S(1)}, f32[8,128]{1,0:T(8,128)S(1)}, u32[]{:S(2)}, u32[]{:S(2)}) collective-permute-start(f32[8,128]{1,0:T(8,128)S(1)} %slice_bitcast_fusion.1), channel_id=1, source_target_pairs={{0,28},{4,8},{8,4},{12,16},{16,12},{20,24},{24,20},{28,0},{1,29},{... | collective-permute-start | bytes 12296 | tf_op jit(solution)/shard_map/ppermute | solution.py:547
  6.5 4.8 %first_main.1 = (f32[72,128]{1,0:T(8,128)S(1)}, f32[64,2,128,128]{3,2,1,0:T(8,128)S(1)}) custom-call(s32[4]{0:T(128)S(1)} %pad_add_fusion.scal, s32[64,2,128,128]{3,2,1,0:T(8,128)} %hbm.1, f32[64,128]{1,0:T(8,128)S(1)} %get-tuple-element.136.mask), custom_call_target="tpu_custom_call" | custom-call | tf_op jit(solution)/shard_map/first_main/pallas_call | solution.py:47
  11.3 1.4 %first_edge.1 = (f32[72,128]{1,0:T(8,128)S(1)}, f32[16,128]{1,0:T(8,128)S(1)}) custom-call(s32[4]{0:T(128)S(1)} %pad_add_fusion.scal, f32[64,2,128,128]{3,2,1,0:T(8,128)S(1)} %get-tuple-element.90.kept, f32[72,128]{1,0:T(8,128)S(1)} %pad_maximum_fusion.u_ref.mask.refs_0_, f32[72,128]{1,0:T(8,128)S(1)} %get-tuple-element.91.inner_v), custom_call_target="tpu_custom_call" | custom-call | tf_op jit(solution)/shard_map/first_edge/pallas_call | solution.py:47
  12.9 2.6 %ratio.3 = (bf16[64,128,256]{2,1,0:T(8,128)(2,1)S(1)}, bf16[64,128,256]{2,1,0:T(8,128)(2,1)S(1)}, f32[72,128]{1,0:T(8,128)S(1)}) custom-call(s32[4]{0:T(128)S(1)} %pad_add_fusion.scal, f32[64,2,128,128]{3,2,1,0:T(8,128)S(1)} %get-tuple-element.90.kept, f32[32,8192]{1,0:T(8,128)S(1)} %copy-done, f32[32,8192]{1,0:T(8,128)S(1)} %copy-done.1, ...), custom_call_target="tpu_custom_call" | custom-call | tf_op jit(solution)/shard_map/ratio/pallas_call | solution.py:47
  15.5 1.2 %collective-permute-done.3 = f32[16,128]{1,0:T(8,128)S(1)} collective-permute-done((f32[16,128]{1,0:T(8,128)S(1)}, f32[16,128]{1,0:T(8,128)S(1)}, u32[]{:S(2)}, u32[]{:S(2)}) %collective-permute-start.3) | collective-permute-done | bytes 8224 | tf_op jit(solution)/shard_map/ppermute | solution.py:547
  16.8 3.7 %collective-permute-start.5 = (f32[72,128]{1,0:T(8,128)S(1)}, f32[72,128]{1,0:T(8,128)S(1)}, u32[]{:S(2)}, u32[]{:S(2)}) collective-permute-start(f32[72,128]{1,0:T(8,128)S(1)} %pad_maximum_fusion.1.after.refs_0_), channel_id=1, source_target_pairs={{0,3},{1,2},{2,1},{3,0},{4,7},{5,6},{6,5},{7,4},{8,11},{9,10},{10,... | collective-permute-start | bytes 110600 | tf_op jit(solution)/shard_map/ppermute | solution.py:541
  20.4 0.8 collective-permute-start.7
  21.2 1.8 %ratio.4 = (bf16[64,128,256]{2,1,0:T(8,128)(2,1)S(1)}, bf16[64,128,256]{2,1,0:T(8,128)(2,1)S(1)}) custom-call(s32[4]{0:T(128)S(1)} %pad_add_fusion.scal, f32[64,2,128,128]{3,2,1,0:T(8,128)S(1)} %get-tuple-element.90.kept, f32[32,8192]{1,0:T(8,128)S(1)} %copy-done, f32[32,8192]{1,0:T(8,128)S(1)} %copy-done.1, ...), custom_call_target="tpu_custom_call", output_to_operand_aliasing={{0}: (5, {}), {1}: (6, {})} | custom-call | tf_op jit(solution)/shard_map/ratio/pallas_call | solution.py:47
  23.0 2.3 %collective-permute-done.6.refs_2_ = f32[72,128]{1,0:T(8,128)S(1)} collective-permute-done((f32[72,128]{1,0:T(8,128)S(1)}, f32[72,128]{1,0:T(8,128)S(1)}, u32[]{:S(2)}, u32[]{:S(2)}) %collective-permute-start.6) | collective-permute-done | bytes 36896 | tf_op jit(solution)/shard_map/ppermute | solution.py:541
  25.3 1.4 %cover_edge.2 = (f32[72,128]{1,0:T(8,128)S(1)}, f32[16,128]{1,0:T(8,128)S(1)}, f32[72,128]{1,0:T(8,128)S(1)}) custom-call(s32[4]{0:T(128)S(1)} %pad_add_fusion.scal, f32[64,2,128,128]{3,2,1,0:T(8,128)S(1)} %get-tuple-element.90.kept, f32[72,128]{1,0:T(8,128)S(1)} %pad_maximum_fusion.u_ref.mask.refs_0_, f32[72,128]{1,0:T(8,128)S(1)} %pad_maximum_fusion.1.after.refs_0_, ...), custom_call_target="tpu_custom_call" | custom-call | tf_op jit(solution)/shard_map/cover_edge/pallas_call | solution.py:47
  26.7 0.8 collective-permute-start.9
  27.6 2.8 %cover_main.2 = f32[72,128]{1,0:T(8,128)S(1)} custom-call(s32[4]{0:T(128)S(1)} %pad_add_fusion.scal, f32[64,2,128,128]{3,2,1,0:T(8,128)S(1)} %get-tuple-element.90.kept, f32[72,128]{1,0:T(8,128)S(1)} %get-tuple-element.100.u_ref.refs_1_, f32[72,128]{1,0:T(8,128)S(1)} %get-tuple-element.101.edge_v), custom_call_target="tpu_custom_call" | custom-call | tf_op jit(solution)/shard_map/cover_main/pallas_call | solution.py:47
  30.7 1.5 %collective-permute-start.10 = (f32[72,128]{1,0:T(8,128)S(1)}, f32[72,128]{1,0:T(8,128)S(1)}, u32[]{:S(2)}, u32[]{:S(2)}) collective-permute-start(f32[72,128]{1,0:T(8,128)S(1)} %pad_maximum_fusion.2.refs_0_), channel_id=1, source_target_pairs={{0,3},{1,2},{2,1},{3,0},{4,7},{5,6},{6,5},{7,4},{8,11},{9,10},{10,... | collective-permute-start | bytes 110600 | tf_op jit(solution)/shard_map/ppermute | solution.py:541
  32.3 0.6 collective-permute-start.11
  32.9 2.3 %collective-permute-start.12 = (f32[72,128]{1,0:T(8,128)S(1)}, f32[72,128]{1,0:T(8,128)S(1)}, u32[]{:S(2)}, u32[]{:S(2)}) collective-permute-start(f32[72,128]{1,0:T(8,128)S(1)} %pad_maximum_fusion.2.refs_0_), channel_id=1, source_target_pairs={{0,1},{1,0},{2,3},{3,2},{4,5},{5,4},{6,7},{7,6},{8,9},{9,8},{10,11... | collective-permute-start | bytes 110600 | tf_op jit(solution)/shard_map/ppermute | solution.py:541
  35.2 0.8 collective-permute-start
  35.9 0.7 collective-permute-done.10.refs_1_
  36.7 0.5 collective-permute-done.11.refs_2_
  37.5 1.4 %cover_edge.3 = (f32[72,128]{1,0:T(8,128)S(1)}, f32[16,128]{1,0:T(8,128)S(1)}, f32[72,128]{1,0:T(8,128)S(1)}) custom-call(s32[4]{0:T(128)S(1)} %pad_add_fusion.scal, f32[64,2,128,128]{3,2,1,0:T(8,128)S(1)} %get-tuple-element.90.kept, f32[72,128]{1,0:T(8,128)S(1)} %pad_maximum_fusion.u_ref.mask.refs_0_, f32[72,128]{1,0:T(8,128)S(1)} %pad_maximum_fusion.2.refs_0_, ...), custom_call_target="tpu_custom_call" | custom-call | tf_op jit(solution)/shard_map/cover_edge/pallas_call | solution.py:47
  38.9 0.8 collective-permute-start.13
  39.7 0.7 collective-permute-start.14
  40.5 2.8 %cover_main.3 = f32[72,128]{1,0:T(8,128)S(1)} custom-call(s32[4]{0:T(128)S(1)} %pad_add_fusion.scal, f32[64,2,128,128]{3,2,1,0:T(8,128)S(1)} %get-tuple-element.90.kept, f32[72,128]{1,0:T(8,128)S(1)} %get-tuple-element.103.u_ref.refs_2_, f32[72,128]{1,0:T(8,128)S(1)} %get-tuple-element.104.edge_v), custom_call_target="tpu_custom_call" | custom-call | tf_op jit(solution)/shard_map/cover_main/pallas_call | solution.py:47
  43.3 2.4 %collective-permute-start.15 = (f32[72,128]{1,0:T(8,128)S(1)}, f32[72,128]{1,0:T(8,128)S(1)}, u32[]{:S(2)}, u32[]{:S(2)}) collective-permute-start(f32[72,128]{1,0:T(8,128)S(1)} %pad_maximum_fusion.3.after.refs_0_), channel_id=1, source_target_pairs={{0,3},{1,2},{2,1},{3,0},{4,7},{5,6},{6,5},{7,4},{8,11},{9,10},{10,... | collective-permute-start | bytes 110600 | tf_op jit(solution)/shard_map/ppermute | solution.py:541
  45.7 0.5 collective-permute-start.16
  46.2 1.6 %collective-permute-start.17 = (f32[72,128]{1,0:T(8,128)S(1)}, f32[72,128]{1,0:T(8,128)S(1)}, u32[]{:S(2)}, u32[]{:S(2)}) collective-permute-start(f32[72,128]{1,0:T(8,128)S(1)} %pad_maximum_fusion.3.after.refs_0_), channel_id=1, source_target_pairs={{0,1},{1,0},{2,3},{3,2},{4,5},{5,4},{6,7},{7,6},{8,9},{9,8},{10,11... | collective-permute-start | bytes 110600 | tf_op jit(solution)/shard_map/ppermute | solution.py:541
  47.8 1.6 %ratio.5 = (bf16[64,128,256]{2,1,0:T(8,128)(2,1)S(1)}, bf16[64,128,256]{2,1,0:T(8,128)(2,1)S(1)}) custom-call(s32[4]{0:T(128)S(1)} %pad_add_fusion.scal, f32[64,2,128,128]{3,2,1,0:T(8,128)S(1)} %get-tuple-element.90.kept, f32[32,8192]{1,0:T(8,128)S(1)} %copy-done, ...), custom_call_target="tpu_custom_call", output_to_operand_aliasing={{0}: (5, {}), {1}: (6, {})} | custom-call | tf_op jit(solution)/shard_map/ratio/pallas_call | solution.py:47
  49.4 1.2 %collective-permute-done.16.refs_2_ = f32[72,128]{1,0:T(8,128)S(1)} collective-permute-done((f32[72,128]{1,0:T(8,128)S(1)}, f32[72,128]{1,0:T(8,128)S(1)}, u32[]{:S(2)}, u32[]{:S(2)}) %collective-permute-start.16) | collective-permute-done | bytes 36896 | tf_op jit(solution)/shard_map/ppermute | solution.py:541
  50.7 1.9 %numer_first.1 = (f32[72,128]{1,0:T(8,128)S(1)}, f32[9,32,128]{2,1,0:T(8,128)S(1)}, f32[16,32,128]{2,1,0:T(8,128)S(1)}) custom-call(s32[4]{0:T(128)S(1)} %pad_add_fusion.scal, bf16[64,128,256]{2,1,0:T(8,128)(2,1)S(1)} %get-tuple-element.107.hi_ref, bf16[64,128,256]{2,1,0:T(8,128)(2,1)S(1)} %get-tuple-element.108.lo_ref, f32[32,8192]{1,0:T(8,128)S(1)} %copy-done, ...), custom_call_target="tpu_custom_call" | custom-call | tf_op jit(solution)/shard_map/numer_first/pallas_call | solution.py:47
  52.6 1.1 %collective-permute-start.19 = (f32[16,32,128]{2,1,0:T(8,128)S(1)}, f32[16,32,128]{2,1,0:T(8,128)S(1)}, u32[]{:S(2)}, u32[]{:S(2)}) collective-permute-start(f32[16,32,128]{2,1,0:T(8,128)S(1)} %get-tuple-element.114), channel_id=1, source_target_pairs={{0,1},{1,0},{2,3},{3,2},{4,5},{5,4},{6,7},{7,6},{8,9},{9,8},{10,11... | collective-permute-start | bytes 786440 | tf_op jit(solution)/shard_map/ppermute | solution.py:541
  53.7 3.3 %numer_col.1 = (f32[8,128]{1,0:T(8,128)S(1)}, f32[16,32,128]{2,1,0:T(8,128)S(1)}, f32[16,32,128]{2,1,0:T(8,128)S(1)}, f32[16,32,128]{2,1,0:T(8,128)S(1)}, f32[16,32,128]{2,1,0:T(8,128)S(1)}) custom-call(s32[4]{0:T(128)S(1)} %pad_add_fusion.scal, bf16[64,128,256]{2,1,0:T(8,128)(2,1)S(1)} %get-tuple-element.107.hi_ref, ...), custom_call_target="tpu_custom_call" | custom-call | tf_op jit(solution)/shard_map/numer_col/pallas_call | solution.py:47
  57.0 1.1 %collective-permute-done.18 = f32[9,32,128]{2,1,0:T(8,128)S(1)} collective-permute-done((f32[9,32,128]{2,1,0:T(8,128)S(1)}, f32[9,32,128]{2,1,0:T(8,128)S(1)}, u32[]{:S(2)}, u32[]{:S(2)}) %collective-permute-start.18) | collective-permute-done | bytes 147488 | tf_op jit(solution)/shard_map/ppermute | solution.py:632
  58.1 1.1 %collective-permute-start.23 = (f32[16,32,128]{2,1,0:T(8,128)S(1)}, f32[16,32,128]{2,1,0:T(8,128)S(1)}, u32[]{:S(2)}, u32[]{:S(2)}) collective-permute-start(f32[16,32,128]{2,1,0:T(8,128)S(1)} %get-tuple-element.128.after), channel_id=1, source_target_pairs={{0,1},{1,0},{2,3},{3,2},{4,5},{5,4},{6,7},{7,6},{8,9},{9,8},{10,11... | collective-permute-start | bytes 786440 | tf_op jit(solution)/shard_map/ppermute | solution.py:541
  59.3 3.5 %numer_row.1 = (f32[16,32,128]{2,1,0:T(8,128)S(1)}, f32[16,32,128]{2,1,0:T(8,128)S(1)}, f32[16,32,128]{2,1,0:T(8,128)S(1)}) custom-call(s32[4]{0:T(128)S(1)} %pad_add_fusion.scal, bf16[64,128,256]{2,1,0:T(8,128)(2,1)S(1)} %get-tuple-element.107.hi_ref, bf16[64,128,256]{2,1,0:T(8,128)(2,1)S(1)} %get-tuple-element.108.lo_ref, ...), custom_call_target="tpu_custom_call" | custom-call | tf_op jit(solution)/shard_map/numer_row/pallas_call | solution.py:47
  62.9 2.4 %collective-permute-start.20 = (f32[16,32,128]{2,1,0:T(8,128)S(1)}, f32[16,32,128]{2,1,0:T(8,128)S(1)}, u32[]{:S(2)}, u32[]{:S(2)}) collective-permute-start(f32[16,32,128]{2,1,0:T(8,128)S(1)} %add.77), channel_id=1, source_target_pairs={{0,3},{1,2},{2,1},{3,0},{4,7},{5,6},{6,5},{7,4},{8,11},{9,10},{10,... | collective-permute-start | bytes 786440 | tf_op jit(solution)/shard_map/ppermute | solution.py:541
  65.2 0.7 coefficient.2
  66.0 0.9 coefficient.3
  67.0 2.1 %collective-permute-start.21 = (f32[16,32,128]{2,1,0:T(8,128)S(1)}, f32[16,32,128]{2,1,0:T(8,128)S(1)}, u32[]{:S(2)}, u32[]{:S(2)}) collective-permute-start(f32[16,32,128]{2,1,0:T(8,128)S(1)} %get-tuple-element.119), channel_id=1, source_target_pairs={{0,1},{1,0},{2,3},{3,2},{4,5},{5,4},{6,7},{7,6},{8,9},{9,8},{10,11... | collective-permute-start | bytes 786440 | tf_op jit(solution)/shard_map/ppermute | solution.py:541
  69.1 1.6 %collective-permute-start.24 = (f32[16,32,128]{2,1,0:T(8,128)S(1)}, f32[16,32,128]{2,1,0:T(8,128)S(1)}, u32[]{:S(2)}, u32[]{:S(2)}) collective-permute-start(f32[16,32,128]{2,1,0:T(8,128)S(1)} %add.81), channel_id=1, source_target_pairs={{0,3},{1,2},{2,1},{3,0},{4,7},{5,6},{6,5},{7,4},{8,11},{9,10},{10,... | collective-permute-start | bytes 786440 | tf_op jit(solution)/shard_map/ppermute | solution.py:541
  70.7 3.9 %collective-permute-done.20.refs_2_ = f32[16,32,128]{2,1,0:T(8,128)S(1)} collective-permute-done((f32[16,32,128]{2,1,0:T(8,128)S(1)}, f32[16,32,128]{2,1,0:T(8,128)S(1)}, u32[]{:S(2)}, u32[]{:S(2)}) %collective-permute-start.20) | collective-permute-done | bytes 262176 | tf_op jit(solution)/shard_map/ppermute | solution.py:541
  74.5 8.9 %all-gather = f32[64,128]{1,0:T(8,128)S(1)} all-gather(f32[8,128]{1,0:T(8,128)S(1)} %get-tuple-element.115), channel_id=2, replica_groups=mesh['genome'=8,'offset'=4] {'genome'}, dimensions={0}, use_global_device_ids=true | all-gather | bytes 36864 | tf_op jit(solution)/shard_map/all_gather | solution.py:652
  83.4 1.2 %collective-permute-done.21.refs_1_ = f32[16,32,128]{2,1,0:T(8,128)S(1)} collective-permute-done((f32[16,32,128]{2,1,0:T(8,128)S(1)}, f32[16,32,128]{2,1,0:T(8,128)S(1)}, u32[]{:S(2)}, u32[]{:S(2)}) %collective-permute-start.21) | collective-permute-done | bytes 262176 | tf_op jit(solution)/shard_map/ppermute | solution.py:541
  84.7 1.3 %update.2 = f32[32,2048]{1,0:T(8,128)} custom-call(s32[4]{0:T(128)S(1)} %pad_add_fusion.scal, f32[8,128]{1,0:T(8,128)S(1)} %bitcast_reduce_fusion.sums, f32[16,32,128]{2,1,0:T(8,128)S(1)} %get-tuple-element.116.times, f32[16,32,128]{2,1,0:T(8,128)S(1)} %get-tuple-element.117.plus, f32[16,32,128]{2,1,0:T(8,128)S(1)} %get-tuple-element.118.refs_0_, ...), custom_call_target="tpu_custom_call" | custom-call | tf_op jit(solution)/shard_map/update/pallas_call | solution.py:47
  86.0 0.6 multiply_bitcast_fusion
  86.6 4.7 %collective-permute-done.24.refs_2_ = f32[16,32,128]{2,1,0:T(8,128)S(1)} collective-permute-done((f32[16,32,128]{2,1,0:T(8,128)S(1)}, f32[16,32,128]{2,1,0:T(8,128)S(1)}, u32[]{:S(2)}, u32[]{:S(2)}) %collective-permute-start.24) | collective-permute-done | bytes 262176 | tf_op jit(solution)/shard_map/ppermute | solution.py:541
  91.3 1.3 %update.3 = f32[32,2048]{1,0:T(8,128)} custom-call(s32[4]{0:T(128)S(1)} %pad_add_fusion.scal, f32[8,128]{1,0:T(8,128)S(1)} %bitcast_reduce_fusion.sums, f32[16,32,128]{2,1,0:T(8,128)S(1)} %get-tuple-element.120.times, f32[16,32,128]{2,1,0:T(8,128)S(1)} %get-tuple-element.121.plus, f32[16,32,128]{2,1,0:T(8,128)S(1)} %get-tuple-element.126.refs_0_, ...), custom_call_target="tpu_custom_call" | custom-call | tf_op jit(solution)/shard_map/update/pallas_call | solution.py:47
  (56 shorter events, 1.7 us)
Async XLA Ops:
  2.4 8.8 %collective-permute-start.1 = (f32[8,128]{1,0:T(8,128)S(1)}, f32[8,128]{1,0:T(8,128)S(1)}, u32[]{:S(2)}, u32[]{:S(2)}) collective-permute-start(f32[8,128]{1,0:T(8,128)S(1)} %slice_bitcast_fusion.1), channel_id=1, source_target_pairs={{0,4},{4,0},{8,12},{12,8},{16,20},{20,16},{24,28},{28,24},{1,5},{5... | collective-permute-start | bytes 12296 | tf_op jit(solution)/shard_map/ppermute | solution.py:546
  2.9 8.4 %collective-permute-start.2 = (f32[8,128]{1,0:T(8,128)S(1)}, f32[8,128]{1,0:T(8,128)S(1)}, u32[]{:S(2)}, u32[]{:S(2)}) collective-permute-start(f32[8,128]{1,0:T(8,128)S(1)} %slice_bitcast_fusion.1), channel_id=1, source_target_pairs={{0,28},{4,8},{8,4},{12,16},{16,12},{20,24},{24,20},{28,0},{1,29},{... | collective-permute-start | bytes 12296 | tf_op jit(solution)/shard_map/ppermute | solution.py:547
  11.3 1.5 %copy-start = (f32[32,8192]{1,0:T(8,128)S(1)}, f32[32,8192]{1,0:T(8,128)}, u32[]{:S(2)}) copy-start(f32[32,8192]{1,0:T(8,128)} %other.1) | copy-start | bytes 3145732
  11.3 1.5 %copy-start.1 = (f32[32,8192]{1,0:T(8,128)S(1)}, f32[32,8192]{1,0:T(8,128)}, u32[]{:S(2)}) copy-start(f32[32,8192]{1,0:T(8,128)} %old_ref.3) | copy-start | bytes 3145732
  12.7 4.0 %collective-permute-start.3 = (f32[16,128]{1,0:T(8,128)S(1)}, f32[16,128]{1,0:T(8,128)S(1)}, u32[]{:S(2)}, u32[]{:S(2)}) collective-permute-start(f32[16,128]{1,0:T(8,128)S(1)} %get-tuple-element.96), channel_id=1, source_target_pairs={{0,28},{4,8},{8,4},{12,16},{16,12},{20,24},{24,20},{28,0},{1,29},{... | collective-permute-start | bytes 24584 | tf_op jit(solution)/shard_map/ppermute | solution.py:547
  12.8 4.0 %collective-permute-start.4 = (f32[16,128]{1,0:T(8,128)S(1)}, f32[16,128]{1,0:T(8,128)S(1)}, u32[]{:S(2)}, u32[]{:S(2)}) collective-permute-start(f32[16,128]{1,0:T(8,128)S(1)} %get-tuple-element.96), channel_id=1, source_target_pairs={{0,4},{4,0},{8,12},{12,8},{16,20},{20,16},{24,28},{28,24},{1,5},{5... | collective-permute-start | bytes 24584 | tf_op jit(solution)/shard_map/ppermute | solution.py:546
  16.8 6.2 %collective-permute-start.5 = (f32[72,128]{1,0:T(8,128)S(1)}, f32[72,128]{1,0:T(8,128)S(1)}, u32[]{:S(2)}, u32[]{:S(2)}) collective-permute-start(f32[72,128]{1,0:T(8,128)S(1)} %pad_maximum_fusion.1.after.refs_0_), channel_id=1, source_target_pairs={{0,3},{1,2},{2,1},{3,0},{4,7},{5,6},{6,5},{7,4},{8,11},{9,10},{10,... | collective-permute-start | bytes 110600 | tf_op jit(solution)/shard_map/ppermute | solution.py:541
  20.4 4.9 %collective-permute-start.6 = (f32[72,128]{1,0:T(8,128)S(1)}, f32[72,128]{1,0:T(8,128)S(1)}, u32[]{:S(2)}, u32[]{:S(2)}) collective-permute-start(f32[72,128]{1,0:T(8,128)S(1)} %pad_maximum_fusion.1.after.refs_0_), channel_id=1, source_target_pairs={{0,2},{1,3},{2,0},{3,1},{4,6},{5,7},{6,4},{7,5},{8,10},{9,11},{10,... | collective-permute-start | bytes 110600 | tf_op jit(solution)/shard_map/ppermute | solution.py:541
  20.4 4.9 %collective-permute-start.7 = (f32[72,128]{1,0:T(8,128)S(1)}, f32[72,128]{1,0:T(8,128)S(1)}, u32[]{:S(2)}, u32[]{:S(2)}) collective-permute-start(f32[72,128]{1,0:T(8,128)S(1)} %pad_maximum_fusion.1.after.refs_0_), channel_id=1, source_target_pairs={{0,1},{1,0},{2,3},{3,2},{4,5},{5,4},{6,7},{7,6},{8,9},{9,8},{10,11... | collective-permute-start | bytes 110600 | tf_op jit(solution)/shard_map/ppermute | solution.py:541
  26.7 4.0 %collective-permute-start.8 = (f32[16,128]{1,0:T(8,128)S(1)}, f32[16,128]{1,0:T(8,128)S(1)}, u32[]{:S(2)}, u32[]{:S(2)}) collective-permute-start(f32[16,128]{1,0:T(8,128)S(1)} %get-tuple-element.102), channel_id=1, source_target_pairs={{0,28},{4,8},{8,4},{12,16},{16,12},{20,24},{24,20},{28,0},{1,29},{... | collective-permute-start | bytes 24584 | tf_op jit(solution)/shard_map/ppermute | solution.py:547
  26.7 4.0 %collective-permute-start.9 = (f32[16,128]{1,0:T(8,128)S(1)}, f32[16,128]{1,0:T(8,128)S(1)}, u32[]{:S(2)}, u32[]{:S(2)}) collective-permute-start(f32[16,128]{1,0:T(8,128)S(1)} %get-tuple-element.102), channel_id=1, source_target_pairs={{0,4},{4,0},{8,12},{12,8},{16,20},{20,16},{24,28},{28,24},{1,5},{5... | collective-permute-start | bytes 24584 | tf_op jit(solution)/shard_map/ppermute | solution.py:546
  30.7 5.9 %collective-permute-start.10 = (f32[72,128]{1,0:T(8,128)S(1)}, f32[72,128]{1,0:T(8,128)S(1)}, u32[]{:S(2)}, u32[]{:S(2)}) collective-permute-start(f32[72,128]{1,0:T(8,128)S(1)} %pad_maximum_fusion.2.refs_0_), channel_id=1, source_target_pairs={{0,3},{1,2},{2,1},{3,0},{4,7},{5,6},{6,5},{7,4},{8,11},{9,10},{10,... | collective-permute-start | bytes 110600 | tf_op jit(solution)/shard_map/ppermute | solution.py:541
  32.3 4.9 %collective-permute-start.11 = (f32[72,128]{1,0:T(8,128)S(1)}, f32[72,128]{1,0:T(8,128)S(1)}, u32[]{:S(2)}, u32[]{:S(2)}) collective-permute-start(f32[72,128]{1,0:T(8,128)S(1)} %pad_maximum_fusion.2.refs_0_), channel_id=1, source_target_pairs={{0,2},{1,3},{2,0},{3,1},{4,6},{5,7},{6,4},{7,5},{8,10},{9,11},{10,... | collective-permute-start | bytes 110600 | tf_op jit(solution)/shard_map/ppermute | solution.py:541
  32.9 4.6 %collective-permute-start.12 = (f32[72,128]{1,0:T(8,128)S(1)}, f32[72,128]{1,0:T(8,128)S(1)}, u32[]{:S(2)}, u32[]{:S(2)}) collective-permute-start(f32[72,128]{1,0:T(8,128)S(1)} %pad_maximum_fusion.2.refs_0_), channel_id=1, source_target_pairs={{0,1},{1,0},{2,3},{3,2},{4,5},{5,4},{6,7},{7,6},{8,9},{9,8},{10,11... | collective-permute-start | bytes 110600 | tf_op jit(solution)/shard_map/ppermute | solution.py:541
  35.2 12.6 %collective-permute-start = (f32[32,1024]{1,0:T(8,128)S(1)}, f32[32,1024]{1,0:T(8,128)S(1)}, u32[]{:S(2)}, u32[]{:S(2)}) collective-permute-start(f32[32,1024]{1,0:T(8,128)S(1)} %slice.207), channel_id=1, source_target_pairs={{0,28},{4,0},{8,4},{12,8},{16,12},{20,16},{24,20},{28,24},{1,29},{... | collective-permute-start | bytes 393224 | tf_op jit(solution)/shard_map/ppermute | solution.py:594
  38.9 4.4 %collective-permute-start.13 = (f32[16,128]{1,0:T(8,128)S(1)}, f32[16,128]{1,0:T(8,128)S(1)}, u32[]{:S(2)}, u32[]{:S(2)}) collective-permute-start(f32[16,128]{1,0:T(8,128)S(1)} %get-tuple-element.105), channel_id=1, source_target_pairs={{0,28},{4,8},{8,4},{12,16},{16,12},{20,24},{24,20},{28,0},{1,29},{... | collective-permute-start | bytes 24584 | tf_op jit(solution)/shard_map/ppermute | solution.py:547
  39.7 3.6 %collective-permute-start.14 = (f32[16,128]{1,0:T(8,128)S(1)}, f32[16,128]{1,0:T(8,128)S(1)}, u32[]{:S(2)}, u32[]{:S(2)}) collective-permute-start(f32[16,128]{1,0:T(8,128)S(1)} %get-tuple-element.105), channel_id=1, source_target_pairs={{0,4},{4,0},{8,12},{12,8},{16,20},{20,16},{24,28},{28,24},{1,5},{5... | collective-permute-start | bytes 24584 | tf_op jit(solution)/shard_map/ppermute | solution.py:546
  43.3 6.1 %collective-permute-start.15 = (f32[72,128]{1,0:T(8,128)S(1)}, f32[72,128]{1,0:T(8,128)S(1)}, u32[]{:S(2)}, u32[]{:S(2)}) collective-permute-start(f32[72,128]{1,0:T(8,128)S(1)} %pad_maximum_fusion.3.after.refs_0_), channel_id=1, source_target_pairs={{0,3},{1,2},{2,1},{3,0},{4,7},{5,6},{6,5},{7,4},{8,11},{9,10},{10,... | collective-permute-start | bytes 110600 | tf_op jit(solution)/shard_map/ppermute | solution.py:541
  45.7 4.9 %collective-permute-start.16 = (f32[72,128]{1,0:T(8,128)S(1)}, f32[72,128]{1,0:T(8,128)S(1)}, u32[]{:S(2)}, u32[]{:S(2)}) collective-permute-start(f32[72,128]{1,0:T(8,128)S(1)} %pad_maximum_fusion.3.after.refs_0_), channel_id=1, source_target_pairs={{0,2},{1,3},{2,0},{3,1},{4,6},{5,7},{6,4},{7,5},{8,10},{9,11},{10,... | collective-permute-start | bytes 110600 | tf_op jit(solution)/shard_map/ppermute | solution.py:541
  46.2 4.5 %collective-permute-start.17 = (f32[72,128]{1,0:T(8,128)S(1)}, f32[72,128]{1,0:T(8,128)S(1)}, u32[]{:S(2)}, u32[]{:S(2)}) collective-permute-start(f32[72,128]{1,0:T(8,128)S(1)} %pad_maximum_fusion.3.after.refs_0_), channel_id=1, source_target_pairs={{0,1},{1,0},{2,3},{3,2},{4,5},{5,4},{6,7},{7,6},{8,9},{9,8},{10,11... | collective-permute-start | bytes 110600 | tf_op jit(solution)/shard_map/ppermute | solution.py:541
  52.6 5.5 %collective-permute-start.18 = (f32[9,32,128]{2,1,0:T(8,128)S(1)}, f32[9,32,128]{2,1,0:T(8,128)S(1)}, u32[]{:S(2)}, u32[]{:S(2)}) collective-permute-start(f32[9,32,128]{2,1,0:T(8,128)S(1)} %get-tuple-element.112), channel_id=1, source_target_pairs={{0,4},{4,8},{8,12},{12,16},{16,20},{20,24},{24,28},{28,0},{1,5},{5... | collective-permute-start | bytes 442376 | tf_op jit(solution)/shard_map/ppermute | solution.py:632
  52.6 10.2 %collective-permute-start.19 = (f32[16,32,128]{2,1,0:T(8,128)S(1)}, f32[16,32,128]{2,1,0:T(8,128)S(1)}, u32[]{:S(2)}, u32[]{:S(2)}) collective-permute-start(f32[16,32,128]{2,1,0:T(8,128)S(1)} %get-tuple-element.114), channel_id=1, source_target_pairs={{0,1},{1,0},{2,3},{3,2},{4,5},{5,4},{6,7},{7,6},{8,9},{9,8},{10,11... | collective-permute-start | bytes 786440 | tf_op jit(solution)/shard_map/ppermute | solution.py:541
  58.1 10.9 %collective-permute-start.23 = (f32[16,32,128]{2,1,0:T(8,128)S(1)}, f32[16,32,128]{2,1,0:T(8,128)S(1)}, u32[]{:S(2)}, u32[]{:S(2)}) collective-permute-start(f32[16,32,128]{2,1,0:T(8,128)S(1)} %get-tuple-element.128.after), channel_id=1, source_target_pairs={{0,1},{1,0},{2,3},{3,2},{4,5},{5,4},{6,7},{7,6},{8,9},{9,8},{10,11... | collective-permute-start | bytes 786440 | tf_op jit(solution)/shard_map/ppermute | solution.py:541
  62.9 11.7 %collective-permute-start.20 = (f32[16,32,128]{2,1,0:T(8,128)S(1)}, f32[16,32,128]{2,1,0:T(8,128)S(1)}, u32[]{:S(2)}, u32[]{:S(2)}) collective-permute-start(f32[16,32,128]{2,1,0:T(8,128)S(1)} %add.77), channel_id=1, source_target_pairs={{0,3},{1,2},{2,1},{3,0},{4,7},{5,6},{6,5},{7,4},{8,11},{9,10},{10,... | collective-permute-start | bytes 786440 | tf_op jit(solution)/shard_map/ppermute | solution.py:541
  66.0 20.7 %collective-permute-start.22 = (f32[16,32,128]{2,1,0:T(8,128)S(1)}, f32[16,32,128]{2,1,0:T(8,128)S(1)}, u32[]{:S(2)}, u32[]{:S(2)}) collective-permute-start(f32[16,32,128]{2,1,0:T(8,128)S(1)} %get-tuple-element.127), channel_id=1, source_target_pairs={{0,1},{1,0},{2,3},{3,2},{4,5},{5,4},{6,7},{7,6},{8,9},{9,8},{10,11... | collective-permute-start | bytes 786440 | tf_op jit(solution)/shard_map/ppermute | solution.py:541
  67.0 17.7 %collective-permute-start.21 = (f32[16,32,128]{2,1,0:T(8,128)S(1)}, f32[16,32,128]{2,1,0:T(8,128)S(1)}, u32[]{:S(2)}, u32[]{:S(2)}) collective-permute-start(f32[16,32,128]{2,1,0:T(8,128)S(1)} %get-tuple-element.119), channel_id=1, source_target_pairs={{0,1},{1,0},{2,3},{3,2},{4,5},{5,4},{6,7},{7,6},{8,9},{9,8},{10,11... | collective-permute-start | bytes 786440 | tf_op jit(solution)/shard_map/ppermute | solution.py:541
  69.1 22.2 %collective-permute-start.24 = (f32[16,32,128]{2,1,0:T(8,128)S(1)}, f32[16,32,128]{2,1,0:T(8,128)S(1)}, u32[]{:S(2)}, u32[]{:S(2)}) collective-permute-start(f32[16,32,128]{2,1,0:T(8,128)S(1)} %add.81), channel_id=1, source_target_pairs={{0,3},{1,2},{2,1},{3,0},{4,7},{5,6},{6,5},{7,4},{8,11},{9,10},{10,... | collective-permute-start | bytes 786440 | tf_op jit(solution)/shard_map/ppermute | solution.py:541
